TPU v7x, 32 devices: a whole 2x2x4 slice. The times are simulated.
32 devices in a mesh: row: 4 (over x, core), col: 8 (over z, y).
Axes of the slice: x: 2, y: 2, z: 4, core: 2. Of those that a mesh axis runs over, the one named last changes fastest.
Arguments:
- left_tiles: bfloat16 [4, 8, 6, 128, 128], P('row', 'col'), may hold values from -6 to 6
- left_index: int32 [4, 8, 6], replicated, may hold values from 0 to 16, as said below
- right_tiles: bfloat16 [4, 8, 2, 3, 128, 128], P('row', 'col'), may hold values from -0.125 to 0.125
- right_index: int32 [4, 8, 2, 3], replicated, may hold values from 0 to 8, as said below
Outputs:
- product: bfloat16 [1024, 1024], P('row', 'col')
Inputs may be any that keep to these rules, and one draw needn't show every extreme that they name: `left_index`: in each block r, c the used slots come first and name distinct positions i * 8 + k; unused slots hold 16. Every block uses at least a third of its 6 slots, some block uses all of them and some block leaves slots unused. `right_index`: in each half block r, c, h the used slots come first and name distinct positions k + j; unused slots hold 8. Every half block uses at least a third of its 3 slots, some uses all of them and some leaves slots unused.
All inputs are finite; a program needn't handle non-finite values.
Results may differ from a plain program's by a relative error of at most 0.001.
Values may be sent and summed in bfloat16 or wider, within the bound.
No kernel may reach another device: no remote copies, remote signals or barrier semaphores. Data moves between devices by JAX's collectives and lax.ppermute only.
A program may use at most 64 MiB of HBM per device.

v0:
```python
import jax
import jax.numpy as jnp
from jax import lax
from jax.sharding import PartitionSpec as P

KT = 8
RT = 2
CT = 1


def passed_along(block, axis, distance):
    devices = range(lax.axis_size(axis))
    route = [((i - distance) % len(devices), i) for i in devices]
    return lax.ppermute(block, axis, route)


def densify(tiles, slots, positions):
    onehot = (slots[:, None] == jnp.arange(positions, dtype=jnp.int32)[None, :]).astype(
        jnp.bfloat16
    )
    return jnp.einsum("sp,sab->pab", onehot, tiles, preferred_element_type=jnp.float32).astype(
        jnp.bfloat16
    )


def multiply(left_now, front_half, left_slots, right_slots):
    tile = left_now.shape[-1]
    right_dense = (
        densify(front_half, right_slots, KT * CT).reshape(KT, CT, tile, tile).transpose(0, 2, 1, 3)
    )
    left_dense = (
        densify(left_now, left_slots, RT * KT).reshape(RT, KT, tile, tile).transpose(0, 2, 1, 3)
    )
    left_dense = left_dense.reshape(RT * tile, KT * tile)
    return jnp.dot(
        left_dense, right_dense.reshape(KT * tile, CT * tile), preferred_element_type=jnp.float32
    )


def lookup(left_index, right_index, row_pos, col_pos, piece):
    zero_pos = jnp.int32(0)
    left_slots = lax.dynamic_slice(
        left_index, (row_pos, piece, zero_pos), (1, 1, left_index.shape[2])
    )[0, 0]
    right_slots = lax.dynamic_slice(
        right_index, (piece // 2, col_pos, piece % 2, zero_pos), (1, 1, 1, right_index.shape[3])
    )[0, 0, 0]
    return (left_slots, right_slots)


def left_forward(left_now):
    return passed_along(left_now, "col", -1)


def right_forward(right_pair):
    arriving = passed_along(right_pair[0], "row", -1)
    return jnp.stack([right_pair[1], arriving])


def shards(left_tiles, left_index, right_tiles, right_index):
    row_count = lax.axis_size("row")
    col_count = lax.axis_size("col")
    row_pos = lax.axis_index("row")
    col_pos = lax.axis_index("col")
    tile = left_tiles.shape[-1]
    start = jnp.zeros((RT * tile, CT * tile), jnp.float32)
    left_now = left_tiles[0, 0]
    right_pair = right_tiles[0, 0]
    for level in range(1, (col_count - 1).bit_length()):
        moved = passed_along(left_now, "col", -(1 << level))
        left_now = jnp.where(row_pos >> level - 1 & 1 == 1, moved, left_now)
    block_shift = col_pos // 2
    for level in range((row_count - 1).bit_length()):
        moved = passed_along(right_pair, "row", -(1 << level))
        right_pair = jnp.where(block_shift >> level & 1 == 1, moved, right_pair)
    stepped = right_forward(right_pair)
    right_pair = jnp.where(col_pos % 2 == 1, stepped, right_pair)
    first_piece = col_pos + 2 * row_pos

    def product_at(left_cur, pair_cur, offset):
        piece = (first_piece + offset) % col_count
        left_slots, right_slots = lookup(left_index, right_index, row_pos, col_pos, piece)
        return multiply(left_cur, pair_cur[0], left_slots, right_slots)

    def advance(offset, carry):
        total, left_cur, pair_cur = carry
        total = total + product_at(left_cur, pair_cur, offset)
        return (total, left_forward(left_cur), right_forward(pair_cur))

    total, left_now, right_pair = lax.fori_loop(
        0, col_count - 1, advance, (start, left_now, right_pair)
    )
    total = total + product_at(left_now, right_pair, col_count - 1)
    return total.astype(jnp.bfloat16)


def solution(mesh):
    return jax.shard_map(
        shards,
        mesh=mesh,
        in_specs=(
            P("row", "col", None, None, None),
            P(),
            P("row", "col", None, None, None, None),
            P(),
        ),
        out_specs=P("row", "col"),
        check_vma=False,
    )
```

profile of v0, /device:TPU:0, one launch (start us, length us, event | category | flops | bytes accessed | tf_op | source)
XLA Modules:
  0.0 108.1 jit_solution(7077304384608211680)
XLA Ops:
  0.0 1.1 %copy.33 = bf16[1,1,2,3,128,128]{5,3,4,2,1,0:T(4,128)(2,1)S(1)} copy(bf16[1,1,2,3,128,128]{5,4,3,2,1,0:T(8,128)(2,1)} %param.8) | data formatting | bytes 393216 | tf_op args[2]
  1.1 2.4 %collective-permute-start.4 = (bf16[2,3,128,128]{3,1,2,0:T(4,128)(2,1)S(1)}, bf16[2,3,128,128]{3,1,2,0:T(4,128)(2,1)S(1)}, u32[]{:S(2)}, u32[]{:S(2)}) collective-permute-start(bf16[2,3,128,128]{3,1,2,0:T(4,128)(2,1)S(1)} %bitcast.87), channel_id=1, source_target_pairs={{8,0},{16,8},{24,16},{0,24},{9,1},{17,9},{25,17},{1,25},{10,2},{18... | collective-permute-start | bytes 589832 | tf_op jit(solution)/shard_map/ppermute | solution.py:14
  3.7 3.7 %collective-permute-start.2 = (bf16[6,128,128]{2,0,1:T(8,128)(2,1)S(1)}, bf16[6,128,128]{2,0,1:T(8,128)(2,1)S(1)}, u32[]{:S(2)}, u32[]{:S(2)}) collective-permute-start(bf16[6,128,128]{2,0,1:T(8,128)(2,1)S(1)} %bitcast.86), channel_id=1, source_target_pairs={{2,0},{3,1},{4,2},{5,3},{6,4},{7,5},{0,6},{1,7},{10,8},{11,9},{12,... | collective-permute-start | bytes 589832 | tf_op jit(solution)/shard_map/ppermute | solution.py:14
  7.6 0.2 dynamic-slice_reduce_fusion.1
  7.8 0.3 dynamic-slice_reduce_fusion
  8.1 0.2 broadcast_select_fusion
  8.4 0.7 collective-permute-start.5
  9.0 3.7 %collective-permute-done.2 = bf16[6,128,128]{2,0,1:T(8,128)(2,1)S(1)} collective-permute-done((bf16[6,128,128]{2,0,1:T(8,128)(2,1)S(1)}, bf16[6,128,128]{2,0,1:T(8,128)(2,1)S(1)}, u32[]{:S(2)}, u32[]{:S(2)}) %collective-permute-start.2) | collective-permute-done | bytes 196640 | tf_op jit(solution)/shard_map/ppermute | solution.py:14
  12.8 1.5 %collective-permute-start.3 = (bf16[6,128,128]{2,0,1:T(8,128)(2,1)S(1)}, bf16[6,128,128]{2,0,1:T(8,128)(2,1)S(1)}, u32[]{:S(2)}, u32[]{:S(2)}) collective-permute-start(bf16[6,128,128]{2,0,1:T(8,128)(2,1)S(1)} %broadcast_select_fusion.2), channel_id=1, source_target_pairs={{4,0},{5,1},{6,2},{7,3},{0,4},{1,5},{2,6},{3,7},{12,8},{13,9},{14,... | collective-permute-start | bytes 589832 | tf_op jit(solution)/shard_map/ppermute | solution.py:14
  14.4 2.7 %collective-permute-done.5 = bf16[2,3,128,128]{3,1,2,0:T(4,128)(2,1)S(1)} collective-permute-done((bf16[2,3,128,128]{3,1,2,0:T(4,128)(2,1)S(1)}, bf16[2,3,128,128]{3,1,2,0:T(4,128)(2,1)S(1)}, u32[]{:S(2)}, u32[]{:S(2)}) %collective-permute-start.5) | collective-permute-done | bytes 196640 | tf_op jit(solution)/shard_map/ppermute | solution.py:14
  17.3 0.6 collective-permute-start.6
  17.9 8.3 %collective-permute-done.3 = bf16[6,128,128]{2,0,1:T(8,128)(2,1)S(1)} collective-permute-done((bf16[6,128,128]{2,0,1:T(8,128)(2,1)S(1)}, bf16[6,128,128]{2,0,1:T(8,128)(2,1)S(1)}, u32[]{:S(2)}, u32[]{:S(2)}) %collective-permute-start.3) | collective-permute-done | bytes 196640 | tf_op jit(solution)/shard_map/ppermute | solution.py:14
  26.3 0.2 maximum_select_fusion
  26.6 79.7 %while.21 = (s32[]{:T(128)}, f32[256,128]{1,0:T(8,128)S(1)}, bf16[6,128,128]{2,0,1:T(8,128)(2,1)S(1)}, bf16[2,3,128,128]{3,1,2,0:T(4,128)(2,1)S(1)}, s32[]{:T(12...) while((s32[]{:T(128)}, f32[256,128]{1,0:T(8,128)S(1)}, ...), condition=%wide.region_1.2_spmd.clone, body=%wide.region_0.1_spmd.clone.sunk | while | flops 71598240 | bytes 6096116 | solution.py:90
  26.7 0.9 collective-permute-start.1
  27.6 4.6 %collective-permute-start = (bf16[6,128,128]{2,0,1:T(8,128)(2,1)S(1)}, bf16[6,128,128]{2,0,1:T(8,128)(2,1)S(1)}, u32[]{:S(2)}, u32[]{:S(2)}) collective-permute-start(bf16[6,128,128]{2,0,1:T(8,128)(2,1)S(1)} %copy.47), channel_id=1, source_target_pairs={{1,0},{2,1},{3,2},{4,3},{5,4},{6,5},{7,6},{0,7},{9,8},{10,9},{11,1... | collective-permute-start | bytes 589832 | tf_op jit(solution)/shard_map/while/body/eval_jaxpr/ppermute | solution.py:14
  32.3 0.5 fusion.39
  32.8 0.3 convolution_convert_fusion.5
  33.2 0.3 convolution_add_fusion.2
  33.5 0.2 pad_maximum_fusion.2
  33.7 2.6 %collective-permute-done = bf16[6,128,128]{2,0,1:T(8,128)(2,1)S(1)} collective-permute-done((bf16[6,128,128]{2,0,1:T(8,128)(2,1)S(1)}, bf16[6,128,128]{2,0,1:T(8,128)(2,1)S(1)}, u32[]{:S(2)}, u32[]{:S(2)}) %collective-permute-start) | collective-permute-done | bytes 196640 | tf_op jit(solution)/shard_map/while/body/eval_jaxpr/ppermute | solution.py:14
  36.5 1.9 %collective-permute-start.1 = (bf16[3,128,128]{2,0,1:T(4,128)(2,1)S(1)}, bf16[3,128,128]{2,0,1:T(4,128)(2,1)S(1)}, u32[]{:S(2)}, u32[]{:S(2)}) collective-permute-start(bf16[3,128,128]{2,0,1:T(4,128)(2,1)S(1)} %get-tuple-element.413), channel_id=1, source_target_pairs={{8,0},{16,8},{24,16},{0,24},{9,1},{17,9},{25,17},{1,25},{10,2},{18... | collective-permute-start | bytes 294920 | tf_op jit(solution)/shard_map/while/body/eval_jaxpr/ppermute | solution.py:14
  38.4 5.2 %collective-permute-start = (bf16[6,128,128]{2,0,1:T(8,128)(2,1)S(1)}, bf16[6,128,128]{2,0,1:T(8,128)(2,1)S(1)}, u32[]{:S(2)}, u32[]{:S(2)}) collective-permute-start(bf16[6,128,128]{2,0,1:T(8,128)(2,1)S(1)} %copy.47), channel_id=1, source_target_pairs={{1,0},{2,1},{3,2},{4,3},{5,4},{6,5},{7,6},{0,7},{9,8},{10,9},{11,1... | collective-permute-start | bytes 589832 | tf_op jit(solution)/shard_map/while/body/eval_jaxpr/ppermute | solution.py:14
  43.6 0.5 fusion.39
  44.2 0.3 convolution_convert_fusion.5
  44.5 0.3 convolution_add_fusion.2
  44.9 0.2 pad_maximum_fusion.2
  45.1 2.9 %collective-permute-done = bf16[6,128,128]{2,0,1:T(8,128)(2,1)S(1)} collective-permute-done((bf16[6,128,128]{2,0,1:T(8,128)(2,1)S(1)}, bf16[6,128,128]{2,0,1:T(8,128)(2,1)S(1)}, u32[]{:S(2)}, u32[]{:S(2)}) %collective-permute-start) | collective-permute-done | bytes 196640 | tf_op jit(solution)/shard_map/while/body/eval_jaxpr/ppermute | solution.py:14
  48.1 1.9 %collective-permute-start.1 = (bf16[3,128,128]{2,0,1:T(4,128)(2,1)S(1)}, bf16[3,128,128]{2,0,1:T(4,128)(2,1)S(1)}, u32[]{:S(2)}, u32[]{:S(2)}) collective-permute-start(bf16[3,128,128]{2,0,1:T(4,128)(2,1)S(1)} %get-tuple-element.413), channel_id=1, source_target_pairs={{8,0},{16,8},{24,16},{0,24},{9,1},{17,9},{25,17},{1,25},{10,2},{18... | collective-permute-start | bytes 294920 | tf_op jit(solution)/shard_map/while/body/eval_jaxpr/ppermute | solution.py:14
  50.0 5.2 %collective-permute-start = (bf16[6,128,128]{2,0,1:T(8,128)(2,1)S(1)}, bf16[6,128,128]{2,0,1:T(8,128)(2,1)S(1)}, u32[]{:S(2)}, u32[]{:S(2)}) collective-permute-start(bf16[6,128,128]{2,0,1:T(8,128)(2,1)S(1)} %copy.47), channel_id=1, source_target_pairs={{1,0},{2,1},{3,2},{4,3},{5,4},{6,5},{7,6},{0,7},{9,8},{10,9},{11,1... | collective-permute-start | bytes 589832 | tf_op jit(solution)/shard_map/while/body/eval_jaxpr/ppermute | solution.py:14
  55.2 0.5 fusion.39
  55.8 0.3 convolution_convert_fusion.5
  56.2 0.3 convolution_add_fusion.2
  56.5 0.2 pad_maximum_fusion.2
  56.7 2.9 %collective-permute-done = bf16[6,128,128]{2,0,1:T(8,128)(2,1)S(1)} collective-permute-done((bf16[6,128,128]{2,0,1:T(8,128)(2,1)S(1)}, bf16[6,128,128]{2,0,1:T(8,128)(2,1)S(1)}, u32[]{:S(2)}, u32[]{:S(2)}) %collective-permute-start) | collective-permute-done | bytes 196640 | tf_op jit(solution)/shard_map/while/body/eval_jaxpr/ppermute | solution.py:14
  59.7 1.9 %collective-permute-start.1 = (bf16[3,128,128]{2,0,1:T(4,128)(2,1)S(1)}, bf16[3,128,128]{2,0,1:T(4,128)(2,1)S(1)}, u32[]{:S(2)}, u32[]{:S(2)}) collective-permute-start(bf16[3,128,128]{2,0,1:T(4,128)(2,1)S(1)} %get-tuple-element.413), channel_id=1, source_target_pairs={{8,0},{16,8},{24,16},{0,24},{9,1},{17,9},{25,17},{1,25},{10,2},{18... | collective-permute-start | bytes 294920 | tf_op jit(solution)/shard_map/while/body/eval_jaxpr/ppermute | solution.py:14
  61.6 5.2 %collective-permute-start = (bf16[6,128,128]{2,0,1:T(8,128)(2,1)S(1)}, bf16[6,128,128]{2,0,1:T(8,128)(2,1)S(1)}, u32[]{:S(2)}, u32[]{:S(2)}) collective-permute-start(bf16[6,128,128]{2,0,1:T(8,128)(2,1)S(1)} %copy.47), channel_id=1, source_target_pairs={{1,0},{2,1},{3,2},{4,3},{5,4},{6,5},{7,6},{0,7},{9,8},{10,9},{11,1... | collective-permute-start | bytes 589832 | tf_op jit(solution)/shard_map/while/body/eval_jaxpr/ppermute | solution.py:14
  66.9 0.5 fusion.39
  67.4 0.3 convolution_convert_fusion.5
  67.8 0.3 convolution_add_fusion.2
  68.2 0.2 pad_maximum_fusion.2
  68.3 2.9 %collective-permute-done = bf16[6,128,128]{2,0,1:T(8,128)(2,1)S(1)} collective-permute-done((bf16[6,128,128]{2,0,1:T(8,128)(2,1)S(1)}, bf16[6,128,128]{2,0,1:T(8,128)(2,1)S(1)}, u32[]{:S(2)}, u32[]{:S(2)}) %collective-permute-start) | collective-permute-done | bytes 196640 | tf_op jit(solution)/shard_map/while/body/eval_jaxpr/ppermute | solution.py:14
  71.4 1.9 %collective-permute-start.1 = (bf16[3,128,128]{2,0,1:T(4,128)(2,1)S(1)}, bf16[3,128,128]{2,0,1:T(4,128)(2,1)S(1)}, u32[]{:S(2)}, u32[]{:S(2)}) collective-permute-start(bf16[3,128,128]{2,0,1:T(4,128)(2,1)S(1)} %get-tuple-element.413), channel_id=1, source_target_pairs={{8,0},{16,8},{24,16},{0,24},{9,1},{17,9},{25,17},{1,25},{10,2},{18... | collective-permute-start | bytes 294920 | tf_op jit(solution)/shard_map/while/body/eval_jaxpr/ppermute | solution.py:14
  73.3 5.2 %collective-permute-start = (bf16[6,128,128]{2,0,1:T(8,128)(2,1)S(1)}, bf16[6,128,128]{2,0,1:T(8,128)(2,1)S(1)}, u32[]{:S(2)}, u32[]{:S(2)}) collective-permute-start(bf16[6,128,128]{2,0,1:T(8,128)(2,1)S(1)} %copy.47), channel_id=1, source_target_pairs={{1,0},{2,1},{3,2},{4,3},{5,4},{6,5},{7,6},{0,7},{9,8},{10,9},{11,1... | collective-permute-start | bytes 589832 | tf_op jit(solution)/shard_map/while/body/eval_jaxpr/ppermute | solution.py:14
  78.5 0.5 fusion.39
  79.1 0.3 convolution_convert_fusion.5
  79.5 0.3 convolution_add_fusion.2
  80.0 2.9 %collective-permute-done = bf16[6,128,128]{2,0,1:T(8,128)(2,1)S(1)} collective-permute-done((bf16[6,128,128]{2,0,1:T(8,128)(2,1)S(1)}, bf16[6,128,128]{2,0,1:T(8,128)(2,1)S(1)}, u32[]{:S(2)}, u32[]{:S(2)}) %collective-permute-start) | collective-permute-done | bytes 196640 | tf_op jit(solution)/shard_map/while/body/eval_jaxpr/ppermute | solution.py:14
  83.0 1.9 %collective-permute-start.1 = (bf16[3,128,128]{2,0,1:T(4,128)(2,1)S(1)}, bf16[3,128,128]{2,0,1:T(4,128)(2,1)S(1)}, u32[]{:S(2)}, u32[]{:S(2)}) collective-permute-start(bf16[3,128,128]{2,0,1:T(4,128)(2,1)S(1)} %get-tuple-element.413), channel_id=1, source_target_pairs={{8,0},{16,8},{24,16},{0,24},{9,1},{17,9},{25,17},{1,25},{10,2},{18... | collective-permute-start | bytes 294920 | tf_op jit(solution)/shard_map/while/body/eval_jaxpr/ppermute | solution.py:14
  84.9 5.2 %collective-permute-start = (bf16[6,128,128]{2,0,1:T(8,128)(2,1)S(1)}, bf16[6,128,128]{2,0,1:T(8,128)(2,1)S(1)}, u32[]{:S(2)}, u32[]{:S(2)}) collective-permute-start(bf16[6,128,128]{2,0,1:T(8,128)(2,1)S(1)} %copy.47), channel_id=1, source_target_pairs={{1,0},{2,1},{3,2},{4,3},{5,4},{6,5},{7,6},{0,7},{9,8},{10,9},{11,1... | collective-permute-start | bytes 589832 | tf_op jit(solution)/shard_map/while/body/eval_jaxpr/ppermute | solution.py:14
  90.2 0.5 fusion.39
  90.7 0.3 convolution_convert_fusion.5
  91.1 0.3 convolution_add_fusion.2
  91.6 2.9 %collective-permute-done = bf16[6,128,128]{2,0,1:T(8,128)(2,1)S(1)} collective-permute-done((bf16[6,128,128]{2,0,1:T(8,128)(2,1)S(1)}, bf16[6,128,128]{2,0,1:T(8,128)(2,1)S(1)}, u32[]{:S(2)}, u32[]{:S(2)}) %collective-permute-start) | collective-permute-done | bytes 196640 | tf_op jit(solution)/shard_map/while/body/eval_jaxpr/ppermute | solution.py:14
  94.7 1.9 %collective-permute-start.1 = (bf16[3,128,128]{2,0,1:T(4,128)(2,1)S(1)}, bf16[3,128,128]{2,0,1:T(4,128)(2,1)S(1)}, u32[]{:S(2)}, u32[]{:S(2)}) collective-permute-start(bf16[3,128,128]{2,0,1:T(4,128)(2,1)S(1)} %get-tuple-element.413), channel_id=1, source_target_pairs={{8,0},{16,8},{24,16},{0,24},{9,1},{17,9},{25,17},{1,25},{10,2},{18... | collective-permute-start | bytes 294920 | tf_op jit(solution)/shard_map/while/body/eval_jaxpr/ppermute | solution.py:14
  96.6 5.2 %collective-permute-start = (bf16[6,128,128]{2,0,1:T(8,128)(2,1)S(1)}, bf16[6,128,128]{2,0,1:T(8,128)(2,1)S(1)}, u32[]{:S(2)}, u32[]{:S(2)}) collective-permute-start(bf16[6,128,128]{2,0,1:T(8,128)(2,1)S(1)} %copy.47), channel_id=1, source_target_pairs={{1,0},{2,1},{3,2},{4,3},{5,4},{6,5},{7,6},{0,7},{9,8},{10,9},{11,1... | collective-permute-start | bytes 589832 | tf_op jit(solution)/shard_map/while/body/eval_jaxpr/ppermute | solution.py:14
  101.8 0.5 fusion.39
  102.4 0.3 convolution_convert_fusion.5
  102.7 0.3 convolution_add_fusion.2
  103.3 2.9 %collective-permute-done = bf16[6,128,128]{2,0,1:T(8,128)(2,1)S(1)} collective-permute-done((bf16[6,128,128]{2,0,1:T(8,128)(2,1)S(1)}, bf16[6,128,128]{2,0,1:T(8,128)(2,1)S(1)}, u32[]{:S(2)}, u32[]{:S(2)}) %collective-permute-start) | collective-permute-done | bytes 196640 | tf_op jit(solution)/shard_map/while/body/eval_jaxpr/ppermute | solution.py:14
  106.2 0.5 fusion.9
  106.7 0.3 convolution_convert_fusion.3
  107.1 0.3 fusion.10
  107.4 0.7 add_convert_fusion
  (72 shorter events, 2.8 us)
Async XLA Ops:
  0.0 3.6 %copy-start.1 = (bf16[1,1,6,128,128]{4,3,2,1,0:T(8,128)(2,1)S(1)}, bf16[1,1,6,128,128]{4,3,2,1,0:T(8,128)(2,1)}, u32[]{:S(2)}) copy-start(bf16[1,1,6,128,128]{4,3,2,1,0:T(8,128)(2,1)} %param.6) | copy-start | bytes 589828
  1.1 7.0 %collective-permute-start.4 = (bf16[2,3,128,128]{3,1,2,0:T(4,128)(2,1)S(1)}, bf16[2,3,128,128]{3,1,2,0:T(4,128)(2,1)S(1)}, u32[]{:S(2)}, u32[]{:S(2)}) collective-permute-start(bf16[2,3,128,128]{3,1,2,0:T(4,128)(2,1)S(1)} %bitcast.87), channel_id=1, source_target_pairs={{8,0},{16,8},{24,16},{0,24},{9,1},{17,9},{25,17},{1,25},{10,2},{18... | collective-permute-start | bytes 589832 | tf_op jit(solution)/shard_map/ppermute | solution.py:14
  3.6 3.8 %copy-start.3 = (s32[4,8,2,3]{1,2,3,0:T(2,128)S(1)}, s32[4,8,2,3]{1,2,3,0:T(2,128)}, u32[]{:S(2)}) copy-start(s32[4,8,2,3]{1,2,3,0:T(2,128)} %param.9) | copy-start | bytes 2308
  3.6 3.9 %copy-start.2 = (s32[4,8,6]{1,0,2:T(4,128)S(1)}, s32[4,8,6]{1,0,2:T(4,128)}, u32[]{:S(2)}) copy-start(s32[4,8,6]{1,0,2:T(4,128)} %param.7) | copy-start | bytes 2308
  3.7 4.4 %copy-start = (bf16[1,1,2,3,128,128]{5,4,3,2,1,0:T(8,128)(2,1)S(1)}, bf16[1,1,2,3,128,128]{5,4,3,2,1,0:T(8,128)(2,1)}, u32[]{:S(2)}) copy-start(bf16[1,1,2,3,128,128]{5,4,3,2,1,0:T(8,128)(2,1)} %param.8) | copy-start | bytes 589828
  3.7 9.0 %collective-permute-start.2 = (bf16[6,128,128]{2,0,1:T(8,128)(2,1)S(1)}, bf16[6,128,128]{2,0,1:T(8,128)(2,1)S(1)}, u32[]{:S(2)}, u32[]{:S(2)}) collective-permute-start(bf16[6,128,128]{2,0,1:T(8,128)(2,1)S(1)} %bitcast.86), channel_id=1, source_target_pairs={{2,0},{3,1},{4,2},{5,3},{6,4},{7,5},{0,6},{1,7},{10,8},{11,9},{12,... | collective-permute-start | bytes 589832 | tf_op jit(solution)/shard_map/ppermute | solution.py:14
  8.4 8.7 %collective-permute-start.5 = (bf16[2,3,128,128]{3,1,2,0:T(4,128)(2,1)S(1)}, bf16[2,3,128,128]{3,1,2,0:T(4,128)(2,1)S(1)}, u32[]{:S(2)}, u32[]{:S(2)}) collective-permute-start(bf16[2,3,128,128]{3,1,2,0:T(4,128)(2,1)S(1)} %broadcast_select_fusion), channel_id=1, source_target_pairs={{16,0},{24,8},{0,16},{8,24},{17,1},{25,9},{1,17},{9,25},{18,2},{26... | collective-permute-start | bytes 589832 | tf_op jit(solution)/shard_map/ppermute | solution.py:14
  12.8 13.5 %collective-permute-start.3 = (bf16[6,128,128]{2,0,1:T(8,128)(2,1)S(1)}, bf16[6,128,128]{2,0,1:T(8,128)(2,1)S(1)}, u32[]{:S(2)}, u32[]{:S(2)}) collective-permute-start(bf16[6,128,128]{2,0,1:T(8,128)(2,1)S(1)} %broadcast_select_fusion.2), channel_id=1, source_target_pairs={{4,0},{5,1},{6,2},{7,3},{0,4},{1,5},{2,6},{3,7},{12,8},{13,9},{14,... | collective-permute-start | bytes 589832 | tf_op jit(solution)/shard_map/ppermute | solution.py:14
  17.3 9.0 %collective-permute-start.6 = (bf16[3,128,128]{2,0,1:T(4,128)(2,1)S(1)}, bf16[3,128,128]{2,0,1:T(4,128)(2,1)S(1)}, u32[]{:S(2)}, u32[]{:S(2)}) collective-permute-start(bf16[3,128,128]{2,0,1:T(4,128)(2,1)S(1)} %get-tuple-element.355), channel_id=1, source_target_pairs={{8,0},{16,8},{24,16},{0,24},{9,1},{17,9},{25,17},{1,25},{10,2},{18... | collective-permute-start | bytes 294920 | tf_op jit(solution)/shard_map/ppermute | solution.py:14
  26.7 6.9 %collective-permute-start.1 = (bf16[3,128,128]{2,0,1:T(4,128)(2,1)S(1)}, bf16[3,128,128]{2,0,1:T(4,128)(2,1)S(1)}, u32[]{:S(2)}, u32[]{:S(2)}) collective-permute-start(bf16[3,128,128]{2,0,1:T(4,128)(2,1)S(1)} %get-tuple-element.413), channel_id=1, source_target_pairs={{8,0},{16,8},{24,16},{0,24},{9,1},{17,9},{25,17},{1,25},{10,2},{18... | collective-permute-start | bytes 294920 | tf_op jit(solution)/shard_map/while/body/eval_jaxpr/ppermute | solution.py:14
  27.6 8.7 %collective-permute-start = (bf16[6,128,128]{2,0,1:T(8,128)(2,1)S(1)}, bf16[6,128,128]{2,0,1:T(8,128)(2,1)S(1)}, u32[]{:S(2)}, u32[]{:S(2)}) collective-permute-start(bf16[6,128,128]{2,0,1:T(8,128)(2,1)S(1)} %copy.47), channel_id=1, source_target_pairs={{1,0},{2,1},{3,2},{4,3},{5,4},{6,5},{7,6},{0,7},{9,8},{10,9},{11,1... | collective-permute-start | bytes 589832 | tf_op jit(solution)/shard_map/while/body/eval_jaxpr/ppermute | solution.py:14
  36.5 8.4 %collective-permute-start.1 = (bf16[3,128,128]{2,0,1:T(4,128)(2,1)S(1)}, bf16[3,128,128]{2,0,1:T(4,128)(2,1)S(1)}, u32[]{:S(2)}, u32[]{:S(2)}) collective-permute-start(bf16[3,128,128]{2,0,1:T(4,128)(2,1)S(1)} %get-tuple-element.413), channel_id=1, source_target_pairs={{8,0},{16,8},{24,16},{0,24},{9,1},{17,9},{25,17},{1,25},{10,2},{18... | collective-permute-start | bytes 294920 | tf_op jit(solution)/shard_map/while/body/eval_jaxpr/ppermute | solution.py:14
  38.4 9.7 %collective-permute-start = (bf16[6,128,128]{2,0,1:T(8,128)(2,1)S(1)}, bf16[6,128,128]{2,0,1:T(8,128)(2,1)S(1)}, u32[]{:S(2)}, u32[]{:S(2)}) collective-permute-start(bf16[6,128,128]{2,0,1:T(8,128)(2,1)S(1)} %copy.47), channel_id=1, source_target_pairs={{1,0},{2,1},{3,2},{4,3},{5,4},{6,5},{7,6},{0,7},{9,8},{10,9},{11,1... | collective-permute-start | bytes 589832 | tf_op jit(solution)/shard_map/while/body/eval_jaxpr/ppermute | solution.py:14
  48.1 8.4 %collective-permute-start.1 = (bf16[3,128,128]{2,0,1:T(4,128)(2,1)S(1)}, bf16[3,128,128]{2,0,1:T(4,128)(2,1)S(1)}, u32[]{:S(2)}, u32[]{:S(2)}) collective-permute-start(bf16[3,128,128]{2,0,1:T(4,128)(2,1)S(1)} %get-tuple-element.413), channel_id=1, source_target_pairs={{8,0},{16,8},{24,16},{0,24},{9,1},{17,9},{25,17},{1,25},{10,2},{18... | collective-permute-start | bytes 294920 | tf_op jit(solution)/shard_map/while/body/eval_jaxpr/ppermute | solution.py:14
  50.0 9.7 %collective-permute-start = (bf16[6,128,128]{2,0,1:T(8,128)(2,1)S(1)}, bf16[6,128,128]{2,0,1:T(8,128)(2,1)S(1)}, u32[]{:S(2)}, u32[]{:S(2)}) collective-permute-start(bf16[6,128,128]{2,0,1:T(8,128)(2,1)S(1)} %copy.47), channel_id=1, source_target_pairs={{1,0},{2,1},{3,2},{4,3},{5,4},{6,5},{7,6},{0,7},{9,8},{10,9},{11,1... | collective-permute-start | bytes 589832 | tf_op jit(solution)/shard_map/while/body/eval_jaxpr/ppermute | solution.py:14
  59.7 8.4 %collective-permute-start.1 = (bf16[3,128,128]{2,0,1:T(4,128)(2,1)S(1)}, bf16[3,128,128]{2,0,1:T(4,128)(2,1)S(1)}, u32[]{:S(2)}, u32[]{:S(2)}) collective-permute-start(bf16[3,128,128]{2,0,1:T(4,128)(2,1)S(1)} %get-tuple-element.413), channel_id=1, source_target_pairs={{8,0},{16,8},{24,16},{0,24},{9,1},{17,9},{25,17},{1,25},{10,2},{18... | collective-permute-start | bytes 294920 | tf_op jit(solution)/shard_map/while/body/eval_jaxpr/ppermute | solution.py:14
  61.6 9.7 %collective-permute-start = (bf16[6,128,128]{2,0,1:T(8,128)(2,1)S(1)}, bf16[6,128,128]{2,0,1:T(8,128)(2,1)S(1)}, u32[]{:S(2)}, u32[]{:S(2)}) collective-permute-start(bf16[6,128,128]{2,0,1:T(8,128)(2,1)S(1)} %copy.47), channel_id=1, source_target_pairs={{1,0},{2,1},{3,2},{4,3},{5,4},{6,5},{7,6},{0,7},{9,8},{10,9},{11,1... | collective-permute-start | bytes 589832 | tf_op jit(solution)/shard_map/while/body/eval_jaxpr/ppermute | solution.py:14
  71.4 8.4 %collective-permute-start.1 = (bf16[3,128,128]{2,0,1:T(4,128)(2,1)S(1)}, bf16[3,128,128]{2,0,1:T(4,128)(2,1)S(1)}, u32[]{:S(2)}, u32[]{:S(2)}) collective-permute-start(bf16[3,128,128]{2,0,1:T(4,128)(2,1)S(1)} %get-tuple-element.413), channel_id=1, source_target_pairs={{8,0},{16,8},{24,16},{0,24},{9,1},{17,9},{25,17},{1,25},{10,2},{18... | collective-permute-start | bytes 294920 | tf_op jit(solution)/shard_map/while/body/eval_jaxpr/ppermute | solution.py:14
  73.3 9.7 %collective-permute-start = (bf16[6,128,128]{2,0,1:T(8,128)(2,1)S(1)}, bf16[6,128,128]{2,0,1:T(8,128)(2,1)S(1)}, u32[]{:S(2)}, u32[]{:S(2)}) collective-permute-start(bf16[6,128,128]{2,0,1:T(8,128)(2,1)S(1)} %copy.47), channel_id=1, source_target_pairs={{1,0},{2,1},{3,2},{4,3},{5,4},{6,5},{7,6},{0,7},{9,8},{10,9},{11,1... | collective-permute-start | bytes 589832 | tf_op jit(solution)/shard_map/while/body/eval_jaxpr/ppermute | solution.py:14
  83.0 8.4 %collective-permute-start.1 = (bf16[3,128,128]{2,0,1:T(4,128)(2,1)S(1)}, bf16[3,128,128]{2,0,1:T(4,128)(2,1)S(1)}, u32[]{:S(2)}, u32[]{:S(2)}) collective-permute-start(bf16[3,128,128]{2,0,1:T(4,128)(2,1)S(1)} %get-tuple-element.413), channel_id=1, source_target_pairs={{8,0},{16,8},{24,16},{0,24},{9,1},{17,9},{25,17},{1,25},{10,2},{18... | collective-permute-start | bytes 294920 | tf_op jit(solution)/shard_map/while/body/eval_jaxpr/ppermute | solution.py:14
  84.9 9.7 %collective-permute-start = (bf16[6,128,128]{2,0,1:T(8,128)(2,1)S(1)}, bf16[6,128,128]{2,0,1:T(8,128)(2,1)S(1)}, u32[]{:S(2)}, u32[]{:S(2)}) collective-permute-start(bf16[6,128,128]{2,0,1:T(8,128)(2,1)S(1)} %copy.47), channel_id=1, source_target_pairs={{1,0},{2,1},{3,2},{4,3},{5,4},{6,5},{7,6},{0,7},{9,8},{10,9},{11,1... | collective-permute-start | bytes 589832 | tf_op jit(solution)/shard_map/while/body/eval_jaxpr/ppermute | solution.py:14
  94.7 8.4 %collective-permute-start.1 = (bf16[3,128,128]{2,0,1:T(4,128)(2,1)S(1)}, bf16[3,128,128]{2,0,1:T(4,128)(2,1)S(1)}, u32[]{:S(2)}, u32[]{:S(2)}) collective-permute-start(bf16[3,128,128]{2,0,1:T(4,128)(2,1)S(1)} %get-tuple-element.413), channel_id=1, source_target_pairs={{8,0},{16,8},{24,16},{0,24},{9,1},{17,9},{25,17},{1,25},{10,2},{18... | collective-permute-start | bytes 294920 | tf_op jit(solution)/shard_map/while/body/eval_jaxpr/ppermute | solution.py:14
  96.6 9.7 %collective-permute-start = (bf16[6,128,128]{2,0,1:T(8,128)(2,1)S(1)}, bf16[6,128,128]{2,0,1:T(8,128)(2,1)S(1)}, u32[]{:S(2)}, u32[]{:S(2)}) collective-permute-start(bf16[6,128,128]{2,0,1:T(8,128)(2,1)S(1)} %copy.47), channel_id=1, source_target_pairs={{1,0},{2,1},{3,2},{4,3},{5,4},{6,5},{7,6},{0,7},{9,8},{10,9},{11,1... | collective-permute-start | bytes 589832 | tf_op jit(solution)/shard_map/while/body/eval_jaxpr/ppermute | solution.py:14
where the time goes:
time: 108 us
  starting transfers between devices  57 us (53%)
  waiting for transfers between devices  35.1 us (32%)
  matrix products  8.81 us (8%)
  local copies, waits for them, and re-layouts  3.61 us (3%)
  other arithmetic  2.69 us (2%)
    ppermute x19, starting transfers between devices, passed_along(): return lax.ppermute(block, axis, route)  57 us
    ppermute x19, waiting for transfers between devices, passed_along(): return lax.ppermute(block, axis, route)  35.1 us
    dot_general x16, matrix products, densify(): jnp.einsum('sp,sab->pab', onehot, tiles, preferred_element_type=jnp.float32)  6.31 us
    dot_general x8, matrix products, multiply(): jnp.dot(left_dense, right_dense.reshape(KT * tile, CT * tile), preferred_...  2.51 us
  transfers between devices with their start and end apart: 19, of which 10 were waited for; matrix products, arithmetic and copies ran while one was open for 10% of the time, Pallas kernels for 0%

commit v1 on v0

v1 whole, which is shorter than its diff:
```python
import jax
import jax.numpy as jnp
from jax import lax
from jax.experimental import pallas as pl
from jax.experimental.pallas import tpu as pltpu
from jax.sharding import PartitionSpec as P

KT = 8
RT = 2


def multiply(row, col, left_index, right_index, left, right):
    pieces, left_slots, tile, _ = left.shape
    right_slots = right.shape[1]

    def kernel(row_ref, col_ref, li_ref, ri_ref, left_ref, right_ref, out_ref, total):
        r = row_ref[0]
        c = col_ref[0]
        total[...] = jnp.zeros_like(total)

        @pl.loop(0, pieces)
        def _(p):
            for s in range(left_slots):
                place = li_ref[r, p, s]
                k = place % KT
                found = jnp.int32(right_slots)
                for t in range(right_slots):
                    found = jnp.where(ri_ref[p // 2, c, p % 2, t] == k, t, found)

                @pl.when(jnp.logical_and(place < RT * KT, found < right_slots))
                def _():
                    i = place // KT
                    total[i] += jnp.dot(
                        left_ref[p, s], right_ref[p, found], preferred_element_type=jnp.float32
                    )

        out_ref[...] = total[...].reshape(RT * tile, tile).astype(out_ref.dtype)

    smem = pl.BlockSpec(memory_space=pltpu.SMEM)
    vmem = pl.BlockSpec(memory_space=pltpu.VMEM)
    return pl.pallas_call(
        kernel,
        out_shape=jax.ShapeDtypeStruct((RT * tile, tile), jnp.bfloat16),
        in_specs=[smem, smem, smem, smem, vmem, vmem],
        out_specs=vmem,
        scratch_shapes=[pltpu.VMEM((RT, tile, tile), jnp.float32)],
        compiler_params=pltpu.CompilerParams(vmem_limit_bytes=32 * 1024 * 1024),
    )(row, col, left_index, right_index, left, right)


def shards(left_tiles, left_index, right_tiles, right_index):
    row = lax.axis_index("row").reshape(1)
    col = lax.axis_index("col").reshape(1)
    left = lax.all_gather(left_tiles[0], "col", axis=0, tiled=True)
    right = lax.all_gather(right_tiles[0, 0], "row", axis=0, tiled=True)
    return multiply(row, col, left_index, right_index, left, right)


def solution(mesh):
    return jax.shard_map(
        shards,
        mesh=mesh,
        in_specs=(
            P("row", "col", None, None, None),
            P(),
            P("row", "col", None, None, None, None),
            P(),
        ),
        out_specs=P("row", "col"),
        check_vma=False,
    )
```

time: 108 us -> 68.3 us (0.63)
  starting transfers between devices: 57 us -> 0.01 us
  between operations: 0.11 us -> 13.4 us
  blocking collectives: 0 us -> 10.2 us
  matrix products: 8.81 us -> 0 us
  Pallas kernels: 0 us -> 3.23 us
  waiting for transfers between devices: 35.1 us -> 38 us
  other arithmetic: 2.69 us -> 0 us
    ppermute x19 -> x0, starting transfers between devices: 57 us -> none  [passed_along(): return lax.ppermute(block, axis, route)]
    all_gather x0 -> x1, waiting for transfers between devices: none -> 37.3 us  [shards(): left = lax.all_gather(left_tiles[0], 'col', axis=0, tiled=True)]
    ppermute x19 -> x0, waiting for transfers between devices: 35.1 us -> none  [passed_along(): return lax.ppermute(block, axis, route)]
    all_gather x0 -> x1, blocking collectives: none -> 10.2 us  [shards(): right = lax.all_gather(right_tiles[0, 0], 'row', axis=0, tiled=True)]
    dot_general x24 -> x0, matrix products: 8.81 us -> none  [the longest x16 6.31 us: densify(): jnp.einsum('sp,sab->pab', onehot, tiles, preferred_element_type=jnp.float32)]
    pallas_call x0 -> x1, Pallas kernels: none -> 3.23 us  [multiply(): pl.pallas_call(kernel, out_shape=jax.ShapeDtypeStruct((RT * tile, tile),...]
    unnamed x12 -> x4, local copies, waits for them, and re-layouts: 1.52 us -> 3.03 us
    another operation x7 -> x0, other arithmetic: 1.29 us -> none  [right_forward(): return jnp.stack([right_pair[1], arriving])]
  transfers between devices with their start and end apart: 19 -> 1, of which waited for: 10 -> 1; matrix products, arithmetic and copies ran while one was open for 10% -> 2% of each run, Pallas kernels for 0% -> 0%
where the time goes in v1:
time: 68.3 us; the launch traced here: 67.9 us
  waiting for transfers between devices  38 us (56%)
  between operations  13.4 us (20%)
  blocking collectives  10.2 us (15%)
  Pallas kernels  3.23 us (5%)
  local copies, waits for them, and re-layouts  3.03 us (4%)
    all_gather x1, waiting for transfers between devices, shards(): left = lax.all_gather(left_tiles[0], 'col', axis=0, tiled=True)  37.3 us
    all_gather x1, blocking collectives, shards(): right = lax.all_gather(right_tiles[0, 0], 'row', axis=0, tiled=True)  10.2 us
    pallas_call x1, Pallas kernels, multiply(): pl.pallas_call(kernel, out_shape=jax.ShapeDtypeStruct((RT * tile, tile),...  3.23 us
    unnamed x4, local copies, waits for them, and re-layouts  3.03 us
  transfers between devices with their start and end apart: 1, of which 1 were waited for; matrix products, arithmetic and copies ran while one was open for 2% of the time, Pallas kernels for 0%

profile of v1, /device:TPU:0, one launch (start us, length us, event | category | flops | bytes accessed | tf_op | source)
XLA Modules:
  0.0 67.9 jit_solution(10193858151340819308)
XLA Ops:
  6.5 0.0 all-gather.4.cloned.1.call-start
  6.5 0.7 %all-gather.4.cloned.1.call-update = ((bf16[1,1,6,128,128]{4,3,2,1,0:T(8,128)(2,1)}), bf16[8,1,6,128,128]{4,3,2,1,0:T(8,128)(2,1)}) async-update(((), (), s32[]{:S(2)}) %all-gather.4.cloned.1.call-start, bf16[1,1,6,128,128]{4,3,2,1,0:T(8,128)(2,1)} %param.4) | async-update | bytes 1966104
  7.3 0.8 %copy.9.li_ref = s32[4,8,6]{2,1,0:T(8,128)S(1)} copy(s32[4,8,6]{1,0,2:T(4,128)} %param.5) | data formatting | bytes 1536 | tf_op args[1]
  8.1 0.8 %copy.10.ri_ref = s32[4,8,2,3]{3,2,1,0:T(2,128)S(1)} copy(s32[4,8,2,3]{1,2,3,0:T(2,128)} %param.7) | data formatting | bytes 1536 | tf_op args[3]
  8.9 10.2 %all-gather.1 = bf16[1,1,8,3,128,128]{5,4,3,1,0,2:T(8,128)(2,1)S(1)} all-gather(bf16[1,1,2,3,128,128]{5,4,3,1,0,2:T(8,128)(2,1)} %bitcast.7), channel_id=3, replica_groups=mesh['row'=4,'col'=8] {'row'}, dimensions={2}, use_global_device_ids=true | all-gather | bytes 983040 | tf_op jit(solution)/shard_map/all_gather | solution.py:55
  19.1 37.3 %all-gather.4.cloned.1.call-done = bf16[8,1,6,128,128]{4,3,2,1,0:T(8,128)(2,1)} async-done(((bf16[1,1,6,128,128]{4,3,2,1,0:T(8,128)(2,1)}), bf16[8,1,6,128,128]{4,3,2,1,0:T(8,128)(2,1)}) %all-gather.4.cloned.1.call-update) | async-done | bytes 1572880 | tf_op jit(solution)/shard_map/all_gather | solution.py:54
  56.5 0.0 copy-start
  56.5 1.4 %copy-done = bf16[8,1,6,128,128]{4,3,2,1,0:T(8,128)(2,1)S(1)} copy-done((bf16[8,1,6,128,128]{4,3,2,1,0:T(8,128)(2,1)S(1)}, bf16[8,1,6,128,128]{4,3,2,1,0:T(8,128)(2,1)}, u32[]{:S(2)}) %copy-start) | copy-done | bytes 1572888
  57.9 3.2 %shard_map.46 = bf16[256,128]{1,0:T(8,128)(2,1)} custom-call(s32[1]{0:T(128)} %bitcast.row_ref, s32[1]{0:T(128)} %bitcast.1.col_ref, s32[4,8,6]{2,1,0:T(8,128)S(1)} %copy.9.li_ref, s32[4,8,2,3]{3,2,1,0:T(2,128)S(1)} %copy.10.ri_ref, bf16[8,6,128,128]{3,2,1,0:T(8,128)(2,1)S(1)} %bitcast.6, bf16[8,3,128,128]{3,2,1,0:T(8,128)(2,1)S(1)} %bitcast.5), custom_call_target="tpu_custom_call" | custom-call | tf_op jit(solution)/shard_map/pallas_call | solution.py:41
Async XLA Ops:
  6.5 49.9 %all-gather.4.cloned.1.call-start = ((), (), s32[]{:S(2)}) async-start(), calls=%async_computation | async-start | bytes 1769472 | tf_op jit(solution)/shard_map/all_gather | solution.py:54
  56.5 1.4 %copy-start = (bf16[8,1,6,128,128]{4,3,2,1,0:T(8,128)(2,1)S(1)}, bf16[8,1,6,128,128]{4,3,2,1,0:T(8,128)(2,1)}, u32[]{:S(2)}) copy-start(bf16[8,1,6,128,128]{4,3,2,1,0:T(8,128)(2,1)} %all-gather.4.cloned.1.call-done) | copy-start | bytes 4718596
Sparse Core Ops, SparseCore 0:
  9.5 46.8 all-gather.3

commit v2 on v1

v2 whole, which is shorter than its diff:
```python
import jax
import jax.numpy as jnp
from jax import lax
from jax.experimental import pallas as pl
from jax.experimental.pallas import tpu as pltpu
from jax.sharding import PartitionSpec as P

KT = 8
RT = 2


def partial_products(place, left_index, right_index, lefts, rights):
    slots, tile, _ = lefts[0].shape
    pairs, right_slots = rights[0].shape[:2]
    inner = len(lefts)

    def kernel(place_ref, li_ref, ri_ref, *refs):
        left_refs, right_refs = refs[:inner], refs[inner : 2 * inner]
        mine_ref, other_ref, total, held = refs[2 * inner :]
        row, z, y = place_ref[0], place_ref[1], place_ref[2]
        total[...] = jnp.zeros_like(total)
        for t in range(inner):
            held[lax.rem(row - t + inner, inner)] = right_refs[t][...]

        for s in range(inner):
            zp = lax.rem(z - s + inner, inner)

            @pl.loop(0, slots)
            def _(slot):
                at = li_ref[row, 2 * zp + y, slot]
                k = lax.rem(at, KT)
                i = lax.div(at, KT)
                for j in range(pairs):
                    c = 2 * z + (y if j == 0 else 1 - y)
                    found = jnp.int32(right_slots)
                    for t in range(right_slots):
                        found = jnp.where(ri_ref[zp, c, y, t] == k, t, found)

                    @pl.when(jnp.logical_and(at < RT * KT, found < right_slots))
                    def _():
                        total[j, i] += jnp.dot(
                            left_refs[s][slot],
                            held[zp, j, found],
                            preferred_element_type=jnp.float32,
                        )

        mine_ref[...] = total[0].reshape(RT * tile, tile)
        other_ref[...] = total[1].reshape(RT * tile, tile)

    smem = pl.BlockSpec(memory_space=pltpu.SMEM)
    vmem = pl.BlockSpec(memory_space=pltpu.VMEM)
    return pl.pallas_call(
        kernel,
        out_shape=[jax.ShapeDtypeStruct((RT * tile, tile), jnp.float32)] * 2,
        in_specs=[smem] * 3 + [vmem] * (2 * inner),
        out_specs=[vmem] * 2,
        scratch_shapes=[
            pltpu.VMEM((pairs, RT, tile, tile), jnp.float32),
            pltpu.VMEM((inner, pairs, right_slots, tile, tile), jnp.bfloat16),
        ],
        compiler_params=pltpu.CompilerParams(vmem_limit_bytes=32 * 1024 * 1024),
    )(place, left_index, right_index, *lefts, *rights)


def shards(left_tiles, left_index, right_tiles, right_index):
    row_count = lax.axis_size("row")
    col_count = lax.axis_size("col")
    row = lax.axis_index("row")
    col = lax.axis_index("col")
    z, y = col // 2, col % 2
    left = left_tiles[0, 0]
    right = right_tiles[0, 0]

    swap = [(c, c ^ 1) for c in range(col_count)]
    given = lax.dynamic_index_in_dim(right, 1 - y, 0, keepdims=True)
    kept = lax.dynamic_index_in_dim(right, y, 0, keepdims=True)
    taken = lax.ppermute(given, "col", swap)

    lefts = [left]
    for s in range(1, col_count // 2):
        route = [(c, (c + 2 * s) % col_count) for c in range(col_count)]
        lefts.append(lax.ppermute(left, "col", route))

    halves = jnp.concatenate([kept, taken])
    rights = [halves]
    for t in range(1, row_count):
        route = [(r, (r + t) % row_count) for r in range(row_count)]
        rights.append(lax.ppermute(halves, "row", route))

    place = jnp.stack([row, z, y])
    mine, other = partial_products(place, left_index, right_index, lefts, rights)
    return (mine + lax.ppermute(other, "col", swap)).astype(jnp.bfloat16)


def solution(mesh):
    return jax.shard_map(
        shards,
        mesh=mesh,
        in_specs=(
            P("row", "col", None, None, None),
            P(),
            P("row", "col", None, None, None, None),
            P(),
        ),
        out_specs=P("row", "col"),
        check_vma=False,
    )
```

time: 68.3 us -> 32.8 us (0.48)
  waiting for transfers between devices: 38 us -> 17.3 us
  between operations: 13.4 us -> 0.05 us
  blocking collectives: 10.2 us -> 0 us
  starting transfers between devices: 0.01 us -> 9.85 us
  local copies, waits for them, and re-layouts: 3.03 us -> 1.84 us
  Pallas kernels: 3.23 us -> 2.48 us
  other arithmetic: 0 us -> 0.74 us
    all_gather x1 -> x0, waiting for transfers between devices: 37.3 us -> none  [shards(): left = lax.all_gather(left_tiles[0], 'col', axis=0, tiled=True)]
    ppermute x0 -> x8, waiting for transfers between devices: none -> 17.3 us  [the longest x3 12.8 us: shards(): lefts.append(lax.ppermute(left, 'col', route))]
    all_gather x1 -> x0, blocking collectives: 10.2 us -> none  [shards(): right = lax.all_gather(right_tiles[0, 0], 'row', axis=0, tiled=True)]
    ppermute x0 -> x8, starting transfers between devices: none -> 9.85 us  [the longest x3 4.61 us: shards(): lefts.append(lax.ppermute(left, 'col', route))]
    unnamed x4 -> x8, local copies, waits for them, and re-layouts: 3.03 us -> 0.84 us
    dynamic_slice x0 -> x1, local copies, waits for them, and re-layouts: none -> 0.99 us  [shards(): kept = lax.dynamic_index_in_dim(right, y, 0, keepdims=True)]
    pallas_call x1, Pallas kernels: 3.23 us -> 2.48 us  [partial_products(): pl.pallas_call(kernel, out_shape=[jax.ShapeDtypeStruct((RT * tile, tile),...]
    unnamed x1 -> x0, waiting for transfers between devices: 0.71 us -> none
  transfers between devices with their start and end apart: 1 -> 8, of which waited for: 1 -> 3; matrix products, arithmetic and copies ran while one was open for 2% -> 1% of each run, Pallas kernels for 0% -> 0%
where the time goes in v2:
time: 32.8 us; the launch traced here: 32.2 us
  waiting for transfers between devices  17.3 us (53%)
  starting transfers between devices  9.85 us (30%)
  Pallas kernels  2.48 us (8%)
  local copies, waits for them, and re-layouts  1.84 us (6%)
  other arithmetic  0.74 us (2%)
    ppermute x3, waiting for transfers between devices, shards(): lefts.append(lax.ppermute(left, 'col', route))  12.8 us
    ppermute x3, starting transfers between devices, shards(): lefts.append(lax.ppermute(left, 'col', route))  4.61 us
    ppermute x1, waiting for transfers between devices, shards(): return (mine + lax.ppermute(other, 'col', swap)).astype(jnp.bfloat16)  4.45 us
    ppermute x1, starting transfers between devices, shards(): taken = lax.ppermute(given, 'col', swap)  3.03 us
    pallas_call x1, Pallas kernels, partial_products(): pl.pallas_call(kernel, out_shape=[jax.ShapeDtypeStruct((RT * tile, tile),...  2.48 us
    ppermute x3, starting transfers between devices, shards(): rights.append(lax.ppermute(halves, 'row', route))  1.62 us
    dynamic_slice x1, local copies, waits for them, and re-layouts, shards(): kept = lax.dynamic_index_in_dim(right, y, 0, keepdims=True)  0.99 us
    unnamed x8, local copies, waits for them, and re-layouts  0.84 us
  transfers between devices with their start and end apart: 8, of which 3 were waited for; matrix products, arithmetic and copies ran while one was open for 1% of the time, Pallas kernels for 0%

profile of v2, /device:TPU:0, one launch (start us, length us, event | category | flops | bytes accessed | tf_op | source)
XLA Modules:
  0.0 32.2 jit_solution(14694260718383661051)
XLA Ops:
  0.0 0.0 copy-start
  0.0 1.0 %dynamic-slice_bitcast_fusion.1 = (bf16[1,3,128,128]{3,2,1,0:T(8,128)(2,1)S(1)}, bf16[1,3,128,128]{3,2,1,0:T(8,128)(2,1)S(1)}) fusion(bf16[1,1,2,3,128,128]{5,4,3,2,1,0:T(8,128)(2,1)} %param.6, s32[]{:T(128)S(6)} %select_n.20, s32[]{:T(128)S(6)} %select_n.21), kind=kLoop, calls=%fused_computation.3 | loop fusion | bytes 393224 | tf_op jit(solution)/shard_map/jit(dynamic_index_in_dim)/dynamic_slice | solution.py:76
  1.0 3.0 %collective-permute-start.3 = (bf16[1,3,128,128]{3,2,1,0:T(8,128)(2,1)S(1)}, bf16[1,3,128,128]{3,2,1,0:T(8,128)(2,1)S(1)}, u32[]{:S(2)}, u32[]{:S(2)}) collective-permute-start(bf16[1,3,128,128]{3,2,1,0:T(8,128)(2,1)S(1)} %get-tuple-element.10), channel_id=1, source_target_pairs={{0,1},{1,0},{2,3},{3,2},{4,5},{5,4},{6,7},{7,6},{8,9},{9,8},{10,11... | collective-permute-start | bytes 294920 | tf_op jit(solution)/shard_map/ppermute | solution.py:77
  4.0 0.0 copy-done
  4.0 3.6 %collective-permute-start.2 = (bf16[6,128,128]{2,1,0:T(8,128)(2,1)S(1)}, bf16[6,128,128]{2,1,0:T(8,128)(2,1)S(1)}, u32[]{:S(2)}, u32[]{:S(2)}) collective-permute-start(bf16[6,128,128]{2,1,0:T(8,128)(2,1)S(1)} %bitcast.8), channel_id=1, source_target_pairs={{0,6},{1,7},{2,0},{3,1},{4,2},{5,3},{6,4},{7,5},{8,14},{9,15},{10,... | collective-permute-start | bytes 589832 | tf_op jit(solution)/shard_map/ppermute | solution.py:82
  7.6 0.0 collective-permute-start.1
  7.6 1.0 %collective-permute-start = (bf16[6,128,128]{2,1,0:T(8,128)(2,1)S(1)}, bf16[6,128,128]{2,1,0:T(8,128)(2,1)S(1)}, u32[]{:S(2)}, u32[]{:S(2)}) collective-permute-start(bf16[6,128,128]{2,1,0:T(8,128)(2,1)S(1)} %bitcast.10), channel_id=1, source_target_pairs={{0,2},{1,3},{2,4},{3,5},{4,6},{5,7},{6,0},{7,1},{8,10},{9,11},{10,... | collective-permute-start | bytes 589832 | tf_op jit(solution)/shard_map/ppermute | solution.py:82
  8.7 0.0 collective-permute-done.3
  8.7 0.0 copy-start.1
  8.7 0.1 collective-permute-start.6
  8.8 1.6 %collective-permute-start.5 = (bf16[2,3,128,128]{3,2,1,0:T(8,128)(2,1)S(1)}, bf16[2,3,128,128]{3,2,1,0:T(8,128)(2,1)S(1)}, u32[]{:S(2)}, u32[]{:S(2)}) collective-permute-start(bf16[2,3,128,128]{3,2,1,0:T(8,128)(2,1)S(1)} %pad_maximum_fusion.refs_4_), channel_id=1, source_target_pairs={{0,16},{8,24},{16,0},{24,8},{1,17},{9,25},{17,1},{25,9},{2,18},{10... | collective-permute-start | bytes 589832 | tf_op jit(solution)/shard_map/ppermute | solution.py:88
  10.3 2.7 %collective-permute-done.2.refs_3_ = bf16[6,128,128]{2,1,0:T(8,128)(2,1)S(1)} collective-permute-done((bf16[6,128,128]{2,1,0:T(8,128)(2,1)S(1)}, bf16[6,128,128]{2,1,0:T(8,128)(2,1)S(1)}, u32[]{:S(2)}, u32[]{:S(2)}) %collective-permute-start.2) | collective-permute-done | bytes 196640 | tf_op jit(solution)/shard_map/ppermute | solution.py:82
  13.0 0.0 collective-permute-start.4
  13.0 0.0 copy-done.1
  13.0 0.0 copy-start.2
  13.0 0.1 copy.5.li_ref
  13.1 0.6 %copy-done.2 = s32[4,8,2,3]{1,2,3,0:T(2,128)S(1)} copy-done((s32[4,8,2,3]{1,2,3,0:T(2,128)S(1)}, s32[4,8,2,3]{1,2,3,0:T(2,128)}, u32[]{:S(2)}) %copy-start.2) | copy-done | bytes 792
  13.7 0.1 copy.6.ri_ref
  13.9 0.1 pad_add_fusion.place_ref
  13.9 10.1 %collective-permute-done.1.refs_2_ = bf16[6,128,128]{2,1,0:T(8,128)(2,1)S(1)} collective-permute-done((bf16[6,128,128]{2,1,0:T(8,128)(2,1)S(1)}, bf16[6,128,128]{2,1,0:T(8,128)(2,1)S(1)}, u32[]{:S(2)}, u32[]{:S(2)}) %collective-permute-start.1) | collective-permute-done | bytes 196640 | tf_op jit(solution)/shard_map/ppermute | solution.py:82
  24.0 0.0 collective-permute-done.refs_1_
  24.1 0.0 collective-permute-done.6.refs_7_
  24.1 0.0 collective-permute-done.5.refs_6_
  24.1 0.0 collective-permute-done.4.refs_5_
  24.1 2.5 %shard_map.46 = (f32[256,128]{1,0:T(8,128)S(1)}, f32[256,128]{1,0:T(8,128)S(1)}) custom-call(s32[3]{0:T(128)S(1)} %pad_add_fusion.place_ref, s32[4,8,6]{2,1,0:T(8,128)S(1)} %copy.5.li_ref, s32[4,8,2,3]{3,2,1,0:T(2,128)S(1)} %copy.6.ri_ref, bf16[6,128,128]{2,1,0:T(8,128)(2,1)S(1)} %bitcast.11, bf16[6,128,128]{2,1,0:T(8,128)(2,1)S(1)} %collective-permute-done.refs_1_, ...), custom_call_target="tpu_custom_call" | custom-call | tf_op jit(solution)/shard_map/pallas_call | solution.py:52
  26.6 0.6 %collective-permute-start.7 = (f32[256,128]{1,0:T(8,128)S(1)}, f32[256,128]{1,0:T(8,128)S(1)}, u32[]{:S(2)}, u32[]{:S(2)}) collective-permute-start(f32[256,128]{1,0:T(8,128)S(1)} %get-tuple-element.8), channel_id=1, source_target_pairs={{0,1},{1,0},{2,3},{3,2},{4,5},{5,4},{6,7},{7,6},{8,9},{9,8},{10,11... | collective-permute-start | bytes 393224 | tf_op jit(solution)/shard_map/ppermute | solution.py:92
  27.1 4.4 %collective-permute-done.7 = f32[256,128]{1,0:T(8,128)S(1)} collective-permute-done((f32[256,128]{1,0:T(8,128)S(1)}, f32[256,128]{1,0:T(8,128)S(1)}, u32[]{:S(2)}, u32[]{:S(2)}) %collective-permute-start.7) | collective-permute-done | bytes 131104 | tf_op jit(solution)/shard_map/ppermute | solution.py:92
  31.6 0.6 %add_convert_fusion = bf16[256,128]{1,0:T(8,128)(2,1)} fusion(f32[256,128]{1,0:T(8,128)S(1)} %get-tuple-element.7, f32[256,128]{1,0:T(8,128)S(1)} %collective-permute-done.7), kind=kLoop, calls=%fused_computation.1 | loop fusion | flops 65536 | bytes 327680 | tf_op jit(solution)/shard_map/convert_element_type | solution.py:92
  (1 shorter events, 0.0 us)
Async XLA Ops:
  0.0 4.0 %copy-start = (bf16[1,1,6,128,128]{4,3,2,1,0:T(8,128)(2,1)S(1)}, bf16[1,1,6,128,128]{4,3,2,1,0:T(8,128)(2,1)}, u32[]{:S(2)}) copy-start(bf16[1,1,6,128,128]{4,3,2,1,0:T(8,128)(2,1)} %param.4) | copy-start | bytes 589828
  1.0 7.7 %collective-permute-start.3 = (bf16[1,3,128,128]{3,2,1,0:T(8,128)(2,1)S(1)}, bf16[1,3,128,128]{3,2,1,0:T(8,128)(2,1)S(1)}, u32[]{:S(2)}, u32[]{:S(2)}) collective-permute-start(bf16[1,3,128,128]{3,2,1,0:T(8,128)(2,1)S(1)} %get-tuple-element.10), channel_id=1, source_target_pairs={{0,1},{1,0},{2,3},{3,2},{4,5},{5,4},{6,7},{7,6},{8,9},{9,8},{10,11... | collective-permute-start | bytes 294920 | tf_op jit(solution)/shard_map/ppermute | solution.py:77
  4.0 9.0 %collective-permute-start.2 = (bf16[6,128,128]{2,1,0:T(8,128)(2,1)S(1)}, bf16[6,128,128]{2,1,0:T(8,128)(2,1)S(1)}, u32[]{:S(2)}, u32[]{:S(2)}) collective-permute-start(bf16[6,128,128]{2,1,0:T(8,128)(2,1)S(1)} %bitcast.8), channel_id=1, source_target_pairs={{0,6},{1,7},{2,0},{3,1},{4,2},{5,3},{6,4},{7,5},{8,14},{9,15},{10,... | collective-permute-start | bytes 589832 | tf_op jit(solution)/shard_map/ppermute | solution.py:82
  7.6 16.4 %collective-permute-start.1 = (bf16[6,128,128]{2,1,0:T(8,128)(2,1)S(1)}, bf16[6,128,128]{2,1,0:T(8,128)(2,1)S(1)}, u32[]{:S(2)}, u32[]{:S(2)}) collective-permute-start(bf16[6,128,128]{2,1,0:T(8,128)(2,1)S(1)} %bitcast.9), channel_id=1, source_target_pairs={{0,4},{1,5},{2,6},{3,7},{4,0},{5,1},{6,2},{7,3},{8,12},{9,13},{10,... | collective-permute-start | bytes 589832 | tf_op jit(solution)/shard_map/ppermute | solution.py:82
  7.6 16.4 %collective-permute-start = (bf16[6,128,128]{2,1,0:T(8,128)(2,1)S(1)}, bf16[6,128,128]{2,1,0:T(8,128)(2,1)S(1)}, u32[]{:S(2)}, u32[]{:S(2)}) collective-permute-start(bf16[6,128,128]{2,1,0:T(8,128)(2,1)S(1)} %bitcast.10), channel_id=1, source_target_pairs={{0,2},{1,3},{2,4},{3,5},{4,6},{5,7},{6,0},{7,1},{8,10},{9,11},{10,... | collective-permute-start | bytes 589832 | tf_op jit(solution)/shard_map/ppermute | solution.py:82
  8.7 4.4 %copy-start.1 = (s32[4,8,6]{1,0,2:T(4,128)S(1)}, s32[4,8,6]{1,0,2:T(4,128)}, u32[]{:S(2)}) copy-start(s32[4,8,6]{1,0,2:T(4,128)} %param.5) | copy-start | bytes 2308
  8.7 15.4 %collective-permute-start.6 = (bf16[2,3,128,128]{3,2,1,0:T(8,128)(2,1)S(1)}, bf16[2,3,128,128]{3,2,1,0:T(8,128)(2,1)S(1)}, u32[]{:S(2)}, u32[]{:S(2)}) collective-permute-start(bf16[2,3,128,128]{3,2,1,0:T(8,128)(2,1)S(1)} %pad_maximum_fusion.refs_4_), channel_id=1, source_target_pairs={{0,24},{8,0},{16,8},{24,16},{1,25},{9,1},{17,9},{25,17},{2,26},{10... | collective-permute-start | bytes 589832 | tf_op jit(solution)/shard_map/ppermute | solution.py:88
  8.8 15.3 %collective-permute-start.5 = (bf16[2,3,128,128]{3,2,1,0:T(8,128)(2,1)S(1)}, bf16[2,3,128,128]{3,2,1,0:T(8,128)(2,1)S(1)}, u32[]{:S(2)}, u32[]{:S(2)}) collective-permute-start(bf16[2,3,128,128]{3,2,1,0:T(8,128)(2,1)S(1)} %pad_maximum_fusion.refs_4_), channel_id=1, source_target_pairs={{0,16},{8,24},{16,0},{24,8},{1,17},{9,25},{17,1},{25,9},{2,18},{10... | collective-permute-start | bytes 589832 | tf_op jit(solution)/shard_map/ppermute | solution.py:88
  13.0 11.0 %collective-permute-start.4 = (bf16[2,3,128,128]{3,2,1,0:T(8,128)(2,1)S(1)}, bf16[2,3,128,128]{3,2,1,0:T(8,128)(2,1)S(1)}, u32[]{:S(2)}, u32[]{:S(2)}) collective-permute-start(bf16[2,3,128,128]{3,2,1,0:T(8,128)(2,1)S(1)} %pad_maximum_fusion.refs_4_), channel_id=1, source_target_pairs={{0,8},{8,16},{16,24},{24,0},{1,9},{9,17},{17,25},{25,1},{2,10},{10... | collective-permute-start | bytes 589832 | tf_op jit(solution)/shard_map/ppermute | solution.py:88
  13.0 0.7 %copy-start.2 = (s32[4,8,2,3]{1,2,3,0:T(2,128)S(1)}, s32[4,8,2,3]{1,2,3,0:T(2,128)}, u32[]{:S(2)}) copy-start(s32[4,8,2,3]{1,2,3,0:T(2,128)} %param.7) | copy-start | bytes 2308
  26.6 5.0 %collective-permute-start.7 = (f32[256,128]{1,0:T(8,128)S(1)}, f32[256,128]{1,0:T(8,128)S(1)}, u32[]{:S(2)}, u32[]{:S(2)}) collective-permute-start(f32[256,128]{1,0:T(8,128)S(1)} %get-tuple-element.8), channel_id=1, source_target_pairs={{0,1},{1,0},{2,3},{3,2},{4,5},{5,4},{6,7},{7,6},{8,9},{9,8},{10,11... | collective-permute-start | bytes 393224 | tf_op jit(solution)/shard_map/ppermute | solution.py:92

commit v3 on v1

v3 whole, which is shorter than its diff:
```python
import jax
import jax.numpy as jnp
from jax import lax
from jax.experimental import pallas as pl
from jax.experimental.pallas import tpu as pltpu
from jax.sharding import PartitionSpec as P

KT = 8
RT = 2
SMEM = pl.BlockSpec(memory_space=pltpu.SMEM)
VMEM = pl.BlockSpec(memory_space=pltpu.VMEM)


def add_block(li_ref, ri_ref, row, zp, y, column, left_ref, right_at, total_ref):
    slots, tile, _ = left_ref.shape
    right_slots = ri_ref.shape[-1]

    @pl.loop(0, slots)
    def _(slot):
        at = li_ref[row, 2 * zp + y, slot]
        k = lax.rem(at, KT)
        i = lax.div(at, KT)
        found = jnp.int32(right_slots)
        for t in range(right_slots):
            found = jnp.where(ri_ref[zp, column, y, t] == k, t, found)

        @pl.when(jnp.logical_and(at < RT * KT, found < right_slots))
        def _():
            rows = pl.ds(pl.multiple_of(i * tile, tile), tile)
            total_ref[rows, :] += jnp.dot(
                left_ref[slot], right_at(found), preferred_element_type=jnp.float32
            )


def first_products(place, left_index, right_index, lefts, kept, taken):
    slots, tile, _ = lefts[0].shape
    count = len(lefts)
    inner = len(kept)
    right_slots = kept[0].shape[1]

    def kernel(place_ref, li_ref, ri_ref, *refs):
        left_refs = refs[:count]
        sides = refs[count : count + inner], refs[count + inner : count + 2 * inner]
        totals = refs[count + 2 * inner : count + 2 * inner + 2]
        lasts = refs[count + 2 * inner + 2 : count + 2 * inner + 4]
        held = refs[-1]
        row, z, y = place_ref[0], place_ref[1], place_ref[2]
        for side in range(2):
            column = 2 * z + (y if side == 0 else 1 - y)
            totals[side][...] = jnp.zeros_like(totals[side])
            for t in range(inner):
                held[side, row ^ t] = sides[side][t][0]
            for s in range(count):
                zp = z ^ s
                add_block(
                    li_ref, ri_ref, row, zp, y, column, left_refs[s],
                    lambda found, side=side, zp=zp: held[side, zp, found], totals[side],
                )
            lasts[side][...] = held[side, z ^ (inner - 1)]

    return pl.pallas_call(
        kernel,
        out_shape=[jax.ShapeDtypeStruct((RT * tile, tile), jnp.float32)] * 2
        + [jax.ShapeDtypeStruct((right_slots, tile, tile), jnp.bfloat16)] * 2,
        in_specs=[SMEM] * 3 + [VMEM] * (count + 2 * inner),
        out_specs=[VMEM] * 4,
        scratch_shapes=[pltpu.VMEM((2, inner, right_slots, tile, tile), jnp.bfloat16)],
        compiler_params=pltpu.CompilerParams(vmem_limit_bytes=32 * 1024 * 1024),
        cost_estimate=pl.CostEstimate(
            flops=4 * count * slots * tile**3, bytes_accessed=2 * count * slots * tile**2, transcendentals=0
        ),
    )(place, left_index, right_index, *lefts, *kept, *taken)


def last_products(place, left_index, right_index, left, right, total, side, inner):
    slots, tile, _ = left.shape

    def kernel(place_ref, li_ref, ri_ref, left_ref, right_ref, total_ref, out_ref):
        row, z, y = place_ref[0], place_ref[1], place_ref[2]
        column = 2 * z + (y if side == 0 else 1 - y)
        out_ref[...] = total_ref[...]
        add_block(
            li_ref, ri_ref, row, z ^ (inner - 1), y, column, left_ref,
            lambda found: right_ref[found], out_ref,
        )

    return pl.pallas_call(
        kernel,
        out_shape=jax.ShapeDtypeStruct(total.shape, total.dtype),
        in_specs=[SMEM] * 3 + [VMEM] * 3,
        out_specs=VMEM,
        compiler_params=pltpu.CompilerParams(vmem_limit_bytes=16 * 1024 * 1024),
        cost_estimate=pl.CostEstimate(
            flops=2 * slots * tile**3, bytes_accessed=2 * slots * tile**2, transcendentals=0
        ),
    )(place, left_index, right_index, left, right, total)


def shards(left_tiles, left_index, right_tiles, right_index):
    row_count = lax.axis_size("row")
    col_count = lax.axis_size("col")
    inner = col_count // 2
    row = lax.axis_index("row")
    col = lax.axis_index("col")
    z, y = col >> 1, col & 1
    right = right_tiles[0, 0]

    def across(block, axis, mask):
        route = [(i, i ^ mask) for i in range(lax.axis_size(axis))]
        return lax.ppermute(block, axis, route)

    lefts = {0: left_tiles[0, 0]}
    distance = inner // 2
    while distance:
        for s in sorted(lefts):
            lefts[s ^ distance] = across(lefts[s], "col", 2 * distance)
        distance //= 2

    given = lax.dynamic_index_in_dim(right, 1 - y, 0, keepdims=True)
    own = lax.dynamic_index_in_dim(right, y, 0, keepdims=True)
    swapped = across(given, "col", 1)
    kept = [own] + [across(own, "row", t) for t in range(1, row_count)]
    taken = [swapped] + [across(swapped, "row", t) for t in range(1, row_count)]

    place = jnp.stack([row, z, y])
    where = (place, left_index, right_index)
    early = [lefts[s] for s in range(inner - 1)]
    mine, other, mine_last, other_last = first_products(*where, early, kept, taken)
    final = lefts[inner - 1]
    other = last_products(*where, final, other_last, other, 1, inner)
    coming = across(other, "col", 1)
    mine = last_products(*where, final, mine_last, mine, 0, inner)
    return (mine + coming).astype(jnp.bfloat16)


def solution(mesh):
    return jax.shard_map(
        shards,
        mesh=mesh,
        in_specs=(
            P("row", "col", None, None, None),
            P(),
            P("row", "col", None, None, None, None),
            P(),
        ),
        out_specs=P("row", "col"),
        check_vma=False,
    )
```

time: 68.3 us -> 32.9 us (0.48)
  waiting for transfers between devices: 38 us -> 10.3 us
  starting transfers between devices: 0.01 us -> 14 us
  between operations: 13.4 us -> 0.04 us
  blocking collectives: 10.2 us -> 0 us
  Pallas kernels: 3.23 us -> 5.78 us
  local copies, waits for them, and re-layouts: 3.03 us -> 1.83 us
  other arithmetic: 0 us -> 0.72 us
    all_gather x1 -> x0, waiting for transfers between devices: 37.3 us -> none  [shards(): left = lax.all_gather(left_tiles[0], 'col', axis=0, tiled=True)]
    ppermute x0 -> x11, starting transfers between devices: none -> 14 us  [across(): return lax.ppermute(block, axis, route)]
    ppermute x0 -> x11, waiting for transfers between devices: none -> 10.3 us  [across(): return lax.ppermute(block, axis, route)]
    all_gather x1 -> x0, blocking collectives: 10.2 us -> none  [shards(): right = lax.all_gather(right_tiles[0, 0], 'row', axis=0, tiled=True)]
    pallas_call x1 -> x3, Pallas kernels: 3.23 us -> 5.78 us  [the longest x2 3.08 us: last_products(): pl.pallas_call(kernel, out_shape=jax.ShapeDtypeStruct(total.shape, total....]
    unnamed x4 -> x8, local copies, waits for them, and re-layouts: 3.03 us -> 0.84 us
    dynamic_slice x0 -> x1, local copies, waits for them, and re-layouts: none -> 0.99 us  [shards(): given = lax.dynamic_index_in_dim(right, 1 - y, 0, keepdims=True)]
    unnamed x1 -> x0, waiting for transfers between devices: 0.71 us -> none
  transfers between devices with their start and end apart: 1 -> 11, of which waited for: 1 -> 5; matrix products, arithmetic and copies ran while one was open for 2% -> 4% of each run, Pallas kernels for 0% -> 13%
where the time goes in v3:
time: 32.9 us; the launch traced here: 32.7 us
  starting transfers between devices  14 us (43%)
  waiting for transfers between devices  10.3 us (31%)
  Pallas kernels  5.78 us (18%)
  local copies, waits for them, and re-layouts  1.83 us (6%)
  other arithmetic  0.72 us (2%)
    ppermute x11, starting transfers between devices, across(): return lax.ppermute(block, axis, route)  14 us
    ppermute x11, waiting for transfers between devices, across(): return lax.ppermute(block, axis, route)  10.3 us
    pallas_call x2, Pallas kernels, last_products(): pl.pallas_call(kernel, out_shape=jax.ShapeDtypeStruct(total.shape, total....  3.08 us
    pallas_call x1, Pallas kernels, first_products(): pl.pallas_call(kernel, out_shape=[jax.ShapeDtypeStruct((RT * tile, tile),...  2.7 us
    dynamic_slice x1, local copies, waits for them, and re-layouts, shards(): given = lax.dynamic_index_in_dim(right, 1 - y, 0, keepdims=True)  0.99 us
    unnamed x8, local copies, waits for them, and re-layouts  0.84 us
  transfers between devices with their start and end apart: 11, of which 5 were waited for; matrix products, arithmetic and copies ran while one was open for 4% of the time, Pallas kernels for 13%

profile of v3, /device:TPU:0, one launch (start us, length us, event | category | flops | bytes accessed | tf_op | source)
XLA Modules:
  0.0 32.7 jit_solution(11409207935465041503)
XLA Ops:
  0.0 4.0 %collective-permute-start = (bf16[6,128,128]{2,1,0:T(8,128)(2,1)}, bf16[6,128,128]{2,1,0:T(8,128)(2,1)S(1)}, u32[]{:S(2)}, u32[]{:S(2)}) collective-permute-start(bf16[6,128,128]{2,1,0:T(8,128)(2,1)} %bitcast.8), channel_id=1, source_target_pairs={{0,4},{1,5},{2,6},{3,7},{4,0},{5,1},{6,2},{7,3},{8,12},{9,13},{10,... | collective-permute-start | bytes 589832 | tf_op jit(solution)/shard_map/ppermute | solution.py:110
  4.0 0.0 copy-start
  4.0 0.0 copy-start.1
  4.0 1.0 %dynamic-slice_bitcast_fusion = (bf16[1,3,128,128]{3,2,1,0:T(8,128)(2,1)S(1)}, bf16[1,3,128,128]{3,2,1,0:T(8,128)(2,1)S(1)}) fusion(bf16[1,1,2,3,128,128]{5,4,3,2,1,0:T(8,128)(2,1)} %param.6, s32[]{:T(128)S(6)} %select_n.8, s32[]{:T(128)S(6)} %select_n.7), kind=kLoop, calls=%fused_computation.1 | loop fusion | bytes 393224 | tf_op jit(solution)/shard_map/jit(dynamic_index_in_dim)/dynamic_slice | solution.py:119
  5.0 1.6 %collective-permute-start.6 = (bf16[1,3,128,128]{3,2,1,0:T(8,128)(2,1)S(1)}, bf16[1,3,128,128]{3,2,1,0:T(8,128)(2,1)S(1)}, u32[]{:S(2)}, u32[]{:S(2)}) collective-permute-start(bf16[1,3,128,128]{3,2,1,0:T(8,128)(2,1)S(1)} %get-tuple-element.13), channel_id=1, source_target_pairs={{0,1},{1,0},{2,3},{3,2},{4,5},{5,4},{6,7},{7,6},{8,9},{9,8},{10,11... | collective-permute-start | bytes 294920 | tf_op jit(solution)/shard_map/ppermute | solution.py:110
  6.6 0.4 %collective-permute-start.5 = (bf16[1,3,128,128]{3,2,1,0:T(8,128)(2,1)S(1)}, bf16[1,3,128,128]{3,2,1,0:T(8,128)(2,1)S(1)}, u32[]{:S(2)}, u32[]{:S(2)}) collective-permute-start(bf16[1,3,128,128]{3,2,1,0:T(8,128)(2,1)S(1)} %get-tuple-element.14.refs_3_), channel_id=1, source_target_pairs={{0,24},{8,16},{16,8},{24,0},{1,25},{9,17},{17,9},{25,1},{2,26},{10... | collective-permute-start | bytes 294920 | tf_op jit(solution)/shard_map/ppermute | solution.py:110
  7.0 1.2 %collective-permute-start.4 = (bf16[1,3,128,128]{3,2,1,0:T(8,128)(2,1)S(1)}, bf16[1,3,128,128]{3,2,1,0:T(8,128)(2,1)S(1)}, u32[]{:S(2)}, u32[]{:S(2)}) collective-permute-start(bf16[1,3,128,128]{3,2,1,0:T(8,128)(2,1)S(1)} %get-tuple-element.14.refs_3_), channel_id=1, source_target_pairs={{0,16},{8,24},{16,0},{24,8},{1,17},{9,25},{17,1},{25,9},{2,18},{10... | collective-permute-start | bytes 294920 | tf_op jit(solution)/shard_map/ppermute | solution.py:110
  8.1 0.3 %collective-permute-start.3 = (bf16[1,3,128,128]{3,2,1,0:T(8,128)(2,1)S(1)}, bf16[1,3,128,128]{3,2,1,0:T(8,128)(2,1)S(1)}, u32[]{:S(2)}, u32[]{:S(2)}) collective-permute-start(bf16[1,3,128,128]{3,2,1,0:T(8,128)(2,1)S(1)} %get-tuple-element.14.refs_3_), channel_id=1, source_target_pairs={{0,8},{8,0},{16,24},{24,16},{1,9},{9,1},{17,25},{25,17},{2,10},{10... | collective-permute-start | bytes 294920 | tf_op jit(solution)/shard_map/ppermute | solution.py:110
  8.5 1.2 %collective-permute-done.6.refs_7_ = bf16[1,3,128,128]{3,2,1,0:T(8,128)(2,1)S(1)} collective-permute-done((bf16[1,3,128,128]{3,2,1,0:T(8,128)(2,1)S(1)}, bf16[1,3,128,128]{3,2,1,0:T(8,128)(2,1)S(1)}, u32[]{:S(2)}, u32[]{:S(2)}) %collective-permute-start.6) | collective-permute-done | bytes 98336 | tf_op jit(solution)/shard_map/ppermute | solution.py:110
  9.7 0.0 copy-done
  9.7 1.6 %collective-permute-start.2 = (bf16[6,128,128]{2,1,0:T(8,128)(2,1)S(1)}, bf16[6,128,128]{2,1,0:T(8,128)(2,1)S(1)}, u32[]{:S(2)}, u32[]{:S(2)}) collective-permute-start(bf16[6,128,128]{2,1,0:T(8,128)(2,1)S(1)} %bitcast.9), channel_id=1, source_target_pairs={{0,2},{1,3},{2,0},{3,1},{4,6},{5,7},{6,4},{7,5},{8,10},{9,11},{10,... | collective-permute-start | bytes 589832 | tf_op jit(solution)/shard_map/ppermute | solution.py:110
  11.3 2.2 %collective-permute-done.refs_2_ = bf16[6,128,128]{2,1,0:T(8,128)(2,1)S(1)} collective-permute-done((bf16[6,128,128]{2,1,0:T(8,128)(2,1)}, bf16[6,128,128]{2,1,0:T(8,128)(2,1)S(1)}, u32[]{:S(2)}, u32[]{:S(2)}) %collective-permute-start) | collective-permute-done | bytes 196640 | tf_op jit(solution)/shard_map/ppermute | solution.py:110
  13.5 0.8 %collective-permute-start.1 = (bf16[6,128,128]{2,1,0:T(8,128)(2,1)S(1)}, bf16[6,128,128]{2,1,0:T(8,128)(2,1)S(1)}, u32[]{:S(2)}, u32[]{:S(2)}) collective-permute-start(bf16[6,128,128]{2,1,0:T(8,128)(2,1)S(1)} %collective-permute-done.refs_2_), channel_id=1, source_target_pairs={{0,2},{1,3},{2,0},{3,1},{4,6},{5,7},{6,4},{7,5},{8,10},{9,11},{10,... | collective-permute-start | bytes 589832 | tf_op jit(solution)/shard_map/ppermute | solution.py:110
  14.2 0.0 copy-done.1
  14.2 0.0 copy-start.2
  14.2 0.1 copy.7.li_ref
  14.3 0.6 %copy-done.2 = s32[4,8,2,3]{1,2,3,0:T(2,128)S(1)} copy-done((s32[4,8,2,3]{1,2,3,0:T(2,128)S(1)}, s32[4,8,2,3]{1,2,3,0:T(2,128)}, u32[]{:S(2)}) %copy-start.2) | copy-done | bytes 792
  14.9 0.1 copy.8.ri_ref
  15.1 0.0 collective-permute-done.5.refs_6_
  15.1 0.9 %collective-permute-start.9 = (bf16[1,3,128,128]{3,2,1,0:T(8,128)(2,1)S(1)}, bf16[1,3,128,128]{3,2,1,0:T(8,128)(2,1)S(1)}, u32[]{:S(2)}, u32[]{:S(2)}) collective-permute-start(bf16[1,3,128,128]{3,2,1,0:T(8,128)(2,1)S(1)} %collective-permute-done.6.refs_7_), channel_id=1, source_target_pairs={{0,24},{8,16},{16,8},{24,0},{1,25},{9,17},{17,9},{25,1},{2,26},{10... | collective-permute-start | bytes 294920 | tf_op jit(solution)/shard_map/ppermute | solution.py:110
  16.0 0.0 collective-permute-done.4.refs_5_
  16.0 0.7 %collective-permute-start.8 = (bf16[1,3,128,128]{3,2,1,0:T(8,128)(2,1)S(1)}, bf16[1,3,128,128]{3,2,1,0:T(8,128)(2,1)S(1)}, u32[]{:S(2)}, u32[]{:S(2)}) collective-permute-start(bf16[1,3,128,128]{3,2,1,0:T(8,128)(2,1)S(1)} %collective-permute-done.6.refs_7_), channel_id=1, source_target_pairs={{0,16},{8,24},{16,0},{24,8},{1,17},{9,25},{17,1},{25,9},{2,18},{10... | collective-permute-start | bytes 294920 | tf_op jit(solution)/shard_map/ppermute | solution.py:110
  16.7 0.0 collective-permute-done.3.refs_4_
  16.7 0.3 collective-permute-start.7
  17.0 0.1 pad_add_fusion.place_ref
  17.1 3.1 %collective-permute-done.9.refs_10_ = bf16[1,3,128,128]{3,2,1,0:T(8,128)(2,1)S(1)} collective-permute-done((bf16[1,3,128,128]{3,2,1,0:T(8,128)(2,1)S(1)}, bf16[1,3,128,128]{3,2,1,0:T(8,128)(2,1)S(1)}, u32[]{:S(2)}, u32[]{:S(2)}) %collective-permute-start.9) | collective-permute-done | bytes 98336 | tf_op jit(solution)/shard_map/ppermute | solution.py:110
  20.2 2.2 %collective-permute-done.8.refs_9_ = bf16[1,3,128,128]{3,2,1,0:T(8,128)(2,1)S(1)} collective-permute-done((bf16[1,3,128,128]{3,2,1,0:T(8,128)(2,1)S(1)}, bf16[1,3,128,128]{3,2,1,0:T(8,128)(2,1)S(1)}, u32[]{:S(2)}, u32[]{:S(2)}) %collective-permute-start.8) | collective-permute-done | bytes 98336 | tf_op jit(solution)/shard_map/ppermute | solution.py:110
  22.3 0.0 collective-permute-done.7.refs_8_
  22.3 0.0 collective-permute-done.2.refs_1_
  22.3 2.7 %shard_map.46 = (f32[256,128]{1,0:T(8,128)S(1)}, f32[256,128]{1,0:T(8,128)S(1)}, bf16[3,128,128]{2,1,0:T(8,128)(2,1)S(1)}, bf16[3,128,128]{2,1,0:T(8,128)(2,1)S(1)}) custom-call(s32[3]{0:T(128)S(1)} %pad_add_fusion.place_ref, s32[4,8,6]{2,1,0:T(8,128)S(1)} %copy.7.li_ref, s32[4,8,2,3]{3,2,1,0:T(2,128)S(1)} %copy.8.ri_ref, bf16[6,128,128]{2,1,0:T(8,128)(2,1)S(1)} %bitcast.10, ...), custom_call_target="tpu_custom_call" | custom-call | flops 150994944 | bytes 589824 | tf_op jit(solution)/shard_map/pallas_call | solution.py:61
  25.0 0.0 collective-permute-done.1.left_ref
  25.1 1.6 %shard_map.48 = f32[256,128]{1,0:T(8,128)S(1)} custom-call(s32[3]{0:T(128)S(1)} %pad_add_fusion.place_ref, s32[4,8,6]{2,1,0:T(8,128)S(1)} %copy.7.li_ref, s32[4,8,2,3]{3,2,1,0:T(2,128)S(1)} %copy.8.ri_ref, bf16[6,128,128]{2,1,0:T(8,128)(2,1)S(1)} %collective-permute-done.1.left_ref, bf16[3,128,128]{2,1,0:T(8,128)(2,1)S(1)} %get-tuple-element.11.right_ref, ...), custom_call_target="tpu_custom_call" | custom-call | flops 25165824 | bytes 196608 | tf_op jit(solution)/shard_map/pallas_call | solution.py:87
  26.6 2.3 %collective-permute-start.10 = (f32[256,128]{1,0:T(8,128)S(1)}, f32[256,128]{1,0:T(8,128)S(1)}, u32[]{:S(2)}, u32[]{:S(2)}) collective-permute-start(f32[256,128]{1,0:T(8,128)S(1)} %shard_map.48), channel_id=1, source_target_pairs={{0,1},{1,0},{2,3},{3,2},{4,5},{5,4},{6,7},{7,6},{8,9},{9,8},{10,11... | collective-permute-start | bytes 393224 | tf_op jit(solution)/shard_map/ppermute | solution.py:110
  28.9 1.5 %shard_map.47 = f32[256,128]{1,0:T(8,128)S(1)} custom-call(s32[3]{0:T(128)S(1)} %pad_add_fusion.place_ref, s32[4,8,6]{2,1,0:T(8,128)S(1)} %copy.7.li_ref, s32[4,8,2,3]{3,2,1,0:T(2,128)S(1)} %copy.8.ri_ref, bf16[6,128,128]{2,1,0:T(8,128)(2,1)S(1)} %collective-permute-done.1.left_ref, bf16[3,128,128]{2,1,0:T(8,128)(2,1)S(1)} %get-tuple-element.9.right_ref, ...), custom_call_target="tpu_custom_call" | custom-call | flops 25165824 | bytes 196608 | tf_op jit(solution)/shard_map/pallas_call | solution.py:87
  30.4 1.6 %collective-permute-done.10 = f32[256,128]{1,0:T(8,128)S(1)} collective-permute-done((f32[256,128]{1,0:T(8,128)S(1)}, f32[256,128]{1,0:T(8,128)S(1)}, u32[]{:S(2)}, u32[]{:S(2)}) %collective-permute-start.10) | collective-permute-done | bytes 131104 | tf_op jit(solution)/shard_map/ppermute | solution.py:110
  32.0 0.6 %add_convert_fusion = bf16[256,128]{1,0:T(8,128)(2,1)} fusion(f32[256,128]{1,0:T(8,128)S(1)} %shard_map.47, f32[256,128]{1,0:T(8,128)S(1)} %collective-permute-done.10), kind=kLoop, calls=%fused_computation | loop fusion | flops 65536 | bytes 327680 | tf_op jit(solution)/shard_map/convert_element_type | solution.py:133
Async XLA Ops:
  0.0 13.5 %collective-permute-start = (bf16[6,128,128]{2,1,0:T(8,128)(2,1)}, bf16[6,128,128]{2,1,0:T(8,128)(2,1)S(1)}, u32[]{:S(2)}, u32[]{:S(2)}) collective-permute-start(bf16[6,128,128]{2,1,0:T(8,128)(2,1)} %bitcast.8), channel_id=1, source_target_pairs={{0,4},{1,5},{2,6},{3,7},{4,0},{5,1},{6,2},{7,3},{8,12},{9,13},{10,... | collective-permute-start | bytes 589832 | tf_op jit(solution)/shard_map/ppermute | solution.py:110
  4.0 5.7 %copy-start = (bf16[1,1,6,128,128]{4,3,2,1,0:T(8,128)(2,1)S(1)}, bf16[1,1,6,128,128]{4,3,2,1,0:T(8,128)(2,1)}, u32[]{:S(2)}) copy-start(bf16[1,1,6,128,128]{4,3,2,1,0:T(8,128)(2,1)} %param.4) | copy-start | bytes 589828
  4.0 10.2 %copy-start.1 = (s32[4,8,6]{1,0,2:T(4,128)S(1)}, s32[4,8,6]{1,0,2:T(4,128)}, u32[]{:S(2)}) copy-start(s32[4,8,6]{1,0,2:T(4,128)} %param.5) | copy-start | bytes 2308
  5.0 4.7 %collective-permute-start.6 = (bf16[1,3,128,128]{3,2,1,0:T(8,128)(2,1)S(1)}, bf16[1,3,128,128]{3,2,1,0:T(8,128)(2,1)S(1)}, u32[]{:S(2)}, u32[]{:S(2)}) collective-permute-start(bf16[1,3,128,128]{3,2,1,0:T(8,128)(2,1)S(1)} %get-tuple-element.13), channel_id=1, source_target_pairs={{0,1},{1,0},{2,3},{3,2},{4,5},{5,4},{6,7},{7,6},{8,9},{9,8},{10,11... | collective-permute-start | bytes 294920 | tf_op jit(solution)/shard_map/ppermute | solution.py:110
  6.6 8.5 %collective-permute-start.5 = (bf16[1,3,128,128]{3,2,1,0:T(8,128)(2,1)S(1)}, bf16[1,3,128,128]{3,2,1,0:T(8,128)(2,1)S(1)}, u32[]{:S(2)}, u32[]{:S(2)}) collective-permute-start(bf16[1,3,128,128]{3,2,1,0:T(8,128)(2,1)S(1)} %get-tuple-element.14.refs_3_), channel_id=1, source_target_pairs={{0,24},{8,16},{16,8},{24,0},{1,25},{9,17},{17,9},{25,1},{2,26},{10... | collective-permute-start | bytes 294920 | tf_op jit(solution)/shard_map/ppermute | solution.py:110
  7.0 9.0 %collective-permute-start.4 = (bf16[1,3,128,128]{3,2,1,0:T(8,128)(2,1)S(1)}, bf16[1,3,128,128]{3,2,1,0:T(8,128)(2,1)S(1)}, u32[]{:S(2)}, u32[]{:S(2)}) collective-permute-start(bf16[1,3,128,128]{3,2,1,0:T(8,128)(2,1)S(1)} %get-tuple-element.14.refs_3_), channel_id=1, source_target_pairs={{0,16},{8,24},{16,0},{24,8},{1,17},{9,25},{17,1},{25,9},{2,18},{10... | collective-permute-start | bytes 294920 | tf_op jit(solution)/shard_map/ppermute | solution.py:110
  8.1 8.6 %collective-permute-start.3 = (bf16[1,3,128,128]{3,2,1,0:T(8,128)(2,1)S(1)}, bf16[1,3,128,128]{3,2,1,0:T(8,128)(2,1)S(1)}, u32[]{:S(2)}, u32[]{:S(2)}) collective-permute-start(bf16[1,3,128,128]{3,2,1,0:T(8,128)(2,1)S(1)} %get-tuple-element.14.refs_3_), channel_id=1, source_target_pairs={{0,8},{8,0},{16,24},{24,16},{1,9},{9,1},{17,25},{25,17},{2,10},{10... | collective-permute-start | bytes 294920 | tf_op jit(solution)/shard_map/ppermute | solution.py:110
  9.7 12.6 %collective-permute-start.2 = (bf16[6,128,128]{2,1,0:T(8,128)(2,1)S(1)}, bf16[6,128,128]{2,1,0:T(8,128)(2,1)S(1)}, u32[]{:S(2)}, u32[]{:S(2)}) collective-permute-start(bf16[6,128,128]{2,1,0:T(8,128)(2,1)S(1)} %bitcast.9), channel_id=1, source_target_pairs={{0,2},{1,3},{2,0},{3,1},{4,6},{5,7},{6,4},{7,5},{8,10},{9,11},{10,... | collective-permute-start | bytes 589832 | tf_op jit(solution)/shard_map/ppermute | solution.py:110
  13.5 11.6 %collective-permute-start.1 = (bf16[6,128,128]{2,1,0:T(8,128)(2,1)S(1)}, bf16[6,128,128]{2,1,0:T(8,128)(2,1)S(1)}, u32[]{:S(2)}, u32[]{:S(2)}) collective-permute-start(bf16[6,128,128]{2,1,0:T(8,128)(2,1)S(1)} %collective-permute-done.refs_2_), channel_id=1, source_target_pairs={{0,2},{1,3},{2,0},{3,1},{4,6},{5,7},{6,4},{7,5},{8,10},{9,11},{10,... | collective-permute-start | bytes 589832 | tf_op jit(solution)/shard_map/ppermute | solution.py:110
  14.2 0.7 %copy-start.2 = (s32[4,8,2,3]{1,2,3,0:T(2,128)S(1)}, s32[4,8,2,3]{1,2,3,0:T(2,128)}, u32[]{:S(2)}) copy-start(s32[4,8,2,3]{1,2,3,0:T(2,128)} %param.7) | copy-start | bytes 2308
  15.1 5.1 %collective-permute-start.9 = (bf16[1,3,128,128]{3,2,1,0:T(8,128)(2,1)S(1)}, bf16[1,3,128,128]{3,2,1,0:T(8,128)(2,1)S(1)}, u32[]{:S(2)}, u32[]{:S(2)}) collective-permute-start(bf16[1,3,128,128]{3,2,1,0:T(8,128)(2,1)S(1)} %collective-permute-done.6.refs_7_), channel_id=1, source_target_pairs={{0,24},{8,16},{16,8},{24,0},{1,25},{9,17},{17,9},{25,1},{2,26},{10... | collective-permute-start | bytes 294920 | tf_op jit(solution)/shard_map/ppermute | solution.py:110
  16.0 6.4 %collective-permute-start.8 = (bf16[1,3,128,128]{3,2,1,0:T(8,128)(2,1)S(1)}, bf16[1,3,128,128]{3,2,1,0:T(8,128)(2,1)S(1)}, u32[]{:S(2)}, u32[]{:S(2)}) collective-permute-start(bf16[1,3,128,128]{3,2,1,0:T(8,128)(2,1)S(1)} %collective-permute-done.6.refs_7_), channel_id=1, source_target_pairs={{0,16},{8,24},{16,0},{24,8},{1,17},{9,25},{17,1},{25,9},{2,18},{10... | collective-permute-start | bytes 294920 | tf_op jit(solution)/shard_map/ppermute | solution.py:110
  16.7 5.6 %collective-permute-start.7 = (bf16[1,3,128,128]{3,2,1,0:T(8,128)(2,1)S(1)}, bf16[1,3,128,128]{3,2,1,0:T(8,128)(2,1)S(1)}, u32[]{:S(2)}, u32[]{:S(2)}) collective-permute-start(bf16[1,3,128,128]{3,2,1,0:T(8,128)(2,1)S(1)} %collective-permute-done.6.refs_7_), channel_id=1, source_target_pairs={{0,8},{8,0},{16,24},{24,16},{1,9},{9,1},{17,25},{25,17},{2,10},{10... | collective-permute-start | bytes 294920 | tf_op jit(solution)/shard_map/ppermute | solution.py:110
  26.6 5.4 %collective-permute-start.10 = (f32[256,128]{1,0:T(8,128)S(1)}, f32[256,128]{1,0:T(8,128)S(1)}, u32[]{:S(2)}, u32[]{:S(2)}) collective-permute-start(f32[256,128]{1,0:T(8,128)S(1)} %shard_map.48), channel_id=1, source_target_pairs={{0,1},{1,0},{2,3},{3,2},{4,5},{5,4},{6,7},{7,6},{8,9},{9,8},{10,11... | collective-permute-start | bytes 393224 | tf_op jit(solution)/shard_map/ppermute | solution.py:110

commit v4 on v3

v4 whole, which is shorter than its diff:
```python
import jax
import jax.numpy as jnp
from jax import lax
from jax.experimental import pallas as pl
from jax.experimental.pallas import tpu as pltpu
from jax.sharding import PartitionSpec as P

KT = 8
RT = 2
SMEM = pl.BlockSpec(memory_space=pltpu.SMEM)
VMEM = pl.BlockSpec(memory_space=pltpu.VMEM)


def match(li_ref, ri_ref, row, zp, y, column, slot):
    right_slots = ri_ref.shape[-1]
    at = li_ref[row, 2 * zp + y, slot]
    k = lax.rem(at, KT)
    code = jnp.int32(0)
    for t in range(right_slots):
        code = jnp.where(ri_ref[zp, column, y, t] == k, 1 + lax.div(at, KT) * right_slots + t, code)
    return jnp.where(at < RT * KT, code, 0)


def add_tile(code, left_tile, right_at, right_slots, total_ref):
    tile = total_ref.shape[1]

    @pl.when(code > 0)
    def _():
        i = lax.div(code - 1, right_slots)
        rows = pl.ds(pl.multiple_of(i * tile, tile), tile)
        total_ref[rows, :] += jnp.dot(
            left_tile(), right_at(lax.rem(code - 1, right_slots)), preferred_element_type=jnp.float32
        )


def first_products(place, left_index, right_index, lefts, rights):
    slots, tile, _ = lefts[0].shape
    count = len(lefts)
    inner = len(rights)
    right_slots = rights[0].shape[1]

    def kernel(place_ref, li_ref, ri_ref, *refs):
        left_refs, right_refs = refs[:count], refs[count : count + inner]
        totals = refs[count + inner : count + inner + 2]
        last_ref, codes_ref, held = refs[count + inner + 2 :]
        row, z, y = place_ref[0], place_ref[1], place_ref[2]
        for t in range(inner):
            held[row ^ t] = right_refs[t][...]
        zl = z ^ (inner - 1)
        last_ref[...] = held[zl]
        for side in range(2):
            column = 2 * z + (y if side == 0 else 1 - y)
            totals[side][...] = jnp.zeros_like(totals[side])
            for slot in range(slots):
                codes_ref[side * slots + slot] = match(li_ref, ri_ref, row, zl, y, column, slot)
            for s in range(count):
                zp = z ^ s

                @pl.loop(0, slots)
                def _(slot):
                    add_tile(
                        match(li_ref, ri_ref, row, zp, y, column, slot),
                        lambda: left_refs[s][slot],
                        lambda found: held[zp, side, found],
                        right_slots,
                        totals[side],
                    )

    return pl.pallas_call(
        kernel,
        out_shape=[jax.ShapeDtypeStruct((RT * tile, tile), jnp.float32)] * 2
        + [
            jax.ShapeDtypeStruct((2, right_slots, tile, tile), jnp.bfloat16),
            jax.ShapeDtypeStruct((2 * slots,), jnp.int32),
        ],
        in_specs=[SMEM] * 3 + [VMEM] * (count + inner),
        out_specs=[VMEM] * 3 + [SMEM],
        scratch_shapes=[pltpu.VMEM((inner, 2, right_slots, tile, tile), jnp.bfloat16)],
        compiler_params=pltpu.CompilerParams(vmem_limit_bytes=32 * 1024 * 1024),
        cost_estimate=pl.CostEstimate(
            flops=4 * count * slots * tile**3, bytes_accessed=2 * count * slots * tile**2, transcendentals=0
        ),
    )(place, left_index, right_index, *lefts, *rights)


def last_products(codes, left, right, total, side):
    slots, tile, _ = left.shape
    right_slots = right.shape[1]

    def kernel(codes_ref, left_ref, right_ref, total_ref, out_ref):
        out_ref[...] = total_ref[...]
        for slot in range(slots):
            add_tile(
                codes_ref[side * slots + slot],
                lambda: left_ref[slot],
                lambda found: right_ref[side, found],
                right_slots,
                out_ref,
            )

    return pl.pallas_call(
        kernel,
        out_shape=jax.ShapeDtypeStruct(total.shape, total.dtype),
        in_specs=[SMEM] + [VMEM] * 3,
        out_specs=VMEM,
        compiler_params=pltpu.CompilerParams(vmem_limit_bytes=16 * 1024 * 1024),
        cost_estimate=pl.CostEstimate(
            flops=2 * slots * tile**3, bytes_accessed=2 * slots * tile**2, transcendentals=0
        ),
    )(codes, left, right, total)


def across(block, axis, mask):
    route = [(i, i ^ mask) for i in range(lax.axis_size(axis))]
    return lax.ppermute(block, axis, route)


def gather(block, axis, unit):
    blocks = {0: block}
    distance = lax.axis_size(axis) // unit // 2
    while distance:
        for s in sorted(blocks):
            blocks[s ^ distance] = across(blocks[s], axis, unit * distance)
        distance //= 2
    return [blocks[s] for s in range(len(blocks))]


def shards(left_tiles, left_index, right_tiles, right_index):
    row = lax.axis_index("row")
    col = lax.axis_index("col")
    z, y = col >> 1, col & 1
    right = right_tiles[0, 0]

    lefts = gather(left_tiles[0, 0], "col", 2)
    given = lax.dynamic_index_in_dim(right, 1 - y, 0, keepdims=True)
    own = lax.dynamic_index_in_dim(right, y, 0, keepdims=True)
    halves = jnp.concatenate([own, across(given, "col", 1)])
    rights = gather(halves, "row", 1)

    place = jnp.stack([row, z, y])
    mine, other, right_last, codes = first_products(place, left_index, right_index, lefts[:-1], rights)
    other = last_products(codes, lefts[-1], right_last, other, 1)
    coming = across(other, "col", 1)
    mine = last_products(codes, lefts[-1], right_last, mine, 0)
    return (mine + coming).astype(jnp.bfloat16)


def solution(mesh):
    return jax.shard_map(
        shards,
        mesh=mesh,
        in_specs=(
            P("row", "col", None, None, None),
            P(),
            P("row", "col", None, None, None, None),
            P(),
        ),
        out_specs=P("row", "col"),
        check_vma=False,
    )
```

time: 32.9 us -> 31.4 us (0.954)
  starting transfers between devices: 14 us -> 11.6 us
  waiting for transfers between devices: 10.3 us -> 12.2 us
  Pallas kernels: 5.78 us -> 4.9 us
    ppermute x11 -> x8, starting transfers between devices: 14 us -> 11.6 us  [across(): return lax.ppermute(block, axis, route)]
    ppermute x11 -> x8, waiting for transfers between devices: 10.3 us -> 12.2 us  [across(): return lax.ppermute(block, axis, route)]
    pallas_call x2, Pallas kernels: 3.08 us -> 1.52 us  [last_products(): pl.pallas_call(kernel, out_shape=jax.ShapeDtypeStruct(total.shape, total....]
    pallas_call x1, Pallas kernels: 2.7 us -> 3.38 us  [first_products(): pl.pallas_call(kernel, out_shape=[jax.ShapeDtypeStruct((RT * tile, tile),...]
  transfers between devices with their start and end apart: 11 -> 8, of which waited for: 5 -> 5; matrix products, arithmetic and copies ran while one was open for 4% -> 1% of each run, Pallas kernels for 13% -> 13%
where the time goes in v4:
time: 31.4 us; the launch traced here: 31.2 us
  waiting for transfers between devices  12.2 us (39%)
  starting transfers between devices  11.6 us (37%)
  Pallas kernels  4.9 us (16%)
  local copies, waits for them, and re-layouts  1.77 us (6%)
  other arithmetic  0.75 us (2%)
    ppermute x8, waiting for transfers between devices, across(): return lax.ppermute(block, axis, route)  12.2 us
    ppermute x8, starting transfers between devices, across(): return lax.ppermute(block, axis, route)  11.6 us
    pallas_call x1, Pallas kernels, first_products(): pl.pallas_call(kernel, out_shape=[jax.ShapeDtypeStruct((RT * tile, tile),...  3.38 us
    pallas_call x2, Pallas kernels, last_products(): pl.pallas_call(kernel, out_shape=jax.ShapeDtypeStruct(total.shape, total....  1.52 us
    dynamic_slice x1, local copies, waits for them, and re-layouts, shards(): own = lax.dynamic_index_in_dim(right, y, 0, keepdims=True)  0.95 us
    unnamed x8, local copies, waits for them, and re-layouts  0.81 us
    convert_element_type x1, other arithmetic, shards(): return (mine + coming).astype(jnp.bfloat16)  0.65 us
  transfers between devices with their start and end apart: 8, of which 5 were waited for; matrix products, arithmetic and copies ran while one was open for 1% of the time, Pallas kernels for 13%

profile of v4, /device:TPU:0, one launch (start us, length us, event | category | flops | bytes accessed | tf_op | source)
XLA Modules:
  0.0 31.2 jit_solution(280006802533243238)
XLA Ops:
  0.0 1.0 %dynamic-slice_bitcast_fusion.1 = (bf16[1,3,128,128]{3,2,1,0:T(8,128)(2,1)S(1)}, bf16[1,3,128,128]{3,2,1,0:T(8,128)(2,1)S(1)}) fusion(bf16[1,1,2,3,128,128]{5,4,3,2,1,0:T(8,128)(2,1)} %param.6, s32[]{:T(128)S(6)} %select_n.7, s32[]{:T(128)S(6)} %select_n.8), kind=kLoop, calls=%fused_computation.3 | loop fusion | bytes 393224 | tf_op jit(solution)/shard_map/jit(dynamic_index_in_dim)/dynamic_slice | solution.py:136
  1.0 3.0 %collective-permute-start.2 = (bf16[1,3,128,128]{3,2,1,0:T(8,128)(2,1)S(1)}, bf16[1,3,128,128]{3,2,1,0:T(8,128)(2,1)S(1)}, u32[]{:S(2)}, u32[]{:S(2)}) collective-permute-start(bf16[1,3,128,128]{3,2,1,0:T(8,128)(2,1)S(1)} %get-tuple-element.14), channel_id=1, source_target_pairs={{0,1},{1,0},{2,3},{3,2},{4,5},{5,4},{6,7},{7,6},{8,9},{9,8},{10,11... | collective-permute-start | bytes 294920 | tf_op jit(solution)/shard_map/ppermute | solution.py:115
  4.0 2.8 %collective-permute-done.2 = bf16[1,3,128,128]{3,2,1,0:T(8,128)(2,1)S(1)} collective-permute-done((bf16[1,3,128,128]{3,2,1,0:T(8,128)(2,1)S(1)}, bf16[1,3,128,128]{3,2,1,0:T(8,128)(2,1)S(1)}, u32[]{:S(2)}, u32[]{:S(2)}) %collective-permute-start.2) | collective-permute-done | bytes 98336 | tf_op jit(solution)/shard_map/ppermute | solution.py:115
  6.8 0.0 copy-start
  6.8 0.0 copy-start.2
  6.8 1.9 %collective-permute-start.4 = (bf16[2,3,128,128]{3,2,1,0:T(8,128)(2,1)S(1)}, bf16[2,3,128,128]{3,2,1,0:T(8,128)(2,1)S(1)}, u32[]{:S(2)}, u32[]{:S(2)}) collective-permute-start(bf16[2,3,128,128]{3,2,1,0:T(8,128)(2,1)S(1)} %pad_maximum_fusion.refs_3_), channel_id=1, source_target_pairs={{0,16},{8,24},{16,0},{24,8},{1,17},{9,25},{17,1},{25,9},{2,18},{10... | collective-permute-start | bytes 589832 | tf_op jit(solution)/shard_map/ppermute | solution.py:115
  8.7 0.0 copy-done
  8.7 2.6 %collective-permute-start.1 = (bf16[6,128,128]{2,1,0:T(8,128)(2,1)S(1)}, bf16[6,128,128]{2,1,0:T(8,128)(2,1)S(1)}, u32[]{:S(2)}, u32[]{:S(2)}) collective-permute-start(bf16[6,128,128]{2,1,0:T(8,128)(2,1)S(1)} %bitcast.8), channel_id=1, source_target_pairs={{0,4},{1,5},{2,6},{3,7},{4,0},{5,1},{6,2},{7,3},{8,12},{9,13},{10,... | collective-permute-start | bytes 589832 | tf_op jit(solution)/shard_map/ppermute | solution.py:115
  11.3 1.6 %collective-permute-start = (bf16[6,128,128]{2,1,0:T(8,128)(2,1)S(1)}, bf16[6,128,128]{2,1,0:T(8,128)(2,1)S(1)}, u32[]{:S(2)}, u32[]{:S(2)}) collective-permute-start(bf16[6,128,128]{2,1,0:T(8,128)(2,1)S(1)} %bitcast.9), channel_id=1, source_target_pairs={{0,2},{1,3},{2,0},{3,1},{4,6},{5,7},{6,4},{7,5},{8,10},{9,11},{10,... | collective-permute-start | bytes 589832 | tf_op jit(solution)/shard_map/ppermute | solution.py:115
  12.8 0.0 collective-permute-start.3
  12.8 0.1 collective-permute-done.4.refs_5_
  13.0 0.4 %collective-permute-start.5 = (bf16[2,3,128,128]{3,2,1,0:T(8,128)(2,1)S(1)}, bf16[2,3,128,128]{3,2,1,0:T(8,128)(2,1)S(1)}, u32[]{:S(2)}, u32[]{:S(2)}) collective-permute-start(bf16[2,3,128,128]{3,2,1,0:T(8,128)(2,1)S(1)} %collective-permute-done.4.refs_5_), channel_id=1, source_target_pairs={{0,8},{8,0},{16,24},{24,16},{1,9},{9,1},{17,25},{25,17},{2,10},{10... | collective-permute-start | bytes 589832 | tf_op jit(solution)/shard_map/ppermute | solution.py:115
  13.4 5.8 %collective-permute-done.1.refs_2_ = bf16[6,128,128]{2,1,0:T(8,128)(2,1)S(1)} collective-permute-done((bf16[6,128,128]{2,1,0:T(8,128)(2,1)S(1)}, bf16[6,128,128]{2,1,0:T(8,128)(2,1)S(1)}, u32[]{:S(2)}, u32[]{:S(2)}) %collective-permute-start.1) | collective-permute-done | bytes 196640 | tf_op jit(solution)/shard_map/ppermute | solution.py:115
  19.1 0.6 %collective-permute-start.6 = (bf16[6,128,128]{2,1,0:T(8,128)(2,1)S(1)}, bf16[6,128,128]{2,1,0:T(8,128)(2,1)S(1)}, u32[]{:S(2)}, u32[]{:S(2)}) collective-permute-start(bf16[6,128,128]{2,1,0:T(8,128)(2,1)S(1)} %collective-permute-done.1.refs_2_), channel_id=1, source_target_pairs={{0,2},{1,3},{2,0},{3,1},{4,6},{5,7},{6,4},{7,5},{8,10},{9,11},{10,... | collective-permute-start | bytes 589832 | tf_op jit(solution)/shard_map/ppermute | solution.py:115
  19.7 0.0 copy-done.2
  19.7 0.0 copy-start.1
  19.7 0.1 copy.6.ri_ref
  19.8 0.6 %copy-done.1 = s32[4,8,6]{1,0,2:T(4,128)S(1)} copy-done((s32[4,8,6]{1,0,2:T(4,128)S(1)}, s32[4,8,6]{1,0,2:T(4,128)}, u32[]{:S(2)}) %copy-start.1) | copy-done | bytes 792
  20.4 0.1 copy.5.li_ref
  20.5 0.1 pad_add_fusion.place_ref
  20.6 0.0 collective-permute-done.refs_1_
  20.6 0.0 collective-permute-done.3.refs_4_
  20.6 0.0 collective-permute-done.5.refs_6_
  20.6 3.4 %shard_map.46 = (f32[256,128]{1,0:T(8,128)S(1)}, f32[256,128]{1,0:T(8,128)S(1)}, bf16[2,3,128,128]{3,2,1,0:T(8,128)(2,1)S(1)}, s32[12]{0:T(128)S(1)}) custom-call(s32[3]{0:T(128)S(1)} %pad_add_fusion.place_ref, s32[4,8,6]{2,1,0:T(8,128)S(1)} %copy.5.li_ref, s32[4,8,2,3]{3,2,1,0:T(2,128)S(1)} %copy.6.ri_ref, bf16[6,128,128]{2,1,0:T(8,128)(2,1)S(1)} %bitcast.10, ...), custom_call_target="tpu_custom_call" | custom-call | flops 150994944 | bytes 589824 | tf_op jit(solution)/shard_map/pallas_call | solution.py:69
  24.0 0.8 %collective-permute-done.6.left_ref = bf16[6,128,128]{2,1,0:T(8,128)(2,1)S(1)} collective-permute-done((bf16[6,128,128]{2,1,0:T(8,128)(2,1)S(1)}, bf16[6,128,128]{2,1,0:T(8,128)(2,1)S(1)}, u32[]{:S(2)}, u32[]{:S(2)}) %collective-permute-start.6) | collective-permute-done | bytes 196640 | tf_op jit(solution)/shard_map/ppermute | solution.py:115
  24.8 0.8 %shard_map.48 = f32[256,128]{1,0:T(8,128)S(1)} custom-call(s32[12]{0:T(128)S(1)} %get-tuple-element.9.codes_ref, bf16[6,128,128]{2,1,0:T(8,128)(2,1)S(1)} %collective-permute-done.6.left_ref, bf16[2,3,128,128]{3,2,1,0:T(8,128)(2,1)S(1)} %get-tuple-element.10.right_ref, f32[256,128]{1,0:T(8,128)S(1)} %get-tuple-element.12.total_ref), custom_call_target="tpu_custom_call" | custom-call | flops 25165824 | bytes 196608 | tf_op jit(solution)/shard_map/pallas_call | solution.py:101
  25.6 1.5 %collective-permute-start.7 = (f32[256,128]{1,0:T(8,128)S(1)}, f32[256,128]{1,0:T(8,128)S(1)}, u32[]{:S(2)}, u32[]{:S(2)}) collective-permute-start(f32[256,128]{1,0:T(8,128)S(1)} %shard_map.48), channel_id=1, source_target_pairs={{0,1},{1,0},{2,3},{3,2},{4,5},{5,4},{6,7},{7,6},{8,9},{9,8},{10,11... | collective-permute-start | bytes 393224 | tf_op jit(solution)/shard_map/ppermute | solution.py:115
  27.1 0.7 %shard_map.47 = f32[256,128]{1,0:T(8,128)S(1)} custom-call(s32[12]{0:T(128)S(1)} %get-tuple-element.9.codes_ref, bf16[6,128,128]{2,1,0:T(8,128)(2,1)S(1)} %collective-permute-done.6.left_ref, bf16[2,3,128,128]{3,2,1,0:T(8,128)(2,1)S(1)} %get-tuple-element.10.right_ref, f32[256,128]{1,0:T(8,128)S(1)} %get-tuple-element.11.total_ref), custom_call_target="tpu_custom_call" | custom-call | flops 25165824 | bytes 196608 | tf_op jit(solution)/shard_map/pallas_call | solution.py:101
  27.8 2.7 %collective-permute-done.7 = f32[256,128]{1,0:T(8,128)S(1)} collective-permute-done((f32[256,128]{1,0:T(8,128)S(1)}, f32[256,128]{1,0:T(8,128)S(1)}, u32[]{:S(2)}, u32[]{:S(2)}) %collective-permute-start.7) | collective-permute-done | bytes 131104 | tf_op jit(solution)/shard_map/ppermute | solution.py:115
  30.6 0.7 %add_convert_fusion = bf16[256,128]{1,0:T(8,128)(2,1)} fusion(f32[256,128]{1,0:T(8,128)S(1)} %shard_map.47, f32[256,128]{1,0:T(8,128)S(1)} %collective-permute-done.7), kind=kLoop, calls=%fused_computation.1 | loop fusion | flops 65536 | bytes 327680 | tf_op jit(solution)/shard_map/convert_element_type | solution.py:145
  (1 shorter events, 0.0 us)
Async XLA Ops:
  1.0 5.8 %collective-permute-start.2 = (bf16[1,3,128,128]{3,2,1,0:T(8,128)(2,1)S(1)}, bf16[1,3,128,128]{3,2,1,0:T(8,128)(2,1)S(1)}, u32[]{:S(2)}, u32[]{:S(2)}) collective-permute-start(bf16[1,3,128,128]{3,2,1,0:T(8,128)(2,1)S(1)} %get-tuple-element.14), channel_id=1, source_target_pairs={{0,1},{1,0},{2,3},{3,2},{4,5},{5,4},{6,7},{7,6},{8,9},{9,8},{10,11... | collective-permute-start | bytes 294920 | tf_op jit(solution)/shard_map/ppermute | solution.py:115
  6.8 1.9 %copy-start = (bf16[1,1,6,128,128]{4,3,2,1,0:T(8,128)(2,1)S(1)}, bf16[1,1,6,128,128]{4,3,2,1,0:T(8,128)(2,1)}, u32[]{:S(2)}) copy-start(bf16[1,1,6,128,128]{4,3,2,1,0:T(8,128)(2,1)} %param.4) | copy-start | bytes 589828
  6.8 12.9 %copy-start.2 = (s32[4,8,2,3]{1,2,3,0:T(2,128)S(1)}, s32[4,8,2,3]{1,2,3,0:T(2,128)}, u32[]{:S(2)}) copy-start(s32[4,8,2,3]{1,2,3,0:T(2,128)} %param.7) | copy-start | bytes 2308
  6.8 6.2 %collective-permute-start.4 = (bf16[2,3,128,128]{3,2,1,0:T(8,128)(2,1)S(1)}, bf16[2,3,128,128]{3,2,1,0:T(8,128)(2,1)S(1)}, u32[]{:S(2)}, u32[]{:S(2)}) collective-permute-start(bf16[2,3,128,128]{3,2,1,0:T(8,128)(2,1)S(1)} %pad_maximum_fusion.refs_3_), channel_id=1, source_target_pairs={{0,16},{8,24},{16,0},{24,8},{1,17},{9,25},{17,1},{25,9},{2,18},{10... | collective-permute-start | bytes 589832 | tf_op jit(solution)/shard_map/ppermute | solution.py:115
  8.7 10.4 %collective-permute-start.1 = (bf16[6,128,128]{2,1,0:T(8,128)(2,1)S(1)}, bf16[6,128,128]{2,1,0:T(8,128)(2,1)S(1)}, u32[]{:S(2)}, u32[]{:S(2)}) collective-permute-start(bf16[6,128,128]{2,1,0:T(8,128)(2,1)S(1)} %bitcast.8), channel_id=1, source_target_pairs={{0,4},{1,5},{2,6},{3,7},{4,0},{5,1},{6,2},{7,3},{8,12},{9,13},{10,... | collective-permute-start | bytes 589832 | tf_op jit(solution)/shard_map/ppermute | solution.py:115
  11.3 9.3 %collective-permute-start = (bf16[6,128,128]{2,1,0:T(8,128)(2,1)S(1)}, bf16[6,128,128]{2,1,0:T(8,128)(2,1)S(1)}, u32[]{:S(2)}, u32[]{:S(2)}) collective-permute-start(bf16[6,128,128]{2,1,0:T(8,128)(2,1)S(1)} %bitcast.9), channel_id=1, source_target_pairs={{0,2},{1,3},{2,0},{3,1},{4,6},{5,7},{6,4},{7,5},{8,10},{9,11},{10,... | collective-permute-start | bytes 589832 | tf_op jit(solution)/shard_map/ppermute | solution.py:115
  12.8 7.7 %collective-permute-start.3 = (bf16[2,3,128,128]{3,2,1,0:T(8,128)(2,1)S(1)}, bf16[2,3,128,128]{3,2,1,0:T(8,128)(2,1)S(1)}, u32[]{:S(2)}, u32[]{:S(2)}) collective-permute-start(bf16[2,3,128,128]{3,2,1,0:T(8,128)(2,1)S(1)} %pad_maximum_fusion.refs_3_), channel_id=1, source_target_pairs={{0,8},{8,0},{16,24},{24,16},{1,9},{9,1},{17,25},{25,17},{2,10},{10... | collective-permute-start | bytes 589832 | tf_op jit(solution)/shard_map/ppermute | solution.py:115
  13.0 7.6 %collective-permute-start.5 = (bf16[2,3,128,128]{3,2,1,0:T(8,128)(2,1)S(1)}, bf16[2,3,128,128]{3,2,1,0:T(8,128)(2,1)S(1)}, u32[]{:S(2)}, u32[]{:S(2)}) collective-permute-start(bf16[2,3,128,128]{3,2,1,0:T(8,128)(2,1)S(1)} %collective-permute-done.4.refs_5_), channel_id=1, source_target_pairs={{0,8},{8,0},{16,24},{24,16},{1,9},{9,1},{17,25},{25,17},{2,10},{10... | collective-permute-start | bytes 589832 | tf_op jit(solution)/shard_map/ppermute | solution.py:115
  19.1 5.7 %collective-permute-start.6 = (bf16[6,128,128]{2,1,0:T(8,128)(2,1)S(1)}, bf16[6,128,128]{2,1,0:T(8,128)(2,1)S(1)}, u32[]{:S(2)}, u32[]{:S(2)}) collective-permute-start(bf16[6,128,128]{2,1,0:T(8,128)(2,1)S(1)} %collective-permute-done.1.refs_2_), channel_id=1, source_target_pairs={{0,2},{1,3},{2,0},{3,1},{4,6},{5,7},{6,4},{7,5},{8,10},{9,11},{10,... | collective-permute-start | bytes 589832 | tf_op jit(solution)/shard_map/ppermute | solution.py:115
  19.7 0.7 %copy-start.1 = (s32[4,8,6]{1,0,2:T(4,128)S(1)}, s32[4,8,6]{1,0,2:T(4,128)}, u32[]{:S(2)}) copy-start(s32[4,8,6]{1,0,2:T(4,128)} %param.5) | copy-start | bytes 2308
  25.6 5.0 %collective-permute-start.7 = (f32[256,128]{1,0:T(8,128)S(1)}, f32[256,128]{1,0:T(8,128)S(1)}, u32[]{:S(2)}, u32[]{:S(2)}) collective-permute-start(f32[256,128]{1,0:T(8,128)S(1)} %shard_map.48), channel_id=1, source_target_pairs={{0,1},{1,0},{2,3},{3,2},{4,5},{5,4},{6,7},{7,6},{8,9},{9,8},{10,11... | collective-permute-start | bytes 393224 | tf_op jit(solution)/shard_map/ppermute | solution.py:115

commit v5 on v4

--- a/solution.py
+++ b/solution.py
@@ -36,17 +36,18 @@
 def first_products(place, left_index, right_index, lefts, rights):
     slots, tile, _ = lefts[0].shape
     count = len(lefts)
-    inner = len(rights)
+    inner = rights[0].shape[0]
     right_slots = rights[0].shape[1]
 
     def kernel(place_ref, li_ref, ri_ref, *refs):
-        left_refs, right_refs = refs[:count], refs[count : count + inner]
-        totals = refs[count + inner : count + inner + 2]
-        last_ref, codes_ref, held = refs[count + inner + 2 :]
+        left_refs, right_refs = refs[:count], refs[count : count + 2]
+        totals = refs[count + 2 : count + 4]
+        last_ref, codes_ref, held = refs[count + 4 :]
         row, z, y = place_ref[0], place_ref[1], place_ref[2]
         for t in range(inner):
-            held[row ^ t] = right_refs[t][...]
-        zl = z ^ (inner - 1)
+            for side in range(2):
+                held[row ^ t, side] = right_refs[t % 2][t - t % 2 + side]
+        zl = lax.rem(z + 1, inner)
         last_ref[...] = held[zl]
         for side in range(2):
             column = 2 * z + (y if side == 0 else 1 - y)
@@ -54,7 +55,7 @@
             for slot in range(slots):
                 codes_ref[side * slots + slot] = match(li_ref, ri_ref, row, zl, y, column, slot)
             for s in range(count):
-                zp = z ^ s
+                zp = lax.rem(z - s + inner, inner)
 
                 @pl.loop(0, slots)
                 def _(slot):
@@ -73,7 +74,7 @@
             jax.ShapeDtypeStruct((2, right_slots, tile, tile), jnp.bfloat16),
             jax.ShapeDtypeStruct((2 * slots,), jnp.int32),
         ],
-        in_specs=[SMEM] * 3 + [VMEM] * (count + inner),
+        in_specs=[SMEM] * 3 + [VMEM] * (count + 2),
         out_specs=[VMEM] * 3 + [SMEM],
         scratch_shapes=[pltpu.VMEM((inner, 2, right_slots, tile, tile), jnp.bfloat16)],
         compiler_params=pltpu.CompilerParams(vmem_limit_bytes=32 * 1024 * 1024),
@@ -115,14 +116,19 @@
     return lax.ppermute(block, axis, route)
 
 
-def gather(block, axis, unit):
-    blocks = {0: block}
-    distance = lax.axis_size(axis) // unit // 2
-    while distance:
-        for s in sorted(blocks):
-            blocks[s ^ distance] = across(blocks[s], axis, unit * distance)
-        distance //= 2
-    return [blocks[s] for s in range(len(blocks))]
+def crossed(block, mask):
+    rows, cols = lax.axis_size("row"), lax.axis_size("col")
+    route = [(r * cols + c, (r ^ mask) * cols + (c ^ 1)) for r in range(rows) for c in range(cols)]
+    return lax.ppermute(block, ("row", "col"), route)
+
+
+def around(block):
+    cols = lax.axis_size("col")
+    route = [(c, (c + 2) % cols) for c in range(cols)]
+    blocks = [block]
+    for _ in range(cols // 2 - 1):
+        blocks.append(lax.ppermute(blocks[-1], "col", route))
+    return blocks
 
 
 def shards(left_tiles, left_index, right_tiles, right_index):
@@ -131,11 +137,15 @@
     z, y = col >> 1, col & 1
     right = right_tiles[0, 0]
 
-    lefts = gather(left_tiles[0, 0], "col", 2)
+    lefts = around(left_tiles[0, 0])
     given = lax.dynamic_index_in_dim(right, 1 - y, 0, keepdims=True)
     own = lax.dynamic_index_in_dim(right, y, 0, keepdims=True)
-    halves = jnp.concatenate([own, across(given, "col", 1)])
-    rights = gather(halves, "row", 1)
+    chips = []
+    for t in range(0, lax.axis_size("row"), 2):
+        chips.append(across(own, "row", t) if t else own)
+        chips.append(crossed(given, t))
+    chips = jnp.concatenate(chips)
+    rights = [chips, across(chips, "row", 1)]
 
     place = jnp.stack([row, z, y])
     mine, other, right_last, codes = first_products(place, left_index, right_index, lefts[:-1], rights)

time: 31.4 us -> 35.1 us (1.12)
  waiting for transfers between devices: 12.2 us -> 19.3 us
  starting transfers between devices: 11.6 us -> 8.42 us
  Pallas kernels: 4.9 us -> 4.5 us
    ppermute x0 -> x5, waiting for transfers between devices: none -> 14.9 us  [the longest x3 13.3 us: around(): blocks.append(lax.ppermute(blocks[-1], 'col', route))]
    ppermute x8 -> x3, starting transfers between devices: 11.6 us -> 3.33 us  [across(): return lax.ppermute(block, axis, route)]
    ppermute x8 -> x3, waiting for transfers between devices: 12.2 us -> 4.45 us  [across(): return lax.ppermute(block, axis, route)]
    ppermute x0 -> x5, starting transfers between devices: none -> 5.09 us  [the longest x2 3.08 us: crossed(): return lax.ppermute(block, ('row', 'col'), route)]
  transfers between devices with their start and end apart: 8 -> 8, of which waited for: 5 -> 6; matrix products, arithmetic and copies ran while one was open for 1% -> 1% of each run, Pallas kernels for 13% -> 11%
where the time goes in v5:
time: 35.1 us; the launch traced here: 34.9 us
  waiting for transfers between devices  19.3 us (55%)
  starting transfers between devices  8.42 us (24%)
  Pallas kernels  4.5 us (13%)
  local copies, waits for them, and re-layouts  1.8 us (5%)
  other arithmetic  0.78 us (2%)
    ppermute x3, waiting for transfers between devices, around(): blocks.append(lax.ppermute(blocks[-1], 'col', route))  13.3 us
    ppermute x3, waiting for transfers between devices, across(): return lax.ppermute(block, axis, route)  4.45 us
    ppermute x3, starting transfers between devices, across(): return lax.ppermute(block, axis, route)  3.33 us
    pallas_call x1, Pallas kernels, first_products(): pl.pallas_call(kernel, out_shape=[jax.ShapeDtypeStruct((RT * tile, tile),...  3.23 us
    ppermute x2, starting transfers between devices, crossed(): return lax.ppermute(block, ('row', 'col'), route)  3.08 us
    ppermute x3, starting transfers between devices, around(): blocks.append(lax.ppermute(blocks[-1], 'col', route))  2.01 us
    ppermute x2, waiting for transfers between devices, crossed(): return lax.ppermute(block, ('row', 'col'), route)  1.6 us
    pallas_call x2, Pallas kernels, last_products(): pl.pallas_call(kernel, out_shape=jax.ShapeDtypeStruct(total.shape, total....  1.27 us
  transfers between devices with their start and end apart: 8, of which 6 were waited for; matrix products, arithmetic and copies ran while one was open for 1% of the time, Pallas kernels for 11%

profile of v5, /device:TPU:0, one launch (start us, length us, event | category | flops | bytes accessed | tf_op | source)
XLA Modules:
  0.0 34.9 jit_solution(13531328943058647419)
XLA Ops:
  0.0 0.0 copy-start
  0.0 1.0 %dynamic-slice_bitcast_fusion.1 = (bf16[1,3,128,128]{3,2,1,0:T(8,128)(2,1)S(1)}, bf16[1,3,128,128]{3,2,1,0:T(8,128)(2,1)S(1)}) fusion(bf16[1,1,2,3,128,128]{5,4,3,2,1,0:T(8,128)(2,1)} %param.6, s32[]{:T(128)S(6)} %select_n.7, s32[]{:T(128)S(6)} %select_n.8), kind=kLoop, calls=%fused_computation.3 | loop fusion | bytes 393224 | tf_op jit(solution)/shard_map/jit(dynamic_index_in_dim)/dynamic_slice | solution.py:142
  1.0 3.0 %collective-permute-start.2 = (bf16[1,3,128,128]{3,2,1,0:T(8,128)(2,1)S(1)}, bf16[1,3,128,128]{3,2,1,0:T(8,128)(2,1)S(1)}, u32[]{:S(2)}, u32[]{:S(2)}) collective-permute-start(bf16[1,3,128,128]{3,2,1,0:T(8,128)(2,1)S(1)} %get-tuple-element.14), channel_id=1, source_target_pairs={{0,1},{1,0},{2,3},{3,2},{4,5},{5,4},{6,7},{7,6},{8,9},{9,8},{10,11... | collective-permute-start | bytes 294920 | tf_op jit(solution)/shard_map/ppermute | solution.py:122
  4.0 1.5 %collective-permute-start.3 = (bf16[1,3,128,128]{3,2,1,0:T(8,128)(2,1)S(1)}, bf16[1,3,128,128]{3,2,1,0:T(8,128)(2,1)S(1)}, u32[]{:S(2)}, u32[]{:S(2)}) collective-permute-start(bf16[1,3,128,128]{3,2,1,0:T(8,128)(2,1)S(1)} %get-tuple-element.13), channel_id=1, source_target_pairs={{0,16},{8,24},{16,0},{24,8},{1,17},{9,25},{17,1},{25,9},{2,18},{10... | collective-permute-start | bytes 294920 | tf_op jit(solution)/shard_map/ppermute | solution.py:116
  5.5 0.0 collective-permute-start.4
  5.6 0.0 copy-done
  5.6 2.0 %collective-permute-start = (bf16[6,128,128]{2,1,0:T(8,128)(2,1)S(1)}, bf16[6,128,128]{2,1,0:T(8,128)(2,1)S(1)}, u32[]{:S(2)}, u32[]{:S(2)}) collective-permute-start(bf16[6,128,128]{2,1,0:T(8,128)(2,1)S(1)} %bitcast.8), channel_id=1, source_target_pairs={{0,2},{1,3},{2,4},{3,5},{4,6},{5,7},{6,0},{7,1},{8,10},{9,11},{10,... | collective-permute-start | bytes 589832 | tf_op jit(solution)/shard_map/ppermute | solution.py:130
  7.6 0.0 collective-permute-done.2
  7.6 1.9 %collective-permute-done.3 = bf16[1,3,128,128]{3,2,1,0:T(8,128)(2,1)S(1)} collective-permute-done((bf16[1,3,128,128]{3,2,1,0:T(8,128)(2,1)S(1)}, bf16[1,3,128,128]{3,2,1,0:T(8,128)(2,1)S(1)}, u32[]{:S(2)}, u32[]{:S(2)}) %collective-permute-start.3) | collective-permute-done | bytes 98336 | tf_op jit(solution)/shard_map/ppermute | solution.py:116
  9.4 1.6 %collective-permute-done.4 = bf16[1,3,128,128]{3,2,1,0:T(8,128)(2,1)S(1)} collective-permute-done((bf16[1,3,128,128]{3,2,1,0:T(8,128)(2,1)S(1)}, bf16[1,3,128,128]{3,2,1,0:T(8,128)(2,1)S(1)}, u32[]{:S(2)}, u32[]{:S(2)}) %collective-permute-start.4) | collective-permute-done | bytes 98336 | tf_op jit(solution)/shard_map/ppermute | solution.py:122
  11.0 0.0 copy-start.2
  11.0 0.1 pad_maximum_fusion.refs_3_
  11.1 0.1 collective-permute-start.5
  11.2 2.5 %collective-permute-done.refs_1_ = bf16[6,128,128]{2,1,0:T(8,128)(2,1)S(1)} collective-permute-done((bf16[6,128,128]{2,1,0:T(8,128)(2,1)S(1)}, bf16[6,128,128]{2,1,0:T(8,128)(2,1)S(1)}, u32[]{:S(2)}, u32[]{:S(2)}) %collective-permute-start) | collective-permute-done | bytes 196640 | tf_op jit(solution)/shard_map/ppermute | solution.py:130
  13.7 0.0 collective-permute-start.1
  13.7 7.5 %collective-permute-done.1.refs_2_ = bf16[6,128,128]{2,1,0:T(8,128)(2,1)S(1)} collective-permute-done((bf16[6,128,128]{2,1,0:T(8,128)(2,1)S(1)}, bf16[6,128,128]{2,1,0:T(8,128)(2,1)S(1)}, u32[]{:S(2)}, u32[]{:S(2)}) %collective-permute-start.1) | collective-permute-done | bytes 196640 | tf_op jit(solution)/shard_map/ppermute | solution.py:130
  21.1 0.0 collective-permute-start.6
  21.1 0.0 copy-done.2
  21.1 0.0 copy-start.1
  21.1 0.1 copy.6.ri_ref
  21.3 0.6 %copy-done.1 = s32[4,8,6]{1,0,2:T(4,128)S(1)} copy-done((s32[4,8,6]{1,0,2:T(4,128)S(1)}, s32[4,8,6]{1,0,2:T(4,128)}, u32[]{:S(2)}) %copy-start.1) | copy-done | bytes 792
  21.8 0.1 copy.5.li_ref
  21.9 0.1 pad_add_fusion.place_ref
  22.0 0.0 collective-permute-done.5.refs_4_
  22.0 3.2 %shard_map.46 = (f32[256,128]{1,0:T(8,128)S(1)}, f32[256,128]{1,0:T(8,128)S(1)}, bf16[2,3,128,128]{3,2,1,0:T(8,128)(2,1)S(1)}, s32[12]{0:T(128)S(1)}) custom-call(s32[3]{0:T(128)S(1)} %pad_add_fusion.place_ref, s32[4,8,6]{2,1,0:T(8,128)S(1)} %copy.5.li_ref, s32[4,8,2,3]{3,2,1,0:T(2,128)S(1)} %copy.6.ri_ref, bf16[6,128,128]{2,1,0:T(8,128)(2,1)S(1)} %bitcast.9, ...), custom_call_target="tpu_custom_call" | custom-call | flops 150994944 | bytes 589824 | tf_op jit(solution)/shard_map/pallas_call | solution.py:70
  25.3 3.3 %collective-permute-done.6.left_ref = bf16[6,128,128]{2,1,0:T(8,128)(2,1)S(1)} collective-permute-done((bf16[6,128,128]{2,1,0:T(8,128)(2,1)S(1)}, bf16[6,128,128]{2,1,0:T(8,128)(2,1)S(1)}, u32[]{:S(2)}, u32[]{:S(2)}) %collective-permute-start.6) | collective-permute-done | bytes 196640 | tf_op jit(solution)/shard_map/ppermute | solution.py:130
  28.6 0.6 %shard_map.48 = f32[256,128]{1,0:T(8,128)S(1)} custom-call(s32[12]{0:T(128)S(1)} %get-tuple-element.9.codes_ref, bf16[6,128,128]{2,1,0:T(8,128)(2,1)S(1)} %collective-permute-done.6.left_ref, bf16[2,3,128,128]{3,2,1,0:T(8,128)(2,1)S(1)} %get-tuple-element.10.right_ref, f32[256,128]{1,0:T(8,128)S(1)} %get-tuple-element.12.total_ref), custom_call_target="tpu_custom_call" | custom-call | flops 25165824 | bytes 196608 | tf_op jit(solution)/shard_map/pallas_call | solution.py:102
  29.2 1.8 %collective-permute-start.7 = (f32[256,128]{1,0:T(8,128)S(1)}, f32[256,128]{1,0:T(8,128)S(1)}, u32[]{:S(2)}, u32[]{:S(2)}) collective-permute-start(f32[256,128]{1,0:T(8,128)S(1)} %shard_map.48), channel_id=1, source_target_pairs={{0,1},{1,0},{2,3},{3,2},{4,5},{5,4},{6,7},{7,6},{8,9},{9,8},{10,11... | collective-permute-start | bytes 393224 | tf_op jit(solution)/shard_map/ppermute | solution.py:116
  31.0 0.7 %shard_map.47 = f32[256,128]{1,0:T(8,128)S(1)} custom-call(s32[12]{0:T(128)S(1)} %get-tuple-element.9.codes_ref, bf16[6,128,128]{2,1,0:T(8,128)(2,1)S(1)} %collective-permute-done.6.left_ref, bf16[2,3,128,128]{3,2,1,0:T(8,128)(2,1)S(1)} %get-tuple-element.10.right_ref, f32[256,128]{1,0:T(8,128)S(1)} %get-tuple-element.11.total_ref), custom_call_target="tpu_custom_call" | custom-call | flops 25165824 | bytes 196608 | tf_op jit(solution)/shard_map/pallas_call | solution.py:102
  31.6 2.6 %collective-permute-done.7 = f32[256,128]{1,0:T(8,128)S(1)} collective-permute-done((f32[256,128]{1,0:T(8,128)S(1)}, f32[256,128]{1,0:T(8,128)S(1)}, u32[]{:S(2)}, u32[]{:S(2)}) %collective-permute-start.7) | collective-permute-done | bytes 131104 | tf_op jit(solution)/shard_map/ppermute | solution.py:116
  34.2 0.7 %add_convert_fusion = bf16[256,128]{1,0:T(8,128)(2,1)} fusion(f32[256,128]{1,0:T(8,128)S(1)} %shard_map.47, f32[256,128]{1,0:T(8,128)S(1)} %collective-permute-done.7), kind=kLoop, calls=%fused_computation.1 | loop fusion | flops 65536 | bytes 327680 | tf_op jit(solution)/shard_map/convert_element_type | solution.py:155
Async XLA Ops:
  0.0 5.6 %copy-start = (bf16[1,1,6,128,128]{4,3,2,1,0:T(8,128)(2,1)S(1)}, bf16[1,1,6,128,128]{4,3,2,1,0:T(8,128)(2,1)}, u32[]{:S(2)}) copy-start(bf16[1,1,6,128,128]{4,3,2,1,0:T(8,128)(2,1)} %param.4) | copy-start | bytes 589828
  1.0 6.6 %collective-permute-start.2 = (bf16[1,3,128,128]{3,2,1,0:T(8,128)(2,1)S(1)}, bf16[1,3,128,128]{3,2,1,0:T(8,128)(2,1)S(1)}, u32[]{:S(2)}, u32[]{:S(2)}) collective-permute-start(bf16[1,3,128,128]{3,2,1,0:T(8,128)(2,1)S(1)} %get-tuple-element.14), channel_id=1, source_target_pairs={{0,1},{1,0},{2,3},{3,2},{4,5},{5,4},{6,7},{7,6},{8,9},{9,8},{10,11... | collective-permute-start | bytes 294920 | tf_op jit(solution)/shard_map/ppermute | solution.py:122
  4.0 5.4 %collective-permute-start.3 = (bf16[1,3,128,128]{3,2,1,0:T(8,128)(2,1)S(1)}, bf16[1,3,128,128]{3,2,1,0:T(8,128)(2,1)S(1)}, u32[]{:S(2)}, u32[]{:S(2)}) collective-permute-start(bf16[1,3,128,128]{3,2,1,0:T(8,128)(2,1)S(1)} %get-tuple-element.13), channel_id=1, source_target_pairs={{0,16},{8,24},{16,0},{24,8},{1,17},{9,25},{17,1},{25,9},{2,18},{10... | collective-permute-start | bytes 294920 | tf_op jit(solution)/shard_map/ppermute | solution.py:116
  5.5 5.5 %collective-permute-start.4 = (bf16[1,3,128,128]{3,2,1,0:T(8,128)(2,1)S(1)}, bf16[1,3,128,128]{3,2,1,0:T(8,128)(2,1)S(1)}, u32[]{:S(2)}, u32[]{:S(2)}) collective-permute-start(bf16[1,3,128,128]{3,2,1,0:T(8,128)(2,1)S(1)} %get-tuple-element.14), channel_id=1, source_target_pairs={{0,17},{1,16},{2,19},{3,18},{4,21},{5,20},{6,23},{7,22},{8,25},{9,... | collective-permute-start | bytes 294920 | tf_op jit(solution)/shard_map/ppermute | solution.py:122
  5.6 8.1 %collective-permute-start = (bf16[6,128,128]{2,1,0:T(8,128)(2,1)S(1)}, bf16[6,128,128]{2,1,0:T(8,128)(2,1)S(1)}, u32[]{:S(2)}, u32[]{:S(2)}) collective-permute-start(bf16[6,128,128]{2,1,0:T(8,128)(2,1)S(1)} %bitcast.8), channel_id=1, source_target_pairs={{0,2},{1,3},{2,4},{3,5},{4,6},{5,7},{6,0},{7,1},{8,10},{9,11},{10,... | collective-permute-start | bytes 589832 | tf_op jit(solution)/shard_map/ppermute | solution.py:130
  11.0 10.1 %copy-start.2 = (s32[4,8,2,3]{1,2,3,0:T(2,128)S(1)}, s32[4,8,2,3]{1,2,3,0:T(2,128)}, u32[]{:S(2)}) copy-start(s32[4,8,2,3]{1,2,3,0:T(2,128)} %param.7) | copy-start | bytes 2308
  11.1 10.9 %collective-permute-start.5 = (bf16[4,3,128,128]{3,2,1,0:T(8,128)(2,1)S(1)}, bf16[4,3,128,128]{3,2,1,0:T(8,128)(2,1)S(1)}, u32[]{:S(2)}, u32[]{:S(2)}) collective-permute-start(bf16[4,3,128,128]{3,2,1,0:T(8,128)(2,1)S(1)} %pad_maximum_fusion.refs_3_), channel_id=1, source_target_pairs={{0,8},{8,0},{16,24},{24,16},{1,9},{9,1},{17,25},{25,17},{2,10},{10... | collective-permute-start | bytes 1179656 | tf_op jit(solution)/shard_map/ppermute | solution.py:116
  13.7 7.5 %collective-permute-start.1 = (bf16[6,128,128]{2,1,0:T(8,128)(2,1)S(1)}, bf16[6,128,128]{2,1,0:T(8,128)(2,1)S(1)}, u32[]{:S(2)}, u32[]{:S(2)}) collective-permute-start(bf16[6,128,128]{2,1,0:T(8,128)(2,1)S(1)} %collective-permute-done.refs_1_), channel_id=1, source_target_pairs={{0,2},{1,3},{2,4},{3,5},{4,6},{5,7},{6,0},{7,1},{8,10},{9,11},{10,... | collective-permute-start | bytes 589832 | tf_op jit(solution)/shard_map/ppermute | solution.py:130
  21.1 7.5 %collective-permute-start.6 = (bf16[6,128,128]{2,1,0:T(8,128)(2,1)S(1)}, bf16[6,128,128]{2,1,0:T(8,128)(2,1)S(1)}, u32[]{:S(2)}, u32[]{:S(2)}) collective-permute-start(bf16[6,128,128]{2,1,0:T(8,128)(2,1)S(1)} %collective-permute-done.1.refs_2_), channel_id=1, source_target_pairs={{0,2},{1,3},{2,4},{3,5},{4,6},{5,7},{6,0},{7,1},{8,10},{9,11},{10,... | collective-permute-start | bytes 589832 | tf_op jit(solution)/shard_map/ppermute | solution.py:130
  21.1 0.7 %copy-start.1 = (s32[4,8,6]{1,0,2:T(4,128)S(1)}, s32[4,8,6]{1,0,2:T(4,128)}, u32[]{:S(2)}) copy-start(s32[4,8,6]{1,0,2:T(4,128)} %param.5) | copy-start | bytes 2308
  29.2 5.0 %collective-permute-start.7 = (f32[256,128]{1,0:T(8,128)S(1)}, f32[256,128]{1,0:T(8,128)S(1)}, u32[]{:S(2)}, u32[]{:S(2)}) collective-permute-start(f32[256,128]{1,0:T(8,128)S(1)} %shard_map.48), channel_id=1, source_target_pairs={{0,1},{1,0},{2,3},{3,2},{4,5},{5,4},{6,7},{7,6},{8,9},{9,8},{10,11... | collective-permute-start | bytes 393224 | tf_op jit(solution)/shard_map/ppermute | solution.py:116

commit v6 on v1

v6 whole, which is shorter than its diff:
```python
import jax
import jax.numpy as jnp
from jax import lax
from jax.experimental import pallas as pl
from jax.experimental.pallas import tpu as pltpu
from jax.sharding import PartitionSpec as P

KT = 8
RT = 2
CUT = 4
SMEM = pl.BlockSpec(memory_space=pltpu.SMEM)
VMEM = pl.BlockSpec(memory_space=pltpu.VMEM)


def find_matches(place, left_index, right_index):
    slots = left_index.shape[-1]
    inner, _, _, right_slots = right_index.shape

    def kernel(place_ref, li_ref, ri_ref, codes_ref):
        row, z, y = place_ref[0], place_ref[1], place_ref[2]

        @pl.loop(0, inner)
        def _(s):
            zp = z ^ s
            for side in range(2):
                column = 2 * z + (y if side == 0 else 1 - y)
                have = [ri_ref[zp, column, y, t] for t in range(right_slots)]
                for slot in range(slots):
                    at = li_ref[row, 2 * zp + y, slot]
                    k = lax.rem(at, KT)
                    first = 1 + lax.div(at, KT) * right_slots
                    code = jnp.int32(0)
                    for t in range(right_slots):
                        code = jnp.where(have[t] == k, first + t, code)
                    codes_ref[(s * 2 + side) * slots + slot] = jnp.where(at < RT * KT, code, 0)

    return pl.pallas_call(
        kernel,
        out_shape=jax.ShapeDtypeStruct((inner * 2 * slots,), jnp.int32),
        in_specs=[SMEM] * 3,
        out_specs=SMEM,
    )(place, left_index, right_index)


def add_part(codes_ref, s, side, start, slots, left_ref, right_at, right_slots, total_ref):
    tile = total_ref.shape[1]

    @pl.loop(0, left_ref.shape[0])
    def _(slot):
        code = codes_ref[(s * 2 + side) * slots + start + slot]

        @pl.when(code > 0)
        def _():
            i = lax.div(code - 1, right_slots)
            rows = pl.ds(pl.multiple_of(i * tile, tile), tile)
            total_ref[rows, :] += jnp.dot(
                left_ref[slot],
                right_at(lax.rem(code - 1, right_slots)),
                preferred_element_type=jnp.float32,
            )


def first_products(place, codes, lefts, rights, slots):
    parts = [(s, part) for s, block in lefts for part in block]
    count = len(parts)
    inner = len(rights)
    _, right_slots, tile, _ = rights[0].shape

    def kernel(place_ref, codes_ref, *refs):
        right_refs = refs[count : count + inner]
        totals = refs[count + inner : count + inner + 2]
        last_ref, held = refs[count + inner + 2 :]
        row, z = place_ref[0], place_ref[1]
        for t in range(inner):
            held[row ^ t] = right_refs[t][...]
        last_ref[...] = held[z ^ (inner - 1)]
        for side in range(2):
            totals[side][...] = jnp.zeros_like(totals[side])
            start, before = 0, None
            for (s, _), left_ref in zip(parts, refs):
                start = start if s == before else 0
                add_part(
                    codes_ref, s, side, start, slots, left_ref,
                    lambda found, s=s: held[z ^ s, side, found], right_slots, totals[side],
                )
                start, before = start + left_ref.shape[0], s

    return pl.pallas_call(
        kernel,
        out_shape=[jax.ShapeDtypeStruct((RT * tile, tile), jnp.float32)] * 2
        + [jax.ShapeDtypeStruct((2, right_slots, tile, tile), jnp.bfloat16)],
        in_specs=[SMEM] * 2 + [VMEM] * (count + inner),
        out_specs=[VMEM] * 3,
        scratch_shapes=[pltpu.VMEM((inner, 2, right_slots, tile, tile), jnp.bfloat16)],
        compiler_params=pltpu.CompilerParams(vmem_limit_bytes=32 * 1024 * 1024),
        cost_estimate=pl.CostEstimate(
            flops=4 * inner * slots * tile**3, bytes_accessed=2 * inner * slots * tile**2, transcendentals=0
        ),
    )(place, codes, *[part for _, part in parts], *rights)


def last_products(codes, s, parts, right, total, side, slots):
    count = len(parts)
    right_slots = right.shape[1]

    def kernel(codes_ref, *refs):
        right_ref, total_ref, out_ref = refs[count:]
        out_ref[...] = total_ref[...]
        start = 0
        for left_ref in refs[:count]:
            add_part(
                codes_ref, s, side, start, slots, left_ref,
                lambda found: right_ref[side, found], right_slots, out_ref,
            )
            start += left_ref.shape[0]

    return pl.pallas_call(
        kernel,
        out_shape=jax.ShapeDtypeStruct(total.shape, total.dtype),
        in_specs=[SMEM] + [VMEM] * (count + 2),
        out_specs=VMEM,
        compiler_params=pltpu.CompilerParams(vmem_limit_bytes=16 * 1024 * 1024),
        cost_estimate=pl.CostEstimate(
            flops=2 * slots * 128**3, bytes_accessed=2 * slots * 128**2, transcendentals=0
        ),
    )(codes, *parts, right, total)


def across(block, axis, mask):
    route = [(i, i ^ mask) for i in range(lax.axis_size(axis))]
    return lax.ppermute(block, axis, route)


def crossed(block, mask):
    rows, cols = lax.axis_size("row"), lax.axis_size("col")
    route = [(r * cols + c, (r ^ mask) * cols + (c ^ 1)) for r in range(rows) for c in range(cols)]
    return lax.ppermute(block, ("row", "col"), route)


def gather(block, cut):
    distance = lax.axis_size("col") // 4
    far_head = across(block[:cut], "col", 2 * distance)
    tail, _ = lax.optimization_barrier((block[cut:], far_head))
    far_tail = across(tail, "col", 2 * distance)
    blocks = {0: (block,), distance: (far_head, far_tail)}
    near = distance // 2
    while near:
        for s in sorted(blocks):
            blocks[s ^ near] = tuple(across(part, "col", 2 * near) for part in blocks[s])
        near //= 2
    return sorted(blocks.items())


def shards(left_tiles, left_index, right_tiles, right_index):
    row = lax.axis_index("row")
    col = lax.axis_index("col")
    z, y = col >> 1, col & 1
    left = left_tiles[0, 0]
    right = right_tiles[0, 0]
    slots = left.shape[0]

    lefts = gather(left, CUT)
    given = lax.dynamic_index_in_dim(right, 1 - y, 0, keepdims=True)
    own = lax.dynamic_index_in_dim(right, y, 0, keepdims=True)
    rights = []
    for t in range(0, lax.axis_size("row"), 2):
        pair = jnp.concatenate([across(own, "row", t) if t else own, crossed(given, t)])
        rights += [pair, across(pair, "row", 1)]

    place = jnp.stack([row, z, y])
    codes = find_matches(place, left_index, right_index)
    mine, other, right_last = first_products(place, codes, lefts[:-1], rights, slots)
    far, final = lefts[-1]
    other = last_products(codes, far, final, right_last, other, 1, slots)
    coming = across(other, "col", 1)
    mine = last_products(codes, far, final, right_last, mine, 0, slots)
    return (mine + coming).astype(jnp.bfloat16)


def solution(mesh):
    return jax.shard_map(
        shards,
        mesh=mesh,
        in_specs=(
            P("row", "col", None, None, None),
            P(),
            P("row", "col", None, None, None, None),
            P(),
        ),
        out_specs=P("row", "col"),
        check_vma=False,
    )
```

time: 68.3 us -> 35.2 us (0.52)
  waiting for transfers between devices: 38 us -> 6.93 us
  starting transfers between devices: 0.01 us -> 17.5 us
  between operations: 13.4 us -> 0.14 us
  blocking collectives: 10.2 us -> 0 us
  Pallas kernels: 3.23 us -> 5.85 us
  other arithmetic: 0 us -> 1.33 us
    all_gather x1 -> x0, waiting for transfers between devices: 37.3 us -> none  [shards(): left = lax.all_gather(left_tiles[0], 'col', axis=0, tiled=True)]
    ppermute x0 -> x11, starting transfers between devices: none -> 17.5 us  [the longest x9 13 us: across(): return lax.ppermute(block, axis, route)]
    all_gather x1 -> x0, blocking collectives: 10.2 us -> none  [shards(): right = lax.all_gather(right_tiles[0, 0], 'row', axis=0, tiled=True)]
    ppermute x0 -> x11, waiting for transfers between devices: none -> 6.93 us  [the longest x9 6.92 us: across(): return lax.ppermute(block, axis, route)]
    pallas_call x1 -> x4, Pallas kernels: 3.23 us -> 5.85 us  [the longest x1 2.35 us: find_matches(): pl.pallas_call(kernel, out_shape=jax.ShapeDtypeStruct((inner * 2 * slots,...]
    dynamic_slice x0 -> x1, local copies, waits for them, and re-layouts: none -> 0.99 us  [shards(): own = lax.dynamic_index_in_dim(right, y, 0, keepdims=True)]
    unnamed x4 -> x13, local copies, waits for them, and re-layouts: 3.03 us -> 2.12 us
    unnamed x1 -> x0, waiting for transfers between devices: 0.71 us -> none
  transfers between devices with their start and end apart: 1 -> 11, of which waited for: 1 -> 3; matrix products, arithmetic and copies ran while one was open for 2% -> 6% of each run, Pallas kernels for 0% -> 15%
where the time goes in v6:
time: 35.2 us; the launch traced here: 34.9 us
  starting transfers between devices  17.5 us (50%)
  waiting for transfers between devices  6.93 us (20%)
  Pallas kernels  5.85 us (17%)
  local copies, waits for them, and re-layouts  3.15 us (9%)
  other arithmetic  1.33 us (4%)
    ppermute x9, starting transfers between devices, across(): return lax.ppermute(block, axis, route)  13 us
    ppermute x9, waiting for transfers between devices, across(): return lax.ppermute(block, axis, route)  6.92 us
    ppermute x2, starting transfers between devices, crossed(): return lax.ppermute(block, ('row', 'col'), route)  4.47 us
    pallas_call x1, Pallas kernels, find_matches(): pl.pallas_call(kernel, out_shape=jax.ShapeDtypeStruct((inner * 2 * slots,...  2.35 us
    unnamed x13, local copies, waits for them, and re-layouts  2.12 us
    pallas_call x1, Pallas kernels, first_products(): pl.pallas_call(kernel, out_shape=[jax.ShapeDtypeStruct((RT * tile, tile),...  2.03 us
    pallas_call x2, Pallas kernels, last_products(): pl.pallas_call(kernel, out_shape=jax.ShapeDtypeStruct(total.shape, total....  1.46 us
    dynamic_slice x1, local copies, waits for them, and re-layouts, shards(): own = lax.dynamic_index_in_dim(right, y, 0, keepdims=True)  0.99 us
  transfers between devices with their start and end apart: 11, of which 3 were waited for; matrix products, arithmetic and copies ran while one was open for 6% of the time, Pallas kernels for 15%

profile of v6, /device:TPU:0, one launch (start us, length us, event | category | flops | bytes accessed | tf_op | source)
XLA Modules:
  0.0 34.9 jit_solution(2507016613443958263)
XLA Ops:
  0.0 0.0 copy-start
  0.0 1.0 %dynamic-slice_bitcast_fusion.1 = (bf16[1,3,128,128]{3,2,1,0:T(8,128)(2,1)S(1)}, bf16[1,3,128,128]{3,2,1,0:T(8,128)(2,1)S(1)}) fusion(bf16[1,1,2,3,128,128]{5,4,3,2,1,0:T(8,128)(2,1)} %param.6, s32[]{:T(128)S(6)} %select_n.7, s32[]{:T(128)S(6)} %select_n.8), kind=kLoop, calls=%fused_computation.4 | loop fusion | bytes 393224 | tf_op jit(solution)/shard_map/jit(dynamic_index_in_dim)/dynamic_slice | solution.py:164
  1.0 4.0 %collective-permute-start.8 = (bf16[1,3,128,128]{3,2,1,0:T(8,128)(2,1)S(1)}, bf16[1,3,128,128]{3,2,1,0:T(8,128)(2,1)S(1)}, u32[]{:S(2)}, u32[]{:S(2)}) collective-permute-start(bf16[1,3,128,128]{3,2,1,0:T(8,128)(2,1)S(1)} %get-tuple-element.14), channel_id=1, source_target_pairs={{0,17},{1,16},{2,19},{3,18},{4,21},{5,20},{6,23},{7,22},{8,25},{9,... | collective-permute-start | bytes 294920 | tf_op jit(solution)/shard_map/ppermute | solution.py:137
  5.0 0.5 %collective-permute-start.5 = (bf16[1,3,128,128]{3,2,1,0:T(8,128)(2,1)S(1)}, bf16[1,3,128,128]{3,2,1,0:T(8,128)(2,1)S(1)}, u32[]{:S(2)}, u32[]{:S(2)}) collective-permute-start(bf16[1,3,128,128]{3,2,1,0:T(8,128)(2,1)S(1)} %get-tuple-element.14), channel_id=1, source_target_pairs={{0,1},{1,0},{2,3},{3,2},{4,5},{5,4},{6,7},{7,6},{8,9},{9,8},{10,11... | collective-permute-start | bytes 294920 | tf_op jit(solution)/shard_map/ppermute | solution.py:137
  5.5 0.1 collective-permute-start.7
  5.6 0.0 copy-done
  5.6 3.1 %collective-permute-start = (bf16[4,128,128]{2,1,0:T(8,128)(2,1)S(1)}, bf16[4,128,128]{2,1,0:T(8,128)(2,1)S(1)}, u32[]{:S(2)}, u32[]{:S(2)}) collective-permute-start(bf16[4,128,128]{2,1,0:T(8,128)(2,1)S(1)} %slice_bitcast_fusion), channel_id=1, source_target_pairs={{0,4},{1,5},{2,6},{3,7},{4,0},{5,1},{6,2},{7,3},{8,12},{9,13},{10,... | collective-permute-start | bytes 393224 | tf_op jit(solution)/shard_map/ppermute | solution.py:131
  8.7 1.6 %collective-permute-start.4 = (bf16[6,128,128]{2,1,0:T(8,128)(2,1)S(1)}, bf16[6,128,128]{2,1,0:T(8,128)(2,1)S(1)}, u32[]{:S(2)}, u32[]{:S(2)}) collective-permute-start(bf16[6,128,128]{2,1,0:T(8,128)(2,1)S(1)} %bitcast.12), channel_id=1, source_target_pairs={{0,2},{1,3},{2,0},{3,1},{4,6},{5,7},{6,4},{7,5},{8,10},{9,11},{10,... | collective-permute-start | bytes 589832 | tf_op jit(solution)/shard_map/ppermute | solution.py:131
  10.2 0.0 collective-permute-done.7
  10.3 0.0 collective-permute-done.8
  10.3 0.1 collective-permute-start.9
  10.4 0.0 collective-permute-done.5
  10.4 0.5 %collective-permute-start.6 = (bf16[2,3,128,128]{3,2,1,0:T(8,128)(2,1)S(1)}, bf16[2,3,128,128]{3,2,1,0:T(8,128)(2,1)S(1)}, u32[]{:S(2)}, u32[]{:S(2)}) collective-permute-start(bf16[2,3,128,128]{3,2,1,0:T(8,128)(2,1)S(1)} %pad_maximum_fusion.refs_4_), channel_id=1, source_target_pairs={{0,8},{8,0},{16,24},{24,16},{1,9},{9,1},{17,25},{25,17},{2,10},{10... | collective-permute-start | bytes 589832 | tf_op jit(solution)/shard_map/ppermute | solution.py:131
  11.0 0.0 copy-start.4
  11.0 2.9 %collective-permute-done.refs_2_ = bf16[4,128,128]{2,1,0:T(8,128)(2,1)S(1)} collective-permute-done((bf16[4,128,128]{2,1,0:T(8,128)(2,1)S(1)}, bf16[4,128,128]{2,1,0:T(8,128)(2,1)S(1)}, u32[]{:S(2)}, u32[]{:S(2)}) %collective-permute-start) | collective-permute-done | bytes 131104 | tf_op jit(solution)/shard_map/ppermute | solution.py:131
  13.8 2.2 %collective-permute-start.2 = (bf16[2,128,128]{2,1,0:T(8,128)(2,1)S(1)}, bf16[2,128,128]{2,1,0:T(8,128)(2,1)S(1)}, u32[]{:S(2)}, u32[]{:S(2)}) collective-permute-start(bf16[2,128,128]{2,1,0:T(8,128)(2,1)S(1)} %slice_bitcast_fusion.1), channel_id=1, source_target_pairs={{0,4},{1,5},{2,6},{3,7},{4,0},{5,1},{6,2},{7,3},{8,12},{9,13},{10,... | collective-permute-start | bytes 196616 | tf_op jit(solution)/shard_map/ppermute | solution.py:131
  16.0 2.3 %collective-permute-start.1 = (bf16[4,128,128]{2,1,0:T(8,128)(2,1)S(1)}, bf16[4,128,128]{2,1,0:T(8,128)(2,1)S(1)}, u32[]{:S(2)}, u32[]{:S(2)}) collective-permute-start(bf16[4,128,128]{2,1,0:T(8,128)(2,1)S(1)} %collective-permute-done.refs_2_), channel_id=1, source_target_pairs={{0,2},{1,3},{2,0},{3,1},{4,6},{5,7},{6,4},{7,5},{8,10},{9,11},{10,... | collective-permute-start | bytes 393224 | tf_op jit(solution)/shard_map/ppermute | solution.py:131
  18.3 1.1 %collective-permute-done.2.refs_3_ = bf16[2,128,128]{2,1,0:T(8,128)(2,1)S(1)} collective-permute-done((bf16[2,128,128]{2,1,0:T(8,128)(2,1)S(1)}, bf16[2,128,128]{2,1,0:T(8,128)(2,1)S(1)}, u32[]{:S(2)}, u32[]{:S(2)}) %collective-permute-start.2) | collective-permute-done | bytes 65568 | tf_op jit(solution)/shard_map/ppermute | solution.py:131
  19.4 1.9 %collective-permute-start.3 = (bf16[2,128,128]{2,1,0:T(8,128)(2,1)S(1)}, bf16[2,128,128]{2,1,0:T(8,128)(2,1)S(1)}, u32[]{:S(2)}, u32[]{:S(2)}) collective-permute-start(bf16[2,128,128]{2,1,0:T(8,128)(2,1)S(1)} %collective-permute-done.2.refs_3_), channel_id=1, source_target_pairs={{0,2},{1,3},{2,0},{3,1},{4,6},{5,7},{6,4},{7,5},{8,10},{9,11},{10,... | collective-permute-start | bytes 196616 | tf_op jit(solution)/shard_map/ppermute | solution.py:131
  21.3 0.7 %pad_add_fusion.place_ref = s32[3]{0:T(128)} fusion(s32[1]{0:T(128)} %bitcast.2, s32[1]{0:T(128)} %bitcast.1, s32[1]{0:T(128)} %bitcast), kind=kLoop, calls=%fused_computation.8 | loop fusion | flops 6 | bytes 24 | tf_op jit(solution)/shard_map/stack | solution.py:170
  21.9 0.0 copy-done.4
  22.0 0.0 copy-start.3
  22.0 0.7 %copy.6.ri_ref = s32[4,8,2,3]{3,2,1,0:T(2,128)} copy(s32[4,8,2,3]{1,2,3,0:T(2,128)S(1)} %copy-done.4) | data formatting | bytes 1536 | tf_op args[3]
  22.7 0.0 copy-done.3
  22.7 0.7 %copy.5.li_ref = s32[4,8,6]{2,1,0:T(8,128)} copy(s32[4,8,6]{1,0,2:T(4,128)S(1)} %copy-done.3) | data formatting | bytes 1536 | tf_op args[1]
  23.4 0.0 copy-start.2
  23.4 2.4 %shard_map.46.codes_ref = s32[48]{0:T(128)} custom-call(s32[3]{0:T(128)} %pad_add_fusion.place_ref, s32[4,8,6]{2,1,0:T(8,128)} %copy.5.li_ref, s32[4,8,2,3]{3,2,1,0:T(2,128)} %copy.6.ri_ref), custom_call_target="tpu_custom_call" | custom-call | tf_op jit(solution)/shard_map/pallas_call | solution.py:37
  25.8 0.0 collective-permute-done.4.refs_1_
  25.8 0.0 collective-permute-done.9.refs_7_
  25.8 0.0 collective-permute-done.6.refs_5_
  25.8 0.0 copy-done.2
  25.8 0.0 copy-start.1
  25.8 0.7 %copy-done.1 = s32[48]{0:T(128)S(1)} copy-done((s32[48]{0:T(128)S(1)}, s32[48]{0:T(128)}, u32[]{:S(2)}) %copy-start.1) | copy-done | bytes 216
  26.5 2.0 %shard_map.47 = (f32[256,128]{1,0:T(8,128)S(1)}, f32[256,128]{1,0:T(8,128)S(1)}, bf16[2,3,128,128]{3,2,1,0:T(8,128)(2,1)S(1)}) custom-call(s32[3]{0:T(128)S(1)} %copy-done.2, s32[48]{0:T(128)S(1)} %copy-done.1, bf16[6,128,128]{2,1,0:T(8,128)(2,1)S(1)} %bitcast.13, bf16[6,128,128]{2,1,0:T(8,128)(2,1)S(1)} %collective-permute-done.4.refs_1_, ...), custom_call_target="tpu_custom_call" | custom-call | flops 201326592 | bytes 786432 | tf_op jit(solution)/shard_map/pallas_call | solution.py:88
  28.5 0.0 collective-permute-done.3.refs_1_
  28.5 0.0 collective-permute-done.1.refs_0_
  28.5 0.6 %shard_map.49 = f32[256,128]{1,0:T(8,128)S(1)} custom-call(s32[48]{0:T(128)S(1)} %copy-done.1, bf16[4,128,128]{2,1,0:T(8,128)(2,1)S(1)} %collective-permute-done.1.refs_0_, bf16[2,128,128]{2,1,0:T(8,128)(2,1)S(1)} %collective-permute-done.3.refs_1_, bf16[2,3,128,128]{3,2,1,0:T(8,128)(2,1)S(1)} %get-tuple-element.10.refs_2_, ...), custom_call_target="tpu_custom_call" | custom-call | flops 25165824 | bytes 196608 | tf_op jit(solution)/shard_map/pallas_call | solution.py:117
  29.2 1.3 %collective-permute-start.10 = (f32[256,128]{1,0:T(8,128)S(1)}, f32[256,128]{1,0:T(8,128)S(1)}, u32[]{:S(2)}, u32[]{:S(2)}) collective-permute-start(f32[256,128]{1,0:T(8,128)S(1)} %shard_map.49), channel_id=1, source_target_pairs={{0,1},{1,0},{2,3},{3,2},{4,5},{5,4},{6,7},{7,6},{8,9},{9,8},{10,11... | collective-permute-start | bytes 393224 | tf_op jit(solution)/shard_map/ppermute | solution.py:131
  30.5 0.8 %shard_map.48 = f32[256,128]{1,0:T(8,128)S(1)} custom-call(s32[48]{0:T(128)S(1)} %copy-done.1, bf16[4,128,128]{2,1,0:T(8,128)(2,1)S(1)} %collective-permute-done.1.refs_0_, bf16[2,128,128]{2,1,0:T(8,128)(2,1)S(1)} %collective-permute-done.3.refs_1_, bf16[2,3,128,128]{3,2,1,0:T(8,128)(2,1)S(1)} %get-tuple-element.10.refs_2_, ...), custom_call_target="tpu_custom_call" | custom-call | flops 25165824 | bytes 196608 | tf_op jit(solution)/shard_map/pallas_call | solution.py:117
  31.3 2.9 %collective-permute-done.10 = f32[256,128]{1,0:T(8,128)S(1)} collective-permute-done((f32[256,128]{1,0:T(8,128)S(1)}, f32[256,128]{1,0:T(8,128)S(1)}, u32[]{:S(2)}, u32[]{:S(2)}) %collective-permute-start.10) | collective-permute-done | bytes 131104 | tf_op jit(solution)/shard_map/ppermute | solution.py:131
  34.2 0.6 %add_convert_fusion = bf16[256,128]{1,0:T(8,128)(2,1)} fusion(f32[256,128]{1,0:T(8,128)S(1)} %shard_map.48, f32[256,128]{1,0:T(8,128)S(1)} %collective-permute-done.10), kind=kLoop, calls=%fused_computation.1 | loop fusion | flops 65536 | bytes 327680 | tf_op jit(solution)/shard_map/convert_element_type | solution.py:177
  (5 shorter events, 0.1 us)
Async XLA Ops:
  0.0 5.6 %copy-start = (bf16[1,1,6,128,128]{4,3,2,1,0:T(8,128)(2,1)S(1)}, bf16[1,1,6,128,128]{4,3,2,1,0:T(8,128)(2,1)}, u32[]{:S(2)}) copy-start(bf16[1,1,6,128,128]{4,3,2,1,0:T(8,128)(2,1)} %param.4) | copy-start | bytes 589828
  1.0 9.3 %collective-permute-start.8 = (bf16[1,3,128,128]{3,2,1,0:T(8,128)(2,1)S(1)}, bf16[1,3,128,128]{3,2,1,0:T(8,128)(2,1)S(1)}, u32[]{:S(2)}, u32[]{:S(2)}) collective-permute-start(bf16[1,3,128,128]{3,2,1,0:T(8,128)(2,1)S(1)} %get-tuple-element.14), channel_id=1, source_target_pairs={{0,17},{1,16},{2,19},{3,18},{4,21},{5,20},{6,23},{7,22},{8,25},{9,... | collective-permute-start | bytes 294920 | tf_op jit(solution)/shard_map/ppermute | solution.py:137
  5.0 5.4 %collective-permute-start.5 = (bf16[1,3,128,128]{3,2,1,0:T(8,128)(2,1)S(1)}, bf16[1,3,128,128]{3,2,1,0:T(8,128)(2,1)S(1)}, u32[]{:S(2)}, u32[]{:S(2)}) collective-permute-start(bf16[1,3,128,128]{3,2,1,0:T(8,128)(2,1)S(1)} %get-tuple-element.14), channel_id=1, source_target_pairs={{0,1},{1,0},{2,3},{3,2},{4,5},{5,4},{6,7},{7,6},{8,9},{9,8},{10,11... | collective-permute-start | bytes 294920 | tf_op jit(solution)/shard_map/ppermute | solution.py:137
  5.5 4.8 %collective-permute-start.7 = (bf16[1,3,128,128]{3,2,1,0:T(8,128)(2,1)S(1)}, bf16[1,3,128,128]{3,2,1,0:T(8,128)(2,1)S(1)}, u32[]{:S(2)}, u32[]{:S(2)}) collective-permute-start(bf16[1,3,128,128]{3,2,1,0:T(8,128)(2,1)S(1)} %get-tuple-element.13), channel_id=1, source_target_pairs={{0,16},{8,24},{16,0},{24,8},{1,17},{9,25},{17,1},{25,9},{2,18},{10... | collective-permute-start | bytes 294920 | tf_op jit(solution)/shard_map/ppermute | solution.py:131
  5.6 8.2 %collective-permute-start = (bf16[4,128,128]{2,1,0:T(8,128)(2,1)S(1)}, bf16[4,128,128]{2,1,0:T(8,128)(2,1)S(1)}, u32[]{:S(2)}, u32[]{:S(2)}) collective-permute-start(bf16[4,128,128]{2,1,0:T(8,128)(2,1)S(1)} %slice_bitcast_fusion), channel_id=1, source_target_pairs={{0,4},{1,5},{2,6},{3,7},{4,0},{5,1},{6,2},{7,3},{8,12},{9,13},{10,... | collective-permute-start | bytes 393224 | tf_op jit(solution)/shard_map/ppermute | solution.py:131
  8.7 17.1 %collective-permute-start.4 = (bf16[6,128,128]{2,1,0:T(8,128)(2,1)S(1)}, bf16[6,128,128]{2,1,0:T(8,128)(2,1)S(1)}, u32[]{:S(2)}, u32[]{:S(2)}) collective-permute-start(bf16[6,128,128]{2,1,0:T(8,128)(2,1)S(1)} %bitcast.12), channel_id=1, source_target_pairs={{0,2},{1,3},{2,0},{3,1},{4,6},{5,7},{6,4},{7,5},{8,10},{9,11},{10,... | collective-permute-start | bytes 589832 | tf_op jit(solution)/shard_map/ppermute | solution.py:131
  10.3 15.5 %collective-permute-start.9 = (bf16[2,3,128,128]{3,2,1,0:T(8,128)(2,1)S(1)}, bf16[2,3,128,128]{3,2,1,0:T(8,128)(2,1)S(1)}, u32[]{:S(2)}, u32[]{:S(2)}) collective-permute-start(bf16[2,3,128,128]{3,2,1,0:T(8,128)(2,1)S(1)} %constant_dynamic-update-slice_fusion.refs_6_), channel_id=1, source_target_pairs={{0,8},{8,0},{16,24},{24,16},{1,9},{9,1},{17,25},{25,17},{2,10},{10... | collective-permute-start | bytes 589832 | tf_op jit(solution)/shard_map/ppermute | solution.py:131
  10.4 15.4 %collective-permute-start.6 = (bf16[2,3,128,128]{3,2,1,0:T(8,128)(2,1)S(1)}, bf16[2,3,128,128]{3,2,1,0:T(8,128)(2,1)S(1)}, u32[]{:S(2)}, u32[]{:S(2)}) collective-permute-start(bf16[2,3,128,128]{3,2,1,0:T(8,128)(2,1)S(1)} %pad_maximum_fusion.refs_4_), channel_id=1, source_target_pairs={{0,8},{8,0},{16,24},{24,16},{1,9},{9,1},{17,25},{25,17},{2,10},{10... | collective-permute-start | bytes 589832 | tf_op jit(solution)/shard_map/ppermute | solution.py:131
  11.0 11.0 %copy-start.4 = (s32[4,8,2,3]{1,2,3,0:T(2,128)S(1)}, s32[4,8,2,3]{1,2,3,0:T(2,128)}, u32[]{:S(2)}) copy-start(s32[4,8,2,3]{1,2,3,0:T(2,128)} %param.7) | copy-start | bytes 2308
  13.8 5.6 %collective-permute-start.2 = (bf16[2,128,128]{2,1,0:T(8,128)(2,1)S(1)}, bf16[2,128,128]{2,1,0:T(8,128)(2,1)S(1)}, u32[]{:S(2)}, u32[]{:S(2)}) collective-permute-start(bf16[2,128,128]{2,1,0:T(8,128)(2,1)S(1)} %slice_bitcast_fusion.1), channel_id=1, source_target_pairs={{0,4},{1,5},{2,6},{3,7},{4,0},{5,1},{6,2},{7,3},{8,12},{9,13},{10,... | collective-permute-start | bytes 196616 | tf_op jit(solution)/shard_map/ppermute | solution.py:131
  16.0 12.5 %collective-permute-start.1 = (bf16[4,128,128]{2,1,0:T(8,128)(2,1)S(1)}, bf16[4,128,128]{2,1,0:T(8,128)(2,1)S(1)}, u32[]{:S(2)}, u32[]{:S(2)}) collective-permute-start(bf16[4,128,128]{2,1,0:T(8,128)(2,1)S(1)} %collective-permute-done.refs_2_), channel_id=1, source_target_pairs={{0,2},{1,3},{2,0},{3,1},{4,6},{5,7},{6,4},{7,5},{8,10},{9,11},{10,... | collective-permute-start | bytes 393224 | tf_op jit(solution)/shard_map/ppermute | solution.py:131
  19.4 9.1 %collective-permute-start.3 = (bf16[2,128,128]{2,1,0:T(8,128)(2,1)S(1)}, bf16[2,128,128]{2,1,0:T(8,128)(2,1)S(1)}, u32[]{:S(2)}, u32[]{:S(2)}) collective-permute-start(bf16[2,128,128]{2,1,0:T(8,128)(2,1)S(1)} %collective-permute-done.2.refs_3_), channel_id=1, source_target_pairs={{0,2},{1,3},{2,0},{3,1},{4,6},{5,7},{6,4},{7,5},{8,10},{9,11},{10,... | collective-permute-start | bytes 196616 | tf_op jit(solution)/shard_map/ppermute | solution.py:131
  22.0 0.7 %copy-start.3 = (s32[4,8,6]{1,0,2:T(4,128)S(1)}, s32[4,8,6]{1,0,2:T(4,128)}, u32[]{:S(2)}) copy-start(s32[4,8,6]{1,0,2:T(4,128)} %param.5) | copy-start | bytes 2308
  23.4 2.4 %copy-start.2 = (s32[3]{0:T(128)S(1)}, s32[3]{0:T(128)}, u32[]{:S(2)}) copy-start(s32[3]{0:T(128)} %pad_add_fusion.place_ref) | copy-start | bytes 40
  25.8 0.7 %copy-start.1 = (s32[48]{0:T(128)S(1)}, s32[48]{0:T(128)}, u32[]{:S(2)}) copy-start(s32[48]{0:T(128)} %shard_map.46.codes_ref) | copy-start | bytes 580
  29.2 5.0 %collective-permute-start.10 = (f32[256,128]{1,0:T(8,128)S(1)}, f32[256,128]{1,0:T(8,128)S(1)}, u32[]{:S(2)}, u32[]{:S(2)}) collective-permute-start(f32[256,128]{1,0:T(8,128)S(1)} %shard_map.49), channel_id=1, source_target_pairs={{0,1},{1,0},{2,3},{3,2},{4,5},{5,4},{6,7},{7,6},{8,9},{9,8},{10,11... | collective-permute-start | bytes 393224 | tf_op jit(solution)/shard_map/ppermute | solution.py:131

commit v7 on v4

--- a/solution.py
+++ b/solution.py
@@ -36,16 +36,17 @@
 def first_products(place, left_index, right_index, lefts, rights):
     slots, tile, _ = lefts[0].shape
     count = len(lefts)
-    inner = len(rights)
-    right_slots = rights[0].shape[1]
+    inner = len(rights) // 2
+    right_slots = rights[0].shape[0]
 
     def kernel(place_ref, li_ref, ri_ref, *refs):
-        left_refs, right_refs = refs[:count], refs[count : count + inner]
-        totals = refs[count + inner : count + inner + 2]
-        last_ref, codes_ref, held = refs[count + inner + 2 :]
+        left_refs, right_refs = refs[:count], refs[count : count + 2 * inner]
+        totals = refs[count + 2 * inner : count + 2 * inner + 2]
+        last_ref, codes_ref, held = refs[count + 2 * inner + 2 :]
         row, z, y = place_ref[0], place_ref[1], place_ref[2]
         for t in range(inner):
-            held[row ^ t] = right_refs[t][...]
+            for side in range(2):
+                held[row ^ t, side] = right_refs[2 * t + side][...]
         zl = z ^ (inner - 1)
         last_ref[...] = held[zl]
         for side in range(2):
@@ -73,7 +74,7 @@
             jax.ShapeDtypeStruct((2, right_slots, tile, tile), jnp.bfloat16),
             jax.ShapeDtypeStruct((2 * slots,), jnp.int32),
         ],
-        in_specs=[SMEM] * 3 + [VMEM] * (count + inner),
+        in_specs=[SMEM] * 3 + [VMEM] * (count + 2 * inner),
         out_specs=[VMEM] * 3 + [SMEM],
         scratch_shapes=[pltpu.VMEM((inner, 2, right_slots, tile, tile), jnp.bfloat16)],
         compiler_params=pltpu.CompilerParams(vmem_limit_bytes=32 * 1024 * 1024),
@@ -115,13 +116,24 @@
     return lax.ppermute(block, axis, route)
 
 
-def gather(block, axis, unit):
+def crossed(block, mask):
+    rows, cols = lax.axis_size("row"), lax.axis_size("col")
+    route = [(r * cols + c, (r ^ mask) * cols + (c ^ 1)) for r in range(rows) for c in range(cols)]
+    return lax.ppermute(block, ("row", "col"), route)
+
+
+def gather(block):
+    distance = lax.axis_size("col") // 4
+    near = [distance // 2**n for n in range(distance.bit_length())]
     blocks = {0: block}
-    distance = lax.axis_size(axis) // unit // 2
-    while distance:
+    for distance in near:
+        blocks[distance] = across(block, "col", 2 * distance)
+    held = lax.optimization_barrier([blocks[d] for d in near])
+    blocks.update(zip(near, held))
+    for n, distance in enumerate(near):
         for s in sorted(blocks):
-            blocks[s ^ distance] = across(blocks[s], axis, unit * distance)
-        distance //= 2
+            if s ^ distance not in blocks and s & (distance - 1) == 0:
+                blocks[s ^ distance] = across(blocks[s], "col", 2 * distance)
     return [blocks[s] for s in range(len(blocks))]
 
 
@@ -131,11 +143,12 @@
     z, y = col >> 1, col & 1
     right = right_tiles[0, 0]
 
-    lefts = gather(left_tiles[0, 0], "col", 2)
-    given = lax.dynamic_index_in_dim(right, 1 - y, 0, keepdims=True)
-    own = lax.dynamic_index_in_dim(right, y, 0, keepdims=True)
-    halves = jnp.concatenate([own, across(given, "col", 1)])
-    rights = gather(halves, "row", 1)
+    lefts = gather(left_tiles[0, 0])
+    given = lax.dynamic_index_in_dim(right, 1 - y, 0, keepdims=False)
+    own = lax.dynamic_index_in_dim(right, y, 0, keepdims=False)
+    rights = []
+    for t in range(lax.axis_size("row")):
+        rights += [across(own, "row", t) if t else own, crossed(given, t)]
 
     place = jnp.stack([row, z, y])
     mine, other, right_last, codes = first_products(place, left_index, right_index, lefts[:-1], rights)

time: 31.4 us -> 35 us (1.11)
  starting transfers between devices: 11.6 us -> 13.7 us
  waiting for transfers between devices: 12.2 us -> 13.5 us
    ppermute x0 -> x4, starting transfers between devices: none -> 5.47 us  [crossed(): return lax.ppermute(block, ('row', 'col'), route)]
    ppermute x8 -> x7, starting transfers between devices: 11.6 us -> 8.19 us  [across(): return lax.ppermute(block, axis, route)]
    ppermute x8 -> x7, waiting for transfers between devices: 12.2 us -> 13.2 us  [across(): return lax.ppermute(block, axis, route)]
    squeeze x0 -> x1, local copies, waits for them, and re-layouts: none -> 0.99 us  [shards(): given = lax.dynamic_index_in_dim(right, 1 - y, 0, keepdims=False)]
    dynamic_slice x1 -> x0, local copies, waits for them, and re-layouts: 0.95 us -> none  [shards(): own = lax.dynamic_index_in_dim(right, y, 0, keepdims=True)]
  transfers between devices with their start and end apart: 8 -> 11, of which waited for: 5 -> 6; matrix products, arithmetic and copies ran while one was open for 1% -> 4% of each run, Pallas kernels for 13% -> 12%
where the time goes in v7:
time: 35 us; the launch traced here: 34.7 us
  starting transfers between devices  13.7 us (39%)
  waiting for transfers between devices  13.5 us (39%)
  Pallas kernels  4.92 us (14%)
  local copies, waits for them, and re-layouts  1.83 us (5%)
  other arithmetic  0.73 us (2%)
    ppermute x7, waiting for transfers between devices, across(): return lax.ppermute(block, axis, route)  13.2 us
    ppermute x7, starting transfers between devices, across(): return lax.ppermute(block, axis, route)  8.19 us
    ppermute x4, starting transfers between devices, crossed(): return lax.ppermute(block, ('row', 'col'), route)  5.47 us
    pallas_call x1, Pallas kernels, first_products(): pl.pallas_call(kernel, out_shape=[jax.ShapeDtypeStruct((RT * tile, tile),...  3.52 us
    pallas_call x2, Pallas kernels, last_products(): pl.pallas_call(kernel, out_shape=jax.ShapeDtypeStruct(total.shape, total....  1.4 us
    squeeze x1, local copies, waits for them, and re-layouts, shards(): given = lax.dynamic_index_in_dim(right, 1 - y, 0, keepdims=False)  0.99 us
    unnamed x8, local copies, waits for them, and re-layouts  0.84 us
  transfers between devices with their start and end apart: 11, of which 6 were waited for; matrix products, arithmetic and copies ran while one was open for 4% of the time, Pallas kernels for 12%

profile of v7, /device:TPU:0, one launch (start us, length us, event | category | flops | bytes accessed | tf_op | source)
XLA Modules:
  0.0 34.7 jit_solution(1941380026244356501)
XLA Ops:
  0.0 3.0 %collective-permute-start.1 = (bf16[6,128,128]{2,1,0:T(8,128)(2,1)}, bf16[6,128,128]{2,1,0:T(8,128)(2,1)S(1)}, u32[]{:S(2)}, u32[]{:S(2)}) collective-permute-start(bf16[6,128,128]{2,1,0:T(8,128)(2,1)} %bitcast.8), channel_id=1, source_target_pairs={{0,2},{1,3},{2,0},{3,1},{4,6},{5,7},{6,4},{7,5},{8,10},{9,11},{10,... | collective-permute-start | bytes 589832 | tf_op jit(solution)/shard_map/ppermute | solution.py:116
  3.0 2.6 %collective-permute-start = (bf16[6,128,128]{2,1,0:T(8,128)(2,1)}, bf16[6,128,128]{2,1,0:T(8,128)(2,1)S(1)}, u32[]{:S(2)}, u32[]{:S(2)}) collective-permute-start(bf16[6,128,128]{2,1,0:T(8,128)(2,1)} %bitcast.9), channel_id=1, source_target_pairs={{0,4},{1,5},{2,6},{3,7},{4,0},{5,1},{6,2},{7,3},{8,12},{9,13},{10,... | collective-permute-start | bytes 589832 | tf_op jit(solution)/shard_map/ppermute | solution.py:116
  5.6 0.0 copy-start.1
  5.6 0.0 copy-start
  5.6 1.0 %dynamic-slice_bitcast_fusion = (bf16[3,128,128]{2,1,0:T(8,128)(2,1)S(1)}, bf16[3,128,128]{2,1,0:T(8,128)(2,1)S(1)}) fusion(bf16[1,1,2,3,128,128]{5,4,3,2,1,0:T(8,128)(2,1)} %param.6, s32[]{:T(128)S(6)} %select_n.8, s32[]{:T(128)S(6)} %select_n.7), kind=kLoop, calls=%fused_computation.1 | loop fusion | bytes 393224 | tf_op jit(solution)/shard_map/jit(dynamic_index_in_dim)/squeeze | solution.py:147
  6.6 1.4 %collective-permute-start.8 = (bf16[3,128,128]{2,1,0:T(8,128)(2,1)S(1)}, bf16[3,128,128]{2,1,0:T(8,128)(2,1)S(1)}, u32[]{:S(2)}, u32[]{:S(2)}) collective-permute-start(bf16[3,128,128]{2,1,0:T(8,128)(2,1)S(1)} %get-tuple-element.17), channel_id=1, source_target_pairs={{0,25},{1,24},{2,27},{3,26},{4,29},{5,28},{6,31},{7,30},{8,17},{9,... | collective-permute-start | bytes 294920 | tf_op jit(solution)/shard_map/ppermute | solution.py:122
  8.0 1.2 %collective-permute-start.6 = (bf16[3,128,128]{2,1,0:T(8,128)(2,1)S(1)}, bf16[3,128,128]{2,1,0:T(8,128)(2,1)S(1)}, u32[]{:S(2)}, u32[]{:S(2)}) collective-permute-start(bf16[3,128,128]{2,1,0:T(8,128)(2,1)S(1)} %get-tuple-element.17), channel_id=1, source_target_pairs={{0,17},{1,16},{2,19},{3,18},{4,21},{5,20},{6,23},{7,22},{8,25},{9,... | collective-permute-start | bytes 294920 | tf_op jit(solution)/shard_map/ppermute | solution.py:122
  9.2 1.4 %collective-permute-start.4 = (bf16[3,128,128]{2,1,0:T(8,128)(2,1)S(1)}, bf16[3,128,128]{2,1,0:T(8,128)(2,1)S(1)}, u32[]{:S(2)}, u32[]{:S(2)}) collective-permute-start(bf16[3,128,128]{2,1,0:T(8,128)(2,1)S(1)} %get-tuple-element.17), channel_id=1, source_target_pairs={{0,9},{1,8},{2,11},{3,10},{4,13},{5,12},{6,15},{7,14},{8,1},{9,0},... | collective-permute-start | bytes 294920 | tf_op jit(solution)/shard_map/ppermute | solution.py:122
  10.6 1.6 %collective-permute-done.1.refs_1_ = bf16[6,128,128]{2,1,0:T(8,128)(2,1)S(1)} collective-permute-done((bf16[6,128,128]{2,1,0:T(8,128)(2,1)}, bf16[6,128,128]{2,1,0:T(8,128)(2,1)S(1)}, u32[]{:S(2)}, u32[]{:S(2)}) %collective-permute-start.1) | collective-permute-done | bytes 196640 | tf_op jit(solution)/shard_map/ppermute | solution.py:116
  12.2 2.6 %collective-permute-done.refs_2_ = bf16[6,128,128]{2,1,0:T(8,128)(2,1)S(1)} collective-permute-done((bf16[6,128,128]{2,1,0:T(8,128)(2,1)}, bf16[6,128,128]{2,1,0:T(8,128)(2,1)S(1)}, u32[]{:S(2)}, u32[]{:S(2)}) %collective-permute-start) | collective-permute-done | bytes 196640 | tf_op jit(solution)/shard_map/ppermute | solution.py:116
  14.8 0.4 %collective-permute-start.9 = (bf16[6,128,128]{2,1,0:T(8,128)(2,1)S(1)}, bf16[6,128,128]{2,1,0:T(8,128)(2,1)S(1)}, u32[]{:S(2)}, u32[]{:S(2)}) collective-permute-start(bf16[6,128,128]{2,1,0:T(8,128)(2,1)S(1)} %collective-permute-done.refs_2_), channel_id=1, source_target_pairs={{0,2},{1,3},{2,0},{3,1},{4,6},{5,7},{6,4},{7,5},{8,10},{9,11},{10,... | collective-permute-start | bytes 589832 | tf_op jit(solution)/shard_map/ppermute | solution.py:116
  15.2 1.5 %collective-permute-start.2 = (bf16[3,128,128]{2,1,0:T(8,128)(2,1)S(1)}, bf16[3,128,128]{2,1,0:T(8,128)(2,1)S(1)}, u32[]{:S(2)}, u32[]{:S(2)}) collective-permute-start(bf16[3,128,128]{2,1,0:T(8,128)(2,1)S(1)} %get-tuple-element.17), channel_id=1, source_target_pairs={{0,1},{1,0},{2,3},{3,2},{4,5},{5,4},{6,7},{7,6},{8,9},{9,8},{10,11... | collective-permute-start | bytes 294920 | tf_op jit(solution)/shard_map/ppermute | solution.py:122
  16.7 0.0 copy-done.1
  16.7 0.0 copy-start.2
  16.7 0.1 copy.5.li_ref
  16.8 0.6 %copy-done.2 = s32[4,8,2,3]{1,2,3,0:T(2,128)S(1)} copy-done((s32[4,8,2,3]{1,2,3,0:T(2,128)S(1)}, s32[4,8,2,3]{1,2,3,0:T(2,128)}, u32[]{:S(2)}) %copy-start.2) | copy-done | bytes 792
  17.4 0.1 copy.6.ri_ref
  17.6 0.0 collective-permute-done.8.refs_10_
  17.6 0.1 collective-permute-start.7
  17.6 0.0 collective-permute-done.6.refs_8_
  17.6 1.6 %collective-permute-start.5 = (bf16[3,128,128]{2,1,0:T(8,128)(2,1)S(1)}, bf16[3,128,128]{2,1,0:T(8,128)(2,1)S(1)}, u32[]{:S(2)}, u32[]{:S(2)}) collective-permute-start(bf16[3,128,128]{2,1,0:T(8,128)(2,1)S(1)} %get-tuple-element.18.refs_3_), channel_id=1, source_target_pairs={{0,16},{8,24},{16,0},{24,8},{1,17},{9,25},{17,1},{25,9},{2,18},{10... | collective-permute-start | bytes 294920 | tf_op jit(solution)/shard_map/ppermute | solution.py:116
  19.2 0.0 collective-permute-done.4.refs_6_
  19.2 0.3 collective-permute-start.3
  19.5 0.1 pad_add_fusion.place_ref
  19.6 0.3 collective-permute-done.2.refs_4_
  19.8 2.8 %collective-permute-done.7.refs_9_ = bf16[3,128,128]{2,1,0:T(8,128)(2,1)S(1)} collective-permute-done((bf16[3,128,128]{2,1,0:T(8,128)(2,1)S(1)}, bf16[3,128,128]{2,1,0:T(8,128)(2,1)S(1)}, u32[]{:S(2)}, u32[]{:S(2)}) %collective-permute-start.7) | collective-permute-done | bytes 98336 | tf_op jit(solution)/shard_map/ppermute | solution.py:116
  22.7 2.2 %collective-permute-done.5.refs_7_ = bf16[3,128,128]{2,1,0:T(8,128)(2,1)S(1)} collective-permute-done((bf16[3,128,128]{2,1,0:T(8,128)(2,1)S(1)}, bf16[3,128,128]{2,1,0:T(8,128)(2,1)S(1)}, u32[]{:S(2)}, u32[]{:S(2)}) %collective-permute-start.5) | collective-permute-done | bytes 98336 | tf_op jit(solution)/shard_map/ppermute | solution.py:116
  24.8 0.0 collective-permute-done.3.refs_5_
  24.8 0.0 copy-done
  24.8 3.5 %shard_map.46 = (f32[256,128]{1,0:T(8,128)S(1)}, f32[256,128]{1,0:T(8,128)S(1)}, bf16[2,3,128,128]{3,2,1,0:T(8,128)(2,1)S(1)}, s32[12]{0:T(128)S(1)}) custom-call(s32[3]{0:T(128)S(1)} %pad_add_fusion.place_ref, s32[4,8,6]{2,1,0:T(8,128)S(1)} %copy.5.li_ref, s32[4,8,2,3]{3,2,1,0:T(2,128)S(1)} %copy.6.ri_ref, bf16[6,128,128]{2,1,0:T(8,128)(2,1)S(1)} %bitcast.10, ...), custom_call_target="tpu_custom_call" | custom-call | flops 150994944 | bytes 589824 | tf_op jit(solution)/shard_map/pallas_call | solution.py:70
  28.4 0.0 collective-permute-done.9.left_ref
  28.4 0.7 %shard_map.48 = f32[256,128]{1,0:T(8,128)S(1)} custom-call(s32[12]{0:T(128)S(1)} %get-tuple-element.13.codes_ref, bf16[6,128,128]{2,1,0:T(8,128)(2,1)S(1)} %collective-permute-done.9.left_ref, bf16[2,3,128,128]{3,2,1,0:T(8,128)(2,1)S(1)} %get-tuple-element.14.right_ref, f32[256,128]{1,0:T(8,128)S(1)} %get-tuple-element.16.total_ref), custom_call_target="tpu_custom_call" | custom-call | flops 25165824 | bytes 196608 | tf_op jit(solution)/shard_map/pallas_call | solution.py:102
  29.1 0.2 collective-permute-start.10
  29.3 0.7 %shard_map.47 = f32[256,128]{1,0:T(8,128)S(1)} custom-call(s32[12]{0:T(128)S(1)} %get-tuple-element.13.codes_ref, bf16[6,128,128]{2,1,0:T(8,128)(2,1)S(1)} %collective-permute-done.9.left_ref, bf16[2,3,128,128]{3,2,1,0:T(8,128)(2,1)S(1)} %get-tuple-element.14.right_ref, f32[256,128]{1,0:T(8,128)S(1)} %get-tuple-element.15.total_ref), custom_call_target="tpu_custom_call" | custom-call | flops 25165824 | bytes 196608 | tf_op jit(solution)/shard_map/pallas_call | solution.py:102
  30.0 4.0 %collective-permute-done.10 = f32[256,128]{1,0:T(8,128)S(1)} collective-permute-done((f32[256,128]{1,0:T(8,128)S(1)}, f32[256,128]{1,0:T(8,128)S(1)}, u32[]{:S(2)}, u32[]{:S(2)}) %collective-permute-start.10) | collective-permute-done | bytes 131104 | tf_op jit(solution)/shard_map/ppermute | solution.py:116
  34.0 0.7 %add_convert_fusion = bf16[256,128]{1,0:T(8,128)(2,1)} fusion(f32[256,128]{1,0:T(8,128)S(1)} %shard_map.47, f32[256,128]{1,0:T(8,128)S(1)} %collective-permute-done.10), kind=kLoop, calls=%fused_computation | loop fusion | flops 65536 | bytes 327680 | tf_op jit(solution)/shard_map/convert_element_type | solution.py:158
Async XLA Ops:
  0.0 12.2 %collective-permute-start.1 = (bf16[6,128,128]{2,1,0:T(8,128)(2,1)}, bf16[6,128,128]{2,1,0:T(8,128)(2,1)S(1)}, u32[]{:S(2)}, u32[]{:S(2)}) collective-permute-start(bf16[6,128,128]{2,1,0:T(8,128)(2,1)} %bitcast.8), channel_id=1, source_target_pairs={{0,2},{1,3},{2,0},{3,1},{4,6},{5,7},{6,4},{7,5},{8,10},{9,11},{10,... | collective-permute-start | bytes 589832 | tf_op jit(solution)/shard_map/ppermute | solution.py:116
  3.0 11.7 %collective-permute-start = (bf16[6,128,128]{2,1,0:T(8,128)(2,1)}, bf16[6,128,128]{2,1,0:T(8,128)(2,1)S(1)}, u32[]{:S(2)}, u32[]{:S(2)}) collective-permute-start(bf16[6,128,128]{2,1,0:T(8,128)(2,1)} %bitcast.9), channel_id=1, source_target_pairs={{0,4},{1,5},{2,6},{3,7},{4,0},{5,1},{6,2},{7,3},{8,12},{9,13},{10,... | collective-permute-start | bytes 589832 | tf_op jit(solution)/shard_map/ppermute | solution.py:116
  5.6 11.1 %copy-start.1 = (s32[4,8,6]{1,0,2:T(4,128)S(1)}, s32[4,8,6]{1,0,2:T(4,128)}, u32[]{:S(2)}) copy-start(s32[4,8,6]{1,0,2:T(4,128)} %param.5) | copy-start | bytes 2308
  5.6 19.2 %copy-start = (bf16[1,1,6,128,128]{4,3,2,1,0:T(8,128)(2,1)S(1)}, bf16[1,1,6,128,128]{4,3,2,1,0:T(8,128)(2,1)}, u32[]{:S(2)}) copy-start(bf16[1,1,6,128,128]{4,3,2,1,0:T(8,128)(2,1)} %param.4) | copy-start | bytes 589828
  6.6 11.0 %collective-permute-start.8 = (bf16[3,128,128]{2,1,0:T(8,128)(2,1)S(1)}, bf16[3,128,128]{2,1,0:T(8,128)(2,1)S(1)}, u32[]{:S(2)}, u32[]{:S(2)}) collective-permute-start(bf16[3,128,128]{2,1,0:T(8,128)(2,1)S(1)} %get-tuple-element.17), channel_id=1, source_target_pairs={{0,25},{1,24},{2,27},{3,26},{4,29},{5,28},{6,31},{7,30},{8,17},{9,... | collective-permute-start | bytes 294920 | tf_op jit(solution)/shard_map/ppermute | solution.py:122
  8.0 9.6 %collective-permute-start.6 = (bf16[3,128,128]{2,1,0:T(8,128)(2,1)S(1)}, bf16[3,128,128]{2,1,0:T(8,128)(2,1)S(1)}, u32[]{:S(2)}, u32[]{:S(2)}) collective-permute-start(bf16[3,128,128]{2,1,0:T(8,128)(2,1)S(1)} %get-tuple-element.17), channel_id=1, source_target_pairs={{0,17},{1,16},{2,19},{3,18},{4,21},{5,20},{6,23},{7,22},{8,25},{9,... | collective-permute-start | bytes 294920 | tf_op jit(solution)/shard_map/ppermute | solution.py:122
  9.2 10.0 %collective-permute-start.4 = (bf16[3,128,128]{2,1,0:T(8,128)(2,1)S(1)}, bf16[3,128,128]{2,1,0:T(8,128)(2,1)S(1)}, u32[]{:S(2)}, u32[]{:S(2)}) collective-permute-start(bf16[3,128,128]{2,1,0:T(8,128)(2,1)S(1)} %get-tuple-element.17), channel_id=1, source_target_pairs={{0,9},{1,8},{2,11},{3,10},{4,13},{5,12},{6,15},{7,14},{8,1},{9,0},... | collective-permute-start | bytes 294920 | tf_op jit(solution)/shard_map/ppermute | solution.py:122
  14.8 13.6 %collective-permute-start.9 = (bf16[6,128,128]{2,1,0:T(8,128)(2,1)S(1)}, bf16[6,128,128]{2,1,0:T(8,128)(2,1)S(1)}, u32[]{:S(2)}, u32[]{:S(2)}) collective-permute-start(bf16[6,128,128]{2,1,0:T(8,128)(2,1)S(1)} %collective-permute-done.refs_2_), channel_id=1, source_target_pairs={{0,2},{1,3},{2,0},{3,1},{4,6},{5,7},{6,4},{7,5},{8,10},{9,11},{10,... | collective-permute-start | bytes 589832 | tf_op jit(solution)/shard_map/ppermute | solution.py:116
  15.2 4.6 %collective-permute-start.2 = (bf16[3,128,128]{2,1,0:T(8,128)(2,1)S(1)}, bf16[3,128,128]{2,1,0:T(8,128)(2,1)S(1)}, u32[]{:S(2)}, u32[]{:S(2)}) collective-permute-start(bf16[3,128,128]{2,1,0:T(8,128)(2,1)S(1)} %get-tuple-element.17), channel_id=1, source_target_pairs={{0,1},{1,0},{2,3},{3,2},{4,5},{5,4},{6,7},{7,6},{8,9},{9,8},{10,11... | collective-permute-start | bytes 294920 | tf_op jit(solution)/shard_map/ppermute | solution.py:122
  16.7 0.7 %copy-start.2 = (s32[4,8,2,3]{1,2,3,0:T(2,128)S(1)}, s32[4,8,2,3]{1,2,3,0:T(2,128)}, u32[]{:S(2)}) copy-start(s32[4,8,2,3]{1,2,3,0:T(2,128)} %param.7) | copy-start | bytes 2308
  17.6 5.1 %collective-permute-start.7 = (bf16[3,128,128]{2,1,0:T(8,128)(2,1)S(1)}, bf16[3,128,128]{2,1,0:T(8,128)(2,1)S(1)}, u32[]{:S(2)}, u32[]{:S(2)}) collective-permute-start(bf16[3,128,128]{2,1,0:T(8,128)(2,1)S(1)} %get-tuple-element.18.refs_3_), channel_id=1, source_target_pairs={{0,24},{8,16},{16,8},{24,0},{1,25},{9,17},{17,9},{25,1},{2,26},{10... | collective-permute-start | bytes 294920 | tf_op jit(solution)/shard_map/ppermute | solution.py:116
  17.6 7.2 %collective-permute-start.5 = (bf16[3,128,128]{2,1,0:T(8,128)(2,1)S(1)}, bf16[3,128,128]{2,1,0:T(8,128)(2,1)S(1)}, u32[]{:S(2)}, u32[]{:S(2)}) collective-permute-start(bf16[3,128,128]{2,1,0:T(8,128)(2,1)S(1)} %get-tuple-element.18.refs_3_), channel_id=1, source_target_pairs={{0,16},{8,24},{16,0},{24,8},{1,17},{9,25},{17,1},{25,9},{2,18},{10... | collective-permute-start | bytes 294920 | tf_op jit(solution)/shard_map/ppermute | solution.py:116
  19.2 5.6 %collective-permute-start.3 = (bf16[3,128,128]{2,1,0:T(8,128)(2,1)S(1)}, bf16[3,128,128]{2,1,0:T(8,128)(2,1)S(1)}, u32[]{:S(2)}, u32[]{:S(2)}) collective-permute-start(bf16[3,128,128]{2,1,0:T(8,128)(2,1)S(1)} %get-tuple-element.18.refs_3_), channel_id=1, source_target_pairs={{0,8},{8,0},{16,24},{24,16},{1,9},{9,1},{17,25},{25,17},{2,10},{10... | collective-permute-start | bytes 294920 | tf_op jit(solution)/shard_map/ppermute | solution.py:116
  29.1 5.0 %collective-permute-start.10 = (f32[256,128]{1,0:T(8,128)S(1)}, f32[256,128]{1,0:T(8,128)S(1)}, u32[]{:S(2)}, u32[]{:S(2)}) collective-permute-start(f32[256,128]{1,0:T(8,128)S(1)} %shard_map.48), channel_id=1, source_target_pairs={{0,1},{1,0},{2,3},{3,2},{4,5},{5,4},{6,7},{7,6},{8,9},{9,8},{10,11... | collective-permute-start | bytes 393224 | tf_op jit(solution)/shard_map/ppermute | solution.py:116

commit v8 on v4

--- a/solution.py
+++ b/solution.py
@@ -11,14 +11,14 @@
 VMEM = pl.BlockSpec(memory_space=pltpu.VMEM)
 
 
-def match(li_ref, ri_ref, row, zp, y, column, slot):
+def match(li_ref, ri_ref, row, zp, there, y, column, slot):
     right_slots = ri_ref.shape[-1]
     at = li_ref[row, 2 * zp + y, slot]
     k = lax.rem(at, KT)
     code = jnp.int32(0)
     for t in range(right_slots):
         code = jnp.where(ri_ref[zp, column, y, t] == k, 1 + lax.div(at, KT) * right_slots + t, code)
-    return jnp.where(at < RT * KT, code, 0)
+    return jnp.where(jnp.logical_and(there, at < RT * KT), code, 0)
 
 
 def add_tile(code, left_tile, right_at, right_slots, total_ref):
@@ -33,7 +33,7 @@
         )
 
 
-def first_products(place, left_index, right_index, lefts, rights):
+def first_products(place, left_index, right_index, names, lefts, last, rights):
     slots, tile, _ = lefts[0].shape
     count = len(lefts)
     inner = len(rights)
@@ -46,25 +46,27 @@
         row, z, y = place_ref[0], place_ref[1], place_ref[2]
         for t in range(inner):
             held[row ^ t] = right_refs[t][...]
-        zl = z ^ (inner - 1)
+        zl, there = origin(z, *last, inner)
         last_ref[...] = held[zl]
         for side in range(2):
             column = 2 * z + (y if side == 0 else 1 - y)
             totals[side][...] = jnp.zeros_like(totals[side])
             for slot in range(slots):
-                codes_ref[side * slots + slot] = match(li_ref, ri_ref, row, zl, y, column, slot)
-            for s in range(count):
-                zp = z ^ s
+                codes_ref[side * slots + slot] = match(li_ref, ri_ref, row, zl, there, y, column, slot)
+            for n, name in enumerate(names):
+                zp, there_n = origin(z, *name, inner)
 
-                @pl.loop(0, slots)
-                def _(slot):
-                    add_tile(
-                        match(li_ref, ri_ref, row, zp, y, column, slot),
-                        lambda: left_refs[s][slot],
-                        lambda found: held[zp, side, found],
-                        right_slots,
-                        totals[side],
-                    )
+                @pl.when(there_n)
+                def _():
+                    @pl.loop(0, slots)
+                    def _(slot):
+                        add_tile(
+                            match(li_ref, ri_ref, row, zp, True, y, column, slot),
+                            lambda: left_refs[n][slot],
+                            lambda found: held[zp, side, found],
+                            right_slots,
+                            totals[side],
+                        )
 
     return pl.pallas_call(
         kernel,
@@ -115,14 +117,35 @@
     return lax.ppermute(block, axis, route)
 
 
-def gather(block, axis, unit):
-    blocks = {0: block}
-    distance = lax.axis_size(axis) // unit // 2
-    while distance:
-        for s in sorted(blocks):
-            blocks[s ^ distance] = across(blocks[s], axis, unit * distance)
-        distance //= 2
-    return [blocks[s] for s in range(len(blocks))]
+def crossed(block, mask):
+    rows, cols = lax.axis_size("row"), lax.axis_size("col")
+    route = [(r * cols + c, (r ^ mask) * cols + (c ^ 1)) for r in range(rows) for c in range(cols)]
+    return lax.ppermute(block, ("row", "col"), route)
+
+
+def spread(block):
+    places = lax.axis_size("col") // 2
+    found = [(0, 0, block)]
+    held = {0: block, 1: block}
+    for step in range(1, places):
+        came = {}
+        for edge in range(2):
+            route = []
+            for i in range(places):
+                j = i + 1 - 2 * ((i + edge) % 2)
+                if 0 <= j < places and 0 <= i - (j - i) * (step - 1) < places:
+                    route += [(2 * i + y, 2 * j + y) for y in range(2)]
+            if route:
+                came[edge] = lax.ppermute(held[1 - edge], "col", route)
+                found.append((edge, step, came[edge]))
+        held = came
+    return found
+
+
+def origin(z, edge, step, places):
+    zp = z + step * (1 - 2 * lax.rem(z + edge, 2))
+    there = jnp.logical_and(zp >= 0, zp < places)
+    return jnp.where(there, zp, z), there
 
 
 def shards(left_tiles, left_index, right_tiles, right_index):
@@ -131,17 +154,23 @@
     z, y = col >> 1, col & 1
     right = right_tiles[0, 0]
 
-    lefts = gather(left_tiles[0, 0], "col", 2)
-    given = lax.dynamic_index_in_dim(right, 1 - y, 0, keepdims=True)
-    own = lax.dynamic_index_in_dim(right, y, 0, keepdims=True)
-    halves = jnp.concatenate([own, across(given, "col", 1)])
-    rights = gather(halves, "row", 1)
+    *early, (*last, final) = spread(left_tiles[0, 0])
+    names = [(edge, step) for edge, step, _ in early]
+    lefts = [block for _, _, block in early]
+    given = lax.dynamic_index_in_dim(right, 1 - y, 0, keepdims=False)
+    own = lax.dynamic_index_in_dim(right, y, 0, keepdims=False)
+    rights = []
+    for t in range(0, lax.axis_size("row"), 2):
+        pair = jnp.stack([across(own, "row", t) if t else own, crossed(given, t)])
+        rights += [pair, across(pair, "row", 1)]
 
     place = jnp.stack([row, z, y])
-    mine, other, right_last, codes = first_products(place, left_index, right_index, lefts[:-1], rights)
-    other = last_products(codes, lefts[-1], right_last, other, 1)
+    mine, other, right_last, codes = first_products(
+        place, left_index, right_index, names, lefts, last, rights
+    )
+    other = last_products(codes, final, right_last, other, 1)
     coming = across(other, "col", 1)
-    mine = last_products(codes, lefts[-1], right_last, mine, 0)
+    mine = last_products(codes, final, right_last, mine, 0)
     return (mine + coming).astype(jnp.bfloat16)
 
 

time: 31.4 us -> 34.9 us (1.11)
  waiting for transfers between devices: 12.2 us -> 14.1 us
  starting transfers between devices: 11.6 us -> 12.6 us
    ppermute x0 -> x7, waiting for transfers between devices: none -> 10.3 us  [the longest x5 8.58 us: spread(): came[edge] = lax.ppermute(held[1 - edge], 'col', route)]
    ppermute x0 -> x7, starting transfers between devices: none -> 9.95 us  [the longest x5 6.93 us: spread(): came[edge] = lax.ppermute(held[1 - edge], 'col', route)]
    ppermute x8 -> x4, starting transfers between devices: 11.6 us -> 2.67 us  [across(): return lax.ppermute(block, axis, route)]
    ppermute x8 -> x4, waiting for transfers between devices: 12.2 us -> 3.8 us  [across(): return lax.ppermute(block, axis, route)]
    squeeze x0 -> x1, local copies, waits for them, and re-layouts: none -> 1.01 us  [shards(): own = lax.dynamic_index_in_dim(right, y, 0, keepdims=False)]
    dynamic_slice x1 -> x0, local copies, waits for them, and re-layouts: 0.95 us -> none  [shards(): own = lax.dynamic_index_in_dim(right, y, 0, keepdims=True)]
  transfers between devices with their start and end apart: 8 -> 11, of which waited for: 5 -> 5; matrix products, arithmetic and copies ran while one was open for 1% -> 4% of each run, Pallas kernels for 13% -> 12%
where the time goes in v8:
time: 34.9 us; the launch traced here: 34.5 us
  waiting for transfers between devices  14.1 us (40%)
  starting transfers between devices  12.6 us (36%)
  Pallas kernels  5.06 us (14%)
  local copies, waits for them, and re-layouts  1.82 us (5%)
  other arithmetic  0.77 us (2%)
    ppermute x5, waiting for transfers between devices, spread(): came[edge] = lax.ppermute(held[1 - edge], 'col', route)  8.58 us
    ppermute x5, starting transfers between devices, spread(): came[edge] = lax.ppermute(held[1 - edge], 'col', route)  6.93 us
    ppermute x4, waiting for transfers between devices, across(): return lax.ppermute(block, axis, route)  3.8 us
    pallas_call x1, Pallas kernels, first_products(): pl.pallas_call(kernel, out_shape=[jax.ShapeDtypeStruct((RT * tile, tile),...  3.65 us
    ppermute x2, starting transfers between devices, crossed(): return lax.ppermute(block, ('row', 'col'), route)  3.02 us
    ppermute x4, starting transfers between devices, across(): return lax.ppermute(block, axis, route)  2.67 us
    ppermute x2, waiting for transfers between devices, crossed(): return lax.ppermute(block, ('row', 'col'), route)  1.71 us
    pallas_call x2, Pallas kernels, last_products(): pl.pallas_call(kernel, out_shape=jax.ShapeDtypeStruct(total.shape, total....  1.41 us
  transfers between devices with their start and end apart: 11, of which 5 were waited for; matrix products, arithmetic and copies ran while one was open for 4% of the time, Pallas kernels for 12%

profile of v8, /device:TPU:0, one launch (start us, length us, event | category | flops | bytes accessed | tf_op | source)
XLA Modules:
  0.0 34.5 jit_solution(11336680893094726680)
XLA Ops:
  0.0 3.0 %collective-permute-start = (bf16[6,128,128]{2,1,0:T(8,128)(2,1)}, bf16[6,128,128]{2,1,0:T(8,128)(2,1)S(1)}, u32[]{:S(2)}, u32[]{:S(2)}) collective-permute-start(bf16[6,128,128]{2,1,0:T(8,128)(2,1)} %bitcast.13), channel_id=1, source_target_pairs={{0,2},{1,3},{2,0},{3,1},{4,6},{5,7},{6,4},{7,5},{8,10},{9,11},{10,... | collective-permute-start | bytes 589832 | tf_op jit(solution)/shard_map/ppermute | solution.py:139
  3.0 0.0 copy-start
  3.0 1.0 %dynamic-slice_bitcast_fusion.1 = (bf16[3,128,128]{2,1,0:T(8,128)(2,1)S(1)}, bf16[3,128,128]{2,1,0:T(8,128)(2,1)S(1)}, bf16[1,3,128,128]{3,2,1,0:T(8,128)(2,1)S(1)}) fusion(bf16[1,1,2,3,128,128]{5,4,3,2,1,0:T(8,128)(2,1)} %param.6, s32[]{:T(128)S(6)} %select_n.7, s32[]{:T(128)S(6)} %select_n.8), kind=kLoop, calls=%fused_computation.4 | loop fusion | bytes 491528 | tf_op jit(solution)/shard_map/jit(dynamic_index_in_dim)/squeeze | solution.py:161
  4.0 2.5 %collective-permute-start.7 = (bf16[3,128,128]{2,1,0:T(8,128)(2,1)S(1)}, bf16[3,128,128]{2,1,0:T(8,128)(2,1)S(1)}, u32[]{:S(2)}, u32[]{:S(2)}) collective-permute-start(bf16[3,128,128]{2,1,0:T(8,128)(2,1)S(1)} %get-tuple-element.14), channel_id=1, source_target_pairs={{0,17},{1,16},{2,19},{3,18},{4,21},{5,20},{6,23},{7,22},{8,25},{9,... | collective-permute-start | bytes 294920 | tf_op jit(solution)/shard_map/ppermute | solution.py:123
  6.6 0.5 %collective-permute-start.6 = (bf16[3,128,128]{2,1,0:T(8,128)(2,1)S(1)}, bf16[3,128,128]{2,1,0:T(8,128)(2,1)S(1)}, u32[]{:S(2)}, u32[]{:S(2)}) collective-permute-start(bf16[3,128,128]{2,1,0:T(8,128)(2,1)S(1)} %get-tuple-element.13), channel_id=1, source_target_pairs={{0,16},{8,24},{16,0},{24,8},{1,17},{9,25},{17,1},{25,9},{2,18},{10... | collective-permute-start | bytes 294920 | tf_op jit(solution)/shard_map/ppermute | solution.py:117
  7.1 0.5 %collective-permute-start.4 = (bf16[3,128,128]{2,1,0:T(8,128)(2,1)S(1)}, bf16[3,128,128]{2,1,0:T(8,128)(2,1)S(1)}, u32[]{:S(2)}, u32[]{:S(2)}) collective-permute-start(bf16[3,128,128]{2,1,0:T(8,128)(2,1)S(1)} %get-tuple-element.14), channel_id=1, source_target_pairs={{0,1},{1,0},{2,3},{3,2},{4,5},{5,4},{6,7},{7,6},{8,9},{9,8},{10,11... | collective-permute-start | bytes 294920 | tf_op jit(solution)/shard_map/ppermute | solution.py:123
  7.6 0.0 copy-done
  7.6 0.7 %collective-permute-start.1 = (bf16[6,128,128]{2,1,0:T(8,128)(2,1)S(1)}, bf16[6,128,128]{2,1,0:T(8,128)(2,1)S(1)}, u32[]{:S(2)}, u32[]{:S(2)}) collective-permute-start(bf16[6,128,128]{2,1,0:T(8,128)(2,1)S(1)} %bitcast.14), channel_id=1, source_target_pairs={{2,4},{3,5},{4,2},{5,3},{10,12},{11,13},{12,10},{13,11},{18,20},{1... | collective-permute-start | bytes 589832 | tf_op jit(solution)/shard_map/ppermute | solution.py:139
  8.3 0.0 collective-permute-done.refs_1_
  8.3 0.7 %collective-permute-start.3 = (bf16[6,128,128]{2,1,0:T(8,128)(2,1)S(1)}, bf16[6,128,128]{2,1,0:T(8,128)(2,1)S(1)}, u32[]{:S(2)}, u32[]{:S(2)}) collective-permute-start(bf16[6,128,128]{2,1,0:T(8,128)(2,1)S(1)} %collective-permute-done.refs_1_), channel_id=1, source_target_pairs={{2,4},{3,5},{4,2},{5,3},{10,12},{11,13},{12,10},{13,11},{18,20},{1... | collective-permute-start | bytes 589832 | tf_op jit(solution)/shard_map/ppermute | solution.py:139
  9.0 1.6 %collective-permute-done.7 = bf16[3,128,128]{2,1,0:T(8,128)(2,1)S(1)} collective-permute-done((bf16[3,128,128]{2,1,0:T(8,128)(2,1)S(1)}, bf16[3,128,128]{2,1,0:T(8,128)(2,1)S(1)}, u32[]{:S(2)}, u32[]{:S(2)}) %collective-permute-start.7) | collective-permute-done | bytes 98336 | tf_op jit(solution)/shard_map/ppermute | solution.py:123
  10.6 1.0 %collective-permute-done.6 = bf16[3,128,128]{2,1,0:T(8,128)(2,1)S(1)} collective-permute-done((bf16[3,128,128]{2,1,0:T(8,128)(2,1)S(1)}, bf16[3,128,128]{2,1,0:T(8,128)(2,1)S(1)}, u32[]{:S(2)}, u32[]{:S(2)}) %collective-permute-start.6) | collective-permute-done | bytes 98336 | tf_op jit(solution)/shard_map/ppermute | solution.py:117
  11.6 0.1 collective-permute-start.8
  11.7 0.1 collective-permute-done.4
  11.8 0.0 copy-start.2
  11.8 0.5 %collective-permute-start.5 = (bf16[2,3,128,128]{3,2,1,0:T(8,128)(2,1)S(1)}, bf16[2,3,128,128]{3,2,1,0:T(8,128)(2,1)S(1)}, u32[]{:S(2)}, u32[]{:S(2)}) collective-permute-start(bf16[2,3,128,128]{3,2,1,0:T(8,128)(2,1)S(1)} %pad_maximum_fusion.refs_5_), channel_id=1, source_target_pairs={{0,8},{8,0},{16,24},{24,16},{1,9},{9,1},{17,25},{25,17},{2,10},{10... | collective-permute-start | bytes 589832 | tf_op jit(solution)/shard_map/ppermute | solution.py:117
  12.3 0.0 collective-permute-done.1.refs_2_
  12.3 1.3 %collective-permute-start.2 = (bf16[6,128,128]{2,1,0:T(8,128)(2,1)S(1)}, bf16[6,128,128]{2,1,0:T(8,128)(2,1)S(1)}, u32[]{:S(2)}, u32[]{:S(2)}) collective-permute-start(bf16[6,128,128]{2,1,0:T(8,128)(2,1)S(1)} %collective-permute-done.1.refs_2_), channel_id=1, source_target_pairs={{2,0},{3,1},{4,6},{5,7},{10,8},{11,9},{12,14},{13,15},{18,16},{19,... | collective-permute-start | bytes 589832 | tf_op jit(solution)/shard_map/ppermute | solution.py:139
  13.6 0.0 collective-permute-done.3.refs_4_
  13.6 1.3 %collective-permute-start.9 = (bf16[6,128,128]{2,1,0:T(8,128)(2,1)S(1)}, bf16[6,128,128]{2,1,0:T(8,128)(2,1)S(1)}, u32[]{:S(2)}, u32[]{:S(2)}) collective-permute-start(bf16[6,128,128]{2,1,0:T(8,128)(2,1)S(1)} %collective-permute-done.3.refs_4_), channel_id=1, source_target_pairs={{2,0},{3,1},{4,6},{5,7},{10,8},{11,9},{12,14},{13,15},{18,16},{19,... | collective-permute-start | bytes 589832 | tf_op jit(solution)/shard_map/ppermute | solution.py:139
  14.9 0.0 copy-done.2
  14.9 0.0 copy-start.1
  14.9 0.1 copy.6.ri_ref
  15.0 0.6 %copy-done.1 = s32[4,8,6]{1,0,2:T(4,128)S(1)} copy-done((s32[4,8,6]{1,0,2:T(4,128)S(1)}, s32[4,8,6]{1,0,2:T(4,128)}, u32[]{:S(2)}) %copy-start.1) | copy-done | bytes 792
  15.6 0.1 copy.5.li_ref
  15.7 0.1 pad_add_fusion.place_ref
  15.8 0.0 collective-permute-done.8.refs_8_
  15.8 0.0 collective-permute-done.5.refs_6_
  15.8 8.6 %collective-permute-done.2.refs_3_ = bf16[6,128,128]{2,1,0:T(8,128)(2,1)S(1)} collective-permute-done((bf16[6,128,128]{2,1,0:T(8,128)(2,1)S(1)}, bf16[6,128,128]{2,1,0:T(8,128)(2,1)S(1)}, u32[]{:S(2)}, u32[]{:S(2)}) %collective-permute-start.2) | collective-permute-done | bytes 196640 | tf_op jit(solution)/shard_map/ppermute | solution.py:139
  24.4 3.6 %shard_map.46 = (f32[256,128]{1,0:T(8,128)S(1)}, f32[256,128]{1,0:T(8,128)S(1)}, bf16[2,3,128,128]{3,2,1,0:T(8,128)(2,1)S(1)}, s32[12]{0:T(128)S(1)}) custom-call(s32[3]{0:T(128)S(1)} %pad_add_fusion.place_ref, s32[4,8,6]{2,1,0:T(8,128)S(1)} %copy.5.li_ref, s32[4,8,2,3]{3,2,1,0:T(2,128)S(1)} %copy.6.ri_ref, bf16[6,128,128]{2,1,0:T(8,128)(2,1)S(1)} %bitcast.15, ...), custom_call_target="tpu_custom_call" | custom-call | flops 251658240 | bytes 983040 | tf_op jit(solution)/shard_map/pallas_call | solution.py:71
  28.0 0.0 collective-permute-done.9.left_ref
  28.0 0.8 %shard_map.48 = f32[256,128]{1,0:T(8,128)S(1)} custom-call(s32[12]{0:T(128)S(1)} %get-tuple-element.9.codes_ref, bf16[6,128,128]{2,1,0:T(8,128)(2,1)S(1)} %collective-permute-done.9.left_ref, bf16[2,3,128,128]{3,2,1,0:T(8,128)(2,1)S(1)} %get-tuple-element.10.right_ref, f32[256,128]{1,0:T(8,128)S(1)} %get-tuple-element.12.total_ref), custom_call_target="tpu_custom_call" | custom-call | flops 25165824 | bytes 196608 | tf_op jit(solution)/shard_map/pallas_call | solution.py:103
  28.9 1.6 %collective-permute-start.10 = (f32[256,128]{1,0:T(8,128)S(1)}, f32[256,128]{1,0:T(8,128)S(1)}, u32[]{:S(2)}, u32[]{:S(2)}) collective-permute-start(f32[256,128]{1,0:T(8,128)S(1)} %shard_map.48), channel_id=1, source_target_pairs={{0,1},{1,0},{2,3},{3,2},{4,5},{5,4},{6,7},{7,6},{8,9},{9,8},{10,11... | collective-permute-start | bytes 393224 | tf_op jit(solution)/shard_map/ppermute | solution.py:117
  30.4 0.6 %shard_map.47 = f32[256,128]{1,0:T(8,128)S(1)} custom-call(s32[12]{0:T(128)S(1)} %get-tuple-element.9.codes_ref, bf16[6,128,128]{2,1,0:T(8,128)(2,1)S(1)} %collective-permute-done.9.left_ref, bf16[2,3,128,128]{3,2,1,0:T(8,128)(2,1)S(1)} %get-tuple-element.10.right_ref, f32[256,128]{1,0:T(8,128)S(1)} %get-tuple-element.11.total_ref), custom_call_target="tpu_custom_call" | custom-call | flops 25165824 | bytes 196608 | tf_op jit(solution)/shard_map/pallas_call | solution.py:103
  31.0 2.8 %collective-permute-done.10 = f32[256,128]{1,0:T(8,128)S(1)} collective-permute-done((f32[256,128]{1,0:T(8,128)S(1)}, f32[256,128]{1,0:T(8,128)S(1)}, u32[]{:S(2)}, u32[]{:S(2)}) %collective-permute-start.10) | collective-permute-done | bytes 131104 | tf_op jit(solution)/shard_map/ppermute | solution.py:117
  33.8 0.7 %add_convert_fusion = bf16[256,128]{1,0:T(8,128)(2,1)} fusion(f32[256,128]{1,0:T(8,128)S(1)} %shard_map.47, f32[256,128]{1,0:T(8,128)S(1)} %collective-permute-done.10), kind=kLoop, calls=%fused_computation.2 | loop fusion | flops 65536 | bytes 327680 | tf_op jit(solution)/shard_map/convert_element_type | solution.py:174
  (2 shorter events, 0.0 us)
Async XLA Ops:
  0.0 8.3 %collective-permute-start = (bf16[6,128,128]{2,1,0:T(8,128)(2,1)}, bf16[6,128,128]{2,1,0:T(8,128)(2,1)S(1)}, u32[]{:S(2)}, u32[]{:S(2)}) collective-permute-start(bf16[6,128,128]{2,1,0:T(8,128)(2,1)} %bitcast.13), channel_id=1, source_target_pairs={{0,2},{1,3},{2,0},{3,1},{4,6},{5,7},{6,4},{7,5},{8,10},{9,11},{10,... | collective-permute-start | bytes 589832 | tf_op jit(solution)/shard_map/ppermute | solution.py:139
  3.0 4.6 %copy-start = (bf16[1,1,6,128,128]{4,3,2,1,0:T(8,128)(2,1)S(1)}, bf16[1,1,6,128,128]{4,3,2,1,0:T(8,128)(2,1)}, u32[]{:S(2)}) copy-start(bf16[1,1,6,128,128]{4,3,2,1,0:T(8,128)(2,1)} %param.4) | copy-start | bytes 589828
  4.0 6.5 %collective-permute-start.7 = (bf16[3,128,128]{2,1,0:T(8,128)(2,1)S(1)}, bf16[3,128,128]{2,1,0:T(8,128)(2,1)S(1)}, u32[]{:S(2)}, u32[]{:S(2)}) collective-permute-start(bf16[3,128,128]{2,1,0:T(8,128)(2,1)S(1)} %get-tuple-element.14), channel_id=1, source_target_pairs={{0,17},{1,16},{2,19},{3,18},{4,21},{5,20},{6,23},{7,22},{8,25},{9,... | collective-permute-start | bytes 294920 | tf_op jit(solution)/shard_map/ppermute | solution.py:123
  6.6 5.0 %collective-permute-start.6 = (bf16[3,128,128]{2,1,0:T(8,128)(2,1)S(1)}, bf16[3,128,128]{2,1,0:T(8,128)(2,1)S(1)}, u32[]{:S(2)}, u32[]{:S(2)}) collective-permute-start(bf16[3,128,128]{2,1,0:T(8,128)(2,1)S(1)} %get-tuple-element.13), channel_id=1, source_target_pairs={{0,16},{8,24},{16,0},{24,8},{1,17},{9,25},{17,1},{25,9},{2,18},{10... | collective-permute-start | bytes 294920 | tf_op jit(solution)/shard_map/ppermute | solution.py:117
  7.1 4.7 %collective-permute-start.4 = (bf16[3,128,128]{2,1,0:T(8,128)(2,1)S(1)}, bf16[3,128,128]{2,1,0:T(8,128)(2,1)S(1)}, u32[]{:S(2)}, u32[]{:S(2)}) collective-permute-start(bf16[3,128,128]{2,1,0:T(8,128)(2,1)S(1)} %get-tuple-element.14), channel_id=1, source_target_pairs={{0,1},{1,0},{2,3},{3,2},{4,5},{5,4},{6,7},{7,6},{8,9},{9,8},{10,11... | collective-permute-start | bytes 294920 | tf_op jit(solution)/shard_map/ppermute | solution.py:123
  7.6 4.7 %collective-permute-start.1 = (bf16[6,128,128]{2,1,0:T(8,128)(2,1)S(1)}, bf16[6,128,128]{2,1,0:T(8,128)(2,1)S(1)}, u32[]{:S(2)}, u32[]{:S(2)}) collective-permute-start(bf16[6,128,128]{2,1,0:T(8,128)(2,1)S(1)} %bitcast.14), channel_id=1, source_target_pairs={{2,4},{3,5},{4,2},{5,3},{10,12},{11,13},{12,10},{13,11},{18,20},{1... | collective-permute-start | bytes 589832 | tf_op jit(solution)/shard_map/ppermute | solution.py:139
  8.3 5.3 %collective-permute-start.3 = (bf16[6,128,128]{2,1,0:T(8,128)(2,1)S(1)}, bf16[6,128,128]{2,1,0:T(8,128)(2,1)S(1)}, u32[]{:S(2)}, u32[]{:S(2)}) collective-permute-start(bf16[6,128,128]{2,1,0:T(8,128)(2,1)S(1)} %collective-permute-done.refs_1_), channel_id=1, source_target_pairs={{2,4},{3,5},{4,2},{5,3},{10,12},{11,13},{12,10},{13,11},{18,20},{1... | collective-permute-start | bytes 589832 | tf_op jit(solution)/shard_map/ppermute | solution.py:139
  11.6 4.2 %collective-permute-start.8 = (bf16[2,3,128,128]{3,2,1,0:T(8,128)(2,1)S(1)}, bf16[2,3,128,128]{3,2,1,0:T(8,128)(2,1)S(1)}, u32[]{:S(2)}, u32[]{:S(2)}) collective-permute-start(bf16[2,3,128,128]{3,2,1,0:T(8,128)(2,1)S(1)} %pad_maximum_fusion.1.refs_7_), channel_id=1, source_target_pairs={{0,8},{8,0},{16,24},{24,16},{1,9},{9,1},{17,25},{25,17},{2,10},{10... | collective-permute-start | bytes 589832 | tf_op jit(solution)/shard_map/ppermute | solution.py:117
  11.8 3.1 %copy-start.2 = (s32[4,8,2,3]{1,2,3,0:T(2,128)S(1)}, s32[4,8,2,3]{1,2,3,0:T(2,128)}, u32[]{:S(2)}) copy-start(s32[4,8,2,3]{1,2,3,0:T(2,128)} %param.7) | copy-start | bytes 2308
  11.8 4.0 %collective-permute-start.5 = (bf16[2,3,128,128]{3,2,1,0:T(8,128)(2,1)S(1)}, bf16[2,3,128,128]{3,2,1,0:T(8,128)(2,1)S(1)}, u32[]{:S(2)}, u32[]{:S(2)}) collective-permute-start(bf16[2,3,128,128]{3,2,1,0:T(8,128)(2,1)S(1)} %pad_maximum_fusion.refs_5_), channel_id=1, source_target_pairs={{0,8},{8,0},{16,24},{24,16},{1,9},{9,1},{17,25},{25,17},{2,10},{10... | collective-permute-start | bytes 589832 | tf_op jit(solution)/shard_map/ppermute | solution.py:117
  12.3 12.1 %collective-permute-start.2 = (bf16[6,128,128]{2,1,0:T(8,128)(2,1)S(1)}, bf16[6,128,128]{2,1,0:T(8,128)(2,1)S(1)}, u32[]{:S(2)}, u32[]{:S(2)}) collective-permute-start(bf16[6,128,128]{2,1,0:T(8,128)(2,1)S(1)} %collective-permute-done.1.refs_2_), channel_id=1, source_target_pairs={{2,0},{3,1},{4,6},{5,7},{10,8},{11,9},{12,14},{13,15},{18,16},{19,... | collective-permute-start | bytes 589832 | tf_op jit(solution)/shard_map/ppermute | solution.py:139
  13.6 14.4 %collective-permute-start.9 = (bf16[6,128,128]{2,1,0:T(8,128)(2,1)S(1)}, bf16[6,128,128]{2,1,0:T(8,128)(2,1)S(1)}, u32[]{:S(2)}, u32[]{:S(2)}) collective-permute-start(bf16[6,128,128]{2,1,0:T(8,128)(2,1)S(1)} %collective-permute-done.3.refs_4_), channel_id=1, source_target_pairs={{2,0},{3,1},{4,6},{5,7},{10,8},{11,9},{12,14},{13,15},{18,16},{19,... | collective-permute-start | bytes 589832 | tf_op jit(solution)/shard_map/ppermute | solution.py:139
  14.9 0.7 %copy-start.1 = (s32[4,8,6]{1,0,2:T(4,128)S(1)}, s32[4,8,6]{1,0,2:T(4,128)}, u32[]{:S(2)}) copy-start(s32[4,8,6]{1,0,2:T(4,128)} %param.5) | copy-start | bytes 2308
  28.9 5.0 %collective-permute-start.10 = (f32[256,128]{1,0:T(8,128)S(1)}, f32[256,128]{1,0:T(8,128)S(1)}, u32[]{:S(2)}, u32[]{:S(2)}) collective-permute-start(f32[256,128]{1,0:T(8,128)S(1)} %shard_map.48), channel_id=1, source_target_pairs={{0,1},{1,0},{2,3},{3,2},{4,5},{5,4},{6,7},{7,6},{8,9},{9,8},{10,11... | collective-permute-start | bytes 393224 | tf_op jit(solution)/shard_map/ppermute | solution.py:117

commit v9 on v6

--- a/solution.py
+++ b/solution.py
@@ -7,7 +7,6 @@
 
 KT = 8
 RT = 2
-CUT = 4
 SMEM = pl.BlockSpec(memory_space=pltpu.SMEM)
 VMEM = pl.BlockSpec(memory_space=pltpu.VMEM)
 
@@ -131,24 +130,16 @@
     return lax.ppermute(block, axis, route)
 
 
-def crossed(block, mask):
-    rows, cols = lax.axis_size("row"), lax.axis_size("col")
-    route = [(r * cols + c, (r ^ mask) * cols + (c ^ 1)) for r in range(rows) for c in range(cols)]
-    return lax.ppermute(block, ("row", "col"), route)
-
-
-def gather(block, cut):
-    distance = lax.axis_size("col") // 4
-    far_head = across(block[:cut], "col", 2 * distance)
-    tail, _ = lax.optimization_barrier((block[cut:], far_head))
-    far_tail = across(tail, "col", 2 * distance)
-    blocks = {0: (block,), distance: (far_head, far_tail)}
-    near = distance // 2
-    while near:
-        for s in sorted(blocks):
-            blocks[s ^ near] = tuple(across(part, "col", 2 * near) for part in blocks[s])
-        near //= 2
-    return sorted(blocks.items())
+def row_gather(right, y):
+    given = lax.dynamic_index_in_dim(right, 1 - y, 0, keepdims=False)
+    own = lax.dynamic_index_in_dim(right, y, 0, keepdims=False)
+    blocks = {0: jnp.stack([own, across(given, "col", 1)])}
+    distance = lax.axis_size("row") // 2
+    while distance:
+        for t in sorted(blocks):
+            blocks[t ^ distance] = across(blocks[t], "row", distance)
+        distance //= 2
+    return [blocks[t] for t in range(len(blocks))]
 
 
 def shards(left_tiles, left_index, right_tiles, right_index):
@@ -158,17 +149,18 @@
     left = left_tiles[0, 0]
     right = right_tiles[0, 0]
     slots = left.shape[0]
+    rows = lax.axis_size("row")
 
-    lefts = gather(left, CUT)
-    given = lax.dynamic_index_in_dim(right, 1 - y, 0, keepdims=True)
-    own = lax.dynamic_index_in_dim(right, y, 0, keepdims=True)
-    rights = []
-    for t in range(0, lax.axis_size("row"), 2):
-        pair = jnp.concatenate([across(own, "row", t) if t else own, crossed(given, t)])
-        rights += [pair, across(pair, "row", 1)]
+    lefts = [(s, (across(left, "col", 2 * s) if s else left,)) for s in range(rows)]
+    place = jnp.stack([row, z, y])
 
-    place = jnp.stack([row, z, y])
-    codes = find_matches(place, left_index, right_index)
+    def right_side():
+        return find_matches(place, left_index, right_index), row_gather(right, y)
+
+    def nothing():
+        return jnp.zeros((rows * 2 * slots,), jnp.int32), [jnp.zeros_like(right)] * rows
+
+    codes, rights = lax.cond(row < rows, right_side, nothing)
     mine, other, right_last = first_products(place, codes, lefts[:-1], rights, slots)
     far, final = lefts[-1]
     other = last_products(codes, far, final, right_last, other, 1, slots)

time: 35.2 us -> 32.9 us (0.935)
  starting transfers between devices: 17.5 us -> 11.5 us
  waiting for transfers between devices: 6.93 us -> 10.5 us
    ppermute x2 -> x0, starting transfers between devices: 4.47 us -> none  [crossed(): return lax.ppermute(block, ('row', 'col'), route)]
    ppermute x9 -> x8, waiting for transfers between devices: 6.92 us -> 10.5 us  [across(): return lax.ppermute(block, axis, route)]
    unnamed x13 -> x6, local copies, waits for them, and re-layouts: 2.12 us -> 0.65 us
    ppermute x9 -> x8, starting transfers between devices: 13 us -> 11.5 us  [across(): return lax.ppermute(block, axis, route)]
    another operation x0 -> x2, local copies, waits for them, and re-layouts: none -> 1.43 us
    another operation x0 -> x1, other arithmetic: none -> 0.7 us  [row_gather(): blocks = {0: jnp.stack([own, across(given, 'col', 1)])}]
    another operation x1, other arithmetic: 0.66 us -> 0.08 us  [shards(): place = jnp.stack([row, z, y])]
  transfers between devices with their start and end apart: 11 -> 8, of which waited for: 3 -> 3; matrix products, arithmetic and copies ran while one was open for 6% -> 10% of each run, Pallas kernels for 15% -> 16%
where the time goes in v9:
time: 32.9 us; the launch traced here: 32.6 us
  starting transfers between devices  11.5 us (35%)
  waiting for transfers between devices  10.5 us (32%)
  Pallas kernels  6.04 us (18%)
  local copies, waits for them, and re-layouts  3.07 us (9%)
  other arithmetic  1.42 us (4%)
    ppermute x8, starting transfers between devices, across(): return lax.ppermute(block, axis, route)  11.5 us
    ppermute x8, waiting for transfers between devices, across(): return lax.ppermute(block, axis, route)  10.5 us
    pallas_call x1, Pallas kernels, find_matches(): pl.pallas_call(kernel, out_shape=jax.ShapeDtypeStruct((inner * 2 * slots,...  2.43 us
    pallas_call x1, Pallas kernels, first_products(): pl.pallas_call(kernel, out_shape=[jax.ShapeDtypeStruct((RT * tile, tile),...  2.28 us
    another operation x2, local copies, waits for them, and re-layouts  1.43 us
    pallas_call x2, Pallas kernels, last_products(): pl.pallas_call(kernel, out_shape=jax.ShapeDtypeStruct(total.shape, total....  1.33 us
    dynamic_slice x1, local copies, waits for them, and re-layouts, row_gather(): own = lax.dynamic_index_in_dim(right, y, 0, keepdims=False)  0.99 us
    another operation x1, other arithmetic, row_gather(): blocks = {0: jnp.stack([own, across(given, 'col', 1)])}  0.7 us
  transfers between devices with their start and end apart: 8, of which 3 were waited for; matrix products, arithmetic and copies ran while one was open for 10% of the time, Pallas kernels for 16%

profile of v9, /device:TPU:0, one launch (start us, length us, event | category | flops | bytes accessed | tf_op | source)
XLA Modules:
  0.0 32.6 jit_solution(9607916828893768929)
XLA Ops:
  0.0 3.0 %collective-permute-start.5 = (bf16[6,128,128]{2,1,0:T(8,128)(2,1)}, bf16[6,128,128]{2,1,0:T(8,128)(2,1)S(1)}, u32[]{:S(2)}, u32[]{:S(2)}) collective-permute-start(bf16[6,128,128]{2,1,0:T(8,128)(2,1)} %bitcast.9), channel_id=1, source_target_pairs={{0,2},{1,3},{2,0},{3,1},{4,6},{5,7},{6,4},{7,5},{8,10},{9,11},{10,... | collective-permute-start | bytes 589832 | tf_op jit(solution)/shard_map/ppermute | solution.py:130
  3.0 2.6 %collective-permute-start.6 = (bf16[6,128,128]{2,1,0:T(8,128)(2,1)}, bf16[6,128,128]{2,1,0:T(8,128)(2,1)S(1)}, u32[]{:S(2)}, u32[]{:S(2)}) collective-permute-start(bf16[6,128,128]{2,1,0:T(8,128)(2,1)} %bitcast.10), channel_id=1, source_target_pairs={{0,4},{1,5},{2,6},{3,7},{4,0},{5,1},{6,2},{7,3},{8,12},{9,13},{10,... | collective-permute-start | bytes 589832 | tf_op jit(solution)/shard_map/ppermute | solution.py:130
  5.6 0.0 collective-permute-start.4
  5.6 0.0 copy-start.1
  5.6 0.0 copy-start.2
  5.6 0.1 pad_add_fusion.place_ref
  5.7 0.6 %copy-done.1 = s32[4,8,6]{1,0,2:T(4,128)S(1)} copy-done((s32[4,8,6]{1,0,2:T(4,128)S(1)}, s32[4,8,6]{1,0,2:T(4,128)}, u32[]{:S(2)}) %copy-start.1) | copy-done | bytes 792
  6.3 0.0 copy-done.2
  6.3 0.0 copy-start
  6.3 16.3 %conditional.1 = (s32[48]{0:T(128)S(1)}, bf16[2,3,128,128]{3,2,1,0:T(8,128)(2,1)}, bf16[2,3,128,128]{3,2,1,0:T(8,128)(2,1)}, bf16[2,3,128,128]{3,2,1,0:T(8,128)(2,1)}, bf16[2,3,128,128]{3,2,1,0:T(8,128)(2,1)}) conditional(s32[]{:T(128)} %convert_element_type.6, () %tuple.13, (s32[3]{0:T(128)S(1)}, s32[4,8,6]{1,0,2:T(4,128)S(1)}, ...), branch_computations={%region_0.0_spmd, %region_1.2_spmd} | conditional | flops 98311 | bytes 3542304 | solution.py:163
  6.3 1.0 %dynamic-slice_bitcast_fusion.1 = (bf16[1,3,128,128]{3,2,1,0:T(8,128)(2,1)S(1)}, bf16[3,128,128]{2,1,0:T(8,128)(2,1)S(1)}) fusion(bf16[1,1,2,3,128,128]{5,4,3,2,1,0:T(8,128)(2,1)} %get-tuple-element.42, s32[]{:T(128)S(6)} %select_n.5, s32[]{:T(128)S(6)} %select_n.6), kind=kLoop, calls=%fused_computation.2 | loop fusion | bytes 393224 | tf_op jit(solution)/shard_map/cond/branch_1_fun/jit(dynamic_index_in_dim)/dynamic_slice | solution.py:135
  7.3 1.8 %collective-permute-start = (bf16[3,128,128]{2,1,0:T(8,128)(2,1)S(1)}, bf16[3,128,128]{2,1,0:T(8,128)(2,1)S(1)}, u32[]{:S(2)}, u32[]{:S(2)}) collective-permute-start(bf16[3,128,128]{2,1,0:T(8,128)(2,1)S(1)} %get-tuple-element.49), channel_id=1, source_target_pairs={{0,1},{1,0},{2,3},{3,2},{4,5},{5,4},{6,7},{7,6},{8,9},{9,8},{10,11... | collective-permute-start | bytes 294920 | tf_op jit(solution)/shard_map/cond/branch_1_fun/ppermute | solution.py:130
  9.1 2.9 %collective-permute-done = bf16[3,128,128]{2,1,0:T(8,128)(2,1)S(1)} collective-permute-done((bf16[3,128,128]{2,1,0:T(8,128)(2,1)S(1)}, bf16[3,128,128]{2,1,0:T(8,128)(2,1)S(1)}, u32[]{:S(2)}, u32[]{:S(2)}) %collective-permute-start) | collective-permute-done | bytes 98336 | tf_op jit(solution)/shard_map/cond/branch_1_fun/ppermute | solution.py:130
  12.0 0.7 %pad_maximum_fusion = bf16[2,3,128,128]{3,2,1,0:T(8,128)(2,1)} fusion(bf16[1,3,128,128]{3,2,1,0:T(8,128)(2,1)S(1)} %bitcast.13, bf16[1,3,128,128]{3,2,1,0:T(8,128)(2,1)S(1)} %get-tuple-element.48), kind=kLoop, calls=%fused_computation | loop fusion | flops 98304 | bytes 393216 | tf_op jit(solution)/shard_map/cond/branch_1_fun/stack | solution.py:136
  12.7 1.7 %collective-permute-start.2 = (bf16[2,3,128,128]{3,2,1,0:T(8,128)(2,1)}, bf16[2,3,128,128]{3,2,1,0:T(8,128)(2,1)}, u32[]{:S(2)}, u32[]{:S(2)}) collective-permute-start(bf16[2,3,128,128]{3,2,1,0:T(8,128)(2,1)} %pad_maximum_fusion), channel_id=1, source_target_pairs={{0,16},{8,24},{16,0},{24,8},{1,17},{9,25},{17,1},{25,9},{2,18},{10... | collective-permute-start | bytes 589832 | tf_op jit(solution)/shard_map/cond/branch_1_fun/ppermute | solution.py:130
  14.4 0.0 collective-permute-start.1
  14.4 4.3 %collective-permute-done.2 = bf16[2,3,128,128]{3,2,1,0:T(8,128)(2,1)} collective-permute-done((bf16[2,3,128,128]{3,2,1,0:T(8,128)(2,1)}, bf16[2,3,128,128]{3,2,1,0:T(8,128)(2,1)}, u32[]{:S(2)}, u32[]{:S(2)}) %collective-permute-start.2) | collective-permute-done | bytes 196640 | tf_op jit(solution)/shard_map/cond/branch_1_fun/ppermute | solution.py:130
  18.7 0.0 collective-permute-start.3
  18.7 0.7 %copy.9.ri_ref = s32[4,8,2,3]{3,2,1,0:T(2,128)} copy(s32[4,8,2,3]{1,2,3,0:T(2,128)S(1)} %get-tuple-element.45) | data formatting | bytes 1536 | tf_op jit(solution)/shard_map
  19.5 0.7 %copy.8.li_ref = s32[4,8,6]{2,1,0:T(8,128)} copy(s32[4,8,6]{1,0,2:T(4,128)S(1)} %get-tuple-element.44) | data formatting | bytes 1536 | tf_op jit(solution)/shard_map
  20.1 2.4 %branch_1_fun.1 = s32[48]{0:T(128)S(1)} custom-call(s32[3]{0:T(128)S(1)} %get-tuple-element.16.place_ref, s32[4,8,6]{2,1,0:T(8,128)} %copy.8.li_ref, s32[4,8,2,3]{3,2,1,0:T(2,128)} %copy.9.ri_ref), custom_call_target="tpu_custom_call" | custom-call | tf_op jit(solution)/shard_map/cond/branch_1_fun/pallas_call | solution.py:36
  22.6 0.0 collective-permute-done.1
  22.6 0.0 collective-permute-done.3
  22.6 0.0 collective-permute-done.5.refs_1_
  22.6 0.0 collective-permute-done.6.refs_2_
  22.6 0.0 copy-done
  22.6 2.3 %shard_map.49 = (f32[256,128]{1,0:T(8,128)S(1)}, f32[256,128]{1,0:T(8,128)S(1)}, bf16[2,3,128,128]{3,2,1,0:T(8,128)(2,1)S(1)}) custom-call(s32[3]{0:T(128)S(1)} %pad_add_fusion.place_ref, s32[48]{0:T(128)S(1)} %get-tuple-element.29.codes_ref, bf16[6,128,128]{2,1,0:T(8,128)(2,1)S(1)} %bitcast.12, bf16[6,128,128]{2,1,0:T(8,128)(2,1)S(1)} %collective-permute-done.5.refs_1_, ...), custom_call_target="tpu_custom_call" | custom-call | flops 201326592 | bytes 786432 | tf_op jit(solution)/shard_map/pallas_call | solution.py:87
  24.9 0.0 collective-permute-done.4.refs_0_
  24.9 0.7 %shard_map.51 = f32[256,128]{1,0:T(8,128)S(1)} custom-call(s32[48]{0:T(128)S(1)} %get-tuple-element.29.codes_ref, bf16[6,128,128]{2,1,0:T(8,128)(2,1)S(1)} %collective-permute-done.4.refs_0_, bf16[2,3,128,128]{3,2,1,0:T(8,128)(2,1)S(1)} %get-tuple-element.34.refs_1_, f32[256,128]{1,0:T(8,128)S(1)} %get-tuple-element.36.refs_2_), custom_call_target="tpu_custom_call" | custom-call | flops 25165824 | bytes 196608 | tf_op jit(solution)/shard_map/pallas_call | solution.py:116
  25.6 2.4 %collective-permute-start.7 = (f32[256,128]{1,0:T(8,128)S(1)}, f32[256,128]{1,0:T(8,128)S(1)}, u32[]{:S(2)}, u32[]{:S(2)}) collective-permute-start(f32[256,128]{1,0:T(8,128)S(1)} %shard_map.51), channel_id=1, source_target_pairs={{0,1},{1,0},{2,3},{3,2},{4,5},{5,4},{6,7},{7,6},{8,9},{9,8},{10,11... | collective-permute-start | bytes 393224 | tf_op jit(solution)/shard_map/ppermute | solution.py:130
  28.0 0.6 %shard_map.50 = f32[256,128]{1,0:T(8,128)S(1)} custom-call(s32[48]{0:T(128)S(1)} %get-tuple-element.29.codes_ref, bf16[6,128,128]{2,1,0:T(8,128)(2,1)S(1)} %collective-permute-done.4.refs_0_, bf16[2,3,128,128]{3,2,1,0:T(8,128)(2,1)S(1)} %get-tuple-element.34.refs_1_, f32[256,128]{1,0:T(8,128)S(1)} %get-tuple-element.35.refs_2_), custom_call_target="tpu_custom_call" | custom-call | flops 25165824 | bytes 196608 | tf_op jit(solution)/shard_map/pallas_call | solution.py:116
  28.7 3.3 %collective-permute-done.7 = f32[256,128]{1,0:T(8,128)S(1)} collective-permute-done((f32[256,128]{1,0:T(8,128)S(1)}, f32[256,128]{1,0:T(8,128)S(1)}, u32[]{:S(2)}, u32[]{:S(2)}) %collective-permute-start.7) | collective-permute-done | bytes 131104 | tf_op jit(solution)/shard_map/ppermute | solution.py:130
  32.0 0.6 %add_convert_fusion = bf16[256,128]{1,0:T(8,128)(2,1)} fusion(f32[256,128]{1,0:T(8,128)S(1)} %shard_map.50, f32[256,128]{1,0:T(8,128)S(1)} %collective-permute-done.7), kind=kLoop, calls=%fused_computation.3 | loop fusion | flops 65536 | bytes 327680 | tf_op jit(solution)/shard_map/convert_element_type | solution.py:169
Async XLA Ops:
  0.0 22.6 %collective-permute-start.5 = (bf16[6,128,128]{2,1,0:T(8,128)(2,1)}, bf16[6,128,128]{2,1,0:T(8,128)(2,1)S(1)}, u32[]{:S(2)}, u32[]{:S(2)}) collective-permute-start(bf16[6,128,128]{2,1,0:T(8,128)(2,1)} %bitcast.9), channel_id=1, source_target_pairs={{0,2},{1,3},{2,0},{3,1},{4,6},{5,7},{6,4},{7,5},{8,10},{9,11},{10,... | collective-permute-start | bytes 589832 | tf_op jit(solution)/shard_map/ppermute | solution.py:130
  3.0 19.6 %collective-permute-start.6 = (bf16[6,128,128]{2,1,0:T(8,128)(2,1)}, bf16[6,128,128]{2,1,0:T(8,128)(2,1)S(1)}, u32[]{:S(2)}, u32[]{:S(2)}) collective-permute-start(bf16[6,128,128]{2,1,0:T(8,128)(2,1)} %bitcast.10), channel_id=1, source_target_pairs={{0,4},{1,5},{2,6},{3,7},{4,0},{5,1},{6,2},{7,3},{8,12},{9,13},{10,... | collective-permute-start | bytes 589832 | tf_op jit(solution)/shard_map/ppermute | solution.py:130
  5.6 19.3 %collective-permute-start.4 = (bf16[6,128,128]{2,1,0:T(8,128)(2,1)}, bf16[6,128,128]{2,1,0:T(8,128)(2,1)S(1)}, u32[]{:S(2)}, u32[]{:S(2)}) collective-permute-start(bf16[6,128,128]{2,1,0:T(8,128)(2,1)} %bitcast.11), channel_id=1, source_target_pairs={{0,6},{1,7},{2,4},{3,5},{4,2},{5,3},{6,0},{7,1},{8,14},{9,15},{10,... | collective-permute-start | bytes 589832 | tf_op jit(solution)/shard_map/ppermute | solution.py:130
  5.6 0.7 %copy-start.1 = (s32[4,8,6]{1,0,2:T(4,128)S(1)}, s32[4,8,6]{1,0,2:T(4,128)}, u32[]{:S(2)}) copy-start(s32[4,8,6]{1,0,2:T(4,128)} %param.7) | copy-start | bytes 2308
  5.6 0.7 %copy-start.2 = (s32[4,8,2,3]{1,2,3,0:T(2,128)S(1)}, s32[4,8,2,3]{1,2,3,0:T(2,128)}, u32[]{:S(2)}) copy-start(s32[4,8,2,3]{1,2,3,0:T(2,128)} %param.9) | copy-start | bytes 2308
  6.3 16.3 %copy-start = (bf16[1,1,6,128,128]{4,3,2,1,0:T(8,128)(2,1)S(1)}, bf16[1,1,6,128,128]{4,3,2,1,0:T(8,128)(2,1)}, u32[]{:S(2)}) copy-start(bf16[1,1,6,128,128]{4,3,2,1,0:T(8,128)(2,1)} %param.6) | copy-start | bytes 589828
  7.3 4.7 %collective-permute-start = (bf16[3,128,128]{2,1,0:T(8,128)(2,1)S(1)}, bf16[3,128,128]{2,1,0:T(8,128)(2,1)S(1)}, u32[]{:S(2)}, u32[]{:S(2)}) collective-permute-start(bf16[3,128,128]{2,1,0:T(8,128)(2,1)S(1)} %get-tuple-element.49), channel_id=1, source_target_pairs={{0,1},{1,0},{2,3},{3,2},{4,5},{5,4},{6,7},{7,6},{8,9},{9,8},{10,11... | collective-permute-start | bytes 294920 | tf_op jit(solution)/shard_map/cond/branch_1_fun/ppermute | solution.py:130
  12.7 6.0 %collective-permute-start.2 = (bf16[2,3,128,128]{3,2,1,0:T(8,128)(2,1)}, bf16[2,3,128,128]{3,2,1,0:T(8,128)(2,1)}, u32[]{:S(2)}, u32[]{:S(2)}) collective-permute-start(bf16[2,3,128,128]{3,2,1,0:T(8,128)(2,1)} %pad_maximum_fusion), channel_id=1, source_target_pairs={{0,16},{8,24},{16,0},{24,8},{1,17},{9,25},{17,1},{25,9},{2,18},{10... | collective-permute-start | bytes 589832 | tf_op jit(solution)/shard_map/cond/branch_1_fun/ppermute | solution.py:130
  14.4 8.2 %collective-permute-start.1 = (bf16[2,3,128,128]{3,2,1,0:T(8,128)(2,1)}, bf16[2,3,128,128]{3,2,1,0:T(8,128)(2,1)}, u32[]{:S(2)}, u32[]{:S(2)}) collective-permute-start(bf16[2,3,128,128]{3,2,1,0:T(8,128)(2,1)} %pad_maximum_fusion), channel_id=1, source_target_pairs={{0,8},{8,0},{16,24},{24,16},{1,9},{9,1},{17,25},{25,17},{2,10},{10... | collective-permute-start | bytes 589832 | tf_op jit(solution)/shard_map/cond/branch_1_fun/ppermute | solution.py:130
  18.7 3.9 %collective-permute-start.3 = (bf16[2,3,128,128]{3,2,1,0:T(8,128)(2,1)}, bf16[2,3,128,128]{3,2,1,0:T(8,128)(2,1)}, u32[]{:S(2)}, u32[]{:S(2)}) collective-permute-start(bf16[2,3,128,128]{3,2,1,0:T(8,128)(2,1)} %collective-permute-done.2), channel_id=1, source_target_pairs={{0,8},{8,0},{16,24},{24,16},{1,9},{9,1},{17,25},{25,17},{2,10},{10... | collective-permute-start | bytes 589832 | tf_op jit(solution)/shard_map/cond/branch_1_fun/ppermute | solution.py:130
  25.6 6.4 %collective-permute-start.7 = (f32[256,128]{1,0:T(8,128)S(1)}, f32[256,128]{1,0:T(8,128)S(1)}, u32[]{:S(2)}, u32[]{:S(2)}) collective-permute-start(f32[256,128]{1,0:T(8,128)S(1)} %shard_map.51), channel_id=1, source_target_pairs={{0,1},{1,0},{2,3},{3,2},{4,5},{5,4},{6,7},{7,6},{8,9},{9,8},{10,11... | collective-permute-start | bytes 393224 | tf_op jit(solution)/shard_map/ppermute | solution.py:130

commit v10 on v9

--- a/solution.py
+++ b/solution.py
@@ -130,16 +130,37 @@
     return lax.ppermute(block, axis, route)
 
 
-def row_gather(right, y):
+def crossed(block, mask):
+    rows, cols = lax.axis_size("row"), lax.axis_size("col")
+    route = [(r * cols + c, (r ^ mask) * cols + (c ^ 1)) for r in range(rows) for c in range(cols)]
+    return lax.ppermute(block, ("row", "col"), route)
+
+
+def gather(block, beside):
+    distance = lax.axis_size("col") // 4
+    steps = [distance >> n for n in range(distance.bit_length())]
+    came = [across(block, "col", 2 * d) for d in steps]
+    came, results = lax.optimization_barrier((came, beside()))
+    blocks = {0: block, **dict(zip(steps, came))}
+    for d in steps:
+        for s in sorted(blocks):
+            if s ^ d not in blocks and s & (d - 1) == 0:
+                blocks[s ^ d] = across(blocks[s], "col", 2 * d)
+    return [(s, (blocks[s],)) for s in range(len(blocks))], results
+
+
+def right_side(place, left_index, right_index, right, y):
+    codes = find_matches(place, left_index, right_index)
     given = lax.dynamic_index_in_dim(right, 1 - y, 0, keepdims=False)
     own = lax.dynamic_index_in_dim(right, y, 0, keepdims=False)
-    blocks = {0: jnp.stack([own, across(given, "col", 1)])}
-    distance = lax.axis_size("row") // 2
-    while distance:
-        for t in sorted(blocks):
-            blocks[t ^ distance] = across(blocks[t], "row", distance)
-        distance //= 2
-    return [blocks[t] for t in range(len(blocks))]
+    pairs = []
+    for t in range(0, lax.axis_size("row"), 2):
+        pairs.append(jnp.stack([across(own, "row", t) if t else own, crossed(given, t)]))
+    codes, pairs = lax.optimization_barrier((codes, pairs))
+    rights = []
+    for pair in pairs:
+        rights += [pair, across(pair, "row", 1)]
+    return codes, rights
 
 
 def shards(left_tiles, left_index, right_tiles, right_index):
@@ -151,16 +172,16 @@
     slots = left.shape[0]
     rows = lax.axis_size("row")
 
-    lefts = [(s, (across(left, "col", 2 * s) if s else left,)) for s in range(rows)]
     place = jnp.stack([row, z, y])
 
-    def right_side():
-        return find_matches(place, left_index, right_index), row_gather(right, y)
-
-    def nothing():
-        return jnp.zeros((rows * 2 * slots,), jnp.int32), [jnp.zeros_like(right)] * rows
-
-    codes, rights = lax.cond(row < rows, right_side, nothing)
+    def right_branch():
+        return lax.cond(
+            row < rows,
+            lambda: right_side(place, left_index, right_index, right, y),
+            lambda: (jnp.zeros((rows * 2 * slots,), jnp.int32), [jnp.zeros_like(right)] * rows),
+        )
+
+    lefts, (codes, rights) = gather(left, right_branch)
     mine, other, right_last = first_products(place, codes, lefts[:-1], rights, slots)
     far, final = lefts[-1]
     other = last_products(codes, far, final, right_last, other, 1, slots)

time: 32.9 us -> 32.3 us (0.982)
  waiting for transfers between devices: 10.5 us -> 8.25 us
  Pallas kernels: 6.04 us -> 7.03 us
  other arithmetic: 1.42 us -> 2.11 us
    ppermute x8 -> x7, starting transfers between devices: 11.5 us -> 8.36 us  [across(): return lax.ppermute(block, axis, route)]
    ppermute x0 -> x2, starting transfers between devices: none -> 3.02 us  [crossed(): return lax.ppermute(block, ('row', 'col'), route)]
    ppermute x8 -> x7, waiting for transfers between devices: 10.5 us -> 8.24 us  [across(): return lax.ppermute(block, axis, route)]
    squeeze x0 -> x1, local copies, waits for them, and re-layouts: none -> 1.01 us  [right_side(): own = lax.dynamic_index_in_dim(right, y, 0, keepdims=False)]
    dynamic_slice x1 -> x0, local copies, waits for them, and re-layouts: 0.99 us -> none  [row_gather(): own = lax.dynamic_index_in_dim(right, y, 0, keepdims=False)]
    another operation x1 -> x2, other arithmetic: 0.7 us -> 1.39 us  [right_side(): jnp.stack([across(own, 'row', t) if t else own, crossed(given, t)])]
    pallas_call x1, Pallas kernels: 2.28 us -> 2.93 us  [first_products(): pl.pallas_call(kernel, out_shape=[jax.ShapeDtypeStruct((RT * tile, tile),...]
    pallas_call x2, Pallas kernels: 1.33 us -> 1.68 us  [last_products(): pl.pallas_call(kernel, out_shape=jax.ShapeDtypeStruct(total.shape, total....]
  transfers between devices with their start and end apart: 8 -> 9, of which waited for: 3 -> 4; matrix products, arithmetic and copies ran while one was open for 10% -> 12% of each run, Pallas kernels for 16% -> 19%
where the time goes in v10:
time: 32.3 us; the launch traced here: 31.9 us
  starting transfers between devices  11.4 us (35%)
  waiting for transfers between devices  8.25 us (26%)
  Pallas kernels  7.03 us (22%)
  local copies, waits for them, and re-layouts  3.09 us (10%)
  other arithmetic  2.11 us (7%)
    ppermute x7, starting transfers between devices, across(): return lax.ppermute(block, axis, route)  8.36 us
    ppermute x7, waiting for transfers between devices, across(): return lax.ppermute(block, axis, route)  8.24 us
    ppermute x2, starting transfers between devices, crossed(): return lax.ppermute(block, ('row', 'col'), route)  3.02 us
    pallas_call x1, Pallas kernels, first_products(): pl.pallas_call(kernel, out_shape=[jax.ShapeDtypeStruct((RT * tile, tile),...  2.93 us
    pallas_call x1, Pallas kernels, find_matches(): pl.pallas_call(kernel, out_shape=jax.ShapeDtypeStruct((inner * 2 * slots,...  2.43 us
    pallas_call x2, Pallas kernels, last_products(): pl.pallas_call(kernel, out_shape=jax.ShapeDtypeStruct(total.shape, total....  1.68 us
    another operation x2, local copies, waits for them, and re-layouts  1.43 us
    another operation x2, other arithmetic, right_side(): jnp.stack([across(own, 'row', t) if t else own, crossed(given, t)])  1.39 us
  transfers between devices with their start and end apart: 9, of which 4 were waited for; matrix products, arithmetic and copies ran while one was open for 12% of the time, Pallas kernels for 19%

profile of v10, /device:TPU:0, one launch (start us, length us, event | category | flops | bytes accessed | tf_op | source)
XLA Modules:
  0.0 31.9 jit_solution(4557820066910391235)
XLA Ops:
  0.0 4.0 %collective-permute-start.5 = (bf16[6,128,128]{2,1,0:T(8,128)(2,1)}, bf16[6,128,128]{2,1,0:T(8,128)(2,1)S(1)}, u32[]{:S(2)}, u32[]{:S(2)}) collective-permute-start(bf16[6,128,128]{2,1,0:T(8,128)(2,1)} %bitcast.13), channel_id=1, source_target_pairs={{0,4},{1,5},{2,6},{3,7},{4,0},{5,1},{6,2},{7,3},{8,12},{9,13},{10,... | collective-permute-start | bytes 589832 | tf_op jit(solution)/shard_map/ppermute | solution.py:130
  4.0 1.6 %collective-permute-start.6 = (bf16[6,128,128]{2,1,0:T(8,128)(2,1)}, bf16[6,128,128]{2,1,0:T(8,128)(2,1)S(1)}, u32[]{:S(2)}, u32[]{:S(2)}) collective-permute-start(bf16[6,128,128]{2,1,0:T(8,128)(2,1)} %bitcast.14), channel_id=1, source_target_pairs={{0,2},{1,3},{2,0},{3,1},{4,6},{5,7},{6,4},{7,5},{8,10},{9,11},{10,... | collective-permute-start | bytes 589832 | tf_op jit(solution)/shard_map/ppermute | solution.py:130
  5.6 0.0 copy-start.1
  5.6 0.0 copy-start.2
  5.6 0.1 pad_add_fusion.place_ref
  5.7 0.6 %copy-done.1 = s32[4,8,6]{1,0,2:T(4,128)S(1)} copy-done((s32[4,8,6]{1,0,2:T(4,128)S(1)}, s32[4,8,6]{1,0,2:T(4,128)}, u32[]{:S(2)}) %copy-start.1) | copy-done | bytes 792
  6.3 0.0 copy-done.2
  6.3 0.0 copy-start
  6.3 11.9 %conditional.1 = (s32[48]{0:T(128)S(1)}, bf16[2,3,128,128]{3,2,1,0:T(8,128)(2,1)}, bf16[2,3,128,128]{3,2,1,0:T(8,128)(2,1)}, bf16[2,3,128,128]{3,2,1,0:T(8,128)(2,1)}, bf16[2,3,128,128]{3,2,1,0:T(8,128)(2,1)}) conditional(s32[]{:T(128)} %convert_element_type.6, () %tuple.15, (s32[3]{0:T(128)S(1)}, s32[4,8,6]{1,0,2:T(4,128)S(1)}, ...), branch_computations={%region_0.0_spmd, %region_1.2_spmd} | conditional | flops 196615 | bytes 4033864 | solution.py:178
  6.3 1.0 %dynamic-slice_bitcast_fusion.1 = (bf16[3,128,128]{2,1,0:T(8,128)(2,1)S(1)}, bf16[3,128,128]{2,1,0:T(8,128)(2,1)S(1)}, bf16[1,3,128,128]{3,2,1,0:T(8,128)(2,1)S(1)}) fusion(bf16[1,1,2,3,128,128]{5,4,3,2,1,0:T(8,128)(2,1)} %get-tuple-element.59, s32[]{:T(128)S(6)} %select_n.5, s32[]{:T(128)S(6)} %select_n.6), kind=kLoop, calls=%fused_computation.3 | loop fusion | bytes 491528 | tf_op jit(solution)/shard_map/cond/branch_1_fun/jit(dynamic_index_in_dim)/squeeze | solution.py:155
  7.4 2.5 %collective-permute-start.2 = (bf16[3,128,128]{2,1,0:T(8,128)(2,1)S(1)}, bf16[3,128,128]{2,1,0:T(8,128)(2,1)S(1)}, u32[]{:S(2)}, u32[]{:S(2)}) collective-permute-start(bf16[3,128,128]{2,1,0:T(8,128)(2,1)S(1)} %get-tuple-element.66), channel_id=1, source_target_pairs={{0,17},{1,16},{2,19},{3,18},{4,21},{5,20},{6,23},{7,22},{8,25},{9,... | collective-permute-start | bytes 294920 | tf_op jit(solution)/shard_map/cond/branch_1_fun/ppermute | solution.py:136
  9.9 0.5 %collective-permute-start.1 = (bf16[3,128,128]{2,1,0:T(8,128)(2,1)S(1)}, bf16[3,128,128]{2,1,0:T(8,128)(2,1)S(1)}, u32[]{:S(2)}, u32[]{:S(2)}) collective-permute-start(bf16[3,128,128]{2,1,0:T(8,128)(2,1)S(1)} %get-tuple-element.65), channel_id=1, source_target_pairs={{0,16},{8,24},{16,0},{24,8},{1,17},{9,25},{17,1},{25,9},{2,18},{10... | collective-permute-start | bytes 294920 | tf_op jit(solution)/shard_map/cond/branch_1_fun/ppermute | solution.py:130
  10.4 0.5 %collective-permute-start = (bf16[3,128,128]{2,1,0:T(8,128)(2,1)S(1)}, bf16[3,128,128]{2,1,0:T(8,128)(2,1)S(1)}, u32[]{:S(2)}, u32[]{:S(2)}) collective-permute-start(bf16[3,128,128]{2,1,0:T(8,128)(2,1)S(1)} %get-tuple-element.66), channel_id=1, source_target_pairs={{0,1},{1,0},{2,3},{3,2},{4,5},{5,4},{6,7},{7,6},{8,9},{9,8},{10,11... | collective-permute-start | bytes 294920 | tf_op jit(solution)/shard_map/cond/branch_1_fun/ppermute | solution.py:136
  10.9 0.7 %copy.9.ri_ref = s32[4,8,2,3]{3,2,1,0:T(2,128)} copy(s32[4,8,2,3]{1,2,3,0:T(2,128)S(1)} %get-tuple-element.62) | data formatting | bytes 1536 | tf_op jit(solution)/shard_map
  11.7 0.7 %copy.8.li_ref = s32[4,8,6]{2,1,0:T(8,128)} copy(s32[4,8,6]{1,0,2:T(4,128)S(1)} %get-tuple-element.61) | data formatting | bytes 1536 | tf_op jit(solution)/shard_map
  12.3 2.4 %branch_1_fun.1 = s32[48]{0:T(128)S(1)} custom-call(s32[3]{0:T(128)S(1)} %get-tuple-element.16.place_ref, s32[4,8,6]{2,1,0:T(8,128)} %copy.8.li_ref, s32[4,8,2,3]{3,2,1,0:T(2,128)} %copy.9.ri_ref), custom_call_target="tpu_custom_call" | custom-call | tf_op jit(solution)/shard_map/cond/branch_1_fun/pallas_call | solution.py:36
  14.8 0.0 collective-permute-done.2
  14.8 0.0 collective-permute-done.1
  14.8 0.7 %pad_maximum_fusion.1 = bf16[2,3,128,128]{3,2,1,0:T(8,128)(2,1)} fusion(bf16[1,3,128,128]{3,2,1,0:T(8,128)(2,1)S(1)} %bitcast.17, bf16[1,3,128,128]{3,2,1,0:T(8,128)(2,1)S(1)} %bitcast.18), kind=kLoop, calls=%fused_computation.1 | loop fusion | flops 98304 | bytes 393216 | tf_op jit(solution)/shard_map/cond/branch_1_fun/stack | solution.py:158
  15.5 0.0 collective-permute-done
  15.5 0.7 %pad_maximum_fusion = bf16[2,3,128,128]{3,2,1,0:T(8,128)(2,1)} fusion(bf16[1,3,128,128]{3,2,1,0:T(8,128)(2,1)S(1)} %bitcast.16, bf16[1,3,128,128]{3,2,1,0:T(8,128)(2,1)S(1)} %get-tuple-element.67), kind=kLoop, calls=%fused_computation | loop fusion | flops 98304 | bytes 393216 | tf_op jit(solution)/shard_map/cond/branch_1_fun/stack | solution.py:158
  16.2 0.0 collective-permute-start.3
  16.2 0.5 %collective-permute-start.4 = (bf16[2,3,128,128]{3,2,1,0:T(8,128)(2,1)}, bf16[2,3,128,128]{3,2,1,0:T(8,128)(2,1)}, u32[]{:S(2)}, u32[]{:S(2)}) collective-permute-start(bf16[2,3,128,128]{3,2,1,0:T(8,128)(2,1)} %pad_maximum_fusion.1), channel_id=1, source_target_pairs={{0,8},{8,0},{16,24},{24,16},{1,9},{9,1},{17,25},{25,17},{2,10},{10... | collective-permute-start | bytes 589832 | tf_op jit(solution)/shard_map/cond/branch_1_fun/ppermute | solution.py:130
  16.7 1.3 %collective-permute-done.3 = bf16[2,3,128,128]{3,2,1,0:T(8,128)(2,1)} collective-permute-done((bf16[2,3,128,128]{3,2,1,0:T(8,128)(2,1)}, bf16[2,3,128,128]{3,2,1,0:T(8,128)(2,1)}, u32[]{:S(2)}, u32[]{:S(2)}) %collective-permute-start.3) | collective-permute-done | bytes 196640 | tf_op jit(solution)/shard_map/cond/branch_1_fun/ppermute | solution.py:130
  18.0 0.3 collective-permute-done.4
  18.3 0.0 collective-permute-done.5.refs_2_
  18.3 0.0 collective-permute-done.6.refs_1_
  18.3 0.5 %collective-permute-start.7 = (bf16[6,128,128]{2,1,0:T(8,128)(2,1)S(1)}, bf16[6,128,128]{2,1,0:T(8,128)(2,1)S(1)}, u32[]{:S(2)}, u32[]{:S(2)}) collective-permute-start(bf16[6,128,128]{2,1,0:T(8,128)(2,1)S(1)} %collective-permute-done.5.refs_2_), channel_id=1, source_target_pairs={{0,2},{1,3},{2,0},{3,1},{4,6},{5,7},{6,4},{7,5},{8,10},{9,11},{10,... | collective-permute-start | bytes 589832 | tf_op jit(solution)/shard_map/ppermute | solution.py:130
  18.7 0.0 copy-done
  18.7 2.9 %shard_map.49 = (f32[256,128]{1,0:T(8,128)S(1)}, f32[256,128]{1,0:T(8,128)S(1)}, bf16[2,3,128,128]{3,2,1,0:T(8,128)(2,1)S(1)}) custom-call(s32[3]{0:T(128)S(1)} %pad_add_fusion.place_ref, s32[48]{0:T(128)S(1)} %get-tuple-element.44.codes_ref, bf16[6,128,128]{2,1,0:T(8,128)(2,1)S(1)} %bitcast.15, bf16[6,128,128]{2,1,0:T(8,128)(2,1)S(1)} %collective-permute-done.6.refs_1_, ...), custom_call_target="tpu_custom_call" | custom-call | flops 201326592 | bytes 786432 | tf_op jit(solution)/shard_map/pallas_call | solution.py:87
  21.7 3.7 %collective-permute-done.7.refs_0_ = bf16[6,128,128]{2,1,0:T(8,128)(2,1)S(1)} collective-permute-done((bf16[6,128,128]{2,1,0:T(8,128)(2,1)S(1)}, bf16[6,128,128]{2,1,0:T(8,128)(2,1)S(1)}, u32[]{:S(2)}, u32[]{:S(2)}) %collective-permute-start.7) | collective-permute-done | bytes 196640 | tf_op jit(solution)/shard_map/ppermute | solution.py:130
  25.3 1.0 %shard_map.51 = f32[256,128]{1,0:T(8,128)S(1)} custom-call(s32[48]{0:T(128)S(1)} %get-tuple-element.44.codes_ref, bf16[6,128,128]{2,1,0:T(8,128)(2,1)S(1)} %collective-permute-done.7.refs_0_, bf16[2,3,128,128]{3,2,1,0:T(8,128)(2,1)S(1)} %get-tuple-element.51.refs_1_, f32[256,128]{1,0:T(8,128)S(1)} %get-tuple-element.53.refs_2_), custom_call_target="tpu_custom_call" | custom-call | flops 25165824 | bytes 196608 | tf_op jit(solution)/shard_map/pallas_call | solution.py:116
  26.3 1.3 %collective-permute-start.8 = (f32[256,128]{1,0:T(8,128)S(1)}, f32[256,128]{1,0:T(8,128)S(1)}, u32[]{:S(2)}, u32[]{:S(2)}) collective-permute-start(f32[256,128]{1,0:T(8,128)S(1)} %shard_map.51), channel_id=1, source_target_pairs={{0,1},{1,0},{2,3},{3,2},{4,5},{5,4},{6,7},{7,6},{8,9},{9,8},{10,11... | collective-permute-start | bytes 393224 | tf_op jit(solution)/shard_map/ppermute | solution.py:130
  27.5 0.7 %shard_map.50 = f32[256,128]{1,0:T(8,128)S(1)} custom-call(s32[48]{0:T(128)S(1)} %get-tuple-element.44.codes_ref, bf16[6,128,128]{2,1,0:T(8,128)(2,1)S(1)} %collective-permute-done.7.refs_0_, bf16[2,3,128,128]{3,2,1,0:T(8,128)(2,1)S(1)} %get-tuple-element.51.refs_1_, f32[256,128]{1,0:T(8,128)S(1)} %get-tuple-element.52.refs_2_), custom_call_target="tpu_custom_call" | custom-call | flops 25165824 | bytes 196608 | tf_op jit(solution)/shard_map/pallas_call | solution.py:116
  28.2 3.0 %collective-permute-done.8 = f32[256,128]{1,0:T(8,128)S(1)} collective-permute-done((f32[256,128]{1,0:T(8,128)S(1)}, f32[256,128]{1,0:T(8,128)S(1)}, u32[]{:S(2)}, u32[]{:S(2)}) %collective-permute-start.8) | collective-permute-done | bytes 131104 | tf_op jit(solution)/shard_map/ppermute | solution.py:130
  31.3 0.6 %add_convert_fusion = bf16[256,128]{1,0:T(8,128)(2,1)} fusion(f32[256,128]{1,0:T(8,128)S(1)} %shard_map.50, f32[256,128]{1,0:T(8,128)S(1)} %collective-permute-done.8), kind=kLoop, calls=%fused_computation.5 | loop fusion | flops 65536 | bytes 327680 | tf_op jit(solution)/shard_map/convert_element_type | solution.py:190
Async XLA Ops:
  0.0 18.3 %collective-permute-start.5 = (bf16[6,128,128]{2,1,0:T(8,128)(2,1)}, bf16[6,128,128]{2,1,0:T(8,128)(2,1)S(1)}, u32[]{:S(2)}, u32[]{:S(2)}) collective-permute-start(bf16[6,128,128]{2,1,0:T(8,128)(2,1)} %bitcast.13), channel_id=1, source_target_pairs={{0,4},{1,5},{2,6},{3,7},{4,0},{5,1},{6,2},{7,3},{8,12},{9,13},{10,... | collective-permute-start | bytes 589832 | tf_op jit(solution)/shard_map/ppermute | solution.py:130
  4.0 14.2 %collective-permute-start.6 = (bf16[6,128,128]{2,1,0:T(8,128)(2,1)}, bf16[6,128,128]{2,1,0:T(8,128)(2,1)S(1)}, u32[]{:S(2)}, u32[]{:S(2)}) collective-permute-start(bf16[6,128,128]{2,1,0:T(8,128)(2,1)} %bitcast.14), channel_id=1, source_target_pairs={{0,2},{1,3},{2,0},{3,1},{4,6},{5,7},{6,4},{7,5},{8,10},{9,11},{10,... | collective-permute-start | bytes 589832 | tf_op jit(solution)/shard_map/ppermute | solution.py:130
  5.6 0.7 %copy-start.1 = (s32[4,8,6]{1,0,2:T(4,128)S(1)}, s32[4,8,6]{1,0,2:T(4,128)}, u32[]{:S(2)}) copy-start(s32[4,8,6]{1,0,2:T(4,128)} %param.7) | copy-start | bytes 2308
  5.6 0.7 %copy-start.2 = (s32[4,8,2,3]{1,2,3,0:T(2,128)S(1)}, s32[4,8,2,3]{1,2,3,0:T(2,128)}, u32[]{:S(2)}) copy-start(s32[4,8,2,3]{1,2,3,0:T(2,128)} %param.9) | copy-start | bytes 2308
  6.3 12.4 %copy-start = (bf16[1,1,6,128,128]{4,3,2,1,0:T(8,128)(2,1)S(1)}, bf16[1,1,6,128,128]{4,3,2,1,0:T(8,128)(2,1)}, u32[]{:S(2)}) copy-start(bf16[1,1,6,128,128]{4,3,2,1,0:T(8,128)(2,1)} %param.6) | copy-start | bytes 589828
  7.4 7.4 %collective-permute-start.2 = (bf16[3,128,128]{2,1,0:T(8,128)(2,1)S(1)}, bf16[3,128,128]{2,1,0:T(8,128)(2,1)S(1)}, u32[]{:S(2)}, u32[]{:S(2)}) collective-permute-start(bf16[3,128,128]{2,1,0:T(8,128)(2,1)S(1)} %get-tuple-element.66), channel_id=1, source_target_pairs={{0,17},{1,16},{2,19},{3,18},{4,21},{5,20},{6,23},{7,22},{8,25},{9,... | collective-permute-start | bytes 294920 | tf_op jit(solution)/shard_map/cond/branch_1_fun/ppermute | solution.py:136
  9.9 4.9 %collective-permute-start.1 = (bf16[3,128,128]{2,1,0:T(8,128)(2,1)S(1)}, bf16[3,128,128]{2,1,0:T(8,128)(2,1)S(1)}, u32[]{:S(2)}, u32[]{:S(2)}) collective-permute-start(bf16[3,128,128]{2,1,0:T(8,128)(2,1)S(1)} %get-tuple-element.65), channel_id=1, source_target_pairs={{0,16},{8,24},{16,0},{24,8},{1,17},{9,25},{17,1},{25,9},{2,18},{10... | collective-permute-start | bytes 294920 | tf_op jit(solution)/shard_map/cond/branch_1_fun/ppermute | solution.py:130
  10.4 5.1 %collective-permute-start = (bf16[3,128,128]{2,1,0:T(8,128)(2,1)S(1)}, bf16[3,128,128]{2,1,0:T(8,128)(2,1)S(1)}, u32[]{:S(2)}, u32[]{:S(2)}) collective-permute-start(bf16[3,128,128]{2,1,0:T(8,128)(2,1)S(1)} %get-tuple-element.66), channel_id=1, source_target_pairs={{0,1},{1,0},{2,3},{3,2},{4,5},{5,4},{6,7},{7,6},{8,9},{9,8},{10,11... | collective-permute-start | bytes 294920 | tf_op jit(solution)/shard_map/cond/branch_1_fun/ppermute | solution.py:136
  16.2 1.8 %collective-permute-start.3 = (bf16[2,3,128,128]{3,2,1,0:T(8,128)(2,1)}, bf16[2,3,128,128]{3,2,1,0:T(8,128)(2,1)}, u32[]{:S(2)}, u32[]{:S(2)}) collective-permute-start(bf16[2,3,128,128]{3,2,1,0:T(8,128)(2,1)} %pad_maximum_fusion), channel_id=1, source_target_pairs={{0,8},{8,0},{16,24},{24,16},{1,9},{9,1},{17,25},{25,17},{2,10},{10... | collective-permute-start | bytes 589832 | tf_op jit(solution)/shard_map/cond/branch_1_fun/ppermute | solution.py:130
  16.2 2.1 %collective-permute-start.4 = (bf16[2,3,128,128]{3,2,1,0:T(8,128)(2,1)}, bf16[2,3,128,128]{3,2,1,0:T(8,128)(2,1)}, u32[]{:S(2)}, u32[]{:S(2)}) collective-permute-start(bf16[2,3,128,128]{3,2,1,0:T(8,128)(2,1)} %pad_maximum_fusion.1), channel_id=1, source_target_pairs={{0,8},{8,0},{16,24},{24,16},{1,9},{9,1},{17,25},{25,17},{2,10},{10... | collective-permute-start | bytes 589832 | tf_op jit(solution)/shard_map/cond/branch_1_fun/ppermute | solution.py:130
  18.3 7.0 %collective-permute-start.7 = (bf16[6,128,128]{2,1,0:T(8,128)(2,1)S(1)}, bf16[6,128,128]{2,1,0:T(8,128)(2,1)S(1)}, u32[]{:S(2)}, u32[]{:S(2)}) collective-permute-start(bf16[6,128,128]{2,1,0:T(8,128)(2,1)S(1)} %collective-permute-done.5.refs_2_), channel_id=1, source_target_pairs={{0,2},{1,3},{2,0},{3,1},{4,6},{5,7},{6,4},{7,5},{8,10},{9,11},{10,... | collective-permute-start | bytes 589832 | tf_op jit(solution)/shard_map/ppermute | solution.py:130
  26.3 5.0 %collective-permute-start.8 = (f32[256,128]{1,0:T(8,128)S(1)}, f32[256,128]{1,0:T(8,128)S(1)}, u32[]{:S(2)}, u32[]{:S(2)}) collective-permute-start(f32[256,128]{1,0:T(8,128)S(1)} %shard_map.51), channel_id=1, source_target_pairs={{0,1},{1,0},{2,3},{3,2},{4,5},{5,4},{6,7},{7,6},{8,9},{9,8},{10,11... | collective-permute-start | bytes 393224 | tf_op jit(solution)/shard_map/ppermute | solution.py:130

commit v11 on v10

--- a/solution.py
+++ b/solution.py
@@ -14,6 +14,8 @@
 def find_matches(place, left_index, right_index):
     slots = left_index.shape[-1]
     inner, _, _, right_slots = right_index.shape
+    left_index = left_index.transpose(2, 0, 1)
+    right_index = right_index.transpose(0, 3, 2, 1)
 
     def kernel(place_ref, li_ref, ri_ref, codes_ref):
         row, z, y = place_ref[0], place_ref[1], place_ref[2]
@@ -23,9 +25,9 @@
             zp = z ^ s
             for side in range(2):
                 column = 2 * z + (y if side == 0 else 1 - y)
-                have = [ri_ref[zp, column, y, t] for t in range(right_slots)]
+                have = [ri_ref[zp, t, y, column] for t in range(right_slots)]
                 for slot in range(slots):
-                    at = li_ref[row, 2 * zp + y, slot]
+                    at = li_ref[slot, row, 2 * zp + y]
                     k = lax.rem(at, KT)
                     first = 1 + lax.div(at, KT) * right_slots
                     code = jnp.int32(0)
@@ -62,16 +64,17 @@
 def first_products(place, codes, lefts, rights, slots):
     parts = [(s, part) for s, block in lefts for part in block]
     count = len(parts)
-    inner = len(rights)
-    _, right_slots, tile, _ = rights[0].shape
+    inner = len(rights) // 2
+    right_slots, tile, _ = rights[0].shape
 
     def kernel(place_ref, codes_ref, *refs):
-        right_refs = refs[count : count + inner]
-        totals = refs[count + inner : count + inner + 2]
-        last_ref, held = refs[count + inner + 2 :]
+        right_refs = refs[count : count + 2 * inner]
+        totals = refs[count + 2 * inner : count + 2 * inner + 2]
+        last_ref, held = refs[count + 2 * inner + 2 :]
         row, z = place_ref[0], place_ref[1]
         for t in range(inner):
-            held[row ^ t] = right_refs[t][...]
+            for side in range(2):
+                held[row ^ t, side] = right_refs[2 * t + side][...]
         last_ref[...] = held[z ^ (inner - 1)]
         for side in range(2):
             totals[side][...] = jnp.zeros_like(totals[side])
@@ -88,7 +91,7 @@
         kernel,
         out_shape=[jax.ShapeDtypeStruct((RT * tile, tile), jnp.float32)] * 2
         + [jax.ShapeDtypeStruct((2, right_slots, tile, tile), jnp.bfloat16)],
-        in_specs=[SMEM] * 2 + [VMEM] * (count + inner),
+        in_specs=[SMEM] * 2 + [VMEM] * (count + 2 * inner),
         out_specs=[VMEM] * 3,
         scratch_shapes=[pltpu.VMEM((inner, 2, right_slots, tile, tile), jnp.bfloat16)],
         compiler_params=pltpu.CompilerParams(vmem_limit_bytes=32 * 1024 * 1024),
@@ -140,27 +143,13 @@
     distance = lax.axis_size("col") // 4
     steps = [distance >> n for n in range(distance.bit_length())]
     came = [across(block, "col", 2 * d) for d in steps]
-    came, results = lax.optimization_barrier((came, beside()))
+    came, beside = lax.optimization_barrier((came, beside))
     blocks = {0: block, **dict(zip(steps, came))}
     for d in steps:
         for s in sorted(blocks):
             if s ^ d not in blocks and s & (d - 1) == 0:
                 blocks[s ^ d] = across(blocks[s], "col", 2 * d)
-    return [(s, (blocks[s],)) for s in range(len(blocks))], results
-
-
-def right_side(place, left_index, right_index, right, y):
-    codes = find_matches(place, left_index, right_index)
-    given = lax.dynamic_index_in_dim(right, 1 - y, 0, keepdims=False)
-    own = lax.dynamic_index_in_dim(right, y, 0, keepdims=False)
-    pairs = []
-    for t in range(0, lax.axis_size("row"), 2):
-        pairs.append(jnp.stack([across(own, "row", t) if t else own, crossed(given, t)]))
-    codes, pairs = lax.optimization_barrier((codes, pairs))
-    rights = []
-    for pair in pairs:
-        rights += [pair, across(pair, "row", 1)]
-    return codes, rights
+    return [(s, (blocks[s],)) for s in range(len(blocks))], beside
 
 
 def shards(left_tiles, left_index, right_tiles, right_index):
@@ -170,18 +159,17 @@
     left = left_tiles[0, 0]
     right = right_tiles[0, 0]
     slots = left.shape[0]
-    rows = lax.axis_size("row")
 
     place = jnp.stack([row, z, y])
+    codes = find_matches(place, left_index, right_index)
+    lefts, codes = gather(left, codes)
+    given = lax.dynamic_index_in_dim(right, 1 - y, 0, keepdims=False)
+    own = lax.dynamic_index_in_dim(right, y, 0, keepdims=False)
+    rights = []
+    for t in range(0, lax.axis_size("row"), 2):
+        pair = [across(own, "row", t) if t else own, crossed(given, t)]
+        rights += pair + [across(half, "row", 1) for half in pair]
 
-    def right_branch():
-        return lax.cond(
-            row < rows,
-            lambda: right_side(place, left_index, right_index, right, y),
-            lambda: (jnp.zeros((rows * 2 * slots,), jnp.int32), [jnp.zeros_like(right)] * rows),
-        )
-
-    lefts, (codes, rights) = gather(left, right_branch)
     mine, other, right_last = first_products(place, codes, lefts[:-1], rights, slots)
     far, final = lefts[-1]
     other = last_products(codes, far, final, right_last, other, 1, slots)

time: 32.3 us -> 27.1 us (0.84)
  Pallas kernels: 7.03 us -> 4.76 us
  local copies, waits for them, and re-layouts: 3.09 us -> 1.66 us
  waiting for transfers between devices: 8.25 us -> 7.19 us
  other arithmetic: 2.11 us -> 1.21 us
  starting transfers between devices: 11.4 us -> 12.1 us
    pallas_call x1, Pallas kernels: 2.93 us -> 1.26 us  [first_products(): pl.pallas_call(kernel, out_shape=[jax.ShapeDtypeStruct((RT * tile, tile),...]
    another operation x2 -> x0, local copies, waits for them, and re-layouts: 1.43 us -> none
    another operation x2 -> x0, other arithmetic: 1.39 us -> none  [right_side(): jnp.stack([across(own, 'row', t) if t else own, crossed(given, t)])]
    ppermute x7 -> x9, waiting for transfers between devices: 8.24 us -> 7.19 us  [across(): return lax.ppermute(block, axis, route)]
    ppermute x7 -> x9, starting transfers between devices: 8.36 us -> 9.03 us  [across(): return lax.ppermute(block, axis, route)]
    another operation x1, other arithmetic: 0.08 us -> 0.56 us  [shards(): place = jnp.stack([row, z, y])]
    pallas_call x1, Pallas kernels: 2.43 us -> 1.97 us  [find_matches(): pl.pallas_call(kernel, out_shape=jax.ShapeDtypeStruct((inner * 2 * slots,...]
  transfers between devices with their start and end apart: 9 -> 11, of which waited for: 4 -> 7; matrix products, arithmetic and copies ran while one was open for 12% -> 6% of each run, Pallas kernels for 19% -> 15%
where the time goes in v11:
time: 27.1 us; the launch traced here: 26.9 us
  starting transfers between devices  12.1 us (45%)
  waiting for transfers between devices  7.19 us (27%)
  Pallas kernels  4.76 us (18%)
  local copies, waits for them, and re-layouts  1.66 us (6%)
  other arithmetic  1.21 us (4%)
    ppermute x9, starting transfers between devices, across(): return lax.ppermute(block, axis, route)  9.03 us
    ppermute x9, waiting for transfers between devices, across(): return lax.ppermute(block, axis, route)  7.19 us
    ppermute x2, starting transfers between devices, crossed(): return lax.ppermute(block, ('row', 'col'), route)  3.02 us
    pallas_call x1, Pallas kernels, find_matches(): pl.pallas_call(kernel, out_shape=jax.ShapeDtypeStruct((inner * 2 * slots,...  1.97 us
    pallas_call x2, Pallas kernels, last_products(): pl.pallas_call(kernel, out_shape=jax.ShapeDtypeStruct(total.shape, total....  1.53 us
    pallas_call x1, Pallas kernels, first_products(): pl.pallas_call(kernel, out_shape=[jax.ShapeDtypeStruct((RT * tile, tile),...  1.26 us
    squeeze x1, local copies, waits for them, and re-layouts, shards(): given = lax.dynamic_index_in_dim(right, 1 - y, 0, keepdims=False)  0.99 us
    unnamed x6, local copies, waits for them, and re-layouts  0.66 us
  transfers between devices with their start and end apart: 11, of which 7 were waited for; matrix products, arithmetic and copies ran while one was open for 6% of the time, Pallas kernels for 15%

profile of v11, /device:TPU:0, one launch (start us, length us, event | category | flops | bytes accessed | tf_op | source)
XLA Modules:
  0.0 26.9 jit_solution(18198206607232949551)
XLA Ops:
  0.0 3.0 %collective-permute-start.1 = (bf16[6,128,128]{2,1,0:T(8,128)(2,1)}, bf16[6,128,128]{2,1,0:T(8,128)(2,1)S(1)}, u32[]{:S(2)}, u32[]{:S(2)}) collective-permute-start(bf16[6,128,128]{2,1,0:T(8,128)(2,1)} %bitcast.10), channel_id=1, source_target_pairs={{0,2},{1,3},{2,0},{3,1},{4,6},{5,7},{6,4},{7,5},{8,10},{9,11},{10,... | collective-permute-start | bytes 589832 | tf_op jit(solution)/shard_map/ppermute | solution.py:133
  3.0 2.6 %collective-permute-start = (bf16[6,128,128]{2,1,0:T(8,128)(2,1)}, bf16[6,128,128]{2,1,0:T(8,128)(2,1)S(1)}, u32[]{:S(2)}, u32[]{:S(2)}) collective-permute-start(bf16[6,128,128]{2,1,0:T(8,128)(2,1)} %bitcast.11), channel_id=1, source_target_pairs={{0,4},{1,5},{2,6},{3,7},{4,0},{5,1},{6,2},{7,3},{8,12},{9,13},{10,... | collective-permute-start | bytes 589832 | tf_op jit(solution)/shard_map/ppermute | solution.py:133
  5.6 0.0 copy-start
  5.6 1.0 %dynamic-slice_bitcast_fusion = (bf16[3,128,128]{2,1,0:T(8,128)(2,1)S(1)}, bf16[3,128,128]{2,1,0:T(8,128)(2,1)S(1)}) fusion(bf16[1,1,2,3,128,128]{5,4,3,2,1,0:T(8,128)(2,1)} %param.6, s32[]{:T(128)S(6)} %select_n.8, s32[]{:T(128)S(6)} %select_n.7), kind=kLoop, calls=%fused_computation.1 | loop fusion | bytes 393224 | tf_op jit(solution)/shard_map/jit(dynamic_index_in_dim)/squeeze | solution.py:166
  6.6 2.5 %collective-permute-start.7 = (bf16[3,128,128]{2,1,0:T(8,128)(2,1)S(1)}, bf16[3,128,128]{2,1,0:T(8,128)(2,1)S(1)}, u32[]{:S(2)}, u32[]{:S(2)}) collective-permute-start(bf16[3,128,128]{2,1,0:T(8,128)(2,1)S(1)} %get-tuple-element.17), channel_id=1, source_target_pairs={{0,17},{1,16},{2,19},{3,18},{4,21},{5,20},{6,23},{7,22},{8,25},{9,... | collective-permute-start | bytes 294920 | tf_op jit(solution)/shard_map/ppermute | solution.py:139
  9.1 0.5 %collective-permute-start.3 = (bf16[3,128,128]{2,1,0:T(8,128)(2,1)S(1)}, bf16[3,128,128]{2,1,0:T(8,128)(2,1)S(1)}, u32[]{:S(2)}, u32[]{:S(2)}) collective-permute-start(bf16[3,128,128]{2,1,0:T(8,128)(2,1)S(1)} %get-tuple-element.17), channel_id=1, source_target_pairs={{0,1},{1,0},{2,3},{3,2},{4,5},{5,4},{6,7},{7,6},{8,9},{9,8},{10,11... | collective-permute-start | bytes 294920 | tf_op jit(solution)/shard_map/ppermute | solution.py:139
  9.6 0.5 %collective-permute-start.6 = (bf16[3,128,128]{2,1,0:T(8,128)(2,1)S(1)}, bf16[3,128,128]{2,1,0:T(8,128)(2,1)S(1)}, u32[]{:S(2)}, u32[]{:S(2)}) collective-permute-start(bf16[3,128,128]{2,1,0:T(8,128)(2,1)S(1)} %get-tuple-element.18.refs_3_), channel_id=1, source_target_pairs={{0,16},{8,24},{16,0},{24,8},{1,17},{9,25},{17,1},{25,9},{2,18},{10... | collective-permute-start | bytes 294920 | tf_op jit(solution)/shard_map/ppermute | solution.py:133
  10.2 0.6 %pad_add_fusion.place_ref = s32[3]{0:T(128)} fusion(s32[1]{0:T(128)} %bitcast.3, s32[1]{0:T(128)} %bitcast.2, s32[1]{0:T(128)} %bitcast.1), kind=kLoop, calls=%fused_computation.3 | loop fusion | flops 6 | bytes 24 | tf_op jit(solution)/shard_map/stack | solution.py:163
  10.7 0.0 copy-start.2
  10.7 2.0 %shard_map.46.codes_ref = s32[48]{0:T(128)} custom-call(s32[3]{0:T(128)} %pad_add_fusion.place_ref, s32[6,4,8]{2,1,0:T(4,128)} %bitcast.13, s32[4,3,2,8]{3,2,1,0:T(2,128)} %bitcast.14), custom_call_target="tpu_custom_call" | custom-call | tf_op jit(solution)/shard_map/pallas_call | solution.py:38
  12.7 0.0 collective-permute-done.1.refs_1_
  12.7 2.1 %collective-permute-done.refs_2_ = bf16[6,128,128]{2,1,0:T(8,128)(2,1)S(1)} collective-permute-done((bf16[6,128,128]{2,1,0:T(8,128)(2,1)}, bf16[6,128,128]{2,1,0:T(8,128)(2,1)S(1)}, u32[]{:S(2)}, u32[]{:S(2)}) %collective-permute-start) | collective-permute-done | bytes 196640 | tf_op jit(solution)/shard_map/ppermute | solution.py:133
  14.8 0.4 %collective-permute-start.2 = (bf16[6,128,128]{2,1,0:T(8,128)(2,1)S(1)}, bf16[6,128,128]{2,1,0:T(8,128)(2,1)S(1)}, u32[]{:S(2)}, u32[]{:S(2)}) collective-permute-start(bf16[6,128,128]{2,1,0:T(8,128)(2,1)S(1)} %collective-permute-done.refs_2_), channel_id=1, source_target_pairs={{0,2},{1,3},{2,0},{3,1},{4,6},{5,7},{6,4},{7,5},{8,10},{9,11},{10,... | collective-permute-start | bytes 589832 | tf_op jit(solution)/shard_map/ppermute | solution.py:133
  15.2 0.0 collective-permute-start.4
  15.2 0.0 collective-permute-done.7.refs_8_
  15.2 0.5 %collective-permute-start.9 = (bf16[3,128,128]{2,1,0:T(8,128)(2,1)S(1)}, bf16[3,128,128]{2,1,0:T(8,128)(2,1)S(1)}, u32[]{:S(2)}, u32[]{:S(2)}) collective-permute-start(bf16[3,128,128]{2,1,0:T(8,128)(2,1)S(1)} %collective-permute-done.7.refs_8_), channel_id=1, source_target_pairs={{0,8},{8,0},{16,24},{24,16},{1,9},{9,1},{17,25},{25,17},{2,10},{10... | collective-permute-start | bytes 294920 | tf_op jit(solution)/shard_map/ppermute | solution.py:133
  15.7 0.0 collective-permute-done.3.refs_4_
  15.7 0.1 collective-permute-start.5
  15.8 0.0 collective-permute-done.6.refs_7_
  15.8 0.4 %collective-permute-start.8 = (bf16[3,128,128]{2,1,0:T(8,128)(2,1)S(1)}, bf16[3,128,128]{2,1,0:T(8,128)(2,1)S(1)}, u32[]{:S(2)}, u32[]{:S(2)}) collective-permute-start(bf16[3,128,128]{2,1,0:T(8,128)(2,1)S(1)} %collective-permute-done.6.refs_7_), channel_id=1, source_target_pairs={{0,8},{8,0},{16,24},{24,16},{1,9},{9,1},{17,25},{25,17},{2,10},{10... | collective-permute-start | bytes 294920 | tf_op jit(solution)/shard_map/ppermute | solution.py:133
  16.2 0.3 collective-permute-done.4.refs_5_
  16.5 0.2 collective-permute-done.9.refs_10_
  16.7 0.4 %collective-permute-done.5.refs_6_ = bf16[3,128,128]{2,1,0:T(8,128)(2,1)S(1)} collective-permute-done((bf16[3,128,128]{2,1,0:T(8,128)(2,1)S(1)}, bf16[3,128,128]{2,1,0:T(8,128)(2,1)S(1)}, u32[]{:S(2)}, u32[]{:S(2)}) %collective-permute-start.5) | collective-permute-done | bytes 98336 | tf_op jit(solution)/shard_map/ppermute | solution.py:133
  17.0 0.2 collective-permute-done.8.refs_9_
  17.2 0.0 copy-done
  17.2 0.0 copy-done.2
  17.2 0.0 copy-start.1
  17.2 0.7 %copy-done.1 = s32[48]{0:T(128)S(1)} copy-done((s32[48]{0:T(128)S(1)}, s32[48]{0:T(128)}, u32[]{:S(2)}) %copy-start.1) | copy-done | bytes 216
  17.8 1.3 %shard_map.47 = (f32[256,128]{1,0:T(8,128)S(1)}, f32[256,128]{1,0:T(8,128)S(1)}, bf16[2,3,128,128]{3,2,1,0:T(8,128)(2,1)S(1)}) custom-call(s32[3]{0:T(128)S(1)} %copy-done.2, s32[48]{0:T(128)S(1)} %copy-done.1, bf16[6,128,128]{2,1,0:T(8,128)(2,1)S(1)} %bitcast.12, bf16[6,128,128]{2,1,0:T(8,128)(2,1)S(1)} %collective-permute-done.1.refs_1_, ...), custom_call_target="tpu_custom_call" | custom-call | flops 201326592 | bytes 786432 | tf_op jit(solution)/shard_map/pallas_call | solution.py:90
  19.1 1.3 %collective-permute-done.2.refs_0_ = bf16[6,128,128]{2,1,0:T(8,128)(2,1)S(1)} collective-permute-done((bf16[6,128,128]{2,1,0:T(8,128)(2,1)S(1)}, bf16[6,128,128]{2,1,0:T(8,128)(2,1)S(1)}, u32[]{:S(2)}, u32[]{:S(2)}) %collective-permute-start.2) | collective-permute-done | bytes 196640 | tf_op jit(solution)/shard_map/ppermute | solution.py:133
  20.4 0.8 %shard_map.49 = f32[256,128]{1,0:T(8,128)S(1)} custom-call(s32[48]{0:T(128)S(1)} %copy-done.1, bf16[6,128,128]{2,1,0:T(8,128)(2,1)S(1)} %collective-permute-done.2.refs_0_, bf16[2,3,128,128]{3,2,1,0:T(8,128)(2,1)S(1)} %get-tuple-element.14.refs_1_, f32[256,128]{1,0:T(8,128)S(1)} %get-tuple-element.16.refs_2_), custom_call_target="tpu_custom_call" | custom-call | flops 25165824 | bytes 196608 | tf_op jit(solution)/shard_map/pallas_call | solution.py:119
  21.3 1.4 %collective-permute-start.10 = (f32[256,128]{1,0:T(8,128)S(1)}, f32[256,128]{1,0:T(8,128)S(1)}, u32[]{:S(2)}, u32[]{:S(2)}) collective-permute-start(f32[256,128]{1,0:T(8,128)S(1)} %shard_map.49), channel_id=1, source_target_pairs={{0,1},{1,0},{2,3},{3,2},{4,5},{5,4},{6,7},{7,6},{8,9},{9,8},{10,11... | collective-permute-start | bytes 393224 | tf_op jit(solution)/shard_map/ppermute | solution.py:133
  22.7 0.7 %shard_map.48 = f32[256,128]{1,0:T(8,128)S(1)} custom-call(s32[48]{0:T(128)S(1)} %copy-done.1, bf16[6,128,128]{2,1,0:T(8,128)(2,1)S(1)} %collective-permute-done.2.refs_0_, bf16[2,3,128,128]{3,2,1,0:T(8,128)(2,1)S(1)} %get-tuple-element.14.refs_1_, f32[256,128]{1,0:T(8,128)S(1)} %get-tuple-element.15.refs_2_), custom_call_target="tpu_custom_call" | custom-call | flops 25165824 | bytes 196608 | tf_op jit(solution)/shard_map/pallas_call | solution.py:119
  23.4 2.9 %collective-permute-done.10 = f32[256,128]{1,0:T(8,128)S(1)} collective-permute-done((f32[256,128]{1,0:T(8,128)S(1)}, f32[256,128]{1,0:T(8,128)S(1)}, u32[]{:S(2)}, u32[]{:S(2)}) %collective-permute-start.10) | collective-permute-done | bytes 131104 | tf_op jit(solution)/shard_map/ppermute | solution.py:133
  26.3 0.7 %add_convert_fusion = bf16[256,128]{1,0:T(8,128)(2,1)} fusion(f32[256,128]{1,0:T(8,128)S(1)} %shard_map.48, f32[256,128]{1,0:T(8,128)S(1)} %collective-permute-done.10), kind=kLoop, calls=%fused_computation | loop fusion | flops 65536 | bytes 327680 | tf_op jit(solution)/shard_map/convert_element_type | solution.py:178
Async XLA Ops:
  0.0 12.7 %collective-permute-start.1 = (bf16[6,128,128]{2,1,0:T(8,128)(2,1)}, bf16[6,128,128]{2,1,0:T(8,128)(2,1)S(1)}, u32[]{:S(2)}, u32[]{:S(2)}) collective-permute-start(bf16[6,128,128]{2,1,0:T(8,128)(2,1)} %bitcast.10), channel_id=1, source_target_pairs={{0,2},{1,3},{2,0},{3,1},{4,6},{5,7},{6,4},{7,5},{8,10},{9,11},{10,... | collective-permute-start | bytes 589832 | tf_op jit(solution)/shard_map/ppermute | solution.py:133
  3.0 11.7 %collective-permute-start = (bf16[6,128,128]{2,1,0:T(8,128)(2,1)}, bf16[6,128,128]{2,1,0:T(8,128)(2,1)S(1)}, u32[]{:S(2)}, u32[]{:S(2)}) collective-permute-start(bf16[6,128,128]{2,1,0:T(8,128)(2,1)} %bitcast.11), channel_id=1, source_target_pairs={{0,4},{1,5},{2,6},{3,7},{4,0},{5,1},{6,2},{7,3},{8,12},{9,13},{10,... | collective-permute-start | bytes 589832 | tf_op jit(solution)/shard_map/ppermute | solution.py:133
  5.6 11.6 %copy-start = (bf16[1,1,6,128,128]{4,3,2,1,0:T(8,128)(2,1)S(1)}, bf16[1,1,6,128,128]{4,3,2,1,0:T(8,128)(2,1)}, u32[]{:S(2)}) copy-start(bf16[1,1,6,128,128]{4,3,2,1,0:T(8,128)(2,1)} %param.4) | copy-start | bytes 589828
  6.6 8.6 %collective-permute-start.7 = (bf16[3,128,128]{2,1,0:T(8,128)(2,1)S(1)}, bf16[3,128,128]{2,1,0:T(8,128)(2,1)S(1)}, u32[]{:S(2)}, u32[]{:S(2)}) collective-permute-start(bf16[3,128,128]{2,1,0:T(8,128)(2,1)S(1)} %get-tuple-element.17), channel_id=1, source_target_pairs={{0,17},{1,16},{2,19},{3,18},{4,21},{5,20},{6,23},{7,22},{8,25},{9,... | collective-permute-start | bytes 294920 | tf_op jit(solution)/shard_map/ppermute | solution.py:139
  9.1 6.6 %collective-permute-start.3 = (bf16[3,128,128]{2,1,0:T(8,128)(2,1)S(1)}, bf16[3,128,128]{2,1,0:T(8,128)(2,1)S(1)}, u32[]{:S(2)}, u32[]{:S(2)}) collective-permute-start(bf16[3,128,128]{2,1,0:T(8,128)(2,1)S(1)} %get-tuple-element.17), channel_id=1, source_target_pairs={{0,1},{1,0},{2,3},{3,2},{4,5},{5,4},{6,7},{7,6},{8,9},{9,8},{10,11... | collective-permute-start | bytes 294920 | tf_op jit(solution)/shard_map/ppermute | solution.py:139
  9.6 6.2 %collective-permute-start.6 = (bf16[3,128,128]{2,1,0:T(8,128)(2,1)S(1)}, bf16[3,128,128]{2,1,0:T(8,128)(2,1)S(1)}, u32[]{:S(2)}, u32[]{:S(2)}) collective-permute-start(bf16[3,128,128]{2,1,0:T(8,128)(2,1)S(1)} %get-tuple-element.18.refs_3_), channel_id=1, source_target_pairs={{0,16},{8,24},{16,0},{24,8},{1,17},{9,25},{17,1},{25,9},{2,18},{10... | collective-permute-start | bytes 294920 | tf_op jit(solution)/shard_map/ppermute | solution.py:133
  10.7 6.5 %copy-start.2 = (s32[3]{0:T(128)S(1)}, s32[3]{0:T(128)}, u32[]{:S(2)}) copy-start(s32[3]{0:T(128)} %pad_add_fusion.place_ref) | copy-start | bytes 40
  14.8 5.7 %collective-permute-start.2 = (bf16[6,128,128]{2,1,0:T(8,128)(2,1)S(1)}, bf16[6,128,128]{2,1,0:T(8,128)(2,1)S(1)}, u32[]{:S(2)}, u32[]{:S(2)}) collective-permute-start(bf16[6,128,128]{2,1,0:T(8,128)(2,1)S(1)} %collective-permute-done.refs_2_), channel_id=1, source_target_pairs={{0,2},{1,3},{2,0},{3,1},{4,6},{5,7},{6,4},{7,5},{8,10},{9,11},{10,... | collective-permute-start | bytes 589832 | tf_op jit(solution)/shard_map/ppermute | solution.py:133
  15.2 1.3 %collective-permute-start.4 = (bf16[3,128,128]{2,1,0:T(8,128)(2,1)S(1)}, bf16[3,128,128]{2,1,0:T(8,128)(2,1)S(1)}, u32[]{:S(2)}, u32[]{:S(2)}) collective-permute-start(bf16[3,128,128]{2,1,0:T(8,128)(2,1)S(1)} %get-tuple-element.18.refs_3_), channel_id=1, source_target_pairs={{0,8},{8,0},{16,24},{24,16},{1,9},{9,1},{17,25},{25,17},{2,10},{10... | collective-permute-start | bytes 294920 | tf_op jit(solution)/shard_map/ppermute | solution.py:133
  15.2 1.5 %collective-permute-start.9 = (bf16[3,128,128]{2,1,0:T(8,128)(2,1)S(1)}, bf16[3,128,128]{2,1,0:T(8,128)(2,1)S(1)}, u32[]{:S(2)}, u32[]{:S(2)}) collective-permute-start(bf16[3,128,128]{2,1,0:T(8,128)(2,1)S(1)} %collective-permute-done.7.refs_8_), channel_id=1, source_target_pairs={{0,8},{8,0},{16,24},{24,16},{1,9},{9,1},{17,25},{25,17},{2,10},{10... | collective-permute-start | bytes 294920 | tf_op jit(solution)/shard_map/ppermute | solution.py:133
  15.7 1.3 %collective-permute-start.5 = (bf16[3,128,128]{2,1,0:T(8,128)(2,1)S(1)}, bf16[3,128,128]{2,1,0:T(8,128)(2,1)S(1)}, u32[]{:S(2)}, u32[]{:S(2)}) collective-permute-start(bf16[3,128,128]{2,1,0:T(8,128)(2,1)S(1)} %collective-permute-done.3.refs_4_), channel_id=1, source_target_pairs={{0,8},{8,0},{16,24},{24,16},{1,9},{9,1},{17,25},{25,17},{2,10},{10... | collective-permute-start | bytes 294920 | tf_op jit(solution)/shard_map/ppermute | solution.py:133
  15.8 1.4 %collective-permute-start.8 = (bf16[3,128,128]{2,1,0:T(8,128)(2,1)S(1)}, bf16[3,128,128]{2,1,0:T(8,128)(2,1)S(1)}, u32[]{:S(2)}, u32[]{:S(2)}) collective-permute-start(bf16[3,128,128]{2,1,0:T(8,128)(2,1)S(1)} %collective-permute-done.6.refs_7_), channel_id=1, source_target_pairs={{0,8},{8,0},{16,24},{24,16},{1,9},{9,1},{17,25},{25,17},{2,10},{10... | collective-permute-start | bytes 294920 | tf_op jit(solution)/shard_map/ppermute | solution.py:133
  17.2 0.7 %copy-start.1 = (s32[48]{0:T(128)S(1)}, s32[48]{0:T(128)}, u32[]{:S(2)}) copy-start(s32[48]{0:T(128)} %shard_map.46.codes_ref) | copy-start | bytes 580
  21.3 5.0 %collective-permute-start.10 = (f32[256,128]{1,0:T(8,128)S(1)}, f32[256,128]{1,0:T(8,128)S(1)}, u32[]{:S(2)}, u32[]{:S(2)}) collective-permute-start(f32[256,128]{1,0:T(8,128)S(1)} %shard_map.49), channel_id=1, source_target_pairs={{0,1},{1,0},{2,3},{3,2},{4,5},{5,4},{6,7},{7,6},{8,9},{9,8},{10,11... | collective-permute-start | bytes 393224 | tf_op jit(solution)/shard_map/ppermute | solution.py:133

commit v12 on v11

--- a/solution.py
+++ b/solution.py
@@ -139,17 +139,18 @@
     return lax.ppermute(block, ("row", "col"), route)
 
 
-def gather(block, beside):
+def gather(block, beside, ahead):
     distance = lax.axis_size("col") // 4
     steps = [distance >> n for n in range(distance.bit_length())]
-    came = [across(block, "col", 2 * d) for d in steps]
-    came, beside = lax.optimization_barrier((came, beside))
+    later, ahead = lax.optimization_barrier((block, ahead))
+    came = [across(later if d == 1 else block, "col", 2 * d) for d in steps]
+    came[:-1], beside = lax.optimization_barrier((came[:-1], beside))
     blocks = {0: block, **dict(zip(steps, came))}
     for d in steps:
         for s in sorted(blocks):
             if s ^ d not in blocks and s & (d - 1) == 0:
                 blocks[s ^ d] = across(blocks[s], "col", 2 * d)
-    return [(s, (blocks[s],)) for s in range(len(blocks))], beside
+    return [(s, (blocks[s],)) for s in range(len(blocks))], beside, ahead
 
 
 def shards(left_tiles, left_index, right_tiles, right_index):
@@ -162,12 +163,15 @@
 
     place = jnp.stack([row, z, y])
     codes = find_matches(place, left_index, right_index)
-    lefts, codes = gather(left, codes)
     given = lax.dynamic_index_in_dim(right, 1 - y, 0, keepdims=False)
     own = lax.dynamic_index_in_dim(right, y, 0, keepdims=False)
+    lefts, codes, (own, given) = gather(left, codes, (own, given))
     rights = []
     for t in range(0, lax.axis_size("row"), 2):
         pair = [across(own, "row", t) if t else own, crossed(given, t)]
+        if not t:
+            pair[0], near = lax.optimization_barrier((pair[0], lefts[1][1]))
+            lefts[1] = (1, near)
         rights += pair + [across(half, "row", 1) for half in pair]
 
     mine, other, right_last = first_products(place, codes, lefts[:-1], rights, slots)

time: 27.1 us -> 26.1 us (0.963)
  waiting for transfers between devices: 7.19 us -> 5.46 us
  starting transfers between devices: 12.1 us -> 12.5 us
    ppermute x9, waiting for transfers between devices: 7.19 us -> 5.45 us  [across(): return lax.ppermute(block, axis, route)]
    ppermute x9, starting transfers between devices: 9.03 us -> 9.52 us  [across(): return lax.ppermute(block, axis, route)]
    pallas_call x1, Pallas kernels: 1.26 us -> 1.7 us  [first_products(): pl.pallas_call(kernel, out_shape=[jax.ShapeDtypeStruct((RT * tile, tile),...]
  transfers between devices with their start and end apart: 11 -> 11, of which waited for: 7 -> 7; matrix products, arithmetic and copies ran while one was open for 6% -> 6% of each run, Pallas kernels for 15% -> 17%
where the time goes in v12:
time: 26.1 us; the launch traced here: 25.9 us
  starting transfers between devices  12.5 us (48%)
  waiting for transfers between devices  5.46 us (21%)
  Pallas kernels  5.01 us (19%)
  local copies, waits for them, and re-layouts  1.68 us (6%)
  other arithmetic  1.21 us (5%)
    ppermute x9, starting transfers between devices, across(): return lax.ppermute(block, axis, route)  9.52 us
    ppermute x9, waiting for transfers between devices, across(): return lax.ppermute(block, axis, route)  5.45 us
    ppermute x2, starting transfers between devices, crossed(): return lax.ppermute(block, ('row', 'col'), route)  2.95 us
    pallas_call x1, Pallas kernels, find_matches(): pl.pallas_call(kernel, out_shape=jax.ShapeDtypeStruct((inner * 2 * slots,...  1.97 us
    pallas_call x1, Pallas kernels, first_products(): pl.pallas_call(kernel, out_shape=[jax.ShapeDtypeStruct((RT * tile, tile),...  1.7 us
    pallas_call x2, Pallas kernels, last_products(): pl.pallas_call(kernel, out_shape=jax.ShapeDtypeStruct(total.shape, total....  1.34 us
    squeeze x1, local copies, waits for them, and re-layouts, shards(): given = lax.dynamic_index_in_dim(right, 1 - y, 0, keepdims=False)  0.99 us
    unnamed x6, local copies, waits for them, and re-layouts  0.68 us
  transfers between devices with their start and end apart: 11, of which 7 were waited for; matrix products, arithmetic and copies ran while one was open for 6% of the time, Pallas kernels for 17%

profile of v12, /device:TPU:0, one launch (start us, length us, event | category | flops | bytes accessed | tf_op | source)
XLA Modules:
  0.0 25.9 jit_solution(10545722286401438902)
XLA Ops:
  0.0 4.0 %collective-permute-start = (bf16[6,128,128]{2,1,0:T(8,128)(2,1)}, bf16[6,128,128]{2,1,0:T(8,128)(2,1)S(1)}, u32[]{:S(2)}, u32[]{:S(2)}) collective-permute-start(bf16[6,128,128]{2,1,0:T(8,128)(2,1)} %bitcast.10), channel_id=1, source_target_pairs={{0,4},{1,5},{2,6},{3,7},{4,0},{5,1},{6,2},{7,3},{8,12},{9,13},{10,... | collective-permute-start | bytes 589832 | tf_op jit(solution)/shard_map/ppermute | solution.py:133
  4.0 0.0 copy-start
  4.0 1.0 %dynamic-slice_bitcast_fusion = (bf16[3,128,128]{2,1,0:T(8,128)(2,1)S(1)}, bf16[3,128,128]{2,1,0:T(8,128)(2,1)S(1)}) fusion(bf16[1,1,2,3,128,128]{5,4,3,2,1,0:T(8,128)(2,1)} %param.6, s32[]{:T(128)S(6)} %select_n.8, s32[]{:T(128)S(6)} %select_n.7), kind=kLoop, calls=%fused_computation.1 | loop fusion | bytes 393224 | tf_op jit(solution)/shard_map/jit(dynamic_index_in_dim)/squeeze | solution.py:166
  5.0 0.0 copy-done
  5.1 1.6 %collective-permute-start.2 = (bf16[6,128,128]{2,1,0:T(8,128)(2,1)S(1)}, bf16[6,128,128]{2,1,0:T(8,128)(2,1)S(1)}, u32[]{:S(2)}, u32[]{:S(2)}) collective-permute-start(bf16[6,128,128]{2,1,0:T(8,128)(2,1)S(1)} %bitcast.11), channel_id=1, source_target_pairs={{0,2},{1,3},{2,0},{3,1},{4,6},{5,7},{6,4},{7,5},{8,10},{9,11},{10,... | collective-permute-start | bytes 589832 | tf_op jit(solution)/shard_map/ppermute | solution.py:133
  6.7 2.4 %collective-permute-start.7 = (bf16[3,128,128]{2,1,0:T(8,128)(2,1)S(1)}, bf16[3,128,128]{2,1,0:T(8,128)(2,1)S(1)}, u32[]{:S(2)}, u32[]{:S(2)}) collective-permute-start(bf16[3,128,128]{2,1,0:T(8,128)(2,1)S(1)} %get-tuple-element.21), channel_id=1, source_target_pairs={{0,17},{1,16},{2,19},{3,18},{4,21},{5,20},{6,23},{7,22},{8,25},{9,... | collective-permute-start | bytes 294920 | tf_op jit(solution)/shard_map/ppermute | solution.py:139
  9.1 0.5 %collective-permute-start.3 = (bf16[3,128,128]{2,1,0:T(8,128)(2,1)S(1)}, bf16[3,128,128]{2,1,0:T(8,128)(2,1)S(1)}, u32[]{:S(2)}, u32[]{:S(2)}) collective-permute-start(bf16[3,128,128]{2,1,0:T(8,128)(2,1)S(1)} %get-tuple-element.21), channel_id=1, source_target_pairs={{0,1},{1,0},{2,3},{3,2},{4,5},{5,4},{6,7},{7,6},{8,9},{9,8},{10,11... | collective-permute-start | bytes 294920 | tf_op jit(solution)/shard_map/ppermute | solution.py:139
  9.6 0.5 %collective-permute-start.6 = (bf16[3,128,128]{2,1,0:T(8,128)(2,1)S(1)}, bf16[3,128,128]{2,1,0:T(8,128)(2,1)S(1)}, u32[]{:S(2)}, u32[]{:S(2)}) collective-permute-start(bf16[3,128,128]{2,1,0:T(8,128)(2,1)S(1)} %get-tuple-element.20.refs_3_), channel_id=1, source_target_pairs={{0,16},{8,24},{16,0},{24,8},{1,17},{9,25},{17,1},{25,9},{2,18},{10... | collective-permute-start | bytes 294920 | tf_op jit(solution)/shard_map/ppermute | solution.py:133
  10.2 0.6 %pad_add_fusion.place_ref = s32[3]{0:T(128)} fusion(s32[1]{0:T(128)} %bitcast.3, s32[1]{0:T(128)} %bitcast.2, s32[1]{0:T(128)} %bitcast.1), kind=kLoop, calls=%fused_computation.3 | loop fusion | flops 6 | bytes 24 | tf_op jit(solution)/shard_map/stack | solution.py:164
  10.7 0.0 copy-start.2
  10.7 2.0 %shard_map.46.codes_ref = s32[48]{0:T(128)} custom-call(s32[3]{0:T(128)} %pad_add_fusion.place_ref, s32[6,4,8]{2,1,0:T(4,128)} %bitcast.13, s32[4,3,2,8]{3,2,1,0:T(2,128)} %bitcast.14), custom_call_target="tpu_custom_call" | custom-call | tf_op jit(solution)/shard_map/pallas_call | solution.py:38
  12.7 0.7 %collective-permute-done.refs_2_ = bf16[6,128,128]{2,1,0:T(8,128)(2,1)S(1)} collective-permute-done((bf16[6,128,128]{2,1,0:T(8,128)(2,1)}, bf16[6,128,128]{2,1,0:T(8,128)(2,1)S(1)}, u32[]{:S(2)}, u32[]{:S(2)}) %collective-permute-start) | collective-permute-done | bytes 196640 | tf_op jit(solution)/shard_map/ppermute | solution.py:133
  13.5 0.8 %collective-permute-start.1 = (bf16[6,128,128]{2,1,0:T(8,128)(2,1)S(1)}, bf16[6,128,128]{2,1,0:T(8,128)(2,1)S(1)}, u32[]{:S(2)}, u32[]{:S(2)}) collective-permute-start(bf16[6,128,128]{2,1,0:T(8,128)(2,1)S(1)} %collective-permute-done.refs_2_), channel_id=1, source_target_pairs={{0,2},{1,3},{2,0},{3,1},{4,6},{5,7},{6,4},{7,5},{8,10},{9,11},{10,... | collective-permute-start | bytes 589832 | tf_op jit(solution)/shard_map/ppermute | solution.py:133
  14.2 0.0 collective-permute-done.6.refs_7_
  14.3 0.0 collective-permute-start.8
  14.3 0.0 collective-permute-done.7.refs_8_
  14.3 0.5 %collective-permute-start.9 = (bf16[3,128,128]{2,1,0:T(8,128)(2,1)S(1)}, bf16[3,128,128]{2,1,0:T(8,128)(2,1)S(1)}, u32[]{:S(2)}, u32[]{:S(2)}) collective-permute-start(bf16[3,128,128]{2,1,0:T(8,128)(2,1)S(1)} %collective-permute-done.7.refs_8_), channel_id=1, source_target_pairs={{0,8},{8,0},{16,24},{24,16},{1,9},{9,1},{17,25},{25,17},{2,10},{10... | collective-permute-start | bytes 294920 | tf_op jit(solution)/shard_map/ppermute | solution.py:133
  14.8 0.0 collective-permute-done.3.refs_4_
  14.8 0.1 collective-permute-start.5
  14.8 0.0 collective-permute-done.2.refs_1_
  14.9 0.4 %collective-permute-start.4 = (bf16[3,128,128]{2,1,0:T(8,128)(2,1)S(1)}, bf16[3,128,128]{2,1,0:T(8,128)(2,1)S(1)}, u32[]{:S(2)}, u32[]{:S(2)}) collective-permute-start(bf16[3,128,128]{2,1,0:T(8,128)(2,1)S(1)} %get-tuple-element.20.refs_3_), channel_id=1, source_target_pairs={{0,8},{8,0},{16,24},{24,16},{1,9},{9,1},{17,25},{25,17},{2,10},{10... | collective-permute-start | bytes 294920 | tf_op jit(solution)/shard_map/ppermute | solution.py:133
  15.3 0.3 %collective-permute-done.8.refs_9_ = bf16[3,128,128]{2,1,0:T(8,128)(2,1)S(1)} collective-permute-done((bf16[3,128,128]{2,1,0:T(8,128)(2,1)S(1)}, bf16[3,128,128]{2,1,0:T(8,128)(2,1)S(1)}, u32[]{:S(2)}, u32[]{:S(2)}) %collective-permute-start.8) | collective-permute-done | bytes 98336 | tf_op jit(solution)/shard_map/ppermute | solution.py:133
  15.6 0.2 collective-permute-done.9.refs_10_
  15.7 0.4 %collective-permute-done.5.refs_6_ = bf16[3,128,128]{2,1,0:T(8,128)(2,1)S(1)} collective-permute-done((bf16[3,128,128]{2,1,0:T(8,128)(2,1)S(1)}, bf16[3,128,128]{2,1,0:T(8,128)(2,1)S(1)}, u32[]{:S(2)}, u32[]{:S(2)}) %collective-permute-start.5) | collective-permute-done | bytes 98336 | tf_op jit(solution)/shard_map/ppermute | solution.py:133
  16.1 0.2 collective-permute-done.4.refs_5_
  16.2 0.0 copy-done.2
  16.2 0.0 copy-start.1
  16.2 0.7 %copy-done.1 = s32[48]{0:T(128)S(1)} copy-done((s32[48]{0:T(128)S(1)}, s32[48]{0:T(128)}, u32[]{:S(2)}) %copy-start.1) | copy-done | bytes 216
  16.9 1.7 %shard_map.47 = (f32[256,128]{1,0:T(8,128)S(1)}, f32[256,128]{1,0:T(8,128)S(1)}, bf16[2,3,128,128]{3,2,1,0:T(8,128)(2,1)S(1)}) custom-call(s32[3]{0:T(128)S(1)} %copy-done.2, s32[48]{0:T(128)S(1)} %copy-done.1, bf16[6,128,128]{2,1,0:T(8,128)(2,1)S(1)} %bitcast.12, bf16[6,128,128]{2,1,0:T(8,128)(2,1)S(1)} %collective-permute-done.2.refs_1_, ...), custom_call_target="tpu_custom_call" | custom-call | flops 201326592 | bytes 786432 | tf_op jit(solution)/shard_map/pallas_call | solution.py:90
  18.6 0.9 %collective-permute-done.1.refs_0_ = bf16[6,128,128]{2,1,0:T(8,128)(2,1)S(1)} collective-permute-done((bf16[6,128,128]{2,1,0:T(8,128)(2,1)S(1)}, bf16[6,128,128]{2,1,0:T(8,128)(2,1)S(1)}, u32[]{:S(2)}, u32[]{:S(2)}) %collective-permute-start.1) | collective-permute-done | bytes 196640 | tf_op jit(solution)/shard_map/ppermute | solution.py:133
  19.5 0.7 %shard_map.49 = f32[256,128]{1,0:T(8,128)S(1)} custom-call(s32[48]{0:T(128)S(1)} %copy-done.1, bf16[6,128,128]{2,1,0:T(8,128)(2,1)S(1)} %collective-permute-done.1.refs_0_, bf16[2,3,128,128]{3,2,1,0:T(8,128)(2,1)S(1)} %get-tuple-element.22.refs_1_, f32[256,128]{1,0:T(8,128)S(1)} %get-tuple-element.24.refs_2_), custom_call_target="tpu_custom_call" | custom-call | flops 25165824 | bytes 196608 | tf_op jit(solution)/shard_map/pallas_call | solution.py:119
  20.2 1.5 %collective-permute-start.10 = (f32[256,128]{1,0:T(8,128)S(1)}, f32[256,128]{1,0:T(8,128)S(1)}, u32[]{:S(2)}, u32[]{:S(2)}) collective-permute-start(f32[256,128]{1,0:T(8,128)S(1)} %shard_map.49), channel_id=1, source_target_pairs={{0,1},{1,0},{2,3},{3,2},{4,5},{5,4},{6,7},{7,6},{8,9},{9,8},{10,11... | collective-permute-start | bytes 393224 | tf_op jit(solution)/shard_map/ppermute | solution.py:133
  21.7 0.6 %shard_map.48 = f32[256,128]{1,0:T(8,128)S(1)} custom-call(s32[48]{0:T(128)S(1)} %copy-done.1, bf16[6,128,128]{2,1,0:T(8,128)(2,1)S(1)} %collective-permute-done.1.refs_0_, bf16[2,3,128,128]{3,2,1,0:T(8,128)(2,1)S(1)} %get-tuple-element.22.refs_1_, f32[256,128]{1,0:T(8,128)S(1)} %get-tuple-element.23.refs_2_), custom_call_target="tpu_custom_call" | custom-call | flops 25165824 | bytes 196608 | tf_op jit(solution)/shard_map/pallas_call | solution.py:119
  22.4 2.8 %collective-permute-done.10 = f32[256,128]{1,0:T(8,128)S(1)} collective-permute-done((f32[256,128]{1,0:T(8,128)S(1)}, f32[256,128]{1,0:T(8,128)S(1)}, u32[]{:S(2)}, u32[]{:S(2)}) %collective-permute-start.10) | collective-permute-done | bytes 131104 | tf_op jit(solution)/shard_map/ppermute | solution.py:133
  25.2 0.7 %add_convert_fusion = bf16[256,128]{1,0:T(8,128)(2,1)} fusion(f32[256,128]{1,0:T(8,128)S(1)} %shard_map.48, f32[256,128]{1,0:T(8,128)S(1)} %collective-permute-done.10), kind=kLoop, calls=%fused_computation | loop fusion | flops 65536 | bytes 327680 | tf_op jit(solution)/shard_map/convert_element_type | solution.py:182
Async XLA Ops:
  0.0 13.5 %collective-permute-start = (bf16[6,128,128]{2,1,0:T(8,128)(2,1)}, bf16[6,128,128]{2,1,0:T(8,128)(2,1)S(1)}, u32[]{:S(2)}, u32[]{:S(2)}) collective-permute-start(bf16[6,128,128]{2,1,0:T(8,128)(2,1)} %bitcast.10), channel_id=1, source_target_pairs={{0,4},{1,5},{2,6},{3,7},{4,0},{5,1},{6,2},{7,3},{8,12},{9,13},{10,... | collective-permute-start | bytes 589832 | tf_op jit(solution)/shard_map/ppermute | solution.py:133
  4.0 1.0 %copy-start = (bf16[1,1,6,128,128]{4,3,2,1,0:T(8,128)(2,1)S(1)}, bf16[1,1,6,128,128]{4,3,2,1,0:T(8,128)(2,1)}, u32[]{:S(2)}) copy-start(bf16[1,1,6,128,128]{4,3,2,1,0:T(8,128)(2,1)} %param.4) | copy-start | bytes 589828
  5.1 9.8 %collective-permute-start.2 = (bf16[6,128,128]{2,1,0:T(8,128)(2,1)S(1)}, bf16[6,128,128]{2,1,0:T(8,128)(2,1)S(1)}, u32[]{:S(2)}, u32[]{:S(2)}) collective-permute-start(bf16[6,128,128]{2,1,0:T(8,128)(2,1)S(1)} %bitcast.11), channel_id=1, source_target_pairs={{0,2},{1,3},{2,0},{3,1},{4,6},{5,7},{6,4},{7,5},{8,10},{9,11},{10,... | collective-permute-start | bytes 589832 | tf_op jit(solution)/shard_map/ppermute | solution.py:133
  6.7 7.6 %collective-permute-start.7 = (bf16[3,128,128]{2,1,0:T(8,128)(2,1)S(1)}, bf16[3,128,128]{2,1,0:T(8,128)(2,1)S(1)}, u32[]{:S(2)}, u32[]{:S(2)}) collective-permute-start(bf16[3,128,128]{2,1,0:T(8,128)(2,1)S(1)} %get-tuple-element.21), channel_id=1, source_target_pairs={{0,17},{1,16},{2,19},{3,18},{4,21},{5,20},{6,23},{7,22},{8,25},{9,... | collective-permute-start | bytes 294920 | tf_op jit(solution)/shard_map/ppermute | solution.py:139
  9.1 5.6 %collective-permute-start.3 = (bf16[3,128,128]{2,1,0:T(8,128)(2,1)S(1)}, bf16[3,128,128]{2,1,0:T(8,128)(2,1)S(1)}, u32[]{:S(2)}, u32[]{:S(2)}) collective-permute-start(bf16[3,128,128]{2,1,0:T(8,128)(2,1)S(1)} %get-tuple-element.21), channel_id=1, source_target_pairs={{0,1},{1,0},{2,3},{3,2},{4,5},{5,4},{6,7},{7,6},{8,9},{9,8},{10,11... | collective-permute-start | bytes 294920 | tf_op jit(solution)/shard_map/ppermute | solution.py:139
  9.6 4.6 %collective-permute-start.6 = (bf16[3,128,128]{2,1,0:T(8,128)(2,1)S(1)}, bf16[3,128,128]{2,1,0:T(8,128)(2,1)S(1)}, u32[]{:S(2)}, u32[]{:S(2)}) collective-permute-start(bf16[3,128,128]{2,1,0:T(8,128)(2,1)S(1)} %get-tuple-element.20.refs_3_), channel_id=1, source_target_pairs={{0,16},{8,24},{16,0},{24,8},{1,17},{9,25},{17,1},{25,9},{2,18},{10... | collective-permute-start | bytes 294920 | tf_op jit(solution)/shard_map/ppermute | solution.py:133
  10.7 5.5 %copy-start.2 = (s32[3]{0:T(128)S(1)}, s32[3]{0:T(128)}, u32[]{:S(2)}) copy-start(s32[3]{0:T(128)} %pad_add_fusion.place_ref) | copy-start | bytes 40
  13.5 6.0 %collective-permute-start.1 = (bf16[6,128,128]{2,1,0:T(8,128)(2,1)S(1)}, bf16[6,128,128]{2,1,0:T(8,128)(2,1)S(1)}, u32[]{:S(2)}, u32[]{:S(2)}) collective-permute-start(bf16[6,128,128]{2,1,0:T(8,128)(2,1)S(1)} %collective-permute-done.refs_2_), channel_id=1, source_target_pairs={{0,2},{1,3},{2,0},{3,1},{4,6},{5,7},{6,4},{7,5},{8,10},{9,11},{10,... | collective-permute-start | bytes 589832 | tf_op jit(solution)/shard_map/ppermute | solution.py:133
  14.3 1.3 %collective-permute-start.8 = (bf16[3,128,128]{2,1,0:T(8,128)(2,1)S(1)}, bf16[3,128,128]{2,1,0:T(8,128)(2,1)S(1)}, u32[]{:S(2)}, u32[]{:S(2)}) collective-permute-start(bf16[3,128,128]{2,1,0:T(8,128)(2,1)S(1)} %collective-permute-done.6.refs_7_), channel_id=1, source_target_pairs={{0,8},{8,0},{16,24},{24,16},{1,9},{9,1},{17,25},{25,17},{2,10},{10... | collective-permute-start | bytes 294920 | tf_op jit(solution)/shard_map/ppermute | solution.py:133
  14.3 1.5 %collective-permute-start.9 = (bf16[3,128,128]{2,1,0:T(8,128)(2,1)S(1)}, bf16[3,128,128]{2,1,0:T(8,128)(2,1)S(1)}, u32[]{:S(2)}, u32[]{:S(2)}) collective-permute-start(bf16[3,128,128]{2,1,0:T(8,128)(2,1)S(1)} %collective-permute-done.7.refs_8_), channel_id=1, source_target_pairs={{0,8},{8,0},{16,24},{24,16},{1,9},{9,1},{17,25},{25,17},{2,10},{10... | collective-permute-start | bytes 294920 | tf_op jit(solution)/shard_map/ppermute | solution.py:133
  14.8 1.3 %collective-permute-start.5 = (bf16[3,128,128]{2,1,0:T(8,128)(2,1)S(1)}, bf16[3,128,128]{2,1,0:T(8,128)(2,1)S(1)}, u32[]{:S(2)}, u32[]{:S(2)}) collective-permute-start(bf16[3,128,128]{2,1,0:T(8,128)(2,1)S(1)} %collective-permute-done.3.refs_4_), channel_id=1, source_target_pairs={{0,8},{8,0},{16,24},{24,16},{1,9},{9,1},{17,25},{25,17},{2,10},{10... | collective-permute-start | bytes 294920 | tf_op jit(solution)/shard_map/ppermute | solution.py:133
  14.9 1.4 %collective-permute-start.4 = (bf16[3,128,128]{2,1,0:T(8,128)(2,1)S(1)}, bf16[3,128,128]{2,1,0:T(8,128)(2,1)S(1)}, u32[]{:S(2)}, u32[]{:S(2)}) collective-permute-start(bf16[3,128,128]{2,1,0:T(8,128)(2,1)S(1)} %get-tuple-element.20.refs_3_), channel_id=1, source_target_pairs={{0,8},{8,0},{16,24},{24,16},{1,9},{9,1},{17,25},{25,17},{2,10},{10... | collective-permute-start | bytes 294920 | tf_op jit(solution)/shard_map/ppermute | solution.py:133
  16.2 0.7 %copy-start.1 = (s32[48]{0:T(128)S(1)}, s32[48]{0:T(128)}, u32[]{:S(2)}) copy-start(s32[48]{0:T(128)} %shard_map.46.codes_ref) | copy-start | bytes 580
  20.2 5.0 %collective-permute-start.10 = (f32[256,128]{1,0:T(8,128)S(1)}, f32[256,128]{1,0:T(8,128)S(1)}, u32[]{:S(2)}, u32[]{:S(2)}) collective-permute-start(f32[256,128]{1,0:T(8,128)S(1)} %shard_map.49), channel_id=1, source_target_pairs={{0,1},{1,0},{2,3},{3,2},{4,5},{5,4},{6,7},{7,6},{8,9},{9,8},{10,11... | collective-permute-start | bytes 393224 | tf_op jit(solution)/shard_map/ppermute | solution.py:133

commit v13 on v12

--- a/solution.py
+++ b/solution.py
@@ -7,18 +7,26 @@
 
 KT = 8
 RT = 2
+BITS = 15
+LEAST = 100
+PAD = 16
 SMEM = pl.BlockSpec(memory_space=pltpu.SMEM)
 VMEM = pl.BlockSpec(memory_space=pltpu.VMEM)
 
 
-def find_matches(place, left_index, right_index):
+def position():
+    col = lax.axis_index("col")
+    return lax.axis_index("row"), col >> 1, col & 1
+
+
+def find_matches(left_index, right_index):
     slots = left_index.shape[-1]
     inner, _, _, right_slots = right_index.shape
     left_index = left_index.transpose(2, 0, 1)
     right_index = right_index.transpose(0, 3, 2, 1)
 
-    def kernel(place_ref, li_ref, ri_ref, codes_ref):
-        row, z, y = place_ref[0], place_ref[1], place_ref[2]
+    def kernel(li_ref, ri_ref, codes_ref):
+        row, z, y = position()
 
         @pl.loop(0, inner)
         def _(s):
@@ -38,9 +46,9 @@
     return pl.pallas_call(
         kernel,
         out_shape=jax.ShapeDtypeStruct((inner * 2 * slots,), jnp.int32),
-        in_specs=[SMEM] * 3,
+        in_specs=[SMEM] * 2,
         out_specs=SMEM,
-    )(place, left_index, right_index)
+    )(left_index, right_index)
 
 
 def add_part(codes_ref, s, side, start, slots, left_ref, right_at, right_slots, total_ref):
@@ -61,17 +69,17 @@
             )
 
 
-def first_products(place, codes, lefts, rights, slots):
+def first_products(codes, lefts, rights, slots):
     parts = [(s, part) for s, block in lefts for part in block]
     count = len(parts)
     inner = len(rights) // 2
     right_slots, tile, _ = rights[0].shape
 
-    def kernel(place_ref, codes_ref, *refs):
+    def kernel(codes_ref, *refs):
         right_refs = refs[count : count + 2 * inner]
         totals = refs[count + 2 * inner : count + 2 * inner + 2]
         last_ref, held = refs[count + 2 * inner + 2 :]
-        row, z = place_ref[0], place_ref[1]
+        row, z, _ = position()
         for t in range(inner):
             for side in range(2):
                 held[row ^ t, side] = right_refs[2 * t + side][...]
@@ -91,41 +99,80 @@
         kernel,
         out_shape=[jax.ShapeDtypeStruct((RT * tile, tile), jnp.float32)] * 2
         + [jax.ShapeDtypeStruct((2, right_slots, tile, tile), jnp.bfloat16)],
-        in_specs=[SMEM] * 2 + [VMEM] * (count + 2 * inner),
+        in_specs=[SMEM] + [VMEM] * (count + 2 * inner),
         out_specs=[VMEM] * 3,
         scratch_shapes=[pltpu.VMEM((inner, 2, right_slots, tile, tile), jnp.bfloat16)],
         compiler_params=pltpu.CompilerParams(vmem_limit_bytes=32 * 1024 * 1024),
         cost_estimate=pl.CostEstimate(
             flops=4 * inner * slots * tile**3, bytes_accessed=2 * inner * slots * tile**2, transcendentals=0
         ),
-    )(place, codes, *[part for _, part in parts], *rights)
-
-
-def last_products(codes, s, parts, right, total, side, slots):
+    )(codes, *[part for _, part in parts], *rights)
+
+
+def last_products(codes, s, parts, right, total, side, slots, finish, out_shape):
     count = len(parts)
     right_slots = right.shape[1]
 
     def kernel(codes_ref, *refs):
-        right_ref, total_ref, out_ref = refs[count:]
-        out_ref[...] = total_ref[...]
+        right_ref, total_ref, out_ref, sum_ref = refs[count:]
+        sum_ref[...] = total_ref[...]
         start = 0
         for left_ref in refs[:count]:
             add_part(
                 codes_ref, s, side, start, slots, left_ref,
-                lambda found: right_ref[side, found], right_slots, out_ref,
+                lambda found: right_ref[side, found], right_slots, sum_ref,
             )
             start += left_ref.shape[0]
-
-    return pl.pallas_call(
-        kernel,
-        out_shape=jax.ShapeDtypeStruct(total.shape, total.dtype),
+        finish(sum_ref, out_ref)
+
+    return pl.pallas_call(
+        kernel,
+        out_shape=out_shape,
         in_specs=[SMEM] + [VMEM] * (count + 2),
         out_specs=VMEM,
+        scratch_shapes=[pltpu.VMEM(total.shape, total.dtype)],
         compiler_params=pltpu.CompilerParams(vmem_limit_bytes=16 * 1024 * 1024),
         cost_estimate=pl.CostEstimate(
             flops=2 * slots * 128**3, bytes_accessed=2 * slots * 128**2, transcendentals=0
         ),
     )(codes, *parts, right, total)
+
+
+def write_sum(sum_ref, out_ref):
+    out_ref[...] = sum_ref[...]
+
+
+def write_coded(sum_ref, out_ref):
+    tile = sum_ref.shape[1]
+    exponents = jnp.zeros((PAD, tile), jnp.float32)
+    for i in range(RT):
+        values = sum_ref[i * tile : (i + 1) * tile, :]
+        largest = jnp.max(jnp.abs(values), axis=0, keepdims=True)
+        exponent = jnp.clip(jnp.floor(jnp.log2(largest)) + 1.0, -LEAST, LEAST)
+        coded = jnp.round(values * jnp.exp2(BITS - exponent))
+        coded = jnp.clip(coded, -(2.0**BITS) + 1.0, 2.0**BITS - 1.0)
+        out_ref[i * tile : (i + 1) * tile, :] = coded.astype(jnp.int32).astype(jnp.int16)
+        at = lax.broadcasted_iota(jnp.int32, (PAD, tile), 0)
+        exponents = jnp.where(at == i, exponent, exponents)
+    out_ref[RT * tile :, :] = exponents.astype(jnp.int32).astype(jnp.int16)
+
+
+def add_coded(total, coded):
+    def kernel(total_ref, coded_ref, out_ref):
+        tile = total_ref.shape[1]
+        exponents = coded_ref[RT * tile :, :].astype(jnp.int32).astype(jnp.float32)
+        for i in range(RT):
+            rows = slice(i * tile, (i + 1) * tile)
+            scale = jnp.exp2(exponents[i : i + 1, :] - BITS)
+            values = coded_ref[rows, :].astype(jnp.int32).astype(jnp.float32)
+            out_ref[rows, :] = (total_ref[rows, :] + values * scale).astype(out_ref.dtype)
+
+    return pl.pallas_call(
+        kernel,
+        out_shape=jax.ShapeDtypeStruct(total.shape, jnp.bfloat16),
+        in_specs=[VMEM] * 2,
+        out_specs=VMEM,
+    )(total, coded)
 
 
 def across(block, axis, mask):
@@ -154,15 +201,12 @@
 
 
 def shards(left_tiles, left_index, right_tiles, right_index):
-    row = lax.axis_index("row")
-    col = lax.axis_index("col")
-    z, y = col >> 1, col & 1
+    y = lax.axis_index("col") & 1
     left = left_tiles[0, 0]
     right = right_tiles[0, 0]
     slots = left.shape[0]
 
-    place = jnp.stack([row, z, y])
-    codes = find_matches(place, left_index, right_index)
+    codes = find_matches(left_index, right_index)
     given = lax.dynamic_index_in_dim(right, 1 - y, 0, keepdims=False)
     own = lax.dynamic_index_in_dim(right, y, 0, keepdims=False)
     lefts, codes, (own, given) = gather(left, codes, (own, given))
@@ -174,12 +218,16 @@
             lefts[1] = (1, near)
         rights += pair + [across(half, "row", 1) for half in pair]
 
-    mine, other, right_last = first_products(place, codes, lefts[:-1], rights, slots)
+    mine, other, right_last = first_products(codes, lefts[:-1], rights, slots)
     far, final = lefts[-1]
-    other = last_products(codes, far, final, right_last, other, 1, slots)
-    coming = across(other, "col", 1)
-    mine = last_products(codes, far, final, right_last, mine, 0, slots)
-    return (mine + coming).astype(jnp.bfloat16)
+    last = (codes, far, final, right_last)
+    rows, tile = mine.shape
+    coded = last_products(
+        *last, other, 1, slots, write_coded, jax.ShapeDtypeStruct((rows + PAD, tile), jnp.int16)
+    )
+    coming = across(coded, "col", 1)
+    mine = last_products(*last, mine, 0, slots, write_sum, jax.ShapeDtypeStruct((rows, tile), jnp.float32))
+    return add_coded(mine, coming)
 
 
 def solution(mesh):

time: 26.1 us -> 27.3 us (1.046); the launches traced: 25.9 us -> 26.8 us
  Pallas kernels: 5.01 us -> 6.66 us
  local copies, waits for them, and re-layouts: 1.68 us -> 2.94 us
  other arithmetic: 1.21 us -> 0 us
  waiting for transfers between devices: 5.46 us -> 4.76 us
    pallas_call x2 -> x3, Pallas kernels: 1.34 us -> 2.92 us  [the longest x1 1.6 us: add_coded(): pl.pallas_call(kernel, out_shape=jax.ShapeDtypeStruct(total.shape, jnp.bf...]
    unnamed x6 -> x8, local copies, waits for them, and re-layouts: 0.68 us -> 1.95 us
    ppermute x2, starting transfers between devices: 2.95 us -> 2 us  [crossed(): return lax.ppermute(block, ('row', 'col'), route)]
    ppermute x9, starting transfers between devices: 9.52 us -> 10.4 us  [across(): return lax.ppermute(block, axis, route)]
    ppermute x9, waiting for transfers between devices: 5.45 us -> 4.64 us  [across(): return lax.ppermute(block, axis, route)]
    convert_element_type x1 -> x0, other arithmetic: 0.65 us -> none  [shards(): return (mine + coming).astype(jnp.bfloat16)]
    another operation x1 -> x0, other arithmetic: 0.56 us -> none  [shards(): place = jnp.stack([row, z, y])]
  transfers between devices with their start and end apart: 11 -> 11, of which waited for: 7 -> 8; matrix products, arithmetic and copies ran while one was open for 6% -> 4% of each run, Pallas kernels for 17% -> 16%
where the time goes in v13:
time: 27.3 us; the launch traced here: 26.8 us
  starting transfers between devices  12.4 us (45%)
  Pallas kernels  6.66 us (24%)
  waiting for transfers between devices  4.76 us (17%)
  local copies, waits for them, and re-layouts  2.94 us (11%)
    ppermute x9, starting transfers between devices, across(): return lax.ppermute(block, axis, route)  10.4 us
    ppermute x9, waiting for transfers between devices, across(): return lax.ppermute(block, axis, route)  4.64 us
    ppermute x2, starting transfers between devices, crossed(): return lax.ppermute(block, ('row', 'col'), route)  2 us
    pallas_call x1, Pallas kernels, find_matches(): pl.pallas_call(kernel, out_shape=jax.ShapeDtypeStruct((inner * 2 * slots,...  1.97 us
    unnamed x8, local copies, waits for them, and re-layouts  1.95 us
    pallas_call x1, Pallas kernels, first_products(): pl.pallas_call(kernel, out_shape=[jax.ShapeDtypeStruct((RT * tile, tile),...  1.77 us
    pallas_call x1, Pallas kernels, add_coded(): pl.pallas_call(kernel, out_shape=jax.ShapeDtypeStruct(total.shape, jnp.bf...  1.6 us
    pallas_call x2, Pallas kernels, last_products(): pl.pallas_call(kernel, out_shape=out_shape, in_specs=[SMEM] + [VMEM] * (c...  1.32 us
  transfers between devices with their start and end apart: 11, of which 8 were waited for; matrix products, arithmetic and copies ran while one was open for 4% of the time, Pallas kernels for 16%

profile of v13, /device:TPU:0, one launch (start us, length us, event | category | flops | bytes accessed | tf_op | source)
XLA Modules:
  0.0 26.8 jit_solution(5413686544612922935)
XLA Ops:
  0.0 4.0 %collective-permute-start = (bf16[6,128,128]{2,1,0:T(8,128)(2,1)}, bf16[6,128,128]{2,1,0:T(8,128)(2,1)S(1)}, u32[]{:S(2)}, u32[]{:S(2)}) collective-permute-start(bf16[6,128,128]{2,1,0:T(8,128)(2,1)} %bitcast.7), channel_id=1, source_target_pairs={{0,4},{1,5},{2,6},{3,7},{4,0},{5,1},{6,2},{7,3},{8,12},{9,13},{10,... | collective-permute-start | bytes 589832 | tf_op jit(solution)/shard_map/ppermute | solution.py:180
  4.0 0.0 copy-start.1
  4.0 1.0 %dynamic-slice_bitcast_fusion = (bf16[3,128,128]{2,1,0:T(8,128)(2,1)S(1)}, bf16[3,128,128]{2,1,0:T(8,128)(2,1)S(1)}) fusion(bf16[1,1,2,3,128,128]{5,4,3,2,1,0:T(8,128)(2,1)} %param.6, s32[]{:T(128)S(6)} %select_n.8, s32[]{:T(128)S(6)} %select_n.7), kind=kLoop, calls=%fused_computation | loop fusion | bytes 393224 | tf_op jit(solution)/shard_map/jit(dynamic_index_in_dim)/squeeze | solution.py:210
  5.0 0.0 copy-done.1
  5.1 1.6 %collective-permute-start.2 = (bf16[6,128,128]{2,1,0:T(8,128)(2,1)S(1)}, bf16[6,128,128]{2,1,0:T(8,128)(2,1)S(1)}, u32[]{:S(2)}, u32[]{:S(2)}) collective-permute-start(bf16[6,128,128]{2,1,0:T(8,128)(2,1)S(1)} %bitcast.8), channel_id=1, source_target_pairs={{0,2},{1,3},{2,0},{3,1},{4,6},{5,7},{6,4},{7,5},{8,10},{9,11},{10,... | collective-permute-start | bytes 589832 | tf_op jit(solution)/shard_map/ppermute | solution.py:180
  6.7 1.5 %collective-permute-start.6 = (bf16[3,128,128]{2,1,0:T(8,128)(2,1)S(1)}, bf16[3,128,128]{2,1,0:T(8,128)(2,1)S(1)}, u32[]{:S(2)}, u32[]{:S(2)}) collective-permute-start(bf16[3,128,128]{2,1,0:T(8,128)(2,1)S(1)} %get-tuple-element.20.refs_3_), channel_id=1, source_target_pairs={{0,16},{8,24},{16,0},{24,8},{1,17},{9,25},{17,1},{25,9},{2,18},{10... | collective-permute-start | bytes 294920 | tf_op jit(solution)/shard_map/ppermute | solution.py:180
  8.2 1.5 %collective-permute-start.7 = (bf16[3,128,128]{2,1,0:T(8,128)(2,1)S(1)}, bf16[3,128,128]{2,1,0:T(8,128)(2,1)S(1)}, u32[]{:S(2)}, u32[]{:S(2)}) collective-permute-start(bf16[3,128,128]{2,1,0:T(8,128)(2,1)S(1)} %get-tuple-element.21), channel_id=1, source_target_pairs={{0,17},{1,16},{2,19},{3,18},{4,21},{5,20},{6,23},{7,22},{8,25},{9,... | collective-permute-start | bytes 294920 | tf_op jit(solution)/shard_map/ppermute | solution.py:186
  9.7 0.5 %collective-permute-start.3 = (bf16[3,128,128]{2,1,0:T(8,128)(2,1)S(1)}, bf16[3,128,128]{2,1,0:T(8,128)(2,1)S(1)}, u32[]{:S(2)}, u32[]{:S(2)}) collective-permute-start(bf16[3,128,128]{2,1,0:T(8,128)(2,1)S(1)} %get-tuple-element.21), channel_id=1, source_target_pairs={{0,1},{1,0},{2,3},{3,2},{4,5},{5,4},{6,7},{7,6},{8,9},{9,8},{10,11... | collective-permute-start | bytes 294920 | tf_op jit(solution)/shard_map/ppermute | solution.py:186
  10.2 2.0 %shard_map.46.codes_ref = s32[48]{0:T(128)} custom-call(s32[6,4,8]{2,1,0:T(4,128)} %bitcast.10, s32[4,3,2,8]{3,2,1,0:T(2,128)} %bitcast.11), custom_call_target="tpu_custom_call" | custom-call | tf_op jit(solution)/shard_map/pallas_call | solution.py:46
  12.2 1.3 %collective-permute-done.refs_2_ = bf16[6,128,128]{2,1,0:T(8,128)(2,1)S(1)} collective-permute-done((bf16[6,128,128]{2,1,0:T(8,128)(2,1)}, bf16[6,128,128]{2,1,0:T(8,128)(2,1)S(1)}, u32[]{:S(2)}, u32[]{:S(2)}) %collective-permute-start) | collective-permute-done | bytes 196640 | tf_op jit(solution)/shard_map/ppermute | solution.py:180
  13.5 0.8 %collective-permute-start.1 = (bf16[6,128,128]{2,1,0:T(8,128)(2,1)S(1)}, bf16[6,128,128]{2,1,0:T(8,128)(2,1)S(1)}, u32[]{:S(2)}, u32[]{:S(2)}) collective-permute-start(bf16[6,128,128]{2,1,0:T(8,128)(2,1)S(1)} %collective-permute-done.refs_2_), channel_id=1, source_target_pairs={{0,2},{1,3},{2,0},{3,1},{4,6},{5,7},{6,4},{7,5},{8,10},{9,11},{10,... | collective-permute-start | bytes 589832 | tf_op jit(solution)/shard_map/ppermute | solution.py:180
  14.2 0.0 collective-permute-done.6.refs_7_
  14.2 0.0 collective-permute-start.8
  14.2 0.0 collective-permute-done.7.refs_8_
  14.2 0.5 %collective-permute-start.9 = (bf16[3,128,128]{2,1,0:T(8,128)(2,1)S(1)}, bf16[3,128,128]{2,1,0:T(8,128)(2,1)S(1)}, u32[]{:S(2)}, u32[]{:S(2)}) collective-permute-start(bf16[3,128,128]{2,1,0:T(8,128)(2,1)S(1)} %collective-permute-done.7.refs_8_), channel_id=1, source_target_pairs={{0,8},{8,0},{16,24},{24,16},{1,9},{9,1},{17,25},{25,17},{2,10},{10... | collective-permute-start | bytes 294920 | tf_op jit(solution)/shard_map/ppermute | solution.py:180
  14.8 0.1 collective-permute-done.3.refs_4_
  14.9 0.0 collective-permute-start.5
  14.9 0.0 collective-permute-done.2.refs_1_
  14.9 0.5 %collective-permute-start.4 = (bf16[3,128,128]{2,1,0:T(8,128)(2,1)S(1)}, bf16[3,128,128]{2,1,0:T(8,128)(2,1)S(1)}, u32[]{:S(2)}, u32[]{:S(2)}) collective-permute-start(bf16[3,128,128]{2,1,0:T(8,128)(2,1)S(1)} %get-tuple-element.20.refs_3_), channel_id=1, source_target_pairs={{0,8},{8,0},{16,24},{24,16},{1,9},{9,1},{17,25},{25,17},{2,10},{10... | collective-permute-start | bytes 294920 | tf_op jit(solution)/shard_map/ppermute | solution.py:180
  15.4 0.1 collective-permute-done.8.refs_9_
  15.5 0.2 collective-permute-done.9.refs_10_
  15.7 0.5 %collective-permute-done.5.refs_6_ = bf16[3,128,128]{2,1,0:T(8,128)(2,1)S(1)} collective-permute-done((bf16[3,128,128]{2,1,0:T(8,128)(2,1)S(1)}, bf16[3,128,128]{2,1,0:T(8,128)(2,1)S(1)}, u32[]{:S(2)}, u32[]{:S(2)}) %collective-permute-start.5) | collective-permute-done | bytes 98336 | tf_op jit(solution)/shard_map/ppermute | solution.py:180
  16.2 0.2 collective-permute-done.4.refs_5_
  16.3 0.0 copy-start.2
  16.3 0.7 %copy-done.2 = s32[48]{0:T(128)S(1)} copy-done((s32[48]{0:T(128)S(1)}, s32[48]{0:T(128)}, u32[]{:S(2)}) %copy-start.2) | copy-done | bytes 216
  17.0 1.8 %shard_map.47 = (f32[256,128]{1,0:T(8,128)S(1)}, f32[256,128]{1,0:T(8,128)S(1)}, bf16[2,3,128,128]{3,2,1,0:T(8,128)(2,1)S(1)}) custom-call(s32[48]{0:T(128)S(1)} %copy-done.2, bf16[6,128,128]{2,1,0:T(8,128)(2,1)S(1)} %bitcast.9, bf16[6,128,128]{2,1,0:T(8,128)(2,1)S(1)} %collective-permute-done.2.refs_1_, ...), custom_call_target="tpu_custom_call" | custom-call | flops 201326592 | bytes 786432 | tf_op jit(solution)/shard_map/pallas_call | solution.py:98
  18.8 0.7 %collective-permute-done.1.refs_0_ = bf16[6,128,128]{2,1,0:T(8,128)(2,1)S(1)} collective-permute-done((bf16[6,128,128]{2,1,0:T(8,128)(2,1)S(1)}, bf16[6,128,128]{2,1,0:T(8,128)(2,1)S(1)}, u32[]{:S(2)}, u32[]{:S(2)}) %collective-permute-start.1) | collective-permute-done | bytes 196640 | tf_op jit(solution)/shard_map/ppermute | solution.py:180
  19.5 0.7 %shard_map.49 = s16[272,128]{1,0:T(8,128)(2,1)S(1)} custom-call(s32[48]{0:T(128)S(1)} %copy-done.2, bf16[6,128,128]{2,1,0:T(8,128)(2,1)S(1)} %collective-permute-done.1.refs_0_, bf16[2,3,128,128]{3,2,1,0:T(8,128)(2,1)S(1)} %get-tuple-element.22.refs_1_, f32[256,128]{1,0:T(8,128)S(1)} %get-tuple-element.24.refs_2_), custom_call_target="tpu_custom_call" | custom-call | flops 25165824 | bytes 196608 | tf_op jit(solution)/shard_map/pallas_call | solution.py:128
  20.2 1.4 %collective-permute-start.10 = (s16[272,128]{1,0:T(8,128)(2,1)S(1)}, s16[272,128]{1,0:T(8,128)(2,1)S(1)}, u32[]{:S(2)}, u32[]{:S(2)}) collective-permute-start(s16[272,128]{1,0:T(8,128)(2,1)S(1)} %shard_map.49), channel_id=1, source_target_pairs={{0,1},{1,0},{2,3},{3,2},{4,5},{5,4},{6,7},{7,6},{8,9},{9,8},{10,11... | collective-permute-start | bytes 208904 | tf_op jit(solution)/shard_map/ppermute | solution.py:180
  21.6 0.6 %shard_map.48.total_ref = f32[256,128]{1,0:T(8,128)S(1)} custom-call(s32[48]{0:T(128)S(1)} %copy-done.2, bf16[6,128,128]{2,1,0:T(8,128)(2,1)S(1)} %collective-permute-done.1.refs_0_, bf16[2,3,128,128]{3,2,1,0:T(8,128)(2,1)S(1)} %get-tuple-element.22.refs_1_, f32[256,128]{1,0:T(8,128)S(1)} %get-tuple-element.23.refs_2_), custom_call_target="tpu_custom_call" | custom-call | flops 25165824 | bytes 196608 | tf_op jit(solution)/shard_map/pallas_call | solution.py:128
  22.2 0.0 copy-start
  22.2 0.6 %copy-done = f32[256,128]{1,0:T(8,128)} copy-done((f32[256,128]{1,0:T(8,128)}, f32[256,128]{1,0:T(8,128)S(1)}, u32[]{:S(2)}) %copy-start) | copy-done | bytes 131096
  22.9 1.7 %collective-permute-done.10.coded_ref = s16[272,128]{1,0:T(8,128)(2,1)S(1)} collective-permute-done((s16[272,128]{1,0:T(8,128)(2,1)S(1)}, s16[272,128]{1,0:T(8,128)(2,1)S(1)}, u32[]{:S(2)}, u32[]{:S(2)}) %collective-permute-start.10) | collective-permute-done | bytes 69664 | tf_op jit(solution)/shard_map/ppermute | solution.py:180
  24.6 0.0 copy-start.3
  24.6 0.6 %copy-done.3 = s16[272,128]{1,0:T(8,128)(2,1)} copy-done((s16[272,128]{1,0:T(8,128)(2,1)}, s16[272,128]{1,0:T(8,128)(2,1)S(1)}, u32[]{:S(2)}) %copy-start.3) | copy-done | bytes 69656
  25.2 1.6 %shard_map.50 = bf16[256,128]{1,0:T(8,128)(2,1)} custom-call(f32[256,128]{1,0:T(8,128)} %copy-done, s16[272,128]{1,0:T(8,128)(2,1)} %copy-done.3), custom_call_target="tpu_custom_call" | custom-call | tf_op jit(solution)/shard_map/pallas_call | solution.py:170
Async XLA Ops:
  0.0 13.5 %collective-permute-start = (bf16[6,128,128]{2,1,0:T(8,128)(2,1)}, bf16[6,128,128]{2,1,0:T(8,128)(2,1)S(1)}, u32[]{:S(2)}, u32[]{:S(2)}) collective-permute-start(bf16[6,128,128]{2,1,0:T(8,128)(2,1)} %bitcast.7), channel_id=1, source_target_pairs={{0,4},{1,5},{2,6},{3,7},{4,0},{5,1},{6,2},{7,3},{8,12},{9,13},{10,... | collective-permute-start | bytes 589832 | tf_op jit(solution)/shard_map/ppermute | solution.py:180
  4.0 1.0 %copy-start.1 = (bf16[1,1,6,128,128]{4,3,2,1,0:T(8,128)(2,1)S(1)}, bf16[1,1,6,128,128]{4,3,2,1,0:T(8,128)(2,1)}, u32[]{:S(2)}) copy-start(bf16[1,1,6,128,128]{4,3,2,1,0:T(8,128)(2,1)} %param.4) | copy-start | bytes 589828
  5.1 9.8 %collective-permute-start.2 = (bf16[6,128,128]{2,1,0:T(8,128)(2,1)S(1)}, bf16[6,128,128]{2,1,0:T(8,128)(2,1)S(1)}, u32[]{:S(2)}, u32[]{:S(2)}) collective-permute-start(bf16[6,128,128]{2,1,0:T(8,128)(2,1)S(1)} %bitcast.8), channel_id=1, source_target_pairs={{0,2},{1,3},{2,0},{3,1},{4,6},{5,7},{6,4},{7,5},{8,10},{9,11},{10,... | collective-permute-start | bytes 589832 | tf_op jit(solution)/shard_map/ppermute | solution.py:180
  6.7 7.6 %collective-permute-start.6 = (bf16[3,128,128]{2,1,0:T(8,128)(2,1)S(1)}, bf16[3,128,128]{2,1,0:T(8,128)(2,1)S(1)}, u32[]{:S(2)}, u32[]{:S(2)}) collective-permute-start(bf16[3,128,128]{2,1,0:T(8,128)(2,1)S(1)} %get-tuple-element.20.refs_3_), channel_id=1, source_target_pairs={{0,16},{8,24},{16,0},{24,8},{1,17},{9,25},{17,1},{25,9},{2,18},{10... | collective-permute-start | bytes 294920 | tf_op jit(solution)/shard_map/ppermute | solution.py:180
  8.2 6.1 %collective-permute-start.7 = (bf16[3,128,128]{2,1,0:T(8,128)(2,1)S(1)}, bf16[3,128,128]{2,1,0:T(8,128)(2,1)S(1)}, u32[]{:S(2)}, u32[]{:S(2)}) collective-permute-start(bf16[3,128,128]{2,1,0:T(8,128)(2,1)S(1)} %get-tuple-element.21), channel_id=1, source_target_pairs={{0,17},{1,16},{2,19},{3,18},{4,21},{5,20},{6,23},{7,22},{8,25},{9,... | collective-permute-start | bytes 294920 | tf_op jit(solution)/shard_map/ppermute | solution.py:186
  9.7 5.2 %collective-permute-start.3 = (bf16[3,128,128]{2,1,0:T(8,128)(2,1)S(1)}, bf16[3,128,128]{2,1,0:T(8,128)(2,1)S(1)}, u32[]{:S(2)}, u32[]{:S(2)}) collective-permute-start(bf16[3,128,128]{2,1,0:T(8,128)(2,1)S(1)} %get-tuple-element.21), channel_id=1, source_target_pairs={{0,1},{1,0},{2,3},{3,2},{4,5},{5,4},{6,7},{7,6},{8,9},{9,8},{10,11... | collective-permute-start | bytes 294920 | tf_op jit(solution)/shard_map/ppermute | solution.py:186
  13.5 6.0 %collective-permute-start.1 = (bf16[6,128,128]{2,1,0:T(8,128)(2,1)S(1)}, bf16[6,128,128]{2,1,0:T(8,128)(2,1)S(1)}, u32[]{:S(2)}, u32[]{:S(2)}) collective-permute-start(bf16[6,128,128]{2,1,0:T(8,128)(2,1)S(1)} %collective-permute-done.refs_2_), channel_id=1, source_target_pairs={{0,2},{1,3},{2,0},{3,1},{4,6},{5,7},{6,4},{7,5},{8,10},{9,11},{10,... | collective-permute-start | bytes 589832 | tf_op jit(solution)/shard_map/ppermute | solution.py:180
  14.2 1.3 %collective-permute-start.8 = (bf16[3,128,128]{2,1,0:T(8,128)(2,1)S(1)}, bf16[3,128,128]{2,1,0:T(8,128)(2,1)S(1)}, u32[]{:S(2)}, u32[]{:S(2)}) collective-permute-start(bf16[3,128,128]{2,1,0:T(8,128)(2,1)S(1)} %collective-permute-done.6.refs_7_), channel_id=1, source_target_pairs={{0,8},{8,0},{16,24},{24,16},{1,9},{9,1},{17,25},{25,17},{2,10},{10... | collective-permute-start | bytes 294920 | tf_op jit(solution)/shard_map/ppermute | solution.py:180
  14.2 1.5 %collective-permute-start.9 = (bf16[3,128,128]{2,1,0:T(8,128)(2,1)S(1)}, bf16[3,128,128]{2,1,0:T(8,128)(2,1)S(1)}, u32[]{:S(2)}, u32[]{:S(2)}) collective-permute-start(bf16[3,128,128]{2,1,0:T(8,128)(2,1)S(1)} %collective-permute-done.7.refs_8_), channel_id=1, source_target_pairs={{0,8},{8,0},{16,24},{24,16},{1,9},{9,1},{17,25},{25,17},{2,10},{10... | collective-permute-start | bytes 294920 | tf_op jit(solution)/shard_map/ppermute | solution.py:180
  14.9 1.3 %collective-permute-start.5 = (bf16[3,128,128]{2,1,0:T(8,128)(2,1)S(1)}, bf16[3,128,128]{2,1,0:T(8,128)(2,1)S(1)}, u32[]{:S(2)}, u32[]{:S(2)}) collective-permute-start(bf16[3,128,128]{2,1,0:T(8,128)(2,1)S(1)} %collective-permute-done.3.refs_4_), channel_id=1, source_target_pairs={{0,8},{8,0},{16,24},{24,16},{1,9},{9,1},{17,25},{25,17},{2,10},{10... | collective-permute-start | bytes 294920 | tf_op jit(solution)/shard_map/ppermute | solution.py:180
  14.9 1.5 %collective-permute-start.4 = (bf16[3,128,128]{2,1,0:T(8,128)(2,1)S(1)}, bf16[3,128,128]{2,1,0:T(8,128)(2,1)S(1)}, u32[]{:S(2)}, u32[]{:S(2)}) collective-permute-start(bf16[3,128,128]{2,1,0:T(8,128)(2,1)S(1)} %get-tuple-element.20.refs_3_), channel_id=1, source_target_pairs={{0,8},{8,0},{16,24},{24,16},{1,9},{9,1},{17,25},{25,17},{2,10},{10... | collective-permute-start | bytes 294920 | tf_op jit(solution)/shard_map/ppermute | solution.py:180
  16.3 0.7 %copy-start.2 = (s32[48]{0:T(128)S(1)}, s32[48]{0:T(128)}, u32[]{:S(2)}) copy-start(s32[48]{0:T(128)} %shard_map.46.codes_ref) | copy-start | bytes 580
  20.2 4.4 %collective-permute-start.10 = (s16[272,128]{1,0:T(8,128)(2,1)S(1)}, s16[272,128]{1,0:T(8,128)(2,1)S(1)}, u32[]{:S(2)}, u32[]{:S(2)}) collective-permute-start(s16[272,128]{1,0:T(8,128)(2,1)S(1)} %shard_map.49), channel_id=1, source_target_pairs={{0,1},{1,0},{2,3},{3,2},{4,5},{5,4},{6,7},{7,6},{8,9},{9,8},{10,11... | collective-permute-start | bytes 208904 | tf_op jit(solution)/shard_map/ppermute | solution.py:180
  22.2 0.7 %copy-start = (f32[256,128]{1,0:T(8,128)}, f32[256,128]{1,0:T(8,128)S(1)}, u32[]{:S(2)}) copy-start(f32[256,128]{1,0:T(8,128)S(1)} %shard_map.48.total_ref) | copy-start | bytes 393220
  24.6 0.6 %copy-start.3 = (s16[272,128]{1,0:T(8,128)(2,1)}, s16[272,128]{1,0:T(8,128)(2,1)S(1)}, u32[]{:S(2)}) copy-start(s16[272,128]{1,0:T(8,128)(2,1)S(1)} %collective-permute-done.10.coded_ref) | copy-start | bytes 208900

commit v14 on v13

--- a/solution.py
+++ b/solution.py
@@ -158,21 +158,10 @@
 
 
 def add_coded(total, coded):
-    def kernel(total_ref, coded_ref, out_ref):
-        tile = total_ref.shape[1]
-        exponents = coded_ref[RT * tile :, :].astype(jnp.int32).astype(jnp.float32)
-        for i in range(RT):
-            rows = slice(i * tile, (i + 1) * tile)
-            scale = jnp.exp2(exponents[i : i + 1, :] - BITS)
-            values = coded_ref[rows, :].astype(jnp.int32).astype(jnp.float32)
-            out_ref[rows, :] = (total_ref[rows, :] + values * scale).astype(out_ref.dtype)
-
-    return pl.pallas_call(
-        kernel,
-        out_shape=jax.ShapeDtypeStruct(total.shape, jnp.bfloat16),
-        in_specs=[VMEM] * 2,
-        out_specs=VMEM,
-    )(total, coded)
+    tile = total.shape[1]
+    exponents = coded[RT * tile : RT * tile + RT].astype(jnp.float32)
+    scale = jnp.repeat(jnp.exp2(exponents - BITS), tile, axis=0)
+    return (total + coded[: RT * tile].astype(jnp.float32) * scale).astype(jnp.bfloat16)
 
 
 def across(block, axis, mask):

time: 27.3 us -> 25.7 us (0.941); the launches traced: 26.8 us -> 25.5 us
  local copies, waits for them, and re-layouts: 2.94 us -> 1.67 us
  Pallas kernels: 6.66 us -> 5.53 us
  other arithmetic: 0 us -> 0.68 us
  waiting for transfers between devices: 4.76 us -> 5.33 us
    pallas_call x1 -> x0, Pallas kernels: 1.6 us -> none  [add_coded(): pl.pallas_call(kernel, out_shape=jax.ShapeDtypeStruct(total.shape, jnp.bf...]
    unnamed x8 -> x4, local copies, waits for them, and re-layouts: 1.95 us -> 0.68 us
    convert_element_type x0 -> x1, other arithmetic: none -> 0.67 us  [add_coded(): (total + coded[:RT * tile].astype(jnp.float32) * scale).astype(jnp.bfloat16)]
    ppermute x9, waiting for transfers between devices: 4.64 us -> 5.2 us  [across(): return lax.ppermute(block, axis, route)]
  transfers between devices with their start and end apart: 11 -> 11, of which waited for: 8 -> 8; matrix products, arithmetic and copies ran while one was open for 4% -> 4% of each run, Pallas kernels for 16% -> 18%
where the time goes in v14:
time: 25.7 us; the launch traced here: 25.5 us
  starting transfers between devices  12.2 us (47%)
  Pallas kernels  5.53 us (22%)
  waiting for transfers between devices  5.33 us (21%)
  local copies, waits for them, and re-layouts  1.67 us (6%)
  other arithmetic  0.68 us (3%)
    ppermute x9, starting transfers between devices, across(): return lax.ppermute(block, axis, route)  10.2 us
    ppermute x9, waiting for transfers between devices, across(): return lax.ppermute(block, axis, route)  5.2 us
    pallas_call x1, Pallas kernels, first_products(): pl.pallas_call(kernel, out_shape=[jax.ShapeDtypeStruct((RT * tile, tile),...  2.02 us
    ppermute x2, starting transfers between devices, crossed(): return lax.ppermute(block, ('row', 'col'), route)  2 us
    pallas_call x1, Pallas kernels, find_matches(): pl.pallas_call(kernel, out_shape=jax.ShapeDtypeStruct((inner * 2 * slots,...  1.97 us
    pallas_call x2, Pallas kernels, last_products(): pl.pallas_call(kernel, out_shape=out_shape, in_specs=[SMEM] + [VMEM] * (c...  1.55 us
    squeeze x1, local copies, waits for them, and re-layouts, shards(): given = lax.dynamic_index_in_dim(right, 1 - y, 0, keepdims=False)  0.99 us
    unnamed x4, local copies, waits for them, and re-layouts  0.68 us
  transfers between devices with their start and end apart: 11, of which 8 were waited for; matrix products, arithmetic and copies ran while one was open for 4% of the time, Pallas kernels for 18%

profile of v14, /device:TPU:0, one launch (start us, length us, event | category | flops | bytes accessed | tf_op | source)
XLA Modules:
  0.0 25.5 jit_solution(8175426733611333900)
XLA Ops:
  0.0 4.0 %collective-permute-start = (bf16[6,128,128]{2,1,0:T(8,128)(2,1)}, bf16[6,128,128]{2,1,0:T(8,128)(2,1)S(1)}, u32[]{:S(2)}, u32[]{:S(2)}) collective-permute-start(bf16[6,128,128]{2,1,0:T(8,128)(2,1)} %bitcast.13), channel_id=1, source_target_pairs={{0,4},{1,5},{2,6},{3,7},{4,0},{5,1},{6,2},{7,3},{8,12},{9,13},{10,... | collective-permute-start | bytes 589832 | tf_op jit(solution)/shard_map/ppermute | solution.py:169
  4.0 0.0 copy-start
  4.0 1.0 %dynamic-slice_bitcast_fusion = (bf16[3,128,128]{2,1,0:T(8,128)(2,1)S(1)}, bf16[3,128,128]{2,1,0:T(8,128)(2,1)S(1)}) fusion(bf16[1,1,2,3,128,128]{5,4,3,2,1,0:T(8,128)(2,1)} %param.6, s32[]{:T(128)S(6)} %select_n.8, s32[]{:T(128)S(6)} %select_n.7), kind=kLoop, calls=%fused_computation.3 | loop fusion | bytes 393224 | tf_op jit(solution)/shard_map/jit(dynamic_index_in_dim)/squeeze | solution.py:199
  5.0 0.0 copy-done
  5.1 1.6 %collective-permute-start.2 = (bf16[6,128,128]{2,1,0:T(8,128)(2,1)S(1)}, bf16[6,128,128]{2,1,0:T(8,128)(2,1)S(1)}, u32[]{:S(2)}, u32[]{:S(2)}) collective-permute-start(bf16[6,128,128]{2,1,0:T(8,128)(2,1)S(1)} %bitcast.14), channel_id=1, source_target_pairs={{0,2},{1,3},{2,0},{3,1},{4,6},{5,7},{6,4},{7,5},{8,10},{9,11},{10,... | collective-permute-start | bytes 589832 | tf_op jit(solution)/shard_map/ppermute | solution.py:169
  6.7 1.5 %collective-permute-start.6 = (bf16[3,128,128]{2,1,0:T(8,128)(2,1)S(1)}, bf16[3,128,128]{2,1,0:T(8,128)(2,1)S(1)}, u32[]{:S(2)}, u32[]{:S(2)}) collective-permute-start(bf16[3,128,128]{2,1,0:T(8,128)(2,1)S(1)} %get-tuple-element.20.refs_3_), channel_id=1, source_target_pairs={{0,16},{8,24},{16,0},{24,8},{1,17},{9,25},{17,1},{25,9},{2,18},{10... | collective-permute-start | bytes 294920 | tf_op jit(solution)/shard_map/ppermute | solution.py:169
  8.2 1.5 %collective-permute-start.7 = (bf16[3,128,128]{2,1,0:T(8,128)(2,1)S(1)}, bf16[3,128,128]{2,1,0:T(8,128)(2,1)S(1)}, u32[]{:S(2)}, u32[]{:S(2)}) collective-permute-start(bf16[3,128,128]{2,1,0:T(8,128)(2,1)S(1)} %get-tuple-element.21), channel_id=1, source_target_pairs={{0,17},{1,16},{2,19},{3,18},{4,21},{5,20},{6,23},{7,22},{8,25},{9,... | collective-permute-start | bytes 294920 | tf_op jit(solution)/shard_map/ppermute | solution.py:175
  9.7 0.5 %collective-permute-start.3 = (bf16[3,128,128]{2,1,0:T(8,128)(2,1)S(1)}, bf16[3,128,128]{2,1,0:T(8,128)(2,1)S(1)}, u32[]{:S(2)}, u32[]{:S(2)}) collective-permute-start(bf16[3,128,128]{2,1,0:T(8,128)(2,1)S(1)} %get-tuple-element.21), channel_id=1, source_target_pairs={{0,1},{1,0},{2,3},{3,2},{4,5},{5,4},{6,7},{7,6},{8,9},{9,8},{10,11... | collective-permute-start | bytes 294920 | tf_op jit(solution)/shard_map/ppermute | solution.py:175
  10.2 2.0 %shard_map.46.codes_ref = s32[48]{0:T(128)} custom-call(s32[6,4,8]{2,1,0:T(4,128)} %bitcast.16, s32[4,3,2,8]{3,2,1,0:T(2,128)} %bitcast.17), custom_call_target="tpu_custom_call" | custom-call | tf_op jit(solution)/shard_map/pallas_call | solution.py:46
  12.2 1.3 %collective-permute-done.refs_2_ = bf16[6,128,128]{2,1,0:T(8,128)(2,1)S(1)} collective-permute-done((bf16[6,128,128]{2,1,0:T(8,128)(2,1)}, bf16[6,128,128]{2,1,0:T(8,128)(2,1)S(1)}, u32[]{:S(2)}, u32[]{:S(2)}) %collective-permute-start) | collective-permute-done | bytes 196640 | tf_op jit(solution)/shard_map/ppermute | solution.py:169
  13.5 0.8 %collective-permute-start.1 = (bf16[6,128,128]{2,1,0:T(8,128)(2,1)S(1)}, bf16[6,128,128]{2,1,0:T(8,128)(2,1)S(1)}, u32[]{:S(2)}, u32[]{:S(2)}) collective-permute-start(bf16[6,128,128]{2,1,0:T(8,128)(2,1)S(1)} %collective-permute-done.refs_2_), channel_id=1, source_target_pairs={{0,2},{1,3},{2,0},{3,1},{4,6},{5,7},{6,4},{7,5},{8,10},{9,11},{10,... | collective-permute-start | bytes 589832 | tf_op jit(solution)/shard_map/ppermute | solution.py:169
  14.2 0.0 collective-permute-done.6.refs_7_
  14.2 0.0 collective-permute-start.8
  14.2 0.0 collective-permute-done.7.refs_8_
  14.2 0.5 %collective-permute-start.9 = (bf16[3,128,128]{2,1,0:T(8,128)(2,1)S(1)}, bf16[3,128,128]{2,1,0:T(8,128)(2,1)S(1)}, u32[]{:S(2)}, u32[]{:S(2)}) collective-permute-start(bf16[3,128,128]{2,1,0:T(8,128)(2,1)S(1)} %collective-permute-done.7.refs_8_), channel_id=1, source_target_pairs={{0,8},{8,0},{16,24},{24,16},{1,9},{9,1},{17,25},{25,17},{2,10},{10... | collective-permute-start | bytes 294920 | tf_op jit(solution)/shard_map/ppermute | solution.py:169
  14.8 0.1 collective-permute-done.3.refs_4_
  14.9 0.0 collective-permute-start.5
  14.9 0.0 collective-permute-done.2.refs_1_
  14.9 0.5 %collective-permute-start.4 = (bf16[3,128,128]{2,1,0:T(8,128)(2,1)S(1)}, bf16[3,128,128]{2,1,0:T(8,128)(2,1)S(1)}, u32[]{:S(2)}, u32[]{:S(2)}) collective-permute-start(bf16[3,128,128]{2,1,0:T(8,128)(2,1)S(1)} %get-tuple-element.20.refs_3_), channel_id=1, source_target_pairs={{0,8},{8,0},{16,24},{24,16},{1,9},{9,1},{17,25},{25,17},{2,10},{10... | collective-permute-start | bytes 294920 | tf_op jit(solution)/shard_map/ppermute | solution.py:169
  15.4 0.1 collective-permute-done.8.refs_9_
  15.5 0.2 collective-permute-done.9.refs_10_
  15.7 0.5 %collective-permute-done.5.refs_6_ = bf16[3,128,128]{2,1,0:T(8,128)(2,1)S(1)} collective-permute-done((bf16[3,128,128]{2,1,0:T(8,128)(2,1)S(1)}, bf16[3,128,128]{2,1,0:T(8,128)(2,1)S(1)}, u32[]{:S(2)}, u32[]{:S(2)}) %collective-permute-start.5) | collective-permute-done | bytes 98336 | tf_op jit(solution)/shard_map/ppermute | solution.py:169
  16.2 0.2 collective-permute-done.4.refs_5_
  16.3 0.0 copy-start.1
  16.3 0.7 %copy-done.1 = s32[48]{0:T(128)S(1)} copy-done((s32[48]{0:T(128)S(1)}, s32[48]{0:T(128)}, u32[]{:S(2)}) %copy-start.1) | copy-done | bytes 216
  17.0 2.0 %shard_map.47 = (f32[256,128]{1,0:T(8,128)S(1)}, f32[256,128]{1,0:T(8,128)S(1)}, bf16[2,3,128,128]{3,2,1,0:T(8,128)(2,1)S(1)}) custom-call(s32[48]{0:T(128)S(1)} %copy-done.1, bf16[6,128,128]{2,1,0:T(8,128)(2,1)S(1)} %bitcast.15, bf16[6,128,128]{2,1,0:T(8,128)(2,1)S(1)} %collective-permute-done.2.refs_1_, ...), custom_call_target="tpu_custom_call" | custom-call | flops 201326592 | bytes 786432 | tf_op jit(solution)/shard_map/pallas_call | solution.py:98
  19.0 0.5 %collective-permute-done.1.refs_0_ = bf16[6,128,128]{2,1,0:T(8,128)(2,1)S(1)} collective-permute-done((bf16[6,128,128]{2,1,0:T(8,128)(2,1)S(1)}, bf16[6,128,128]{2,1,0:T(8,128)(2,1)S(1)}, u32[]{:S(2)}, u32[]{:S(2)}) %collective-permute-start.1) | collective-permute-done | bytes 196640 | tf_op jit(solution)/shard_map/ppermute | solution.py:169
  19.5 0.9 %shard_map.49 = s16[272,128]{1,0:T(8,128)(2,1)S(1)} custom-call(s32[48]{0:T(128)S(1)} %copy-done.1, bf16[6,128,128]{2,1,0:T(8,128)(2,1)S(1)} %collective-permute-done.1.refs_0_, bf16[2,3,128,128]{3,2,1,0:T(8,128)(2,1)S(1)} %get-tuple-element.22.refs_1_, f32[256,128]{1,0:T(8,128)S(1)} %get-tuple-element.24.refs_2_), custom_call_target="tpu_custom_call" | custom-call | flops 25165824 | bytes 196608 | tf_op jit(solution)/shard_map/pallas_call | solution.py:128
  20.4 1.3 %collective-permute-start.10 = (s16[272,128]{1,0:T(8,128)(2,1)S(1)}, s16[272,128]{1,0:T(8,128)(2,1)S(1)}, u32[]{:S(2)}, u32[]{:S(2)}) collective-permute-start(s16[272,128]{1,0:T(8,128)(2,1)S(1)} %shard_map.49), channel_id=1, source_target_pairs={{0,1},{1,0},{2,3},{3,2},{4,5},{5,4},{6,7},{7,6},{8,9},{9,8},{10,11... | collective-permute-start | bytes 208904 | tf_op jit(solution)/shard_map/ppermute | solution.py:169
  21.7 0.6 %shard_map.48 = f32[256,128]{1,0:T(8,128)S(1)} custom-call(s32[48]{0:T(128)S(1)} %copy-done.1, bf16[6,128,128]{2,1,0:T(8,128)(2,1)S(1)} %collective-permute-done.1.refs_0_, bf16[2,3,128,128]{3,2,1,0:T(8,128)(2,1)S(1)} %get-tuple-element.22.refs_1_, f32[256,128]{1,0:T(8,128)S(1)} %get-tuple-element.23.refs_2_), custom_call_target="tpu_custom_call" | custom-call | flops 25165824 | bytes 196608 | tf_op jit(solution)/shard_map/pallas_call | solution.py:128
  22.3 2.5 %collective-permute-done.10 = s16[272,128]{1,0:T(8,128)(2,1)S(1)} collective-permute-done((s16[272,128]{1,0:T(8,128)(2,1)S(1)}, s16[272,128]{1,0:T(8,128)(2,1)S(1)}, u32[]{:S(2)}, u32[]{:S(2)}) %collective-permute-start.10) | collective-permute-done | bytes 69664 | tf_op jit(solution)/shard_map/ppermute | solution.py:169
  24.8 0.7 %fusion.1 = bf16[256,128]{1,0:T(8,128)(2,1)} fusion(f32[256,128]{1,0:T(8,128)S(1)} %shard_map.48, s16[272,128]{1,0:T(8,128)(2,1)S(1)} %collective-permute-done.10, f32[2,128]{1,0:T(2,128)S(1)} %multiply_exponential_fusion), kind=kLoop, calls=%fused_computation.2 | loop fusion | flops 131072 | bytes 263168 | tf_op jit(solution)/shard_map/convert_element_type | solution.py:164
  (1 shorter events, 0.0 us)
Async XLA Ops:
  0.0 13.5 %collective-permute-start = (bf16[6,128,128]{2,1,0:T(8,128)(2,1)}, bf16[6,128,128]{2,1,0:T(8,128)(2,1)S(1)}, u32[]{:S(2)}, u32[]{:S(2)}) collective-permute-start(bf16[6,128,128]{2,1,0:T(8,128)(2,1)} %bitcast.13), channel_id=1, source_target_pairs={{0,4},{1,5},{2,6},{3,7},{4,0},{5,1},{6,2},{7,3},{8,12},{9,13},{10,... | collective-permute-start | bytes 589832 | tf_op jit(solution)/shard_map/ppermute | solution.py:169
  4.0 1.0 %copy-start = (bf16[1,1,6,128,128]{4,3,2,1,0:T(8,128)(2,1)S(1)}, bf16[1,1,6,128,128]{4,3,2,1,0:T(8,128)(2,1)}, u32[]{:S(2)}) copy-start(bf16[1,1,6,128,128]{4,3,2,1,0:T(8,128)(2,1)} %param.4) | copy-start | bytes 589828
  5.1 9.8 %collective-permute-start.2 = (bf16[6,128,128]{2,1,0:T(8,128)(2,1)S(1)}, bf16[6,128,128]{2,1,0:T(8,128)(2,1)S(1)}, u32[]{:S(2)}, u32[]{:S(2)}) collective-permute-start(bf16[6,128,128]{2,1,0:T(8,128)(2,1)S(1)} %bitcast.14), channel_id=1, source_target_pairs={{0,2},{1,3},{2,0},{3,1},{4,6},{5,7},{6,4},{7,5},{8,10},{9,11},{10,... | collective-permute-start | bytes 589832 | tf_op jit(solution)/shard_map/ppermute | solution.py:169
  6.7 7.6 %collective-permute-start.6 = (bf16[3,128,128]{2,1,0:T(8,128)(2,1)S(1)}, bf16[3,128,128]{2,1,0:T(8,128)(2,1)S(1)}, u32[]{:S(2)}, u32[]{:S(2)}) collective-permute-start(bf16[3,128,128]{2,1,0:T(8,128)(2,1)S(1)} %get-tuple-element.20.refs_3_), channel_id=1, source_target_pairs={{0,16},{8,24},{16,0},{24,8},{1,17},{9,25},{17,1},{25,9},{2,18},{10... | collective-permute-start | bytes 294920 | tf_op jit(solution)/shard_map/ppermute | solution.py:169
  8.2 6.1 %collective-permute-start.7 = (bf16[3,128,128]{2,1,0:T(8,128)(2,1)S(1)}, bf16[3,128,128]{2,1,0:T(8,128)(2,1)S(1)}, u32[]{:S(2)}, u32[]{:S(2)}) collective-permute-start(bf16[3,128,128]{2,1,0:T(8,128)(2,1)S(1)} %get-tuple-element.21), channel_id=1, source_target_pairs={{0,17},{1,16},{2,19},{3,18},{4,21},{5,20},{6,23},{7,22},{8,25},{9,... | collective-permute-start | bytes 294920 | tf_op jit(solution)/shard_map/ppermute | solution.py:175
  9.7 5.2 %collective-permute-start.3 = (bf16[3,128,128]{2,1,0:T(8,128)(2,1)S(1)}, bf16[3,128,128]{2,1,0:T(8,128)(2,1)S(1)}, u32[]{:S(2)}, u32[]{:S(2)}) collective-permute-start(bf16[3,128,128]{2,1,0:T(8,128)(2,1)S(1)} %get-tuple-element.21), channel_id=1, source_target_pairs={{0,1},{1,0},{2,3},{3,2},{4,5},{5,4},{6,7},{7,6},{8,9},{9,8},{10,11... | collective-permute-start | bytes 294920 | tf_op jit(solution)/shard_map/ppermute | solution.py:175
  13.5 6.0 %collective-permute-start.1 = (bf16[6,128,128]{2,1,0:T(8,128)(2,1)S(1)}, bf16[6,128,128]{2,1,0:T(8,128)(2,1)S(1)}, u32[]{:S(2)}, u32[]{:S(2)}) collective-permute-start(bf16[6,128,128]{2,1,0:T(8,128)(2,1)S(1)} %collective-permute-done.refs_2_), channel_id=1, source_target_pairs={{0,2},{1,3},{2,0},{3,1},{4,6},{5,7},{6,4},{7,5},{8,10},{9,11},{10,... | collective-permute-start | bytes 589832 | tf_op jit(solution)/shard_map/ppermute | solution.py:169
  14.2 1.3 %collective-permute-start.8 = (bf16[3,128,128]{2,1,0:T(8,128)(2,1)S(1)}, bf16[3,128,128]{2,1,0:T(8,128)(2,1)S(1)}, u32[]{:S(2)}, u32[]{:S(2)}) collective-permute-start(bf16[3,128,128]{2,1,0:T(8,128)(2,1)S(1)} %collective-permute-done.6.refs_7_), channel_id=1, source_target_pairs={{0,8},{8,0},{16,24},{24,16},{1,9},{9,1},{17,25},{25,17},{2,10},{10... | collective-permute-start | bytes 294920 | tf_op jit(solution)/shard_map/ppermute | solution.py:169
  14.2 1.5 %collective-permute-start.9 = (bf16[3,128,128]{2,1,0:T(8,128)(2,1)S(1)}, bf16[3,128,128]{2,1,0:T(8,128)(2,1)S(1)}, u32[]{:S(2)}, u32[]{:S(2)}) collective-permute-start(bf16[3,128,128]{2,1,0:T(8,128)(2,1)S(1)} %collective-permute-done.7.refs_8_), channel_id=1, source_target_pairs={{0,8},{8,0},{16,24},{24,16},{1,9},{9,1},{17,25},{25,17},{2,10},{10... | collective-permute-start | bytes 294920 | tf_op jit(solution)/shard_map/ppermute | solution.py:169
  14.9 1.3 %collective-permute-start.5 = (bf16[3,128,128]{2,1,0:T(8,128)(2,1)S(1)}, bf16[3,128,128]{2,1,0:T(8,128)(2,1)S(1)}, u32[]{:S(2)}, u32[]{:S(2)}) collective-permute-start(bf16[3,128,128]{2,1,0:T(8,128)(2,1)S(1)} %collective-permute-done.3.refs_4_), channel_id=1, source_target_pairs={{0,8},{8,0},{16,24},{24,16},{1,9},{9,1},{17,25},{25,17},{2,10},{10... | collective-permute-start | bytes 294920 | tf_op jit(solution)/shard_map/ppermute | solution.py:169
  14.9 1.5 %collective-permute-start.4 = (bf16[3,128,128]{2,1,0:T(8,128)(2,1)S(1)}, bf16[3,128,128]{2,1,0:T(8,128)(2,1)S(1)}, u32[]{:S(2)}, u32[]{:S(2)}) collective-permute-start(bf16[3,128,128]{2,1,0:T(8,128)(2,1)S(1)} %get-tuple-element.20.refs_3_), channel_id=1, source_target_pairs={{0,8},{8,0},{16,24},{24,16},{1,9},{9,1},{17,25},{25,17},{2,10},{10... | collective-permute-start | bytes 294920 | tf_op jit(solution)/shard_map/ppermute | solution.py:169
  16.3 0.7 %copy-start.1 = (s32[48]{0:T(128)S(1)}, s32[48]{0:T(128)}, u32[]{:S(2)}) copy-start(s32[48]{0:T(128)} %shard_map.46.codes_ref) | copy-start | bytes 580
  20.4 4.4 %collective-permute-start.10 = (s16[272,128]{1,0:T(8,128)(2,1)S(1)}, s16[272,128]{1,0:T(8,128)(2,1)S(1)}, u32[]{:S(2)}, u32[]{:S(2)}) collective-permute-start(s16[272,128]{1,0:T(8,128)(2,1)S(1)} %shard_map.49), channel_id=1, source_target_pairs={{0,1},{1,0},{2,3},{3,2},{4,5},{5,4},{6,7},{7,6},{8,9},{9,8},{10,11... | collective-permute-start | bytes 208904 | tf_op jit(solution)/shard_map/ppermute | solution.py:169

commit v15 on v14

--- a/solution.py
+++ b/solution.py
@@ -175,10 +175,10 @@
     return lax.ppermute(block, ("row", "col"), route)
 
 
-def gather(block, beside, ahead):
+def gather(block, beside, place):
     distance = lax.axis_size("col") // 4
     steps = [distance >> n for n in range(distance.bit_length())]
-    later, ahead = lax.optimization_barrier((block, ahead))
+    later, _ = lax.optimization_barrier((block, place))
     came = [across(later if d == 1 else block, "col", 2 * d) for d in steps]
     came[:-1], beside = lax.optimization_barrier((came[:-1], beside))
     blocks = {0: block, **dict(zip(steps, came))}
@@ -186,7 +186,7 @@
         for s in sorted(blocks):
             if s ^ d not in blocks and s & (d - 1) == 0:
                 blocks[s ^ d] = across(blocks[s], "col", 2 * d)
-    return [(s, (blocks[s],)) for s in range(len(blocks))], beside, ahead
+    return [(s, (blocks[s],)) for s in range(len(blocks))], beside
 
 
 def shards(left_tiles, left_index, right_tiles, right_index):
@@ -198,7 +198,7 @@
     codes = find_matches(left_index, right_index)
     given = lax.dynamic_index_in_dim(right, 1 - y, 0, keepdims=False)
     own = lax.dynamic_index_in_dim(right, y, 0, keepdims=False)
-    lefts, codes, (own, given) = gather(left, codes, (own, given))
+    lefts, codes = gather(left, codes, y)
     rights = []
     for t in range(0, lax.axis_size("row"), 2):
         pair = [across(own, "row", t) if t else own, crossed(given, t)]

time: 25.7 us -> 25.8 us (level)
  Pallas kernels: 5.53 us -> 4.87 us
  waiting for transfers between devices: 5.33 us -> 5.92 us
    ppermute x2, starting transfers between devices: 2 us -> 3.02 us  [crossed(): return lax.ppermute(block, ('row', 'col'), route)]
    ppermute x9, starting transfers between devices: 10.2 us -> 9.26 us  [across(): return lax.ppermute(block, axis, route)]
    ppermute x9, waiting for transfers between devices: 5.2 us -> 5.92 us  [across(): return lax.ppermute(block, axis, route)]
    pallas_call x1, Pallas kernels: 2.02 us -> 1.36 us  [first_products(): pl.pallas_call(kernel, out_shape=[jax.ShapeDtypeStruct((RT * tile, tile),...]
  transfers between devices with their start and end apart: 11 -> 11, of which waited for: 8 -> 7; matrix products, arithmetic and copies ran while one was open for 4% -> 4% of each run, Pallas kernels for 18% -> 16%
where the time goes in v15:
time: 25.8 us; the launch traced here: 25.5 us
  starting transfers between devices  12.3 us (48%)
  waiting for transfers between devices  5.92 us (23%)
  Pallas kernels  4.87 us (19%)
  local copies, waits for them, and re-layouts  1.65 us (6%)
  other arithmetic  0.68 us (3%)
    ppermute x9, starting transfers between devices, across(): return lax.ppermute(block, axis, route)  9.26 us
    ppermute x9, waiting for transfers between devices, across(): return lax.ppermute(block, axis, route)  5.92 us
    ppermute x2, starting transfers between devices, crossed(): return lax.ppermute(block, ('row', 'col'), route)  3.02 us
    pallas_call x1, Pallas kernels, find_matches(): pl.pallas_call(kernel, out_shape=jax.ShapeDtypeStruct((inner * 2 * slots,...  1.97 us
    pallas_call x2, Pallas kernels, last_products(): pl.pallas_call(kernel, out_shape=out_shape, in_specs=[SMEM] + [VMEM] * (c...  1.53 us
    pallas_call x1, Pallas kernels, first_products(): pl.pallas_call(kernel, out_shape=[jax.ShapeDtypeStruct((RT * tile, tile),...  1.36 us
    squeeze x1, local copies, waits for them, and re-layouts, shards(): given = lax.dynamic_index_in_dim(right, 1 - y, 0, keepdims=False)  0.99 us
    convert_element_type x1, other arithmetic, add_coded(): (total + coded[:RT * tile].astype(jnp.float32) * scale).astype(jnp.bfloat16)  0.67 us
  transfers between devices with their start and end apart: 11, of which 7 were waited for; matrix products, arithmetic and copies ran while one was open for 4% of the time, Pallas kernels for 16%

profile of v15, /device:TPU:0, one launch (start us, length us, event | category | flops | bytes accessed | tf_op | source)
XLA Modules:
  0.0 25.5 jit_solution(7152733849854736920)
XLA Ops:
  0.0 4.0 %collective-permute-start = (bf16[6,128,128]{2,1,0:T(8,128)(2,1)}, bf16[6,128,128]{2,1,0:T(8,128)(2,1)S(1)}, u32[]{:S(2)}, u32[]{:S(2)}) collective-permute-start(bf16[6,128,128]{2,1,0:T(8,128)(2,1)} %bitcast.13), channel_id=1, source_target_pairs={{0,4},{1,5},{2,6},{3,7},{4,0},{5,1},{6,2},{7,3},{8,12},{9,13},{10,... | collective-permute-start | bytes 589832 | tf_op jit(solution)/shard_map/ppermute | solution.py:169
  4.0 1.6 %collective-permute-start.2 = (bf16[6,128,128]{2,1,0:T(8,128)(2,1)}, bf16[6,128,128]{2,1,0:T(8,128)(2,1)S(1)}, u32[]{:S(2)}, u32[]{:S(2)}) collective-permute-start(bf16[6,128,128]{2,1,0:T(8,128)(2,1)} %bitcast.14), channel_id=1, source_target_pairs={{0,2},{1,3},{2,0},{3,1},{4,6},{5,7},{6,4},{7,5},{8,10},{9,11},{10,... | collective-permute-start | bytes 589832 | tf_op jit(solution)/shard_map/ppermute | solution.py:169
  5.6 0.0 copy-start
  5.6 1.0 %dynamic-slice_bitcast_fusion = (bf16[3,128,128]{2,1,0:T(8,128)(2,1)S(1)}, bf16[3,128,128]{2,1,0:T(8,128)(2,1)S(1)}) fusion(bf16[1,1,2,3,128,128]{5,4,3,2,1,0:T(8,128)(2,1)} %param.6, s32[]{:T(128)S(6)} %select_n.8, s32[]{:T(128)S(6)} %select_n.7), kind=kLoop, calls=%fused_computation.3 | loop fusion | bytes 393224 | tf_op jit(solution)/shard_map/jit(dynamic_index_in_dim)/squeeze | solution.py:199
  6.6 2.5 %collective-permute-start.7 = (bf16[3,128,128]{2,1,0:T(8,128)(2,1)S(1)}, bf16[3,128,128]{2,1,0:T(8,128)(2,1)S(1)}, u32[]{:S(2)}, u32[]{:S(2)}) collective-permute-start(bf16[3,128,128]{2,1,0:T(8,128)(2,1)S(1)} %get-tuple-element.21), channel_id=1, source_target_pairs={{0,17},{1,16},{2,19},{3,18},{4,21},{5,20},{6,23},{7,22},{8,25},{9,... | collective-permute-start | bytes 294920 | tf_op jit(solution)/shard_map/ppermute | solution.py:175
  9.1 0.5 %collective-permute-start.3 = (bf16[3,128,128]{2,1,0:T(8,128)(2,1)S(1)}, bf16[3,128,128]{2,1,0:T(8,128)(2,1)S(1)}, u32[]{:S(2)}, u32[]{:S(2)}) collective-permute-start(bf16[3,128,128]{2,1,0:T(8,128)(2,1)S(1)} %get-tuple-element.21), channel_id=1, source_target_pairs={{0,1},{1,0},{2,3},{3,2},{4,5},{5,4},{6,7},{7,6},{8,9},{9,8},{10,11... | collective-permute-start | bytes 294920 | tf_op jit(solution)/shard_map/ppermute | solution.py:175
  9.6 0.5 %collective-permute-start.6 = (bf16[3,128,128]{2,1,0:T(8,128)(2,1)S(1)}, bf16[3,128,128]{2,1,0:T(8,128)(2,1)S(1)}, u32[]{:S(2)}, u32[]{:S(2)}) collective-permute-start(bf16[3,128,128]{2,1,0:T(8,128)(2,1)S(1)} %get-tuple-element.17.refs_3_), channel_id=1, source_target_pairs={{0,16},{8,24},{16,0},{24,8},{1,17},{9,25},{17,1},{25,9},{2,18},{10... | collective-permute-start | bytes 294920 | tf_op jit(solution)/shard_map/ppermute | solution.py:169
  10.2 2.0 %shard_map.46.codes_ref = s32[48]{0:T(128)} custom-call(s32[6,4,8]{2,1,0:T(4,128)} %bitcast.16, s32[4,3,2,8]{3,2,1,0:T(2,128)} %bitcast.17), custom_call_target="tpu_custom_call" | custom-call | tf_op jit(solution)/shard_map/pallas_call | solution.py:46
  12.1 1.3 %collective-permute-done.refs_2_ = bf16[6,128,128]{2,1,0:T(8,128)(2,1)S(1)} collective-permute-done((bf16[6,128,128]{2,1,0:T(8,128)(2,1)}, bf16[6,128,128]{2,1,0:T(8,128)(2,1)S(1)}, u32[]{:S(2)}, u32[]{:S(2)}) %collective-permute-start) | collective-permute-done | bytes 196640 | tf_op jit(solution)/shard_map/ppermute | solution.py:169
  13.5 0.7 %collective-permute-start.1 = (bf16[6,128,128]{2,1,0:T(8,128)(2,1)S(1)}, bf16[6,128,128]{2,1,0:T(8,128)(2,1)S(1)}, u32[]{:S(2)}, u32[]{:S(2)}) collective-permute-start(bf16[6,128,128]{2,1,0:T(8,128)(2,1)S(1)} %collective-permute-done.refs_2_), channel_id=1, source_target_pairs={{0,2},{1,3},{2,0},{3,1},{4,6},{5,7},{6,4},{7,5},{8,10},{9,11},{10,... | collective-permute-start | bytes 589832 | tf_op jit(solution)/shard_map/ppermute | solution.py:169
  14.2 0.0 collective-permute-done.7.refs_8_
  14.2 0.0 collective-permute-start.9
  14.2 0.0 collective-permute-done.3.refs_4_
  14.2 0.5 %collective-permute-start.5 = (bf16[3,128,128]{2,1,0:T(8,128)(2,1)S(1)}, bf16[3,128,128]{2,1,0:T(8,128)(2,1)S(1)}, u32[]{:S(2)}, u32[]{:S(2)}) collective-permute-start(bf16[3,128,128]{2,1,0:T(8,128)(2,1)S(1)} %collective-permute-done.3.refs_4_), channel_id=1, source_target_pairs={{0,8},{8,0},{16,24},{24,16},{1,9},{9,1},{17,25},{25,17},{2,10},{10... | collective-permute-start | bytes 294920 | tf_op jit(solution)/shard_map/ppermute | solution.py:169
  14.7 0.0 collective-permute-done.6.refs_7_
  14.7 0.1 collective-permute-start.8
  14.8 0.0 collective-permute-done.2.refs_1_
  14.8 0.4 %collective-permute-start.4 = (bf16[3,128,128]{2,1,0:T(8,128)(2,1)S(1)}, bf16[3,128,128]{2,1,0:T(8,128)(2,1)S(1)}, u32[]{:S(2)}, u32[]{:S(2)}) collective-permute-start(bf16[3,128,128]{2,1,0:T(8,128)(2,1)S(1)} %get-tuple-element.17.refs_3_), channel_id=1, source_target_pairs={{0,8},{8,0},{16,24},{24,16},{1,9},{9,1},{17,25},{25,17},{2,10},{10... | collective-permute-start | bytes 294920 | tf_op jit(solution)/shard_map/ppermute | solution.py:169
  15.2 0.3 %collective-permute-done.9.refs_10_ = bf16[3,128,128]{2,1,0:T(8,128)(2,1)S(1)} collective-permute-done((bf16[3,128,128]{2,1,0:T(8,128)(2,1)S(1)}, bf16[3,128,128]{2,1,0:T(8,128)(2,1)S(1)}, u32[]{:S(2)}, u32[]{:S(2)}) %collective-permute-start.9) | collective-permute-done | bytes 98336 | tf_op jit(solution)/shard_map/ppermute | solution.py:169
  15.5 0.2 collective-permute-done.5.refs_6_
  15.7 0.4 %collective-permute-done.8.refs_9_ = bf16[3,128,128]{2,1,0:T(8,128)(2,1)S(1)} collective-permute-done((bf16[3,128,128]{2,1,0:T(8,128)(2,1)S(1)}, bf16[3,128,128]{2,1,0:T(8,128)(2,1)S(1)}, u32[]{:S(2)}, u32[]{:S(2)}) %collective-permute-start.8) | collective-permute-done | bytes 98336 | tf_op jit(solution)/shard_map/ppermute | solution.py:169
  16.0 0.2 collective-permute-done.4.refs_5_
  16.2 0.0 copy-done
  16.2 0.0 copy-start.1
  16.2 0.7 %copy-done.1 = s32[48]{0:T(128)S(1)} copy-done((s32[48]{0:T(128)S(1)}, s32[48]{0:T(128)}, u32[]{:S(2)}) %copy-start.1) | copy-done | bytes 216
  16.8 1.4 %shard_map.47 = (f32[256,128]{1,0:T(8,128)S(1)}, f32[256,128]{1,0:T(8,128)S(1)}, bf16[2,3,128,128]{3,2,1,0:T(8,128)(2,1)S(1)}) custom-call(s32[48]{0:T(128)S(1)} %copy-done.1, bf16[6,128,128]{2,1,0:T(8,128)(2,1)S(1)} %bitcast.15, bf16[6,128,128]{2,1,0:T(8,128)(2,1)S(1)} %collective-permute-done.2.refs_1_, ...), custom_call_target="tpu_custom_call" | custom-call | flops 201326592 | bytes 786432 | tf_op jit(solution)/shard_map/pallas_call | solution.py:98
  18.2 1.3 %collective-permute-done.1.refs_0_ = bf16[6,128,128]{2,1,0:T(8,128)(2,1)S(1)} collective-permute-done((bf16[6,128,128]{2,1,0:T(8,128)(2,1)S(1)}, bf16[6,128,128]{2,1,0:T(8,128)(2,1)S(1)}, u32[]{:S(2)}, u32[]{:S(2)}) %collective-permute-start.1) | collective-permute-done | bytes 196640 | tf_op jit(solution)/shard_map/ppermute | solution.py:169
  19.5 0.9 %shard_map.49 = s16[272,128]{1,0:T(8,128)(2,1)S(1)} custom-call(s32[48]{0:T(128)S(1)} %copy-done.1, bf16[6,128,128]{2,1,0:T(8,128)(2,1)S(1)} %collective-permute-done.1.refs_0_, bf16[2,3,128,128]{3,2,1,0:T(8,128)(2,1)S(1)} %get-tuple-element.18.refs_1_, f32[256,128]{1,0:T(8,128)S(1)} %get-tuple-element.20.refs_2_), custom_call_target="tpu_custom_call" | custom-call | flops 25165824 | bytes 196608 | tf_op jit(solution)/shard_map/pallas_call | solution.py:128
  20.4 1.4 %collective-permute-start.10 = (s16[272,128]{1,0:T(8,128)(2,1)S(1)}, s16[272,128]{1,0:T(8,128)(2,1)S(1)}, u32[]{:S(2)}, u32[]{:S(2)}) collective-permute-start(s16[272,128]{1,0:T(8,128)(2,1)S(1)} %shard_map.49), channel_id=1, source_target_pairs={{0,1},{1,0},{2,3},{3,2},{4,5},{5,4},{6,7},{7,6},{8,9},{9,8},{10,11... | collective-permute-start | bytes 208904 | tf_op jit(solution)/shard_map/ppermute | solution.py:169
  21.8 0.6 %shard_map.48 = f32[256,128]{1,0:T(8,128)S(1)} custom-call(s32[48]{0:T(128)S(1)} %copy-done.1, bf16[6,128,128]{2,1,0:T(8,128)(2,1)S(1)} %collective-permute-done.1.refs_0_, bf16[2,3,128,128]{3,2,1,0:T(8,128)(2,1)S(1)} %get-tuple-element.18.refs_1_, f32[256,128]{1,0:T(8,128)S(1)} %get-tuple-element.19.refs_2_), custom_call_target="tpu_custom_call" | custom-call | flops 25165824 | bytes 196608 | tf_op jit(solution)/shard_map/pallas_call | solution.py:128
  22.4 2.4 %collective-permute-done.10 = s16[272,128]{1,0:T(8,128)(2,1)S(1)} collective-permute-done((s16[272,128]{1,0:T(8,128)(2,1)S(1)}, s16[272,128]{1,0:T(8,128)(2,1)S(1)}, u32[]{:S(2)}, u32[]{:S(2)}) %collective-permute-start.10) | collective-permute-done | bytes 69664 | tf_op jit(solution)/shard_map/ppermute | solution.py:169
  24.8 0.7 %fusion.1 = bf16[256,128]{1,0:T(8,128)(2,1)} fusion(f32[256,128]{1,0:T(8,128)S(1)} %shard_map.48, s16[272,128]{1,0:T(8,128)(2,1)S(1)} %collective-permute-done.10, f32[2,128]{1,0:T(2,128)S(1)} %multiply_exponential_fusion), kind=kLoop, calls=%fused_computation.2 | loop fusion | flops 131072 | bytes 263168 | tf_op jit(solution)/shard_map/convert_element_type | solution.py:164
  (1 shorter events, 0.0 us)
Async XLA Ops:
  0.0 13.5 %collective-permute-start = (bf16[6,128,128]{2,1,0:T(8,128)(2,1)}, bf16[6,128,128]{2,1,0:T(8,128)(2,1)S(1)}, u32[]{:S(2)}, u32[]{:S(2)}) collective-permute-start(bf16[6,128,128]{2,1,0:T(8,128)(2,1)} %bitcast.13), channel_id=1, source_target_pairs={{0,4},{1,5},{2,6},{3,7},{4,0},{5,1},{6,2},{7,3},{8,12},{9,13},{10,... | collective-permute-start | bytes 589832 | tf_op jit(solution)/shard_map/ppermute | solution.py:169
  4.0 10.7 %collective-permute-start.2 = (bf16[6,128,128]{2,1,0:T(8,128)(2,1)}, bf16[6,128,128]{2,1,0:T(8,128)(2,1)S(1)}, u32[]{:S(2)}, u32[]{:S(2)}) collective-permute-start(bf16[6,128,128]{2,1,0:T(8,128)(2,1)} %bitcast.14), channel_id=1, source_target_pairs={{0,2},{1,3},{2,0},{3,1},{4,6},{5,7},{6,4},{7,5},{8,10},{9,11},{10,... | collective-permute-start | bytes 589832 | tf_op jit(solution)/shard_map/ppermute | solution.py:169
  5.6 10.6 %copy-start = (bf16[1,1,6,128,128]{4,3,2,1,0:T(8,128)(2,1)S(1)}, bf16[1,1,6,128,128]{4,3,2,1,0:T(8,128)(2,1)}, u32[]{:S(2)}) copy-start(bf16[1,1,6,128,128]{4,3,2,1,0:T(8,128)(2,1)} %param.4) | copy-start | bytes 589828
  6.6 7.6 %collective-permute-start.7 = (bf16[3,128,128]{2,1,0:T(8,128)(2,1)S(1)}, bf16[3,128,128]{2,1,0:T(8,128)(2,1)S(1)}, u32[]{:S(2)}, u32[]{:S(2)}) collective-permute-start(bf16[3,128,128]{2,1,0:T(8,128)(2,1)S(1)} %get-tuple-element.21), channel_id=1, source_target_pairs={{0,17},{1,16},{2,19},{3,18},{4,21},{5,20},{6,23},{7,22},{8,25},{9,... | collective-permute-start | bytes 294920 | tf_op jit(solution)/shard_map/ppermute | solution.py:175
  9.1 5.1 %collective-permute-start.3 = (bf16[3,128,128]{2,1,0:T(8,128)(2,1)S(1)}, bf16[3,128,128]{2,1,0:T(8,128)(2,1)S(1)}, u32[]{:S(2)}, u32[]{:S(2)}) collective-permute-start(bf16[3,128,128]{2,1,0:T(8,128)(2,1)S(1)} %get-tuple-element.21), channel_id=1, source_target_pairs={{0,1},{1,0},{2,3},{3,2},{4,5},{5,4},{6,7},{7,6},{8,9},{9,8},{10,11... | collective-permute-start | bytes 294920 | tf_op jit(solution)/shard_map/ppermute | solution.py:175
  9.6 5.1 %collective-permute-start.6 = (bf16[3,128,128]{2,1,0:T(8,128)(2,1)S(1)}, bf16[3,128,128]{2,1,0:T(8,128)(2,1)S(1)}, u32[]{:S(2)}, u32[]{:S(2)}) collective-permute-start(bf16[3,128,128]{2,1,0:T(8,128)(2,1)S(1)} %get-tuple-element.17.refs_3_), channel_id=1, source_target_pairs={{0,16},{8,24},{16,0},{24,8},{1,17},{9,25},{17,1},{25,9},{2,18},{10... | collective-permute-start | bytes 294920 | tf_op jit(solution)/shard_map/ppermute | solution.py:169
  13.5 6.0 %collective-permute-start.1 = (bf16[6,128,128]{2,1,0:T(8,128)(2,1)S(1)}, bf16[6,128,128]{2,1,0:T(8,128)(2,1)S(1)}, u32[]{:S(2)}, u32[]{:S(2)}) collective-permute-start(bf16[6,128,128]{2,1,0:T(8,128)(2,1)S(1)} %collective-permute-done.refs_2_), channel_id=1, source_target_pairs={{0,2},{1,3},{2,0},{3,1},{4,6},{5,7},{6,4},{7,5},{8,10},{9,11},{10,... | collective-permute-start | bytes 589832 | tf_op jit(solution)/shard_map/ppermute | solution.py:169
  14.2 1.3 %collective-permute-start.9 = (bf16[3,128,128]{2,1,0:T(8,128)(2,1)S(1)}, bf16[3,128,128]{2,1,0:T(8,128)(2,1)S(1)}, u32[]{:S(2)}, u32[]{:S(2)}) collective-permute-start(bf16[3,128,128]{2,1,0:T(8,128)(2,1)S(1)} %collective-permute-done.7.refs_8_), channel_id=1, source_target_pairs={{0,8},{8,0},{16,24},{24,16},{1,9},{9,1},{17,25},{25,17},{2,10},{10... | collective-permute-start | bytes 294920 | tf_op jit(solution)/shard_map/ppermute | solution.py:169
  14.2 1.5 %collective-permute-start.5 = (bf16[3,128,128]{2,1,0:T(8,128)(2,1)S(1)}, bf16[3,128,128]{2,1,0:T(8,128)(2,1)S(1)}, u32[]{:S(2)}, u32[]{:S(2)}) collective-permute-start(bf16[3,128,128]{2,1,0:T(8,128)(2,1)S(1)} %collective-permute-done.3.refs_4_), channel_id=1, source_target_pairs={{0,8},{8,0},{16,24},{24,16},{1,9},{9,1},{17,25},{25,17},{2,10},{10... | collective-permute-start | bytes 294920 | tf_op jit(solution)/shard_map/ppermute | solution.py:169
  14.7 1.3 %collective-permute-start.8 = (bf16[3,128,128]{2,1,0:T(8,128)(2,1)S(1)}, bf16[3,128,128]{2,1,0:T(8,128)(2,1)S(1)}, u32[]{:S(2)}, u32[]{:S(2)}) collective-permute-start(bf16[3,128,128]{2,1,0:T(8,128)(2,1)S(1)} %collective-permute-done.6.refs_7_), channel_id=1, source_target_pairs={{0,8},{8,0},{16,24},{24,16},{1,9},{9,1},{17,25},{25,17},{2,10},{10... | collective-permute-start | bytes 294920 | tf_op jit(solution)/shard_map/ppermute | solution.py:169
  14.8 1.4 %collective-permute-start.4 = (bf16[3,128,128]{2,1,0:T(8,128)(2,1)S(1)}, bf16[3,128,128]{2,1,0:T(8,128)(2,1)S(1)}, u32[]{:S(2)}, u32[]{:S(2)}) collective-permute-start(bf16[3,128,128]{2,1,0:T(8,128)(2,1)S(1)} %get-tuple-element.17.refs_3_), channel_id=1, source_target_pairs={{0,8},{8,0},{16,24},{24,16},{1,9},{9,1},{17,25},{25,17},{2,10},{10... | collective-permute-start | bytes 294920 | tf_op jit(solution)/shard_map/ppermute | solution.py:169
  16.2 0.7 %copy-start.1 = (s32[48]{0:T(128)S(1)}, s32[48]{0:T(128)}, u32[]{:S(2)}) copy-start(s32[48]{0:T(128)} %shard_map.46.codes_ref) | copy-start | bytes 580
  20.4 4.4 %collective-permute-start.10 = (s16[272,128]{1,0:T(8,128)(2,1)S(1)}, s16[272,128]{1,0:T(8,128)(2,1)S(1)}, u32[]{:S(2)}, u32[]{:S(2)}) collective-permute-start(s16[272,128]{1,0:T(8,128)(2,1)S(1)} %shard_map.49), channel_id=1, source_target_pairs={{0,1},{1,0},{2,3},{3,2},{4,5},{5,4},{6,7},{7,6},{8,9},{9,8},{10,11... | collective-permute-start | bytes 208904 | tf_op jit(solution)/shard_map/ppermute | solution.py:169

commit v16 on v15

--- a/solution.py
+++ b/solution.py
@@ -83,7 +83,21 @@
         for t in range(inner):
             for side in range(2):
                 held[row ^ t, side] = right_refs[2 * t + side][...]
-        last_ref[...] = held[z ^ (inner - 1)]
+        at = z ^ (inner - 1)
+        last_ref[...] = jnp.zeros_like(last_ref)
+        for side in range(2):
+
+            @pl.loop(0, slots)
+            def _(slot):
+                code = codes_ref[((inner - 1) * 2 + side) * slots + slot]
+
+                @pl.when(code > 0)
+                def _():
+                    rows = pl.ds(pl.multiple_of(slot * tile, tile), tile)
+                    i = lax.div(code - 1, right_slots)
+                    columns = pl.ds(pl.multiple_of(i * tile, tile), tile)
+                    last_ref[side, rows, columns] = held[at, side, lax.rem(code - 1, right_slots)]
+
         for side in range(2):
             totals[side][...] = jnp.zeros_like(totals[side])
             start, before = 0, None
@@ -98,7 +112,7 @@
     return pl.pallas_call(
         kernel,
         out_shape=[jax.ShapeDtypeStruct((RT * tile, tile), jnp.float32)] * 2
-        + [jax.ShapeDtypeStruct((2, right_slots, tile, tile), jnp.bfloat16)],
+        + [jax.ShapeDtypeStruct((2, slots * tile, RT * tile), jnp.bfloat16)],
         in_specs=[SMEM] + [VMEM] * (count + 2 * inner),
         out_specs=[VMEM] * 3,
         scratch_shapes=[pltpu.VMEM((inner, 2, right_slots, tile, tile), jnp.bfloat16)],
@@ -109,44 +123,45 @@
     )(codes, *[part for _, part in parts], *rights)
 
 
-def last_products(codes, s, parts, right, total, side, slots, finish, out_shape):
-    count = len(parts)
-    right_slots = right.shape[1]
-
-    def kernel(codes_ref, *refs):
-        right_ref, total_ref, out_ref, sum_ref = refs[count:]
-        sum_ref[...] = total_ref[...]
-        start = 0
-        for left_ref in refs[:count]:
-            add_part(
-                codes_ref, s, side, start, slots, left_ref,
-                lambda found: right_ref[side, found], right_slots, sum_ref,
+def last_products(parts, right, total, side, finish, out_shape):
+    (left,) = parts
+    slots, tile, _ = left.shape
+
+    def kernel(left_ref, right_ref, total_ref, out_ref):
+        added = jnp.zeros((tile, RT * tile), jnp.float32)
+        for slot in range(0, slots, 2):
+            both = min(2, slots - slot)
+            tiles = [left_ref[slot + n] for n in range(both)]
+            added += jnp.dot(
+                jnp.concatenate(tiles, axis=1),
+                right_ref[side, slot * tile : (slot + both) * tile, :],
+                preferred_element_type=jnp.float32,
             )
-            start += left_ref.shape[0]
-        finish(sum_ref, out_ref)
+        sums = [
+            total_ref[i * tile : (i + 1) * tile, :] + added[:, i * tile : (i + 1) * tile] for i in range(RT)
+        ]
+        finish(sums, out_ref)
 
     return pl.pallas_call(
         kernel,
         out_shape=out_shape,
-        in_specs=[SMEM] + [VMEM] * (count + 2),
+        in_specs=[VMEM] * 3,
         out_specs=VMEM,
-        scratch_shapes=[pltpu.VMEM(total.shape, total.dtype)],
         compiler_params=pltpu.CompilerParams(vmem_limit_bytes=16 * 1024 * 1024),
         cost_estimate=pl.CostEstimate(
-            flops=2 * slots * 128**3, bytes_accessed=2 * slots * 128**2, transcendentals=0
+            flops=2 * slots * tile**3, bytes_accessed=2 * slots * tile**2, transcendentals=0
         ),
-    )(codes, *parts, right, total)
-
-
-def write_sum(sum_ref, out_ref):
-    out_ref[...] = sum_ref[...]
-
-
-def write_coded(sum_ref, out_ref):
-    tile = sum_ref.shape[1]
+    )(left, right, total)
+
+
+def write_sum(sums, out_ref):
+    out_ref[...] = jnp.concatenate(sums)
+
+
+def write_coded(sums, out_ref):
+    tile = out_ref.shape[1]
     exponents = jnp.zeros((PAD, tile), jnp.float32)
-    for i in range(RT):
-        values = sum_ref[i * tile : (i + 1) * tile, :]
+    for i, values in enumerate(sums):
         largest = jnp.max(jnp.abs(values), axis=0, keepdims=True)
         exponent = jnp.clip(jnp.floor(jnp.log2(largest)) + 1.0, -LEAST, LEAST)
         coded = jnp.round(values * jnp.exp2(BITS - exponent))
@@ -208,14 +223,13 @@
         rights += pair + [across(half, "row", 1) for half in pair]
 
     mine, other, right_last = first_products(codes, lefts[:-1], rights, slots)
-    far, final = lefts[-1]
-    last = (codes, far, final, right_last)
+    last = (lefts[-1][1], right_last)
     rows, tile = mine.shape
     coded = last_products(
-        *last, other, 1, slots, write_coded, jax.ShapeDtypeStruct((rows + PAD, tile), jnp.int16)
+        *last, other, 1, write_coded, jax.ShapeDtypeStruct((rows + PAD, tile), jnp.int16)
     )
     coming = across(coded, "col", 1)
-    mine = last_products(*last, mine, 0, slots, write_sum, jax.ShapeDtypeStruct((rows, tile), jnp.float32))
+    mine = last_products(*last, mine, 0, write_sum, jax.ShapeDtypeStruct((rows, tile), jnp.float32))
     return add_coded(mine, coming)
 
 

time: 25.8 us -> 25.2 us (0.977)
  Pallas kernels: 4.87 us -> 4.17 us
    pallas_call x2, Pallas kernels: 1.53 us -> 0.47 us  [last_products(): pl.pallas_call(kernel, out_shape=out_shape, in_specs=[VMEM] * 3, out_spec...]
    pallas_call x1, Pallas kernels: 1.36 us -> 1.73 us  [first_products(): pl.pallas_call(kernel, out_shape=[jax.ShapeDtypeStruct((RT * tile, tile),...]
where the time goes in v16:
time: 25.2 us; the launch traced here: 24.9 us
  starting transfers between devices  12.3 us (49%)
  waiting for transfers between devices  6.07 us (24%)
  Pallas kernels  4.17 us (17%)
  local copies, waits for them, and re-layouts  1.65 us (7%)
  other arithmetic  0.68 us (3%)
    ppermute x9, starting transfers between devices, across(): return lax.ppermute(block, axis, route)  9.25 us
    ppermute x9, waiting for transfers between devices, across(): return lax.ppermute(block, axis, route)  6.06 us
    ppermute x2, starting transfers between devices, crossed(): return lax.ppermute(block, ('row', 'col'), route)  3.02 us
    pallas_call x1, Pallas kernels, find_matches(): pl.pallas_call(kernel, out_shape=jax.ShapeDtypeStruct((inner * 2 * slots,...  1.97 us
    pallas_call x1, Pallas kernels, first_products(): pl.pallas_call(kernel, out_shape=[jax.ShapeDtypeStruct((RT * tile, tile),...  1.73 us
    squeeze x1, local copies, waits for them, and re-layouts, shards(): given = lax.dynamic_index_in_dim(right, 1 - y, 0, keepdims=False)  0.99 us
    convert_element_type x1, other arithmetic, add_coded(): (total + coded[:RT * tile].astype(jnp.float32) * scale).astype(jnp.bfloat16)  0.67 us
    unnamed x4, local copies, waits for them, and re-layouts  0.66 us
  transfers between devices with their start and end apart: 11, of which 7 were waited for; matrix products, arithmetic and copies ran while one was open for 4% of the time, Pallas kernels for 16%

profile of v16, /device:TPU:0, one launch (start us, length us, event | category | flops | bytes accessed | tf_op | source)
XLA Modules:
  0.0 24.9 jit_solution(12542343318565185962)
XLA Ops:
  0.0 4.0 %collective-permute-start = (bf16[6,128,128]{2,1,0:T(8,128)(2,1)}, bf16[6,128,128]{2,1,0:T(8,128)(2,1)S(1)}, u32[]{:S(2)}, u32[]{:S(2)}) collective-permute-start(bf16[6,128,128]{2,1,0:T(8,128)(2,1)} %bitcast.13), channel_id=1, source_target_pairs={{0,4},{1,5},{2,6},{3,7},{4,0},{5,1},{6,2},{7,3},{8,12},{9,13},{10,... | collective-permute-start | bytes 589832 | tf_op jit(solution)/shard_map/ppermute | solution.py:184
  4.0 1.6 %collective-permute-start.2 = (bf16[6,128,128]{2,1,0:T(8,128)(2,1)}, bf16[6,128,128]{2,1,0:T(8,128)(2,1)S(1)}, u32[]{:S(2)}, u32[]{:S(2)}) collective-permute-start(bf16[6,128,128]{2,1,0:T(8,128)(2,1)} %bitcast.14), channel_id=1, source_target_pairs={{0,2},{1,3},{2,0},{3,1},{4,6},{5,7},{6,4},{7,5},{8,10},{9,11},{10,... | collective-permute-start | bytes 589832 | tf_op jit(solution)/shard_map/ppermute | solution.py:184
  5.6 0.0 copy-start
  5.6 1.0 %dynamic-slice_bitcast_fusion = (bf16[3,128,128]{2,1,0:T(8,128)(2,1)S(1)}, bf16[3,128,128]{2,1,0:T(8,128)(2,1)S(1)}) fusion(bf16[1,1,2,3,128,128]{5,4,3,2,1,0:T(8,128)(2,1)} %param.6, s32[]{:T(128)S(6)} %select_n.8, s32[]{:T(128)S(6)} %select_n.7), kind=kLoop, calls=%fused_computation.3 | loop fusion | bytes 393224 | tf_op jit(solution)/shard_map/jit(dynamic_index_in_dim)/squeeze | solution.py:214
  6.6 2.5 %collective-permute-start.7 = (bf16[3,128,128]{2,1,0:T(8,128)(2,1)S(1)}, bf16[3,128,128]{2,1,0:T(8,128)(2,1)S(1)}, u32[]{:S(2)}, u32[]{:S(2)}) collective-permute-start(bf16[3,128,128]{2,1,0:T(8,128)(2,1)S(1)} %get-tuple-element.21), channel_id=1, source_target_pairs={{0,17},{1,16},{2,19},{3,18},{4,21},{5,20},{6,23},{7,22},{8,25},{9,... | collective-permute-start | bytes 294920 | tf_op jit(solution)/shard_map/ppermute | solution.py:190
  9.1 0.5 %collective-permute-start.3 = (bf16[3,128,128]{2,1,0:T(8,128)(2,1)S(1)}, bf16[3,128,128]{2,1,0:T(8,128)(2,1)S(1)}, u32[]{:S(2)}, u32[]{:S(2)}) collective-permute-start(bf16[3,128,128]{2,1,0:T(8,128)(2,1)S(1)} %get-tuple-element.21), channel_id=1, source_target_pairs={{0,1},{1,0},{2,3},{3,2},{4,5},{5,4},{6,7},{7,6},{8,9},{9,8},{10,11... | collective-permute-start | bytes 294920 | tf_op jit(solution)/shard_map/ppermute | solution.py:190
  9.6 0.5 %collective-permute-start.6 = (bf16[3,128,128]{2,1,0:T(8,128)(2,1)S(1)}, bf16[3,128,128]{2,1,0:T(8,128)(2,1)S(1)}, u32[]{:S(2)}, u32[]{:S(2)}) collective-permute-start(bf16[3,128,128]{2,1,0:T(8,128)(2,1)S(1)} %get-tuple-element.17.refs_3_), channel_id=1, source_target_pairs={{0,16},{8,24},{16,0},{24,8},{1,17},{9,25},{17,1},{25,9},{2,18},{10... | collective-permute-start | bytes 294920 | tf_op jit(solution)/shard_map/ppermute | solution.py:184
  10.2 2.0 %shard_map.46.codes_ref = s32[48]{0:T(128)} custom-call(s32[6,4,8]{2,1,0:T(4,128)} %bitcast.16, s32[4,3,2,8]{3,2,1,0:T(2,128)} %bitcast.17), custom_call_target="tpu_custom_call" | custom-call | tf_op jit(solution)/shard_map/pallas_call | solution.py:46
  12.1 1.3 %collective-permute-done.refs_2_ = bf16[6,128,128]{2,1,0:T(8,128)(2,1)S(1)} collective-permute-done((bf16[6,128,128]{2,1,0:T(8,128)(2,1)}, bf16[6,128,128]{2,1,0:T(8,128)(2,1)S(1)}, u32[]{:S(2)}, u32[]{:S(2)}) %collective-permute-start) | collective-permute-done | bytes 196640 | tf_op jit(solution)/shard_map/ppermute | solution.py:184
  13.5 0.7 %collective-permute-start.1 = (bf16[6,128,128]{2,1,0:T(8,128)(2,1)S(1)}, bf16[6,128,128]{2,1,0:T(8,128)(2,1)S(1)}, u32[]{:S(2)}, u32[]{:S(2)}) collective-permute-start(bf16[6,128,128]{2,1,0:T(8,128)(2,1)S(1)} %collective-permute-done.refs_2_), channel_id=1, source_target_pairs={{0,2},{1,3},{2,0},{3,1},{4,6},{5,7},{6,4},{7,5},{8,10},{9,11},{10,... | collective-permute-start | bytes 589832 | tf_op jit(solution)/shard_map/ppermute | solution.py:184
  14.2 0.0 collective-permute-done.7.refs_8_
  14.2 0.0 collective-permute-start.9
  14.2 0.0 collective-permute-done.3.refs_4_
  14.2 0.5 %collective-permute-start.5 = (bf16[3,128,128]{2,1,0:T(8,128)(2,1)S(1)}, bf16[3,128,128]{2,1,0:T(8,128)(2,1)S(1)}, u32[]{:S(2)}, u32[]{:S(2)}) collective-permute-start(bf16[3,128,128]{2,1,0:T(8,128)(2,1)S(1)} %collective-permute-done.3.refs_4_), channel_id=1, source_target_pairs={{0,8},{8,0},{16,24},{24,16},{1,9},{9,1},{17,25},{25,17},{2,10},{10... | collective-permute-start | bytes 294920 | tf_op jit(solution)/shard_map/ppermute | solution.py:184
  14.7 0.0 collective-permute-done.6.refs_7_
  14.7 0.1 collective-permute-start.8
  14.8 0.0 collective-permute-done.2.refs_1_
  14.8 0.4 %collective-permute-start.4 = (bf16[3,128,128]{2,1,0:T(8,128)(2,1)S(1)}, bf16[3,128,128]{2,1,0:T(8,128)(2,1)S(1)}, u32[]{:S(2)}, u32[]{:S(2)}) collective-permute-start(bf16[3,128,128]{2,1,0:T(8,128)(2,1)S(1)} %get-tuple-element.17.refs_3_), channel_id=1, source_target_pairs={{0,8},{8,0},{16,24},{24,16},{1,9},{9,1},{17,25},{25,17},{2,10},{10... | collective-permute-start | bytes 294920 | tf_op jit(solution)/shard_map/ppermute | solution.py:184
  15.2 0.3 %collective-permute-done.9.refs_10_ = bf16[3,128,128]{2,1,0:T(8,128)(2,1)S(1)} collective-permute-done((bf16[3,128,128]{2,1,0:T(8,128)(2,1)S(1)}, bf16[3,128,128]{2,1,0:T(8,128)(2,1)S(1)}, u32[]{:S(2)}, u32[]{:S(2)}) %collective-permute-start.9) | collective-permute-done | bytes 98336 | tf_op jit(solution)/shard_map/ppermute | solution.py:184
  15.5 0.2 collective-permute-done.5.refs_6_
  15.7 0.4 %collective-permute-done.8.refs_9_ = bf16[3,128,128]{2,1,0:T(8,128)(2,1)S(1)} collective-permute-done((bf16[3,128,128]{2,1,0:T(8,128)(2,1)S(1)}, bf16[3,128,128]{2,1,0:T(8,128)(2,1)S(1)}, u32[]{:S(2)}, u32[]{:S(2)}) %collective-permute-start.8) | collective-permute-done | bytes 98336 | tf_op jit(solution)/shard_map/ppermute | solution.py:184
  16.0 0.2 collective-permute-done.4.refs_5_
  16.2 0.0 copy-done
  16.2 0.0 copy-start.1
  16.2 0.7 %copy-done.1 = s32[48]{0:T(128)S(1)} copy-done((s32[48]{0:T(128)S(1)}, s32[48]{0:T(128)}, u32[]{:S(2)}) %copy-start.1) | copy-done | bytes 216
  16.8 1.7 %shard_map.47 = (f32[256,128]{1,0:T(8,128)S(1)}, f32[256,128]{1,0:T(8,128)S(1)}, bf16[2,768,256]{2,1,0:T(8,128)(2,1)S(1)}) custom-call(s32[48]{0:T(128)S(1)} %copy-done.1, bf16[6,128,128]{2,1,0:T(8,128)(2,1)S(1)} %bitcast.15, bf16[6,128,128]{2,1,0:T(8,128)(2,1)S(1)} %collective-permute-done.2.refs_1_, bf16[6,128,128]{2,1,0:T(8,128)(2,1)S(1)} %collective-permute-done.refs_2_, ...), custom_call_target="tpu_custom_call" | custom-call | flops 201326592 | bytes 786432 | tf_op jit(solution)/shard_map/pallas_call | solution.py:112
  18.6 0.9 %collective-permute-done.1.left_ref = bf16[6,128,128]{2,1,0:T(8,128)(2,1)S(1)} collective-permute-done((bf16[6,128,128]{2,1,0:T(8,128)(2,1)S(1)}, bf16[6,128,128]{2,1,0:T(8,128)(2,1)S(1)}, u32[]{:S(2)}, u32[]{:S(2)}) %collective-permute-start.1) | collective-permute-done | bytes 196640 | tf_op jit(solution)/shard_map/ppermute | solution.py:184
  19.5 0.3 %shard_map.49 = s16[272,128]{1,0:T(8,128)(2,1)S(1)} custom-call(bf16[6,128,128]{2,1,0:T(8,128)(2,1)S(1)} %collective-permute-done.1.left_ref, bf16[2,768,256]{2,1,0:T(8,128)(2,1)S(1)} %get-tuple-element.18.right_ref, f32[256,128]{1,0:T(8,128)S(1)} %get-tuple-element.20.total_ref), custom_call_target="tpu_custom_call" | custom-call | flops 25165824 | bytes 196608 | tf_op jit(solution)/shard_map/pallas_call | solution.py:145
  19.8 1.4 %collective-permute-start.10 = (s16[272,128]{1,0:T(8,128)(2,1)S(1)}, s16[272,128]{1,0:T(8,128)(2,1)S(1)}, u32[]{:S(2)}, u32[]{:S(2)}) collective-permute-start(s16[272,128]{1,0:T(8,128)(2,1)S(1)} %shard_map.49), channel_id=1, source_target_pairs={{0,1},{1,0},{2,3},{3,2},{4,5},{5,4},{6,7},{7,6},{8,9},{9,8},{10,11... | collective-permute-start | bytes 208904 | tf_op jit(solution)/shard_map/ppermute | solution.py:184
  21.1 0.2 shard_map.48
  21.3 2.9 %collective-permute-done.10 = s16[272,128]{1,0:T(8,128)(2,1)S(1)} collective-permute-done((s16[272,128]{1,0:T(8,128)(2,1)S(1)}, s16[272,128]{1,0:T(8,128)(2,1)S(1)}, u32[]{:S(2)}, u32[]{:S(2)}) %collective-permute-start.10) | collective-permute-done | bytes 69664 | tf_op jit(solution)/shard_map/ppermute | solution.py:184
  24.2 0.7 %fusion.1 = bf16[256,128]{1,0:T(8,128)(2,1)} fusion(f32[256,128]{1,0:T(8,128)S(1)} %shard_map.48, s16[272,128]{1,0:T(8,128)(2,1)S(1)} %collective-permute-done.10, f32[2,128]{1,0:T(2,128)S(1)} %multiply_exponential_fusion), kind=kLoop, calls=%fused_computation.2 | loop fusion | flops 131072 | bytes 263168 | tf_op jit(solution)/shard_map/convert_element_type | solution.py:179
  (1 shorter events, 0.0 us)
Async XLA Ops:
  0.0 13.5 %collective-permute-start = (bf16[6,128,128]{2,1,0:T(8,128)(2,1)}, bf16[6,128,128]{2,1,0:T(8,128)(2,1)S(1)}, u32[]{:S(2)}, u32[]{:S(2)}) collective-permute-start(bf16[6,128,128]{2,1,0:T(8,128)(2,1)} %bitcast.13), channel_id=1, source_target_pairs={{0,4},{1,5},{2,6},{3,7},{4,0},{5,1},{6,2},{7,3},{8,12},{9,13},{10,... | collective-permute-start | bytes 589832 | tf_op jit(solution)/shard_map/ppermute | solution.py:184
  4.0 10.7 %collective-permute-start.2 = (bf16[6,128,128]{2,1,0:T(8,128)(2,1)}, bf16[6,128,128]{2,1,0:T(8,128)(2,1)S(1)}, u32[]{:S(2)}, u32[]{:S(2)}) collective-permute-start(bf16[6,128,128]{2,1,0:T(8,128)(2,1)} %bitcast.14), channel_id=1, source_target_pairs={{0,2},{1,3},{2,0},{3,1},{4,6},{5,7},{6,4},{7,5},{8,10},{9,11},{10,... | collective-permute-start | bytes 589832 | tf_op jit(solution)/shard_map/ppermute | solution.py:184
  5.6 10.6 %copy-start = (bf16[1,1,6,128,128]{4,3,2,1,0:T(8,128)(2,1)S(1)}, bf16[1,1,6,128,128]{4,3,2,1,0:T(8,128)(2,1)}, u32[]{:S(2)}) copy-start(bf16[1,1,6,128,128]{4,3,2,1,0:T(8,128)(2,1)} %param.4) | copy-start | bytes 589828
  6.6 7.6 %collective-permute-start.7 = (bf16[3,128,128]{2,1,0:T(8,128)(2,1)S(1)}, bf16[3,128,128]{2,1,0:T(8,128)(2,1)S(1)}, u32[]{:S(2)}, u32[]{:S(2)}) collective-permute-start(bf16[3,128,128]{2,1,0:T(8,128)(2,1)S(1)} %get-tuple-element.21), channel_id=1, source_target_pairs={{0,17},{1,16},{2,19},{3,18},{4,21},{5,20},{6,23},{7,22},{8,25},{9,... | collective-permute-start | bytes 294920 | tf_op jit(solution)/shard_map/ppermute | solution.py:190
  9.1 5.1 %collective-permute-start.3 = (bf16[3,128,128]{2,1,0:T(8,128)(2,1)S(1)}, bf16[3,128,128]{2,1,0:T(8,128)(2,1)S(1)}, u32[]{:S(2)}, u32[]{:S(2)}) collective-permute-start(bf16[3,128,128]{2,1,0:T(8,128)(2,1)S(1)} %get-tuple-element.21), channel_id=1, source_target_pairs={{0,1},{1,0},{2,3},{3,2},{4,5},{5,4},{6,7},{7,6},{8,9},{9,8},{10,11... | collective-permute-start | bytes 294920 | tf_op jit(solution)/shard_map/ppermute | solution.py:190
  9.6 5.1 %collective-permute-start.6 = (bf16[3,128,128]{2,1,0:T(8,128)(2,1)S(1)}, bf16[3,128,128]{2,1,0:T(8,128)(2,1)S(1)}, u32[]{:S(2)}, u32[]{:S(2)}) collective-permute-start(bf16[3,128,128]{2,1,0:T(8,128)(2,1)S(1)} %get-tuple-element.17.refs_3_), channel_id=1, source_target_pairs={{0,16},{8,24},{16,0},{24,8},{1,17},{9,25},{17,1},{25,9},{2,18},{10... | collective-permute-start | bytes 294920 | tf_op jit(solution)/shard_map/ppermute | solution.py:184
  13.5 6.0 %collective-permute-start.1 = (bf16[6,128,128]{2,1,0:T(8,128)(2,1)S(1)}, bf16[6,128,128]{2,1,0:T(8,128)(2,1)S(1)}, u32[]{:S(2)}, u32[]{:S(2)}) collective-permute-start(bf16[6,128,128]{2,1,0:T(8,128)(2,1)S(1)} %collective-permute-done.refs_2_), channel_id=1, source_target_pairs={{0,2},{1,3},{2,0},{3,1},{4,6},{5,7},{6,4},{7,5},{8,10},{9,11},{10,... | collective-permute-start | bytes 589832 | tf_op jit(solution)/shard_map/ppermute | solution.py:184
  14.2 1.3 %collective-permute-start.9 = (bf16[3,128,128]{2,1,0:T(8,128)(2,1)S(1)}, bf16[3,128,128]{2,1,0:T(8,128)(2,1)S(1)}, u32[]{:S(2)}, u32[]{:S(2)}) collective-permute-start(bf16[3,128,128]{2,1,0:T(8,128)(2,1)S(1)} %collective-permute-done.7.refs_8_), channel_id=1, source_target_pairs={{0,8},{8,0},{16,24},{24,16},{1,9},{9,1},{17,25},{25,17},{2,10},{10... | collective-permute-start | bytes 294920 | tf_op jit(solution)/shard_map/ppermute | solution.py:184
  14.2 1.5 %collective-permute-start.5 = (bf16[3,128,128]{2,1,0:T(8,128)(2,1)S(1)}, bf16[3,128,128]{2,1,0:T(8,128)(2,1)S(1)}, u32[]{:S(2)}, u32[]{:S(2)}) collective-permute-start(bf16[3,128,128]{2,1,0:T(8,128)(2,1)S(1)} %collective-permute-done.3.refs_4_), channel_id=1, source_target_pairs={{0,8},{8,0},{16,24},{24,16},{1,9},{9,1},{17,25},{25,17},{2,10},{10... | collective-permute-start | bytes 294920 | tf_op jit(solution)/shard_map/ppermute | solution.py:184
  14.7 1.3 %collective-permute-start.8 = (bf16[3,128,128]{2,1,0:T(8,128)(2,1)S(1)}, bf16[3,128,128]{2,1,0:T(8,128)(2,1)S(1)}, u32[]{:S(2)}, u32[]{:S(2)}) collective-permute-start(bf16[3,128,128]{2,1,0:T(8,128)(2,1)S(1)} %collective-permute-done.6.refs_7_), channel_id=1, source_target_pairs={{0,8},{8,0},{16,24},{24,16},{1,9},{9,1},{17,25},{25,17},{2,10},{10... | collective-permute-start | bytes 294920 | tf_op jit(solution)/shard_map/ppermute | solution.py:184
  14.8 1.4 %collective-permute-start.4 = (bf16[3,128,128]{2,1,0:T(8,128)(2,1)S(1)}, bf16[3,128,128]{2,1,0:T(8,128)(2,1)S(1)}, u32[]{:S(2)}, u32[]{:S(2)}) collective-permute-start(bf16[3,128,128]{2,1,0:T(8,128)(2,1)S(1)} %get-tuple-element.17.refs_3_), channel_id=1, source_target_pairs={{0,8},{8,0},{16,24},{24,16},{1,9},{9,1},{17,25},{25,17},{2,10},{10... | collective-permute-start | bytes 294920 | tf_op jit(solution)/shard_map/ppermute | solution.py:184
  16.2 0.7 %copy-start.1 = (s32[48]{0:T(128)S(1)}, s32[48]{0:T(128)}, u32[]{:S(2)}) copy-start(s32[48]{0:T(128)} %shard_map.46.codes_ref) | copy-start | bytes 580
  19.8 4.4 %collective-permute-start.10 = (s16[272,128]{1,0:T(8,128)(2,1)S(1)}, s16[272,128]{1,0:T(8,128)(2,1)S(1)}, u32[]{:S(2)}, u32[]{:S(2)}) collective-permute-start(s16[272,128]{1,0:T(8,128)(2,1)S(1)} %shard_map.49), channel_id=1, source_target_pairs={{0,1},{1,0},{2,3},{3,2},{4,5},{5,4},{6,7},{7,6},{8,9},{9,8},{10,11... | collective-permute-start | bytes 208904 | tf_op jit(solution)/shard_map/ppermute | solution.py:184

commit v17 on v16

--- a/solution.py
+++ b/solution.py
@@ -48,6 +48,7 @@
         out_shape=jax.ShapeDtypeStruct((inner * 2 * slots,), jnp.int32),
         in_specs=[SMEM] * 2,
         out_specs=SMEM,
+        compiler_params=pltpu.CompilerParams(vmem_limit_bytes=2 * 1024 * 1024),
     )(left_index, right_index)
 
 
@@ -173,10 +174,22 @@
 
 
 def add_coded(total, coded):
-    tile = total.shape[1]
-    exponents = coded[RT * tile : RT * tile + RT].astype(jnp.float32)
-    scale = jnp.repeat(jnp.exp2(exponents - BITS), tile, axis=0)
-    return (total + coded[: RT * tile].astype(jnp.float32) * scale).astype(jnp.bfloat16)
+    def kernel(total_ref, coded_ref, out_ref):
+        tile = total_ref.shape[1]
+        exponents = coded_ref[RT * tile :, :].astype(jnp.int32).astype(jnp.float32)
+        for i in range(RT):
+            rows = slice(i * tile, (i + 1) * tile)
+            scale = jnp.exp2(exponents[i : i + 1, :] - BITS)
+            values = coded_ref[rows, :].astype(jnp.int32).astype(jnp.float32)
+            out_ref[rows, :] = (total_ref[rows, :] + values * scale).astype(out_ref.dtype)
+
+    return pl.pallas_call(
+        kernel,
+        out_shape=jax.ShapeDtypeStruct(total.shape, jnp.bfloat16),
+        in_specs=[VMEM] * 2,
+        out_specs=VMEM,
+        compiler_params=pltpu.CompilerParams(vmem_limit_bytes=8 * 1024 * 1024),
+    )(total, coded)
 
 
 def across(block, axis, mask):

time: 25.2 us -> 24.9 us (0.988)
  other arithmetic: 0.68 us -> 0 us
  local copies, waits for them, and re-layouts: 1.65 us -> 1 us
  Pallas kernels: 4.17 us -> 4.81 us
  waiting for transfers between devices: 6.07 us -> 6.67 us
    convert_element_type x1 -> x0, other arithmetic: 0.67 us -> none  [add_coded(): (total + coded[:RT * tile].astype(jnp.float32) * scale).astype(jnp.bfloat16)]
    pallas_call x0 -> x1, Pallas kernels: none -> 0.65 us  [add_coded(): pl.pallas_call(kernel, out_shape=jax.ShapeDtypeStruct(total.shape, jnp.bf...]
    unnamed x4 -> x6, local copies, waits for them, and re-layouts: 0.66 us -> 0.01 us
    ppermute x9, waiting for transfers between devices: 6.06 us -> 6.66 us  [across(): return lax.ppermute(block, axis, route)]
where the time goes in v17:
time: 24.9 us; the launch traced here: 24.8 us
  starting transfers between devices  12.3 us (49%)
  waiting for transfers between devices  6.67 us (27%)
  Pallas kernels  4.81 us (19%)
  local copies, waits for them, and re-layouts  1 us (4%)
    ppermute x9, starting transfers between devices, across(): return lax.ppermute(block, axis, route)  9.25 us
    ppermute x9, waiting for transfers between devices, across(): return lax.ppermute(block, axis, route)  6.66 us
    ppermute x2, starting transfers between devices, crossed(): return lax.ppermute(block, ('row', 'col'), route)  3.02 us
    pallas_call x1, Pallas kernels, find_matches(): pl.pallas_call(kernel, out_shape=jax.ShapeDtypeStruct((inner * 2 * slots,...  1.92 us
    pallas_call x1, Pallas kernels, first_products(): pl.pallas_call(kernel, out_shape=[jax.ShapeDtypeStruct((RT * tile, tile),...  1.77 us
    squeeze x1, local copies, waits for them, and re-layouts, shards(): given = lax.dynamic_index_in_dim(right, 1 - y, 0, keepdims=False)  0.99 us
    pallas_call x1, Pallas kernels, add_coded(): pl.pallas_call(kernel, out_shape=jax.ShapeDtypeStruct(total.shape, jnp.bf...  0.65 us
  transfers between devices with their start and end apart: 11, of which 7 were waited for; matrix products, arithmetic and copies ran while one was open for 4% of the time, Pallas kernels for 16%

profile of v17, /device:TPU:0, one launch (start us, length us, event | category | flops | bytes accessed | tf_op | source)
XLA Modules:
  0.0 24.8 jit_solution(11829291078003047773)
XLA Ops:
  0.0 4.0 %collective-permute-start = (bf16[6,128,128]{2,1,0:T(8,128)(2,1)}, bf16[6,128,128]{2,1,0:T(8,128)(2,1)S(1)}, u32[]{:S(2)}, u32[]{:S(2)}) collective-permute-start(bf16[6,128,128]{2,1,0:T(8,128)(2,1)} %bitcast.7), channel_id=1, source_target_pairs={{0,4},{1,5},{2,6},{3,7},{4,0},{5,1},{6,2},{7,3},{8,12},{9,13},{10,... | collective-permute-start | bytes 589832 | tf_op jit(solution)/shard_map/ppermute | solution.py:197
  4.0 1.6 %collective-permute-start.2 = (bf16[6,128,128]{2,1,0:T(8,128)(2,1)}, bf16[6,128,128]{2,1,0:T(8,128)(2,1)S(1)}, u32[]{:S(2)}, u32[]{:S(2)}) collective-permute-start(bf16[6,128,128]{2,1,0:T(8,128)(2,1)} %bitcast.8), channel_id=1, source_target_pairs={{0,2},{1,3},{2,0},{3,1},{4,6},{5,7},{6,4},{7,5},{8,10},{9,11},{10,... | collective-permute-start | bytes 589832 | tf_op jit(solution)/shard_map/ppermute | solution.py:197
  5.6 0.0 copy-start.1
  5.6 0.0 copy-start.2
  5.6 0.0 copy-start
  5.6 1.0 %dynamic-slice_bitcast_fusion = (bf16[3,128,128]{2,1,0:T(8,128)(2,1)S(1)}, bf16[3,128,128]{2,1,0:T(8,128)(2,1)S(1)}) fusion(bf16[1,1,2,3,128,128]{5,4,3,2,1,0:T(8,128)(2,1)} %param.6, s32[]{:T(128)S(6)} %select_n.8, s32[]{:T(128)S(6)} %select_n.7), kind=kLoop, calls=%fused_computation | loop fusion | bytes 393224 | tf_op jit(solution)/shard_map/jit(dynamic_index_in_dim)/squeeze | solution.py:227
  6.6 2.5 %collective-permute-start.7 = (bf16[3,128,128]{2,1,0:T(8,128)(2,1)S(1)}, bf16[3,128,128]{2,1,0:T(8,128)(2,1)S(1)}, u32[]{:S(2)}, u32[]{:S(2)}) collective-permute-start(bf16[3,128,128]{2,1,0:T(8,128)(2,1)S(1)} %get-tuple-element.21), channel_id=1, source_target_pairs={{0,17},{1,16},{2,19},{3,18},{4,21},{5,20},{6,23},{7,22},{8,25},{9,... | collective-permute-start | bytes 294920 | tf_op jit(solution)/shard_map/ppermute | solution.py:203
  9.1 0.5 %collective-permute-start.3 = (bf16[3,128,128]{2,1,0:T(8,128)(2,1)S(1)}, bf16[3,128,128]{2,1,0:T(8,128)(2,1)S(1)}, u32[]{:S(2)}, u32[]{:S(2)}) collective-permute-start(bf16[3,128,128]{2,1,0:T(8,128)(2,1)S(1)} %get-tuple-element.21), channel_id=1, source_target_pairs={{0,1},{1,0},{2,3},{3,2},{4,5},{5,4},{6,7},{7,6},{8,9},{9,8},{10,11... | collective-permute-start | bytes 294920 | tf_op jit(solution)/shard_map/ppermute | solution.py:203
  9.6 0.5 %collective-permute-start.6 = (bf16[3,128,128]{2,1,0:T(8,128)(2,1)S(1)}, bf16[3,128,128]{2,1,0:T(8,128)(2,1)S(1)}, u32[]{:S(2)}, u32[]{:S(2)}) collective-permute-start(bf16[3,128,128]{2,1,0:T(8,128)(2,1)S(1)} %get-tuple-element.17.refs_3_), channel_id=1, source_target_pairs={{0,16},{8,24},{16,0},{24,8},{1,17},{9,25},{17,1},{25,9},{2,18},{10... | collective-permute-start | bytes 294920 | tf_op jit(solution)/shard_map/ppermute | solution.py:197
  10.2 0.0 copy-done.1
  10.2 0.0 copy-done.2
  10.2 1.9 %shard_map.46.codes_ref = s32[48]{0:T(128)S(1)} custom-call(s32[6,4,8]{2,1,0:T(4,128)S(1)} %bitcast.10, s32[4,3,2,8]{3,2,1,0:T(2,128)S(1)} %bitcast.11), custom_call_target="tpu_custom_call" | custom-call | tf_op jit(solution)/shard_map/pallas_call | solution.py:46
  12.1 1.4 %collective-permute-done.refs_2_ = bf16[6,128,128]{2,1,0:T(8,128)(2,1)S(1)} collective-permute-done((bf16[6,128,128]{2,1,0:T(8,128)(2,1)}, bf16[6,128,128]{2,1,0:T(8,128)(2,1)S(1)}, u32[]{:S(2)}, u32[]{:S(2)}) %collective-permute-start) | collective-permute-done | bytes 196640 | tf_op jit(solution)/shard_map/ppermute | solution.py:197
  13.5 0.7 %collective-permute-start.1 = (bf16[6,128,128]{2,1,0:T(8,128)(2,1)S(1)}, bf16[6,128,128]{2,1,0:T(8,128)(2,1)S(1)}, u32[]{:S(2)}, u32[]{:S(2)}) collective-permute-start(bf16[6,128,128]{2,1,0:T(8,128)(2,1)S(1)} %collective-permute-done.refs_2_), channel_id=1, source_target_pairs={{0,2},{1,3},{2,0},{3,1},{4,6},{5,7},{6,4},{7,5},{8,10},{9,11},{10,... | collective-permute-start | bytes 589832 | tf_op jit(solution)/shard_map/ppermute | solution.py:197
  14.2 0.0 collective-permute-done.7.refs_8_
  14.2 0.0 collective-permute-start.9
  14.2 0.0 collective-permute-done.3.refs_4_
  14.2 0.5 %collective-permute-start.5 = (bf16[3,128,128]{2,1,0:T(8,128)(2,1)S(1)}, bf16[3,128,128]{2,1,0:T(8,128)(2,1)S(1)}, u32[]{:S(2)}, u32[]{:S(2)}) collective-permute-start(bf16[3,128,128]{2,1,0:T(8,128)(2,1)S(1)} %collective-permute-done.3.refs_4_), channel_id=1, source_target_pairs={{0,8},{8,0},{16,24},{24,16},{1,9},{9,1},{17,25},{25,17},{2,10},{10... | collective-permute-start | bytes 294920 | tf_op jit(solution)/shard_map/ppermute | solution.py:197
  14.7 0.0 collective-permute-done.6.refs_7_
  14.7 0.1 collective-permute-start.8
  14.8 0.0 collective-permute-done.2.refs_1_
  14.8 0.4 %collective-permute-start.4 = (bf16[3,128,128]{2,1,0:T(8,128)(2,1)S(1)}, bf16[3,128,128]{2,1,0:T(8,128)(2,1)S(1)}, u32[]{:S(2)}, u32[]{:S(2)}) collective-permute-start(bf16[3,128,128]{2,1,0:T(8,128)(2,1)S(1)} %get-tuple-element.17.refs_3_), channel_id=1, source_target_pairs={{0,8},{8,0},{16,24},{24,16},{1,9},{9,1},{17,25},{25,17},{2,10},{10... | collective-permute-start | bytes 294920 | tf_op jit(solution)/shard_map/ppermute | solution.py:197
  15.2 0.3 %collective-permute-done.9.refs_10_ = bf16[3,128,128]{2,1,0:T(8,128)(2,1)S(1)} collective-permute-done((bf16[3,128,128]{2,1,0:T(8,128)(2,1)S(1)}, bf16[3,128,128]{2,1,0:T(8,128)(2,1)S(1)}, u32[]{:S(2)}, u32[]{:S(2)}) %collective-permute-start.9) | collective-permute-done | bytes 98336 | tf_op jit(solution)/shard_map/ppermute | solution.py:197
  15.5 0.2 collective-permute-done.5.refs_6_
  15.7 0.4 %collective-permute-done.8.refs_9_ = bf16[3,128,128]{2,1,0:T(8,128)(2,1)S(1)} collective-permute-done((bf16[3,128,128]{2,1,0:T(8,128)(2,1)S(1)}, bf16[3,128,128]{2,1,0:T(8,128)(2,1)S(1)}, u32[]{:S(2)}, u32[]{:S(2)}) %collective-permute-start.8) | collective-permute-done | bytes 98336 | tf_op jit(solution)/shard_map/ppermute | solution.py:197
  16.0 0.2 collective-permute-done.4.refs_5_
  16.2 0.0 copy-done
  16.2 1.8 %shard_map.47 = (f32[256,128]{1,0:T(8,128)S(1)}, f32[256,128]{1,0:T(8,128)S(1)}, bf16[2,768,256]{2,1,0:T(8,128)(2,1)S(1)}) custom-call(s32[48]{0:T(128)S(1)} %shard_map.46.codes_ref, bf16[6,128,128]{2,1,0:T(8,128)(2,1)S(1)} %bitcast.9, bf16[6,128,128]{2,1,0:T(8,128)(2,1)S(1)} %collective-permute-done.2.refs_1_, ...), custom_call_target="tpu_custom_call" | custom-call | flops 201326592 | bytes 786432 | tf_op jit(solution)/shard_map/pallas_call | solution.py:113
  17.9 1.6 %collective-permute-done.1.left_ref = bf16[6,128,128]{2,1,0:T(8,128)(2,1)S(1)} collective-permute-done((bf16[6,128,128]{2,1,0:T(8,128)(2,1)S(1)}, bf16[6,128,128]{2,1,0:T(8,128)(2,1)S(1)}, u32[]{:S(2)}, u32[]{:S(2)}) %collective-permute-start.1) | collective-permute-done | bytes 196640 | tf_op jit(solution)/shard_map/ppermute | solution.py:197
  19.5 0.3 %shard_map.49 = s16[272,128]{1,0:T(8,128)(2,1)S(1)} custom-call(bf16[6,128,128]{2,1,0:T(8,128)(2,1)S(1)} %collective-permute-done.1.left_ref, bf16[2,768,256]{2,1,0:T(8,128)(2,1)S(1)} %get-tuple-element.18.right_ref, f32[256,128]{1,0:T(8,128)S(1)} %get-tuple-element.20.total_ref), custom_call_target="tpu_custom_call" | custom-call | flops 25165824 | bytes 196608 | tf_op jit(solution)/shard_map/pallas_call | solution.py:146
  19.8 1.4 %collective-permute-start.10 = (s16[272,128]{1,0:T(8,128)(2,1)S(1)}, s16[272,128]{1,0:T(8,128)(2,1)S(1)}, u32[]{:S(2)}, u32[]{:S(2)}) collective-permute-start(s16[272,128]{1,0:T(8,128)(2,1)S(1)} %shard_map.49), channel_id=1, source_target_pairs={{0,1},{1,0},{2,3},{3,2},{4,5},{5,4},{6,7},{7,6},{8,9},{9,8},{10,11... | collective-permute-start | bytes 208904 | tf_op jit(solution)/shard_map/ppermute | solution.py:197
  21.1 0.2 shard_map.48.total_ref
  21.3 2.8 %collective-permute-done.10.coded_ref = s16[272,128]{1,0:T(8,128)(2,1)S(1)} collective-permute-done((s16[272,128]{1,0:T(8,128)(2,1)S(1)}, s16[272,128]{1,0:T(8,128)(2,1)S(1)}, u32[]{:S(2)}, u32[]{:S(2)}) %collective-permute-start.10) | collective-permute-done | bytes 69664 | tf_op jit(solution)/shard_map/ppermute | solution.py:197
  24.1 0.7 %shard_map.50 = bf16[256,128]{1,0:T(8,128)(2,1)} custom-call(f32[256,128]{1,0:T(8,128)S(1)} %shard_map.48.total_ref, s16[272,128]{1,0:T(8,128)(2,1)S(1)} %collective-permute-done.10.coded_ref), custom_call_target="tpu_custom_call" | custom-call | tf_op jit(solution)/shard_map/pallas_call | solution.py:186
Async XLA Ops:
  0.0 13.5 %collective-permute-start = (bf16[6,128,128]{2,1,0:T(8,128)(2,1)}, bf16[6,128,128]{2,1,0:T(8,128)(2,1)S(1)}, u32[]{:S(2)}, u32[]{:S(2)}) collective-permute-start(bf16[6,128,128]{2,1,0:T(8,128)(2,1)} %bitcast.7), channel_id=1, source_target_pairs={{0,4},{1,5},{2,6},{3,7},{4,0},{5,1},{6,2},{7,3},{8,12},{9,13},{10,... | collective-permute-start | bytes 589832 | tf_op jit(solution)/shard_map/ppermute | solution.py:197
  4.0 10.7 %collective-permute-start.2 = (bf16[6,128,128]{2,1,0:T(8,128)(2,1)}, bf16[6,128,128]{2,1,0:T(8,128)(2,1)S(1)}, u32[]{:S(2)}, u32[]{:S(2)}) collective-permute-start(bf16[6,128,128]{2,1,0:T(8,128)(2,1)} %bitcast.8), channel_id=1, source_target_pairs={{0,2},{1,3},{2,0},{3,1},{4,6},{5,7},{6,4},{7,5},{8,10},{9,11},{10,... | collective-permute-start | bytes 589832 | tf_op jit(solution)/shard_map/ppermute | solution.py:197
  5.6 4.6 %copy-start.1 = (s32[4,8,6]{1,0,2:T(4,128)S(1)}, s32[4,8,6]{1,0,2:T(4,128)}, u32[]{:S(2)}) copy-start(s32[4,8,6]{1,0,2:T(4,128)} %param.5) | copy-start | bytes 2308
  5.6 4.6 %copy-start.2 = (s32[4,8,2,3]{1,2,3,0:T(2,128)S(1)}, s32[4,8,2,3]{1,2,3,0:T(2,128)}, u32[]{:S(2)}) copy-start(s32[4,8,2,3]{1,2,3,0:T(2,128)} %param.7) | copy-start | bytes 2308
  5.6 10.6 %copy-start = (bf16[1,1,6,128,128]{4,3,2,1,0:T(8,128)(2,1)S(1)}, bf16[1,1,6,128,128]{4,3,2,1,0:T(8,128)(2,1)}, u32[]{:S(2)}) copy-start(bf16[1,1,6,128,128]{4,3,2,1,0:T(8,128)(2,1)} %param.4) | copy-start | bytes 589828
  6.6 7.6 %collective-permute-start.7 = (bf16[3,128,128]{2,1,0:T(8,128)(2,1)S(1)}, bf16[3,128,128]{2,1,0:T(8,128)(2,1)S(1)}, u32[]{:S(2)}, u32[]{:S(2)}) collective-permute-start(bf16[3,128,128]{2,1,0:T(8,128)(2,1)S(1)} %get-tuple-element.21), channel_id=1, source_target_pairs={{0,17},{1,16},{2,19},{3,18},{4,21},{5,20},{6,23},{7,22},{8,25},{9,... | collective-permute-start | bytes 294920 | tf_op jit(solution)/shard_map/ppermute | solution.py:203
  9.1 5.1 %collective-permute-start.3 = (bf16[3,128,128]{2,1,0:T(8,128)(2,1)S(1)}, bf16[3,128,128]{2,1,0:T(8,128)(2,1)S(1)}, u32[]{:S(2)}, u32[]{:S(2)}) collective-permute-start(bf16[3,128,128]{2,1,0:T(8,128)(2,1)S(1)} %get-tuple-element.21), channel_id=1, source_target_pairs={{0,1},{1,0},{2,3},{3,2},{4,5},{5,4},{6,7},{7,6},{8,9},{9,8},{10,11... | collective-permute-start | bytes 294920 | tf_op jit(solution)/shard_map/ppermute | solution.py:203
  9.6 5.1 %collective-permute-start.6 = (bf16[3,128,128]{2,1,0:T(8,128)(2,1)S(1)}, bf16[3,128,128]{2,1,0:T(8,128)(2,1)S(1)}, u32[]{:S(2)}, u32[]{:S(2)}) collective-permute-start(bf16[3,128,128]{2,1,0:T(8,128)(2,1)S(1)} %get-tuple-element.17.refs_3_), channel_id=1, source_target_pairs={{0,16},{8,24},{16,0},{24,8},{1,17},{9,25},{17,1},{25,9},{2,18},{10... | collective-permute-start | bytes 294920 | tf_op jit(solution)/shard_map/ppermute | solution.py:197
  13.5 6.0 %collective-permute-start.1 = (bf16[6,128,128]{2,1,0:T(8,128)(2,1)S(1)}, bf16[6,128,128]{2,1,0:T(8,128)(2,1)S(1)}, u32[]{:S(2)}, u32[]{:S(2)}) collective-permute-start(bf16[6,128,128]{2,1,0:T(8,128)(2,1)S(1)} %collective-permute-done.refs_2_), channel_id=1, source_target_pairs={{0,2},{1,3},{2,0},{3,1},{4,6},{5,7},{6,4},{7,5},{8,10},{9,11},{10,... | collective-permute-start | bytes 589832 | tf_op jit(solution)/shard_map/ppermute | solution.py:197
  14.2 1.3 %collective-permute-start.9 = (bf16[3,128,128]{2,1,0:T(8,128)(2,1)S(1)}, bf16[3,128,128]{2,1,0:T(8,128)(2,1)S(1)}, u32[]{:S(2)}, u32[]{:S(2)}) collective-permute-start(bf16[3,128,128]{2,1,0:T(8,128)(2,1)S(1)} %collective-permute-done.7.refs_8_), channel_id=1, source_target_pairs={{0,8},{8,0},{16,24},{24,16},{1,9},{9,1},{17,25},{25,17},{2,10},{10... | collective-permute-start | bytes 294920 | tf_op jit(solution)/shard_map/ppermute | solution.py:197
  14.2 1.5 %collective-permute-start.5 = (bf16[3,128,128]{2,1,0:T(8,128)(2,1)S(1)}, bf16[3,128,128]{2,1,0:T(8,128)(2,1)S(1)}, u32[]{:S(2)}, u32[]{:S(2)}) collective-permute-start(bf16[3,128,128]{2,1,0:T(8,128)(2,1)S(1)} %collective-permute-done.3.refs_4_), channel_id=1, source_target_pairs={{0,8},{8,0},{16,24},{24,16},{1,9},{9,1},{17,25},{25,17},{2,10},{10... | collective-permute-start | bytes 294920 | tf_op jit(solution)/shard_map/ppermute | solution.py:197
  14.7 1.3 %collective-permute-start.8 = (bf16[3,128,128]{2,1,0:T(8,128)(2,1)S(1)}, bf16[3,128,128]{2,1,0:T(8,128)(2,1)S(1)}, u32[]{:S(2)}, u32[]{:S(2)}) collective-permute-start(bf16[3,128,128]{2,1,0:T(8,128)(2,1)S(1)} %collective-permute-done.6.refs_7_), channel_id=1, source_target_pairs={{0,8},{8,0},{16,24},{24,16},{1,9},{9,1},{17,25},{25,17},{2,10},{10... | collective-permute-start | bytes 294920 | tf_op jit(solution)/shard_map/ppermute | solution.py:197
  14.8 1.4 %collective-permute-start.4 = (bf16[3,128,128]{2,1,0:T(8,128)(2,1)S(1)}, bf16[3,128,128]{2,1,0:T(8,128)(2,1)S(1)}, u32[]{:S(2)}, u32[]{:S(2)}) collective-permute-start(bf16[3,128,128]{2,1,0:T(8,128)(2,1)S(1)} %get-tuple-element.17.refs_3_), channel_id=1, source_target_pairs={{0,8},{8,0},{16,24},{24,16},{1,9},{9,1},{17,25},{25,17},{2,10},{10... | collective-permute-start | bytes 294920 | tf_op jit(solution)/shard_map/ppermute | solution.py:197
  19.8 4.4 %collective-permute-start.10 = (s16[272,128]{1,0:T(8,128)(2,1)S(1)}, s16[272,128]{1,0:T(8,128)(2,1)S(1)}, u32[]{:S(2)}, u32[]{:S(2)}) collective-permute-start(s16[272,128]{1,0:T(8,128)(2,1)S(1)} %shard_map.49), channel_id=1, source_target_pairs={{0,1},{1,0},{2,3},{3,2},{4,5},{5,4},{6,7},{7,6},{8,9},{9,8},{10,11... | collective-permute-start | bytes 208904 | tf_op jit(solution)/shard_map/ppermute | solution.py:197

commit v18 on v17

--- a/solution.py
+++ b/solution.py
@@ -125,14 +125,16 @@
 
 
 def last_products(parts, right, total, side, finish, out_shape):
-    (left,) = parts
-    slots, tile, _ = left.shape
-
-    def kernel(left_ref, right_ref, total_ref, out_ref):
+    slots, tile, _ = parts[0].shape
+
+    def kernel(odd_ref, even_ref, right_ref, total_ref, out_ref):
+        odd = lax.axis_index("row") & 1
         added = jnp.zeros((tile, RT * tile), jnp.float32)
         for slot in range(0, slots, 2):
             both = min(2, slots - slot)
-            tiles = [left_ref[slot + n] for n in range(both)]
+            tiles = [
+                jnp.where(odd == 1, odd_ref[slot + n], even_ref[slot + n]) for n in range(both)
+            ]
             added += jnp.dot(
                 jnp.concatenate(tiles, axis=1),
                 right_ref[side, slot * tile : (slot + both) * tile, :],
@@ -146,13 +148,13 @@
     return pl.pallas_call(
         kernel,
         out_shape=out_shape,
-        in_specs=[VMEM] * 3,
+        in_specs=[VMEM] * 4,
         out_specs=VMEM,
         compiler_params=pltpu.CompilerParams(vmem_limit_bytes=16 * 1024 * 1024),
         cost_estimate=pl.CostEstimate(
             flops=2 * slots * tile**3, bytes_accessed=2 * slots * tile**2, transcendentals=0
         ),
-    )(left, right, total)
+    )(*parts, right, total)
 
 
 def write_sum(sums, out_ref):
@@ -203,6 +205,17 @@
     return lax.ppermute(block, ("row", "col"), route)
 
 
+def passed_on(block):
+    rows, cols = lax.axis_size("row"), lax.axis_size("col")
+    moved = []
+    for core in range(2):
+        route = [
+            (r * cols + c, r * cols + (c ^ 2 if r % 2 == core else c)) for r in range(rows) for c in range(cols)
+        ]
+        moved.append(lax.ppermute(block, ("row", "col"), route))
+    return moved[::-1]
+
+
 def gather(block, beside, place):
     distance = lax.axis_size("col") // 4
     steps = [distance >> n for n in range(distance.bit_length())]
@@ -212,9 +225,10 @@
     blocks = {0: block, **dict(zip(steps, came))}
     for d in steps:
         for s in sorted(blocks):
-            if s ^ d not in blocks and s & (d - 1) == 0:
+            if s ^ d not in blocks and s & (d - 1) == 0 and s ^ d != 2 * distance - 1:
                 blocks[s ^ d] = across(blocks[s], "col", 2 * d)
-    return [(s, (blocks[s],)) for s in range(len(blocks))], beside
+    found = [(s, (blocks[s],)) for s in range(2 * distance - 1)]
+    return found + [(2 * distance - 1, passed_on(blocks[2 * distance - 2]))], beside
 
 
 def shards(left_tiles, left_index, right_tiles, right_index):

time: 24.9 us -> 29.6 us (1.19)
  starting transfers between devices: 12.3 us -> 15.2 us
  waiting for transfers between devices: 6.67 us -> 8.3 us
    ppermute x9 -> x8, waiting for transfers between devices: 6.66 us -> 3.32 us  [across(): return lax.ppermute(block, axis, route)]
    ppermute x0 -> x2, starting transfers between devices: none -> 3.03 us  [passed_on(): moved.append(lax.ppermute(block, ('row', 'col'), route))]
    ppermute x0 -> x2, waiting for transfers between devices: none -> 2.62 us  [passed_on(): moved.append(lax.ppermute(block, ('row', 'col'), route))]
    ppermute x2, waiting for transfers between devices: 0.01 us -> 2.36 us  [crossed(): return lax.ppermute(block, ('row', 'col'), route)]
    ppermute x9 -> x8, starting transfers between devices: 9.25 us -> 9.1 us  [across(): return lax.ppermute(block, axis, route)]
  transfers between devices with their start and end apart: 11 -> 12, of which waited for: 7 -> 6; matrix products, arithmetic and copies ran while one was open for 4% -> 3% of each run, Pallas kernels for 16% -> 14%
where the time goes in v18:
time: 29.6 us; the launch traced here: 29.5 us
  starting transfers between devices  15.2 us (51%)
  waiting for transfers between devices  8.3 us (28%)
  Pallas kernels  4.92 us (17%)
  local copies, waits for them, and re-layouts  1 us (3%)
    ppermute x8, starting transfers between devices, across(): return lax.ppermute(block, axis, route)  9.1 us
    ppermute x8, waiting for transfers between devices, across(): return lax.ppermute(block, axis, route)  3.32 us
    ppermute x2, starting transfers between devices, passed_on(): moved.append(lax.ppermute(block, ('row', 'col'), route))  3.03 us
    ppermute x2, starting transfers between devices, crossed(): return lax.ppermute(block, ('row', 'col'), route)  3.02 us
    ppermute x2, waiting for transfers between devices, passed_on(): moved.append(lax.ppermute(block, ('row', 'col'), route))  2.62 us
    ppermute x2, waiting for transfers between devices, crossed(): return lax.ppermute(block, ('row', 'col'), route)  2.36 us
    pallas_call x1, Pallas kernels, find_matches(): pl.pallas_call(kernel, out_shape=jax.ShapeDtypeStruct((inner * 2 * slots,...  1.92 us
    pallas_call x1, Pallas kernels, first_products(): pl.pallas_call(kernel, out_shape=[jax.ShapeDtypeStruct((RT * tile, tile),...  1.87 us
  transfers between devices with their start and end apart: 12, of which 6 were waited for; matrix products, arithmetic and copies ran while one was open for 3% of the time, Pallas kernels for 14%

profile of v18, /device:TPU:0, one launch (start us, length us, event | category | flops | bytes accessed | tf_op | source)
XLA Modules:
  0.0 29.5 jit_solution(5850132190325056794)
XLA Ops:
  0.0 4.0 %collective-permute-start = (bf16[6,128,128]{2,1,0:T(8,128)(2,1)}, bf16[6,128,128]{2,1,0:T(8,128)(2,1)S(1)}, u32[]{:S(2)}, u32[]{:S(2)}) collective-permute-start(bf16[6,128,128]{2,1,0:T(8,128)(2,1)} %bitcast.7), channel_id=1, source_target_pairs={{0,4},{1,5},{2,6},{3,7},{4,0},{5,1},{6,2},{7,3},{8,12},{9,13},{10,... | collective-permute-start | bytes 589832 | tf_op jit(solution)/shard_map/ppermute | solution.py:199
  4.0 1.6 %collective-permute-start.3 = (bf16[6,128,128]{2,1,0:T(8,128)(2,1)}, bf16[6,128,128]{2,1,0:T(8,128)(2,1)S(1)}, u32[]{:S(2)}, u32[]{:S(2)}) collective-permute-start(bf16[6,128,128]{2,1,0:T(8,128)(2,1)} %bitcast.8), channel_id=1, source_target_pairs={{0,2},{1,3},{2,0},{3,1},{4,6},{5,7},{6,4},{7,5},{8,10},{9,11},{10,... | collective-permute-start | bytes 589832 | tf_op jit(solution)/shard_map/ppermute | solution.py:199
  5.6 0.0 copy-start.1
  5.6 0.0 copy-start.2
  5.6 0.0 copy-start
  5.6 1.0 %dynamic-slice_bitcast_fusion = (bf16[3,128,128]{2,1,0:T(8,128)(2,1)S(1)}, bf16[3,128,128]{2,1,0:T(8,128)(2,1)S(1)}) fusion(bf16[1,1,2,3,128,128]{5,4,3,2,1,0:T(8,128)(2,1)} %param.6, s32[]{:T(128)S(6)} %select_n.8, s32[]{:T(128)S(6)} %select_n.7), kind=kLoop, calls=%fused_computation | loop fusion | bytes 393224 | tf_op jit(solution)/shard_map/jit(dynamic_index_in_dim)/squeeze | solution.py:241
  6.6 2.5 %collective-permute-start.8 = (bf16[3,128,128]{2,1,0:T(8,128)(2,1)S(1)}, bf16[3,128,128]{2,1,0:T(8,128)(2,1)S(1)}, u32[]{:S(2)}, u32[]{:S(2)}) collective-permute-start(bf16[3,128,128]{2,1,0:T(8,128)(2,1)S(1)} %get-tuple-element.21), channel_id=1, source_target_pairs={{0,17},{1,16},{2,19},{3,18},{4,21},{5,20},{6,23},{7,22},{8,25},{9,... | collective-permute-start | bytes 294920 | tf_op jit(solution)/shard_map/ppermute | solution.py:205
  9.1 0.5 %collective-permute-start.4 = (bf16[3,128,128]{2,1,0:T(8,128)(2,1)S(1)}, bf16[3,128,128]{2,1,0:T(8,128)(2,1)S(1)}, u32[]{:S(2)}, u32[]{:S(2)}) collective-permute-start(bf16[3,128,128]{2,1,0:T(8,128)(2,1)S(1)} %get-tuple-element.21), channel_id=1, source_target_pairs={{0,1},{1,0},{2,3},{3,2},{4,5},{5,4},{6,7},{7,6},{8,9},{9,8},{10,11... | collective-permute-start | bytes 294920 | tf_op jit(solution)/shard_map/ppermute | solution.py:205
  9.6 0.5 %collective-permute-start.7 = (bf16[3,128,128]{2,1,0:T(8,128)(2,1)S(1)}, bf16[3,128,128]{2,1,0:T(8,128)(2,1)S(1)}, u32[]{:S(2)}, u32[]{:S(2)}) collective-permute-start(bf16[3,128,128]{2,1,0:T(8,128)(2,1)S(1)} %get-tuple-element.17.refs_3_), channel_id=1, source_target_pairs={{0,16},{8,24},{16,0},{24,8},{1,17},{9,25},{17,1},{25,9},{2,18},{10... | collective-permute-start | bytes 294920 | tf_op jit(solution)/shard_map/ppermute | solution.py:199
  10.2 2.4 %collective-permute-done.8.refs_8_ = bf16[3,128,128]{2,1,0:T(8,128)(2,1)S(1)} collective-permute-done((bf16[3,128,128]{2,1,0:T(8,128)(2,1)S(1)}, bf16[3,128,128]{2,1,0:T(8,128)(2,1)S(1)}, u32[]{:S(2)}, u32[]{:S(2)}) %collective-permute-start.8) | collective-permute-done | bytes 98336 | tf_op jit(solution)/shard_map/ppermute | solution.py:205
  12.5 0.0 collective-permute-start.10
  12.5 0.0 copy-done.1
  12.5 0.0 copy-done.2
  12.5 1.9 %shard_map.46.codes_ref = s32[48]{0:T(128)S(1)} custom-call(s32[6,4,8]{2,1,0:T(4,128)S(1)} %bitcast.10, s32[4,3,2,8]{3,2,1,0:T(2,128)S(1)} %bitcast.11), custom_call_target="tpu_custom_call" | custom-call | tf_op jit(solution)/shard_map/pallas_call | solution.py:46
  14.5 0.0 collective-permute-done.refs_2_
  14.5 2.4 %collective-permute-start.2 = (bf16[6,128,128]{2,1,0:T(8,128)(2,1)S(1)}, bf16[6,128,128]{2,1,0:T(8,128)(2,1)S(1)}, u32[]{:S(2)}, u32[]{:S(2)}) collective-permute-start(bf16[6,128,128]{2,1,0:T(8,128)(2,1)S(1)} %collective-permute-done.refs_2_), channel_id=1, source_target_pairs={{0,2},{1,3},{2,0},{3,1},{4,6},{5,7},{6,4},{7,5},{8,8},{9,9},{10,10... | collective-permute-start | bytes 589832 | tf_op jit(solution)/shard_map/ppermute | solution.py:215
  16.8 0.0 collective-permute-done.4.refs_4_
  16.9 0.7 %collective-permute-start.1 = (bf16[6,128,128]{2,1,0:T(8,128)(2,1)S(1)}, bf16[6,128,128]{2,1,0:T(8,128)(2,1)S(1)}, u32[]{:S(2)}, u32[]{:S(2)}) collective-permute-start(bf16[6,128,128]{2,1,0:T(8,128)(2,1)S(1)} %collective-permute-done.refs_2_), channel_id=1, source_target_pairs={{0,0},{1,1},{2,2},{3,3},{4,4},{5,5},{6,6},{7,7},{8,10},{9,11},{10,... | collective-permute-start | bytes 589832 | tf_op jit(solution)/shard_map/ppermute | solution.py:215
  17.5 0.0 collective-permute-done.7.refs_7_
  17.6 0.3 collective-permute-start.6
  17.8 0.0 collective-permute-done.3.refs_1_
  17.8 0.3 collective-permute-start.9
  18.1 0.0 collective-permute-done.10.refs_10_
  18.1 0.2 collective-permute-start.5
  18.4 0.6 %collective-permute-done.6.refs_6_ = bf16[3,128,128]{2,1,0:T(8,128)(2,1)S(1)} collective-permute-done((bf16[3,128,128]{2,1,0:T(8,128)(2,1)S(1)}, bf16[3,128,128]{2,1,0:T(8,128)(2,1)S(1)}, u32[]{:S(2)}, u32[]{:S(2)}) %collective-permute-start.6) | collective-permute-done | bytes 98336 | tf_op jit(solution)/shard_map/ppermute | solution.py:199
  18.9 0.2 collective-permute-done.9.refs_9_
  19.1 0.3 collective-permute-done.5.refs_5_
  19.4 0.0 copy-done
  19.4 1.9 %shard_map.47 = (f32[256,128]{1,0:T(8,128)S(1)}, f32[256,128]{1,0:T(8,128)S(1)}, bf16[2,768,256]{2,1,0:T(8,128)(2,1)S(1)}) custom-call(s32[48]{0:T(128)S(1)} %shard_map.46.codes_ref, bf16[6,128,128]{2,1,0:T(8,128)(2,1)S(1)} %bitcast.9, bf16[6,128,128]{2,1,0:T(8,128)(2,1)S(1)} %collective-permute-done.3.refs_1_, ...), custom_call_target="tpu_custom_call" | custom-call | flops 201326592 | bytes 786432 | tf_op jit(solution)/shard_map/pallas_call | solution.py:113
  21.3 2.6 %collective-permute-done.2.even_ref = bf16[6,128,128]{2,1,0:T(8,128)(2,1)S(1)} collective-permute-done((bf16[6,128,128]{2,1,0:T(8,128)(2,1)S(1)}, bf16[6,128,128]{2,1,0:T(8,128)(2,1)S(1)}, u32[]{:S(2)}, u32[]{:S(2)}) %collective-permute-start.2) | collective-permute-done | bytes 196640 | tf_op jit(solution)/shard_map/ppermute | solution.py:215
  23.9 0.0 collective-permute-done.1.odd_ref
  23.9 0.3 shard_map.49
  24.2 2.2 %collective-permute-start.11 = (s16[272,128]{1,0:T(8,128)(2,1)S(1)}, s16[272,128]{1,0:T(8,128)(2,1)S(1)}, u32[]{:S(2)}, u32[]{:S(2)}) collective-permute-start(s16[272,128]{1,0:T(8,128)(2,1)S(1)} %shard_map.49), channel_id=1, source_target_pairs={{0,1},{1,0},{2,3},{3,2},{4,5},{5,4},{6,7},{7,6},{8,9},{9,8},{10,11... | collective-permute-start | bytes 208904 | tf_op jit(solution)/shard_map/ppermute | solution.py:199
  26.4 0.2 shard_map.48.total_ref
  26.6 2.2 %collective-permute-done.11.coded_ref = s16[272,128]{1,0:T(8,128)(2,1)S(1)} collective-permute-done((s16[272,128]{1,0:T(8,128)(2,1)S(1)}, s16[272,128]{1,0:T(8,128)(2,1)S(1)}, u32[]{:S(2)}, u32[]{:S(2)}) %collective-permute-start.11) | collective-permute-done | bytes 69664 | tf_op jit(solution)/shard_map/ppermute | solution.py:199
  28.8 0.7 %shard_map.50 = bf16[256,128]{1,0:T(8,128)(2,1)} custom-call(f32[256,128]{1,0:T(8,128)S(1)} %shard_map.48.total_ref, s16[272,128]{1,0:T(8,128)(2,1)S(1)} %collective-permute-done.11.coded_ref), custom_call_target="tpu_custom_call" | custom-call | tf_op jit(solution)/shard_map/pallas_call | solution.py:188
Async XLA Ops:
  0.0 14.5 %collective-permute-start = (bf16[6,128,128]{2,1,0:T(8,128)(2,1)}, bf16[6,128,128]{2,1,0:T(8,128)(2,1)S(1)}, u32[]{:S(2)}, u32[]{:S(2)}) collective-permute-start(bf16[6,128,128]{2,1,0:T(8,128)(2,1)} %bitcast.7), channel_id=1, source_target_pairs={{0,4},{1,5},{2,6},{3,7},{4,0},{5,1},{6,2},{7,3},{8,12},{9,13},{10,... | collective-permute-start | bytes 589832 | tf_op jit(solution)/shard_map/ppermute | solution.py:199
  4.0 13.8 %collective-permute-start.3 = (bf16[6,128,128]{2,1,0:T(8,128)(2,1)}, bf16[6,128,128]{2,1,0:T(8,128)(2,1)S(1)}, u32[]{:S(2)}, u32[]{:S(2)}) collective-permute-start(bf16[6,128,128]{2,1,0:T(8,128)(2,1)} %bitcast.8), channel_id=1, source_target_pairs={{0,2},{1,3},{2,0},{3,1},{4,6},{5,7},{6,4},{7,5},{8,10},{9,11},{10,... | collective-permute-start | bytes 589832 | tf_op jit(solution)/shard_map/ppermute | solution.py:199
  5.6 6.9 %copy-start.1 = (s32[4,8,6]{1,0,2:T(4,128)S(1)}, s32[4,8,6]{1,0,2:T(4,128)}, u32[]{:S(2)}) copy-start(s32[4,8,6]{1,0,2:T(4,128)} %param.5) | copy-start | bytes 2308
  5.6 6.9 %copy-start.2 = (s32[4,8,2,3]{1,2,3,0:T(2,128)S(1)}, s32[4,8,2,3]{1,2,3,0:T(2,128)}, u32[]{:S(2)}) copy-start(s32[4,8,2,3]{1,2,3,0:T(2,128)} %param.7) | copy-start | bytes 2308
  5.6 13.8 %copy-start = (bf16[1,1,6,128,128]{4,3,2,1,0:T(8,128)(2,1)S(1)}, bf16[1,1,6,128,128]{4,3,2,1,0:T(8,128)(2,1)}, u32[]{:S(2)}) copy-start(bf16[1,1,6,128,128]{4,3,2,1,0:T(8,128)(2,1)} %param.4) | copy-start | bytes 589828
  6.6 5.9 %collective-permute-start.8 = (bf16[3,128,128]{2,1,0:T(8,128)(2,1)S(1)}, bf16[3,128,128]{2,1,0:T(8,128)(2,1)S(1)}, u32[]{:S(2)}, u32[]{:S(2)}) collective-permute-start(bf16[3,128,128]{2,1,0:T(8,128)(2,1)S(1)} %get-tuple-element.21), channel_id=1, source_target_pairs={{0,17},{1,16},{2,19},{3,18},{4,21},{5,20},{6,23},{7,22},{8,25},{9,... | collective-permute-start | bytes 294920 | tf_op jit(solution)/shard_map/ppermute | solution.py:205
  9.1 7.7 %collective-permute-start.4 = (bf16[3,128,128]{2,1,0:T(8,128)(2,1)S(1)}, bf16[3,128,128]{2,1,0:T(8,128)(2,1)S(1)}, u32[]{:S(2)}, u32[]{:S(2)}) collective-permute-start(bf16[3,128,128]{2,1,0:T(8,128)(2,1)S(1)} %get-tuple-element.21), channel_id=1, source_target_pairs={{0,1},{1,0},{2,3},{3,2},{4,5},{5,4},{6,7},{7,6},{8,9},{9,8},{10,11... | collective-permute-start | bytes 294920 | tf_op jit(solution)/shard_map/ppermute | solution.py:205
  9.6 7.9 %collective-permute-start.7 = (bf16[3,128,128]{2,1,0:T(8,128)(2,1)S(1)}, bf16[3,128,128]{2,1,0:T(8,128)(2,1)S(1)}, u32[]{:S(2)}, u32[]{:S(2)}) collective-permute-start(bf16[3,128,128]{2,1,0:T(8,128)(2,1)S(1)} %get-tuple-element.17.refs_3_), channel_id=1, source_target_pairs={{0,16},{8,24},{16,0},{24,8},{1,17},{9,25},{17,1},{25,9},{2,18},{10... | collective-permute-start | bytes 294920 | tf_op jit(solution)/shard_map/ppermute | solution.py:199
  12.5 5.6 %collective-permute-start.10 = (bf16[3,128,128]{2,1,0:T(8,128)(2,1)S(1)}, bf16[3,128,128]{2,1,0:T(8,128)(2,1)S(1)}, u32[]{:S(2)}, u32[]{:S(2)}) collective-permute-start(bf16[3,128,128]{2,1,0:T(8,128)(2,1)S(1)} %collective-permute-done.8.refs_8_), channel_id=1, source_target_pairs={{0,8},{8,0},{16,24},{24,16},{1,9},{9,1},{17,25},{25,17},{2,10},{10... | collective-permute-start | bytes 294920 | tf_op jit(solution)/shard_map/ppermute | solution.py:199
  14.5 9.4 %collective-permute-start.2 = (bf16[6,128,128]{2,1,0:T(8,128)(2,1)S(1)}, bf16[6,128,128]{2,1,0:T(8,128)(2,1)S(1)}, u32[]{:S(2)}, u32[]{:S(2)}) collective-permute-start(bf16[6,128,128]{2,1,0:T(8,128)(2,1)S(1)} %collective-permute-done.refs_2_), channel_id=1, source_target_pairs={{0,2},{1,3},{2,0},{3,1},{4,6},{5,7},{6,4},{7,5},{8,8},{9,9},{10,10... | collective-permute-start | bytes 589832 | tf_op jit(solution)/shard_map/ppermute | solution.py:215
  16.9 7.1 %collective-permute-start.1 = (bf16[6,128,128]{2,1,0:T(8,128)(2,1)S(1)}, bf16[6,128,128]{2,1,0:T(8,128)(2,1)S(1)}, u32[]{:S(2)}, u32[]{:S(2)}) collective-permute-start(bf16[6,128,128]{2,1,0:T(8,128)(2,1)S(1)} %collective-permute-done.refs_2_), channel_id=1, source_target_pairs={{0,0},{1,1},{2,2},{3,3},{4,4},{5,5},{6,6},{7,7},{8,10},{9,11},{10,... | collective-permute-start | bytes 589832 | tf_op jit(solution)/shard_map/ppermute | solution.py:215
  17.6 1.4 %collective-permute-start.6 = (bf16[3,128,128]{2,1,0:T(8,128)(2,1)S(1)}, bf16[3,128,128]{2,1,0:T(8,128)(2,1)S(1)}, u32[]{:S(2)}, u32[]{:S(2)}) collective-permute-start(bf16[3,128,128]{2,1,0:T(8,128)(2,1)S(1)} %collective-permute-done.4.refs_4_), channel_id=1, source_target_pairs={{0,8},{8,0},{16,24},{24,16},{1,9},{9,1},{17,25},{25,17},{2,10},{10... | collective-permute-start | bytes 294920 | tf_op jit(solution)/shard_map/ppermute | solution.py:199
  17.8 1.3 %collective-permute-start.9 = (bf16[3,128,128]{2,1,0:T(8,128)(2,1)S(1)}, bf16[3,128,128]{2,1,0:T(8,128)(2,1)S(1)}, u32[]{:S(2)}, u32[]{:S(2)}) collective-permute-start(bf16[3,128,128]{2,1,0:T(8,128)(2,1)S(1)} %collective-permute-done.7.refs_7_), channel_id=1, source_target_pairs={{0,8},{8,0},{16,24},{24,16},{1,9},{9,1},{17,25},{25,17},{2,10},{10... | collective-permute-start | bytes 294920 | tf_op jit(solution)/shard_map/ppermute | solution.py:199
  18.1 1.3 %collective-permute-start.5 = (bf16[3,128,128]{2,1,0:T(8,128)(2,1)S(1)}, bf16[3,128,128]{2,1,0:T(8,128)(2,1)S(1)}, u32[]{:S(2)}, u32[]{:S(2)}) collective-permute-start(bf16[3,128,128]{2,1,0:T(8,128)(2,1)S(1)} %get-tuple-element.17.refs_3_), channel_id=1, source_target_pairs={{0,8},{8,0},{16,24},{24,16},{1,9},{9,1},{17,25},{25,17},{2,10},{10... | collective-permute-start | bytes 294920 | tf_op jit(solution)/shard_map/ppermute | solution.py:199
  24.2 4.6 %collective-permute-start.11 = (s16[272,128]{1,0:T(8,128)(2,1)S(1)}, s16[272,128]{1,0:T(8,128)(2,1)S(1)}, u32[]{:S(2)}, u32[]{:S(2)}) collective-permute-start(s16[272,128]{1,0:T(8,128)(2,1)S(1)} %shard_map.49), channel_id=1, source_target_pairs={{0,1},{1,0},{2,3},{3,2},{4,5},{5,4},{6,7},{7,6},{8,9},{9,8},{10,11... | collective-permute-start | bytes 208904 | tf_op jit(solution)/shard_map/ppermute | solution.py:199

commit v19 on v17

--- a/solution.py
+++ b/solution.py
@@ -173,9 +173,10 @@
     out_ref[RT * tile :, :] = exponents.astype(jnp.int32).astype(jnp.int16)
 
 
-def add_coded(total, coded):
-    def kernel(total_ref, coded_ref, out_ref):
+def add_coded(total, both):
+    def kernel(total_ref, both_ref, out_ref):
         tile = total_ref.shape[1]
+        coded_ref = both_ref.at[1 - position()[2]]
         exponents = coded_ref[RT * tile :, :].astype(jnp.int32).astype(jnp.float32)
         for i in range(RT):
             rows = slice(i * tile, (i + 1) * tile)
@@ -189,7 +190,7 @@
         in_specs=[VMEM] * 2,
         out_specs=VMEM,
         compiler_params=pltpu.CompilerParams(vmem_limit_bytes=8 * 1024 * 1024),
-    )(total, coded)
+    )(total, both)
 
 
 def across(block, axis, mask):
@@ -241,9 +242,10 @@
     coded = last_products(
         *last, other, 1, write_coded, jax.ShapeDtypeStruct((rows + PAD, tile), jnp.int16)
     )
-    coming = across(coded, "col", 1)
+    pairs = [[2 * z, 2 * z + 1] for z in range(lax.axis_size("col") // 2)]
+    both = lax.all_gather(coded, "col", axis_index_groups=pairs)
     mine = last_products(*last, mine, 0, write_sum, jax.ShapeDtypeStruct((rows, tile), jnp.float32))
-    return add_coded(mine, coming)
+    return add_coded(mine, both)
 
 
 def solution(mesh):

time: 24.9 us -> 25.8 us (1.036)
  blocking collectives: 0 us -> 4.99 us
  waiting for transfers between devices: 6.67 us -> 3.93 us
  starting transfers between devices: 12.3 us -> 10.9 us
    all_gather x0 -> x1, blocking collectives: none -> 4.99 us  [shards(): both = lax.all_gather(coded, 'col', axis_index_groups=pairs)]
    ppermute x9 -> x8, waiting for transfers between devices: 6.66 us -> 3.92 us  [across(): return lax.ppermute(block, axis, route)]
    ppermute x9 -> x8, starting transfers between devices: 9.25 us -> 7.89 us  [across(): return lax.ppermute(block, axis, route)]
  transfers between devices with their start and end apart: 11 -> 10, of which waited for: 7 -> 6; matrix products, arithmetic and copies ran while one was open for 4% -> 4% of each run, Pallas kernels for 16% -> 14%
where the time goes in v19:
time: 25.8 us; the launch traced here: 25.6 us
  starting transfers between devices  10.9 us (42%)
  blocking collectives  4.99 us (19%)
  Pallas kernels  4.76 us (18%)
  waiting for transfers between devices  3.93 us (15%)
  local copies, waits for them, and re-layouts  1 us (4%)
    ppermute x8, starting transfers between devices, across(): return lax.ppermute(block, axis, route)  7.89 us
    all_gather x1, blocking collectives, shards(): both = lax.all_gather(coded, 'col', axis_index_groups=pairs)  4.99 us
    ppermute x8, waiting for transfers between devices, across(): return lax.ppermute(block, axis, route)  3.92 us
    ppermute x2, starting transfers between devices, crossed(): return lax.ppermute(block, ('row', 'col'), route)  3.02 us
    pallas_call x1, Pallas kernels, find_matches(): pl.pallas_call(kernel, out_shape=jax.ShapeDtypeStruct((inner * 2 * slots,...  1.92 us
    pallas_call x1, Pallas kernels, first_products(): pl.pallas_call(kernel, out_shape=[jax.ShapeDtypeStruct((RT * tile, tile),...  1.7 us
    squeeze x1, local copies, waits for them, and re-layouts, shards(): given = lax.dynamic_index_in_dim(right, 1 - y, 0, keepdims=False)  0.99 us
    pallas_call x1, Pallas kernels, add_coded(): pl.pallas_call(kernel, out_shape=jax.ShapeDtypeStruct(total.shape, jnp.bf...  0.66 us
  transfers between devices with their start and end apart: 10, of which 6 were waited for; matrix products, arithmetic and copies ran while one was open for 4% of the time, Pallas kernels for 14%

profile of v19, /device:TPU:0, one launch (start us, length us, event | category | flops | bytes accessed | tf_op | source)
XLA Modules:
  0.0 25.6 jit_solution(14307117694458779381)
XLA Ops:
  0.0 4.0 %collective-permute-start = (bf16[6,128,128]{2,1,0:T(8,128)(2,1)}, bf16[6,128,128]{2,1,0:T(8,128)(2,1)S(1)}, u32[]{:S(2)}, u32[]{:S(2)}) collective-permute-start(bf16[6,128,128]{2,1,0:T(8,128)(2,1)} %bitcast.9), channel_id=1, source_target_pairs={{0,4},{1,5},{2,6},{3,7},{4,0},{5,1},{6,2},{7,3},{8,12},{9,13},{10,... | collective-permute-start | bytes 589832 | tf_op jit(solution)/shard_map/ppermute | solution.py:198
  4.0 1.6 %collective-permute-start.2 = (bf16[6,128,128]{2,1,0:T(8,128)(2,1)}, bf16[6,128,128]{2,1,0:T(8,128)(2,1)S(1)}, u32[]{:S(2)}, u32[]{:S(2)}) collective-permute-start(bf16[6,128,128]{2,1,0:T(8,128)(2,1)} %bitcast.10), channel_id=1, source_target_pairs={{0,2},{1,3},{2,0},{3,1},{4,6},{5,7},{6,4},{7,5},{8,10},{9,11},{10,... | collective-permute-start | bytes 589832 | tf_op jit(solution)/shard_map/ppermute | solution.py:198
  5.6 0.0 copy-start.1
  5.6 0.0 copy-start.2
  5.6 0.0 copy-start
  5.6 1.0 %dynamic-slice_bitcast_fusion = (bf16[3,128,128]{2,1,0:T(8,128)(2,1)S(1)}, bf16[3,128,128]{2,1,0:T(8,128)(2,1)S(1)}) fusion(bf16[1,1,2,3,128,128]{5,4,3,2,1,0:T(8,128)(2,1)} %param.6, s32[]{:T(128)S(6)} %select_n.8, s32[]{:T(128)S(6)} %select_n.7), kind=kLoop, calls=%fused_computation | loop fusion | bytes 393224 | tf_op jit(solution)/shard_map/jit(dynamic_index_in_dim)/squeeze | solution.py:228
  6.6 2.5 %collective-permute-start.7 = (bf16[3,128,128]{2,1,0:T(8,128)(2,1)S(1)}, bf16[3,128,128]{2,1,0:T(8,128)(2,1)S(1)}, u32[]{:S(2)}, u32[]{:S(2)}) collective-permute-start(bf16[3,128,128]{2,1,0:T(8,128)(2,1)S(1)} %get-tuple-element.21), channel_id=1, source_target_pairs={{0,17},{1,16},{2,19},{3,18},{4,21},{5,20},{6,23},{7,22},{8,25},{9,... | collective-permute-start | bytes 294920 | tf_op jit(solution)/shard_map/ppermute | solution.py:204
  9.1 0.5 %collective-permute-start.3 = (bf16[3,128,128]{2,1,0:T(8,128)(2,1)S(1)}, bf16[3,128,128]{2,1,0:T(8,128)(2,1)S(1)}, u32[]{:S(2)}, u32[]{:S(2)}) collective-permute-start(bf16[3,128,128]{2,1,0:T(8,128)(2,1)S(1)} %get-tuple-element.21), channel_id=1, source_target_pairs={{0,1},{1,0},{2,3},{3,2},{4,5},{5,4},{6,7},{7,6},{8,9},{9,8},{10,11... | collective-permute-start | bytes 294920 | tf_op jit(solution)/shard_map/ppermute | solution.py:204
  9.6 0.5 %collective-permute-start.6 = (bf16[3,128,128]{2,1,0:T(8,128)(2,1)S(1)}, bf16[3,128,128]{2,1,0:T(8,128)(2,1)S(1)}, u32[]{:S(2)}, u32[]{:S(2)}) collective-permute-start(bf16[3,128,128]{2,1,0:T(8,128)(2,1)S(1)} %get-tuple-element.17.refs_3_), channel_id=1, source_target_pairs={{0,16},{8,24},{16,0},{24,8},{1,17},{9,25},{17,1},{25,9},{2,18},{10... | collective-permute-start | bytes 294920 | tf_op jit(solution)/shard_map/ppermute | solution.py:198
  10.2 0.0 copy-done.1
  10.2 0.0 copy-done.2
  10.2 1.9 %shard_map.46.codes_ref = s32[48]{0:T(128)S(1)} custom-call(s32[6,4,8]{2,1,0:T(4,128)S(1)} %bitcast.12, s32[4,3,2,8]{3,2,1,0:T(2,128)S(1)} %bitcast.13), custom_call_target="tpu_custom_call" | custom-call | tf_op jit(solution)/shard_map/pallas_call | solution.py:46
  12.1 1.4 %collective-permute-done.refs_2_ = bf16[6,128,128]{2,1,0:T(8,128)(2,1)S(1)} collective-permute-done((bf16[6,128,128]{2,1,0:T(8,128)(2,1)}, bf16[6,128,128]{2,1,0:T(8,128)(2,1)S(1)}, u32[]{:S(2)}, u32[]{:S(2)}) %collective-permute-start) | collective-permute-done | bytes 196640 | tf_op jit(solution)/shard_map/ppermute | solution.py:198
  13.5 0.7 %collective-permute-start.1 = (bf16[6,128,128]{2,1,0:T(8,128)(2,1)S(1)}, bf16[6,128,128]{2,1,0:T(8,128)(2,1)S(1)}, u32[]{:S(2)}, u32[]{:S(2)}) collective-permute-start(bf16[6,128,128]{2,1,0:T(8,128)(2,1)S(1)} %collective-permute-done.refs_2_), channel_id=1, source_target_pairs={{0,2},{1,3},{2,0},{3,1},{4,6},{5,7},{6,4},{7,5},{8,10},{9,11},{10,... | collective-permute-start | bytes 589832 | tf_op jit(solution)/shard_map/ppermute | solution.py:198
  14.2 0.0 collective-permute-done.7.refs_8_
  14.2 0.0 collective-permute-start.9
  14.2 0.0 collective-permute-done.3.refs_4_
  14.2 0.5 %collective-permute-start.5 = (bf16[3,128,128]{2,1,0:T(8,128)(2,1)S(1)}, bf16[3,128,128]{2,1,0:T(8,128)(2,1)S(1)}, u32[]{:S(2)}, u32[]{:S(2)}) collective-permute-start(bf16[3,128,128]{2,1,0:T(8,128)(2,1)S(1)} %collective-permute-done.3.refs_4_), channel_id=1, source_target_pairs={{0,8},{8,0},{16,24},{24,16},{1,9},{9,1},{17,25},{25,17},{2,10},{10... | collective-permute-start | bytes 294920 | tf_op jit(solution)/shard_map/ppermute | solution.py:198
  14.7 0.0 collective-permute-done.6.refs_7_
  14.7 0.1 collective-permute-start.8
  14.8 0.0 collective-permute-done.2.refs_1_
  14.8 0.4 %collective-permute-start.4 = (bf16[3,128,128]{2,1,0:T(8,128)(2,1)S(1)}, bf16[3,128,128]{2,1,0:T(8,128)(2,1)S(1)}, u32[]{:S(2)}, u32[]{:S(2)}) collective-permute-start(bf16[3,128,128]{2,1,0:T(8,128)(2,1)S(1)} %get-tuple-element.17.refs_3_), channel_id=1, source_target_pairs={{0,8},{8,0},{16,24},{24,16},{1,9},{9,1},{17,25},{25,17},{2,10},{10... | collective-permute-start | bytes 294920 | tf_op jit(solution)/shard_map/ppermute | solution.py:198
  15.2 0.3 %collective-permute-done.9.refs_10_ = bf16[3,128,128]{2,1,0:T(8,128)(2,1)S(1)} collective-permute-done((bf16[3,128,128]{2,1,0:T(8,128)(2,1)S(1)}, bf16[3,128,128]{2,1,0:T(8,128)(2,1)S(1)}, u32[]{:S(2)}, u32[]{:S(2)}) %collective-permute-start.9) | collective-permute-done | bytes 98336 | tf_op jit(solution)/shard_map/ppermute | solution.py:198
  15.5 0.2 collective-permute-done.5.refs_6_
  15.7 0.4 %collective-permute-done.8.refs_9_ = bf16[3,128,128]{2,1,0:T(8,128)(2,1)S(1)} collective-permute-done((bf16[3,128,128]{2,1,0:T(8,128)(2,1)S(1)}, bf16[3,128,128]{2,1,0:T(8,128)(2,1)S(1)}, u32[]{:S(2)}, u32[]{:S(2)}) %collective-permute-start.8) | collective-permute-done | bytes 98336 | tf_op jit(solution)/shard_map/ppermute | solution.py:198
  16.0 0.2 collective-permute-done.4.refs_5_
  16.2 0.0 copy-done
  16.2 1.7 %shard_map.47 = (f32[256,128]{1,0:T(8,128)S(1)}, f32[256,128]{1,0:T(8,128)S(1)}, bf16[2,768,256]{2,1,0:T(8,128)(2,1)S(1)}) custom-call(s32[48]{0:T(128)S(1)} %shard_map.46.codes_ref, bf16[6,128,128]{2,1,0:T(8,128)(2,1)S(1)} %bitcast.11, bf16[6,128,128]{2,1,0:T(8,128)(2,1)S(1)} %collective-permute-done.2.refs_1_, ...), custom_call_target="tpu_custom_call" | custom-call | flops 201326592 | bytes 786432 | tf_op jit(solution)/shard_map/pallas_call | solution.py:113
  17.9 1.6 %collective-permute-done.1.left_ref = bf16[6,128,128]{2,1,0:T(8,128)(2,1)S(1)} collective-permute-done((bf16[6,128,128]{2,1,0:T(8,128)(2,1)S(1)}, bf16[6,128,128]{2,1,0:T(8,128)(2,1)S(1)}, u32[]{:S(2)}, u32[]{:S(2)}) %collective-permute-start.1) | collective-permute-done | bytes 196640 | tf_op jit(solution)/shard_map/ppermute | solution.py:198
  19.5 0.3 %shard_map.49 = s16[272,128]{1,0:T(8,128)(2,1)S(1)} custom-call(bf16[6,128,128]{2,1,0:T(8,128)(2,1)S(1)} %collective-permute-done.1.left_ref, bf16[2,768,256]{2,1,0:T(8,128)(2,1)S(1)} %get-tuple-element.18.right_ref, f32[256,128]{1,0:T(8,128)S(1)} %get-tuple-element.20.total_ref), custom_call_target="tpu_custom_call" | custom-call | flops 25165824 | bytes 196608 | tf_op jit(solution)/shard_map/pallas_call | solution.py:146
  19.8 5.0 %all-gather = s16[544,128]{1,0:T(8,128)(2,1)S(1)} all-gather(s16[272,128]{1,0:T(8,128)(2,1)S(1)} %shard_map.49), channel_id=2, replica_groups={{0,1},{2,3},{4,5},{6,7},{8,9},{10,11},{12,13},{14,15},{16,17},{18,19},{..., dimensions={0}, use_global_device_ids=true | all-gather | bytes 208896 | tf_op jit(solution)/shard_map/all_gather | solution.py:246
  24.8 0.2 shard_map.48.total_ref
  25.0 0.7 %shard_map.50 = bf16[256,128]{1,0:T(8,128)(2,1)} custom-call(f32[256,128]{1,0:T(8,128)S(1)} %shard_map.48.total_ref, s16[2,272,128]{2,1,0:T(8,128)(2,1)S(1)} %bitcast.8), custom_call_target="tpu_custom_call" | custom-call | tf_op jit(solution)/shard_map/pallas_call | solution.py:187
Async XLA Ops:
  0.0 13.5 %collective-permute-start = (bf16[6,128,128]{2,1,0:T(8,128)(2,1)}, bf16[6,128,128]{2,1,0:T(8,128)(2,1)S(1)}, u32[]{:S(2)}, u32[]{:S(2)}) collective-permute-start(bf16[6,128,128]{2,1,0:T(8,128)(2,1)} %bitcast.9), channel_id=1, source_target_pairs={{0,4},{1,5},{2,6},{3,7},{4,0},{5,1},{6,2},{7,3},{8,12},{9,13},{10,... | collective-permute-start | bytes 589832 | tf_op jit(solution)/shard_map/ppermute | solution.py:198
  4.0 10.7 %collective-permute-start.2 = (bf16[6,128,128]{2,1,0:T(8,128)(2,1)}, bf16[6,128,128]{2,1,0:T(8,128)(2,1)S(1)}, u32[]{:S(2)}, u32[]{:S(2)}) collective-permute-start(bf16[6,128,128]{2,1,0:T(8,128)(2,1)} %bitcast.10), channel_id=1, source_target_pairs={{0,2},{1,3},{2,0},{3,1},{4,6},{5,7},{6,4},{7,5},{8,10},{9,11},{10,... | collective-permute-start | bytes 589832 | tf_op jit(solution)/shard_map/ppermute | solution.py:198
  5.6 4.6 %copy-start.1 = (s32[4,8,6]{1,0,2:T(4,128)S(1)}, s32[4,8,6]{1,0,2:T(4,128)}, u32[]{:S(2)}) copy-start(s32[4,8,6]{1,0,2:T(4,128)} %param.5) | copy-start | bytes 2308
  5.6 4.6 %copy-start.2 = (s32[4,8,2,3]{1,2,3,0:T(2,128)S(1)}, s32[4,8,2,3]{1,2,3,0:T(2,128)}, u32[]{:S(2)}) copy-start(s32[4,8,2,3]{1,2,3,0:T(2,128)} %param.7) | copy-start | bytes 2308
  5.6 10.6 %copy-start = (bf16[1,1,6,128,128]{4,3,2,1,0:T(8,128)(2,1)S(1)}, bf16[1,1,6,128,128]{4,3,2,1,0:T(8,128)(2,1)}, u32[]{:S(2)}) copy-start(bf16[1,1,6,128,128]{4,3,2,1,0:T(8,128)(2,1)} %param.4) | copy-start | bytes 589828
  6.6 7.6 %collective-permute-start.7 = (bf16[3,128,128]{2,1,0:T(8,128)(2,1)S(1)}, bf16[3,128,128]{2,1,0:T(8,128)(2,1)S(1)}, u32[]{:S(2)}, u32[]{:S(2)}) collective-permute-start(bf16[3,128,128]{2,1,0:T(8,128)(2,1)S(1)} %get-tuple-element.21), channel_id=1, source_target_pairs={{0,17},{1,16},{2,19},{3,18},{4,21},{5,20},{6,23},{7,22},{8,25},{9,... | collective-permute-start | bytes 294920 | tf_op jit(solution)/shard_map/ppermute | solution.py:204
  9.1 5.1 %collective-permute-start.3 = (bf16[3,128,128]{2,1,0:T(8,128)(2,1)S(1)}, bf16[3,128,128]{2,1,0:T(8,128)(2,1)S(1)}, u32[]{:S(2)}, u32[]{:S(2)}) collective-permute-start(bf16[3,128,128]{2,1,0:T(8,128)(2,1)S(1)} %get-tuple-element.21), channel_id=1, source_target_pairs={{0,1},{1,0},{2,3},{3,2},{4,5},{5,4},{6,7},{7,6},{8,9},{9,8},{10,11... | collective-permute-start | bytes 294920 | tf_op jit(solution)/shard_map/ppermute | solution.py:204
  9.6 5.1 %collective-permute-start.6 = (bf16[3,128,128]{2,1,0:T(8,128)(2,1)S(1)}, bf16[3,128,128]{2,1,0:T(8,128)(2,1)S(1)}, u32[]{:S(2)}, u32[]{:S(2)}) collective-permute-start(bf16[3,128,128]{2,1,0:T(8,128)(2,1)S(1)} %get-tuple-element.17.refs_3_), channel_id=1, source_target_pairs={{0,16},{8,24},{16,0},{24,8},{1,17},{9,25},{17,1},{25,9},{2,18},{10... | collective-permute-start | bytes 294920 | tf_op jit(solution)/shard_map/ppermute | solution.py:198
  13.5 6.0 %collective-permute-start.1 = (bf16[6,128,128]{2,1,0:T(8,128)(2,1)S(1)}, bf16[6,128,128]{2,1,0:T(8,128)(2,1)S(1)}, u32[]{:S(2)}, u32[]{:S(2)}) collective-permute-start(bf16[6,128,128]{2,1,0:T(8,128)(2,1)S(1)} %collective-permute-done.refs_2_), channel_id=1, source_target_pairs={{0,2},{1,3},{2,0},{3,1},{4,6},{5,7},{6,4},{7,5},{8,10},{9,11},{10,... | collective-permute-start | bytes 589832 | tf_op jit(solution)/shard_map/ppermute | solution.py:198
  14.2 1.3 %collective-permute-start.9 = (bf16[3,128,128]{2,1,0:T(8,128)(2,1)S(1)}, bf16[3,128,128]{2,1,0:T(8,128)(2,1)S(1)}, u32[]{:S(2)}, u32[]{:S(2)}) collective-permute-start(bf16[3,128,128]{2,1,0:T(8,128)(2,1)S(1)} %collective-permute-done.7.refs_8_), channel_id=1, source_target_pairs={{0,8},{8,0},{16,24},{24,16},{1,9},{9,1},{17,25},{25,17},{2,10},{10... | collective-permute-start | bytes 294920 | tf_op jit(solution)/shard_map/ppermute | solution.py:198
  14.2 1.5 %collective-permute-start.5 = (bf16[3,128,128]{2,1,0:T(8,128)(2,1)S(1)}, bf16[3,128,128]{2,1,0:T(8,128)(2,1)S(1)}, u32[]{:S(2)}, u32[]{:S(2)}) collective-permute-start(bf16[3,128,128]{2,1,0:T(8,128)(2,1)S(1)} %collective-permute-done.3.refs_4_), channel_id=1, source_target_pairs={{0,8},{8,0},{16,24},{24,16},{1,9},{9,1},{17,25},{25,17},{2,10},{10... | collective-permute-start | bytes 294920 | tf_op jit(solution)/shard_map/ppermute | solution.py:198
  14.7 1.3 %collective-permute-start.8 = (bf16[3,128,128]{2,1,0:T(8,128)(2,1)S(1)}, bf16[3,128,128]{2,1,0:T(8,128)(2,1)S(1)}, u32[]{:S(2)}, u32[]{:S(2)}) collective-permute-start(bf16[3,128,128]{2,1,0:T(8,128)(2,1)S(1)} %collective-permute-done.6.refs_7_), channel_id=1, source_target_pairs={{0,8},{8,0},{16,24},{24,16},{1,9},{9,1},{17,25},{25,17},{2,10},{10... | collective-permute-start | bytes 294920 | tf_op jit(solution)/shard_map/ppermute | solution.py:198
  14.8 1.4 %collective-permute-start.4 = (bf16[3,128,128]{2,1,0:T(8,128)(2,1)S(1)}, bf16[3,128,128]{2,1,0:T(8,128)(2,1)S(1)}, u32[]{:S(2)}, u32[]{:S(2)}) collective-permute-start(bf16[3,128,128]{2,1,0:T(8,128)(2,1)S(1)} %get-tuple-element.17.refs_3_), channel_id=1, source_target_pairs={{0,8},{8,0},{16,24},{24,16},{1,9},{9,1},{17,25},{25,17},{2,10},{10... | collective-permute-start | bytes 294920 | tf_op jit(solution)/shard_map/ppermute | solution.py:198

commit v20 on v17

--- a/solution.py
+++ b/solution.py
@@ -70,7 +70,7 @@
             )
 
 
-def first_products(codes, lefts, rights, slots):
+def first_products(codes, lefts, last, rights, slots):
     parts = [(s, part) for s, block in lefts for part in block]
     count = len(parts)
     inner = len(rights) // 2
@@ -84,13 +84,13 @@
         for t in range(inner):
             for side in range(2):
                 held[row ^ t, side] = right_refs[2 * t + side][...]
-        at = z ^ (inner - 1)
+        at = z ^ last
         last_ref[...] = jnp.zeros_like(last_ref)
         for side in range(2):
 
             @pl.loop(0, slots)
             def _(slot):
-                code = codes_ref[((inner - 1) * 2 + side) * slots + slot]
+                code = codes_ref[(last * 2 + side) * slots + slot]
 
                 @pl.when(code > 0)
                 def _():
@@ -204,17 +204,20 @@
 
 
 def gather(block, beside, place):
-    distance = lax.axis_size("col") // 4
-    steps = [distance >> n for n in range(distance.bit_length())]
+    places = lax.axis_size("col") // 2
+    steps = [places >> n for n in range(1, places.bit_length() - 2)] + [3, 1]
     later, _ = lax.optimization_barrier((block, place))
     came = [across(later if d == 1 else block, "col", 2 * d) for d in steps]
     came[:-1], beside = lax.optimization_barrier((came[:-1], beside))
     blocks = {0: block, **dict(zip(steps, came))}
+    spanned = [0]
     for d in steps:
-        for s in sorted(blocks):
-            if s ^ d not in blocks and s & (d - 1) == 0:
-                blocks[s ^ d] = across(blocks[s], "col", 2 * d)
-    return [(s, (blocks[s],)) for s in range(len(blocks))], beside
+        for s in spanned[1:]:
+            blocks[s ^ d] = across(blocks[s], "col", 2 * d)
+        spanned += [s ^ d for s in spanned]
+    last = spanned[-1]
+    order = [s for s in sorted(blocks) if s != last] + [last]
+    return [(s, (blocks[s],)) for s in order], beside
 
 
 def shards(left_tiles, left_index, right_tiles, right_index):
@@ -235,7 +238,7 @@
             lefts[1] = (1, near)
         rights += pair + [across(half, "row", 1) for half in pair]
 
-    mine, other, right_last = first_products(codes, lefts[:-1], rights, slots)
+    mine, other, right_last = first_products(codes, lefts[:-1], lefts[-1][0], rights, slots)
     last = (lefts[-1][1], right_last)
     rows, tile = mine.shape
     coded = last_products(

time: 24.9 us -> 24.1 us (0.968)
  waiting for transfers between devices: 6.67 us -> 4.31 us
  starting transfers between devices: 12.3 us -> 13.7 us
    ppermute x9, waiting for transfers between devices: 6.66 us -> 4.3 us  [across(): return lax.ppermute(block, axis, route)]
    ppermute x9, starting transfers between devices: 9.25 us -> 10.7 us  [across(): return lax.ppermute(block, axis, route)]
  transfers between devices with their start and end apart: 11 -> 11, of which waited for: 7 -> 6; matrix products, arithmetic and copies ran while one was open for 4% -> 4% of each run, Pallas kernels for 16% -> 17%
where the time goes in v20:
time: 24.1 us; the launch traced here: 24 us
  starting transfers between devices  13.7 us (57%)
  Pallas kernels  4.87 us (20%)
  waiting for transfers between devices  4.31 us (18%)
  local copies, waits for them, and re-layouts  1.01 us (4%)
    ppermute x9, starting transfers between devices, across(): return lax.ppermute(block, axis, route)  10.7 us
    ppermute x9, waiting for transfers between devices, across(): return lax.ppermute(block, axis, route)  4.3 us
    ppermute x2, starting transfers between devices, crossed(): return lax.ppermute(block, ('row', 'col'), route)  3.02 us
    pallas_call x1, Pallas kernels, find_matches(): pl.pallas_call(kernel, out_shape=jax.ShapeDtypeStruct((inner * 2 * slots,...  1.92 us
    pallas_call x1, Pallas kernels, first_products(): pl.pallas_call(kernel, out_shape=[jax.ShapeDtypeStruct((RT * tile, tile),...  1.83 us
    squeeze x1, local copies, waits for them, and re-layouts, shards(): given = lax.dynamic_index_in_dim(right, 1 - y, 0, keepdims=False)  1 us
    pallas_call x1, Pallas kernels, add_coded(): pl.pallas_call(kernel, out_shape=jax.ShapeDtypeStruct(total.shape, jnp.bf...  0.65 us
  transfers between devices with their start and end apart: 11, of which 6 were waited for; matrix products, arithmetic and copies ran while one was open for 4% of the time, Pallas kernels for 17%

profile of v20, /device:TPU:0, one launch (start us, length us, event | category | flops | bytes accessed | tf_op | source)
XLA Modules:
  0.0 24.0 jit_solution(5840065006522868405)
XLA Ops:
  0.0 5.0 %collective-permute-start = (bf16[6,128,128]{2,1,0:T(8,128)(2,1)}, bf16[6,128,128]{2,1,0:T(8,128)(2,1)S(1)}, u32[]{:S(2)}, u32[]{:S(2)}) collective-permute-start(bf16[6,128,128]{2,1,0:T(8,128)(2,1)} %bitcast.7), channel_id=1, source_target_pairs={{0,6},{1,7},{2,4},{3,5},{4,2},{5,3},{6,0},{7,1},{8,14},{9,15},{10,... | collective-permute-start | bytes 589832 | tf_op jit(solution)/shard_map/ppermute | solution.py:197
  5.0 0.0 collective-permute-start.2
  5.1 0.0 copy-start.1
  5.1 0.0 copy-start.2
  5.1 0.0 copy-start
  5.1 1.0 %dynamic-slice_bitcast_fusion = (bf16[3,128,128]{2,1,0:T(8,128)(2,1)S(1)}, bf16[3,128,128]{2,1,0:T(8,128)(2,1)S(1)}) fusion(bf16[1,1,2,3,128,128]{5,4,3,2,1,0:T(8,128)(2,1)} %param.6, s32[]{:T(128)S(6)} %select_n.8, s32[]{:T(128)S(6)} %select_n.7), kind=kLoop, calls=%fused_computation | loop fusion | bytes 393224 | tf_op jit(solution)/shard_map/jit(dynamic_index_in_dim)/squeeze | solution.py:230
  6.1 2.5 %collective-permute-start.7 = (bf16[3,128,128]{2,1,0:T(8,128)(2,1)S(1)}, bf16[3,128,128]{2,1,0:T(8,128)(2,1)S(1)}, u32[]{:S(2)}, u32[]{:S(2)}) collective-permute-start(bf16[3,128,128]{2,1,0:T(8,128)(2,1)S(1)} %get-tuple-element.21), channel_id=1, source_target_pairs={{0,17},{1,16},{2,19},{3,18},{4,21},{5,20},{6,23},{7,22},{8,25},{9,... | collective-permute-start | bytes 294920 | tf_op jit(solution)/shard_map/ppermute | solution.py:203
  8.6 0.5 %collective-permute-start.3 = (bf16[3,128,128]{2,1,0:T(8,128)(2,1)S(1)}, bf16[3,128,128]{2,1,0:T(8,128)(2,1)S(1)}, u32[]{:S(2)}, u32[]{:S(2)}) collective-permute-start(bf16[3,128,128]{2,1,0:T(8,128)(2,1)S(1)} %get-tuple-element.21), channel_id=1, source_target_pairs={{0,1},{1,0},{2,3},{3,2},{4,5},{5,4},{6,7},{7,6},{8,9},{9,8},{10,11... | collective-permute-start | bytes 294920 | tf_op jit(solution)/shard_map/ppermute | solution.py:203
  9.1 0.5 %collective-permute-start.6 = (bf16[3,128,128]{2,1,0:T(8,128)(2,1)S(1)}, bf16[3,128,128]{2,1,0:T(8,128)(2,1)S(1)}, u32[]{:S(2)}, u32[]{:S(2)}) collective-permute-start(bf16[3,128,128]{2,1,0:T(8,128)(2,1)S(1)} %get-tuple-element.17.refs_3_), channel_id=1, source_target_pairs={{0,16},{8,24},{16,0},{24,8},{1,17},{9,25},{17,1},{25,9},{2,18},{10... | collective-permute-start | bytes 294920 | tf_op jit(solution)/shard_map/ppermute | solution.py:197
  9.6 0.0 copy-done.1
  9.6 0.0 copy-done.2
  9.6 1.9 %shard_map.46.codes_ref = s32[48]{0:T(128)S(1)} custom-call(s32[6,4,8]{2,1,0:T(4,128)S(1)} %bitcast.10, s32[4,3,2,8]{3,2,1,0:T(2,128)S(1)} %bitcast.11), custom_call_target="tpu_custom_call" | custom-call | tf_op jit(solution)/shard_map/pallas_call | solution.py:46
  11.6 0.0 collective-permute-done.refs_2_
  11.6 2.5 %collective-permute-start.1 = (bf16[6,128,128]{2,1,0:T(8,128)(2,1)S(1)}, bf16[6,128,128]{2,1,0:T(8,128)(2,1)S(1)}, u32[]{:S(2)}, u32[]{:S(2)}) collective-permute-start(bf16[6,128,128]{2,1,0:T(8,128)(2,1)S(1)} %collective-permute-done.refs_2_), channel_id=1, source_target_pairs={{0,2},{1,3},{2,0},{3,1},{4,6},{5,7},{6,4},{7,5},{8,10},{9,11},{10,... | collective-permute-start | bytes 589832 | tf_op jit(solution)/shard_map/ppermute | solution.py:197
  14.1 0.0 collective-permute-done.7.refs_8_
  14.1 0.0 collective-permute-start.9
  14.1 0.0 collective-permute-done.3.refs_4_
  14.1 0.5 %collective-permute-start.5 = (bf16[3,128,128]{2,1,0:T(8,128)(2,1)S(1)}, bf16[3,128,128]{2,1,0:T(8,128)(2,1)S(1)}, u32[]{:S(2)}, u32[]{:S(2)}) collective-permute-start(bf16[3,128,128]{2,1,0:T(8,128)(2,1)S(1)} %collective-permute-done.3.refs_4_), channel_id=1, source_target_pairs={{0,8},{8,0},{16,24},{24,16},{1,9},{9,1},{17,25},{25,17},{2,10},{10... | collective-permute-start | bytes 294920 | tf_op jit(solution)/shard_map/ppermute | solution.py:197
  14.6 0.0 collective-permute-done.6.refs_7_
  14.6 0.1 collective-permute-start.8
  14.7 0.0 collective-permute-done.2.refs_1_
  14.7 0.4 %collective-permute-start.4 = (bf16[3,128,128]{2,1,0:T(8,128)(2,1)S(1)}, bf16[3,128,128]{2,1,0:T(8,128)(2,1)S(1)}, u32[]{:S(2)}, u32[]{:S(2)}) collective-permute-start(bf16[3,128,128]{2,1,0:T(8,128)(2,1)S(1)} %get-tuple-element.17.refs_3_), channel_id=1, source_target_pairs={{0,8},{8,0},{16,24},{24,16},{1,9},{9,1},{17,25},{25,17},{2,10},{10... | collective-permute-start | bytes 294920 | tf_op jit(solution)/shard_map/ppermute | solution.py:197
  15.1 0.3 %collective-permute-done.9.refs_10_ = bf16[3,128,128]{2,1,0:T(8,128)(2,1)S(1)} collective-permute-done((bf16[3,128,128]{2,1,0:T(8,128)(2,1)S(1)}, bf16[3,128,128]{2,1,0:T(8,128)(2,1)S(1)}, u32[]{:S(2)}, u32[]{:S(2)}) %collective-permute-start.9) | collective-permute-done | bytes 98336 | tf_op jit(solution)/shard_map/ppermute | solution.py:197
  15.4 0.2 collective-permute-done.5.refs_6_
  15.6 0.4 %collective-permute-done.8.refs_9_ = bf16[3,128,128]{2,1,0:T(8,128)(2,1)S(1)} collective-permute-done((bf16[3,128,128]{2,1,0:T(8,128)(2,1)S(1)}, bf16[3,128,128]{2,1,0:T(8,128)(2,1)S(1)}, u32[]{:S(2)}, u32[]{:S(2)}) %collective-permute-start.8) | collective-permute-done | bytes 98336 | tf_op jit(solution)/shard_map/ppermute | solution.py:197
  15.9 0.2 collective-permute-done.4.refs_5_
  16.1 0.0 copy-done
  16.1 1.8 %shard_map.47 = (f32[256,128]{1,0:T(8,128)S(1)}, f32[256,128]{1,0:T(8,128)S(1)}, bf16[2,768,256]{2,1,0:T(8,128)(2,1)S(1)}) custom-call(s32[48]{0:T(128)S(1)} %shard_map.46.codes_ref, bf16[6,128,128]{2,1,0:T(8,128)(2,1)S(1)} %bitcast.9, bf16[6,128,128]{2,1,0:T(8,128)(2,1)S(1)} %collective-permute-done.2.refs_1_, ...), custom_call_target="tpu_custom_call" | custom-call | flops 201326592 | bytes 786432 | tf_op jit(solution)/shard_map/pallas_call | solution.py:113
  17.9 0.8 %collective-permute-done.1.left_ref = bf16[6,128,128]{2,1,0:T(8,128)(2,1)S(1)} collective-permute-done((bf16[6,128,128]{2,1,0:T(8,128)(2,1)S(1)}, bf16[6,128,128]{2,1,0:T(8,128)(2,1)S(1)}, u32[]{:S(2)}, u32[]{:S(2)}) %collective-permute-start.1) | collective-permute-done | bytes 196640 | tf_op jit(solution)/shard_map/ppermute | solution.py:197
  18.7 0.3 %shard_map.49 = s16[272,128]{1,0:T(8,128)(2,1)S(1)} custom-call(bf16[6,128,128]{2,1,0:T(8,128)(2,1)S(1)} %collective-permute-done.1.left_ref, bf16[2,768,256]{2,1,0:T(8,128)(2,1)S(1)} %get-tuple-element.18.right_ref, f32[256,128]{1,0:T(8,128)S(1)} %get-tuple-element.20.total_ref), custom_call_target="tpu_custom_call" | custom-call | flops 25165824 | bytes 196608 | tf_op jit(solution)/shard_map/pallas_call | solution.py:146
  19.0 1.6 %collective-permute-start.10 = (s16[272,128]{1,0:T(8,128)(2,1)S(1)}, s16[272,128]{1,0:T(8,128)(2,1)S(1)}, u32[]{:S(2)}, u32[]{:S(2)}) collective-permute-start(s16[272,128]{1,0:T(8,128)(2,1)S(1)} %shard_map.49), channel_id=1, source_target_pairs={{0,1},{1,0},{2,3},{3,2},{4,5},{5,4},{6,7},{7,6},{8,9},{9,8},{10,11... | collective-permute-start | bytes 208904 | tf_op jit(solution)/shard_map/ppermute | solution.py:197
  20.5 0.2 shard_map.48.total_ref
  20.8 2.6 %collective-permute-done.10.coded_ref = s16[272,128]{1,0:T(8,128)(2,1)S(1)} collective-permute-done((s16[272,128]{1,0:T(8,128)(2,1)S(1)}, s16[272,128]{1,0:T(8,128)(2,1)S(1)}, u32[]{:S(2)}, u32[]{:S(2)}) %collective-permute-start.10) | collective-permute-done | bytes 69664 | tf_op jit(solution)/shard_map/ppermute | solution.py:197
  23.3 0.7 %shard_map.50 = bf16[256,128]{1,0:T(8,128)(2,1)} custom-call(f32[256,128]{1,0:T(8,128)S(1)} %shard_map.48.total_ref, s16[272,128]{1,0:T(8,128)(2,1)S(1)} %collective-permute-done.10.coded_ref), custom_call_target="tpu_custom_call" | custom-call | tf_op jit(solution)/shard_map/pallas_call | solution.py:186
Async XLA Ops:
  0.0 11.6 %collective-permute-start = (bf16[6,128,128]{2,1,0:T(8,128)(2,1)}, bf16[6,128,128]{2,1,0:T(8,128)(2,1)S(1)}, u32[]{:S(2)}, u32[]{:S(2)}) collective-permute-start(bf16[6,128,128]{2,1,0:T(8,128)(2,1)} %bitcast.7), channel_id=1, source_target_pairs={{0,6},{1,7},{2,4},{3,5},{4,2},{5,3},{6,0},{7,1},{8,14},{9,15},{10,... | collective-permute-start | bytes 589832 | tf_op jit(solution)/shard_map/ppermute | solution.py:197
  5.0 9.6 %collective-permute-start.2 = (bf16[6,128,128]{2,1,0:T(8,128)(2,1)}, bf16[6,128,128]{2,1,0:T(8,128)(2,1)S(1)}, u32[]{:S(2)}, u32[]{:S(2)}) collective-permute-start(bf16[6,128,128]{2,1,0:T(8,128)(2,1)} %bitcast.8), channel_id=1, source_target_pairs={{0,2},{1,3},{2,0},{3,1},{4,6},{5,7},{6,4},{7,5},{8,10},{9,11},{10,... | collective-permute-start | bytes 589832 | tf_op jit(solution)/shard_map/ppermute | solution.py:197
  5.1 4.6 %copy-start.1 = (s32[4,8,6]{1,0,2:T(4,128)S(1)}, s32[4,8,6]{1,0,2:T(4,128)}, u32[]{:S(2)}) copy-start(s32[4,8,6]{1,0,2:T(4,128)} %param.5) | copy-start | bytes 2308
  5.1 4.6 %copy-start.2 = (s32[4,8,2,3]{1,2,3,0:T(2,128)S(1)}, s32[4,8,2,3]{1,2,3,0:T(2,128)}, u32[]{:S(2)}) copy-start(s32[4,8,2,3]{1,2,3,0:T(2,128)} %param.7) | copy-start | bytes 2308
  5.1 11.0 %copy-start = (bf16[1,1,6,128,128]{4,3,2,1,0:T(8,128)(2,1)S(1)}, bf16[1,1,6,128,128]{4,3,2,1,0:T(8,128)(2,1)}, u32[]{:S(2)}) copy-start(bf16[1,1,6,128,128]{4,3,2,1,0:T(8,128)(2,1)} %param.4) | copy-start | bytes 589828
  6.1 8.0 %collective-permute-start.7 = (bf16[3,128,128]{2,1,0:T(8,128)(2,1)S(1)}, bf16[3,128,128]{2,1,0:T(8,128)(2,1)S(1)}, u32[]{:S(2)}, u32[]{:S(2)}) collective-permute-start(bf16[3,128,128]{2,1,0:T(8,128)(2,1)S(1)} %get-tuple-element.21), channel_id=1, source_target_pairs={{0,17},{1,16},{2,19},{3,18},{4,21},{5,20},{6,23},{7,22},{8,25},{9,... | collective-permute-start | bytes 294920 | tf_op jit(solution)/shard_map/ppermute | solution.py:203
  8.6 5.5 %collective-permute-start.3 = (bf16[3,128,128]{2,1,0:T(8,128)(2,1)S(1)}, bf16[3,128,128]{2,1,0:T(8,128)(2,1)S(1)}, u32[]{:S(2)}, u32[]{:S(2)}) collective-permute-start(bf16[3,128,128]{2,1,0:T(8,128)(2,1)S(1)} %get-tuple-element.21), channel_id=1, source_target_pairs={{0,1},{1,0},{2,3},{3,2},{4,5},{5,4},{6,7},{7,6},{8,9},{9,8},{10,11... | collective-permute-start | bytes 294920 | tf_op jit(solution)/shard_map/ppermute | solution.py:203
  9.1 5.5 %collective-permute-start.6 = (bf16[3,128,128]{2,1,0:T(8,128)(2,1)S(1)}, bf16[3,128,128]{2,1,0:T(8,128)(2,1)S(1)}, u32[]{:S(2)}, u32[]{:S(2)}) collective-permute-start(bf16[3,128,128]{2,1,0:T(8,128)(2,1)S(1)} %get-tuple-element.17.refs_3_), channel_id=1, source_target_pairs={{0,16},{8,24},{16,0},{24,8},{1,17},{9,25},{17,1},{25,9},{2,18},{10... | collective-permute-start | bytes 294920 | tf_op jit(solution)/shard_map/ppermute | solution.py:197
  11.6 7.1 %collective-permute-start.1 = (bf16[6,128,128]{2,1,0:T(8,128)(2,1)S(1)}, bf16[6,128,128]{2,1,0:T(8,128)(2,1)S(1)}, u32[]{:S(2)}, u32[]{:S(2)}) collective-permute-start(bf16[6,128,128]{2,1,0:T(8,128)(2,1)S(1)} %collective-permute-done.refs_2_), channel_id=1, source_target_pairs={{0,2},{1,3},{2,0},{3,1},{4,6},{5,7},{6,4},{7,5},{8,10},{9,11},{10,... | collective-permute-start | bytes 589832 | tf_op jit(solution)/shard_map/ppermute | solution.py:197
  14.1 1.3 %collective-permute-start.9 = (bf16[3,128,128]{2,1,0:T(8,128)(2,1)S(1)}, bf16[3,128,128]{2,1,0:T(8,128)(2,1)S(1)}, u32[]{:S(2)}, u32[]{:S(2)}) collective-permute-start(bf16[3,128,128]{2,1,0:T(8,128)(2,1)S(1)} %collective-permute-done.7.refs_8_), channel_id=1, source_target_pairs={{0,8},{8,0},{16,24},{24,16},{1,9},{9,1},{17,25},{25,17},{2,10},{10... | collective-permute-start | bytes 294920 | tf_op jit(solution)/shard_map/ppermute | solution.py:197
  14.1 1.5 %collective-permute-start.5 = (bf16[3,128,128]{2,1,0:T(8,128)(2,1)S(1)}, bf16[3,128,128]{2,1,0:T(8,128)(2,1)S(1)}, u32[]{:S(2)}, u32[]{:S(2)}) collective-permute-start(bf16[3,128,128]{2,1,0:T(8,128)(2,1)S(1)} %collective-permute-done.3.refs_4_), channel_id=1, source_target_pairs={{0,8},{8,0},{16,24},{24,16},{1,9},{9,1},{17,25},{25,17},{2,10},{10... | collective-permute-start | bytes 294920 | tf_op jit(solution)/shard_map/ppermute | solution.py:197
  14.6 1.3 %collective-permute-start.8 = (bf16[3,128,128]{2,1,0:T(8,128)(2,1)S(1)}, bf16[3,128,128]{2,1,0:T(8,128)(2,1)S(1)}, u32[]{:S(2)}, u32[]{:S(2)}) collective-permute-start(bf16[3,128,128]{2,1,0:T(8,128)(2,1)S(1)} %collective-permute-done.6.refs_7_), channel_id=1, source_target_pairs={{0,8},{8,0},{16,24},{24,16},{1,9},{9,1},{17,25},{25,17},{2,10},{10... | collective-permute-start | bytes 294920 | tf_op jit(solution)/shard_map/ppermute | solution.py:197
  14.7 1.4 %collective-permute-start.4 = (bf16[3,128,128]{2,1,0:T(8,128)(2,1)S(1)}, bf16[3,128,128]{2,1,0:T(8,128)(2,1)S(1)}, u32[]{:S(2)}, u32[]{:S(2)}) collective-permute-start(bf16[3,128,128]{2,1,0:T(8,128)(2,1)S(1)} %get-tuple-element.17.refs_3_), channel_id=1, source_target_pairs={{0,8},{8,0},{16,24},{24,16},{1,9},{9,1},{17,25},{25,17},{2,10},{10... | collective-permute-start | bytes 294920 | tf_op jit(solution)/shard_map/ppermute | solution.py:197
  19.0 4.4 %collective-permute-start.10 = (s16[272,128]{1,0:T(8,128)(2,1)S(1)}, s16[272,128]{1,0:T(8,128)(2,1)S(1)}, u32[]{:S(2)}, u32[]{:S(2)}) collective-permute-start(s16[272,128]{1,0:T(8,128)(2,1)S(1)} %shard_map.49), channel_id=1, source_target_pairs={{0,1},{1,0},{2,3},{3,2},{4,5},{5,4},{6,7},{7,6},{8,9},{9,8},{10,11... | collective-permute-start | bytes 208904 | tf_op jit(solution)/shard_map/ppermute | solution.py:197

commit v21 on v20

--- a/solution.py
+++ b/solution.py
@@ -203,12 +203,11 @@
     return lax.ppermute(block, ("row", "col"), route)
 
 
-def gather(block, beside, place):
+def gather(block, beside):
     places = lax.axis_size("col") // 2
     steps = [places >> n for n in range(1, places.bit_length() - 2)] + [3, 1]
-    later, _ = lax.optimization_barrier((block, place))
-    came = [across(later if d == 1 else block, "col", 2 * d) for d in steps]
-    came[:-1], beside = lax.optimization_barrier((came[:-1], beside))
+    came = [across(block, "col", 2 * d) for d in steps]
+    came, beside = lax.optimization_barrier((came, beside))
     blocks = {0: block, **dict(zip(steps, came))}
     spanned = [0]
     for d in steps:
@@ -229,7 +228,7 @@
     codes = find_matches(left_index, right_index)
     given = lax.dynamic_index_in_dim(right, 1 - y, 0, keepdims=False)
     own = lax.dynamic_index_in_dim(right, y, 0, keepdims=False)
-    lefts, codes = gather(left, codes, y)
+    lefts, codes = gather(left, codes)
     rights = []
     for t in range(0, lax.axis_size("row"), 2):
         pair = [across(own, "row", t) if t else own, crossed(given, t)]

time: 24.1 us -> 25.8 us (1.071)
  waiting for transfers between devices: 4.31 us -> 7.66 us
  starting transfers between devices: 13.7 us -> 12.3 us
    ppermute x9, waiting for transfers between devices: 4.3 us -> 7.65 us  [across(): return lax.ppermute(block, axis, route)]
    ppermute x9, starting transfers between devices: 10.7 us -> 9.24 us  [across(): return lax.ppermute(block, axis, route)]
  transfers between devices with their start and end apart: 11 -> 11, of which waited for: 6 -> 7; matrix products, arithmetic and copies ran while one was open for 4% -> 4% of each run, Pallas kernels for 17% -> 15%
where the time goes in v21:
time: 25.8 us; the launch traced here: 25.7 us
  starting transfers between devices  12.3 us (48%)
  waiting for transfers between devices  7.66 us (30%)
  Pallas kernels  4.66 us (18%)
  local copies, waits for them, and re-layouts  1 us (4%)
    ppermute x9, starting transfers between devices, across(): return lax.ppermute(block, axis, route)  9.24 us
    ppermute x9, waiting for transfers between devices, across(): return lax.ppermute(block, axis, route)  7.65 us
    ppermute x2, starting transfers between devices, crossed(): return lax.ppermute(block, ('row', 'col'), route)  3.02 us
    pallas_call x1, Pallas kernels, find_matches(): pl.pallas_call(kernel, out_shape=jax.ShapeDtypeStruct((inner * 2 * slots,...  1.92 us
    pallas_call x1, Pallas kernels, first_products(): pl.pallas_call(kernel, out_shape=[jax.ShapeDtypeStruct((RT * tile, tile),...  1.62 us
    squeeze x1, local copies, waits for them, and re-layouts, shards(): given = lax.dynamic_index_in_dim(right, 1 - y, 0, keepdims=False)  0.99 us
    pallas_call x1, Pallas kernels, add_coded(): pl.pallas_call(kernel, out_shape=jax.ShapeDtypeStruct(total.shape, jnp.bf...  0.65 us
  transfers between devices with their start and end apart: 11, of which 7 were waited for; matrix products, arithmetic and copies ran while one was open for 4% of the time, Pallas kernels for 15%

profile of v21, /device:TPU:0, one launch (start us, length us, event | category | flops | bytes accessed | tf_op | source)
XLA Modules:
  0.0 25.7 jit_solution(4357470943853509390)
XLA Ops:
  0.0 3.0 %collective-permute-start.1 = (bf16[6,128,128]{2,1,0:T(8,128)(2,1)}, bf16[6,128,128]{2,1,0:T(8,128)(2,1)S(1)}, u32[]{:S(2)}, u32[]{:S(2)}) collective-permute-start(bf16[6,128,128]{2,1,0:T(8,128)(2,1)} %bitcast.7), channel_id=1, source_target_pairs={{0,2},{1,3},{2,0},{3,1},{4,6},{5,7},{6,4},{7,5},{8,10},{9,11},{10,... | collective-permute-start | bytes 589832 | tf_op jit(solution)/shard_map/ppermute | solution.py:197
  3.0 2.5 %collective-permute-start = (bf16[6,128,128]{2,1,0:T(8,128)(2,1)}, bf16[6,128,128]{2,1,0:T(8,128)(2,1)S(1)}, u32[]{:S(2)}, u32[]{:S(2)}) collective-permute-start(bf16[6,128,128]{2,1,0:T(8,128)(2,1)} %bitcast.8), channel_id=1, source_target_pairs={{0,6},{1,7},{2,4},{3,5},{4,2},{5,3},{6,0},{7,1},{8,14},{9,15},{10,... | collective-permute-start | bytes 589832 | tf_op jit(solution)/shard_map/ppermute | solution.py:197
  5.5 0.0 copy-start.1
  5.5 0.0 copy-start.2
  5.5 0.0 copy-start
  5.5 1.0 %dynamic-slice_bitcast_fusion = (bf16[3,128,128]{2,1,0:T(8,128)(2,1)S(1)}, bf16[3,128,128]{2,1,0:T(8,128)(2,1)S(1)}) fusion(bf16[1,1,2,3,128,128]{5,4,3,2,1,0:T(8,128)(2,1)} %param.6, s32[]{:T(128)S(6)} %select_n.8, s32[]{:T(128)S(6)} %select_n.7), kind=kLoop, calls=%fused_computation | loop fusion | bytes 393224 | tf_op jit(solution)/shard_map/jit(dynamic_index_in_dim)/squeeze | solution.py:229
  6.5 2.5 %collective-permute-start.7 = (bf16[3,128,128]{2,1,0:T(8,128)(2,1)S(1)}, bf16[3,128,128]{2,1,0:T(8,128)(2,1)S(1)}, u32[]{:S(2)}, u32[]{:S(2)}) collective-permute-start(bf16[3,128,128]{2,1,0:T(8,128)(2,1)S(1)} %get-tuple-element.21), channel_id=1, source_target_pairs={{0,17},{1,16},{2,19},{3,18},{4,21},{5,20},{6,23},{7,22},{8,25},{9,... | collective-permute-start | bytes 294920 | tf_op jit(solution)/shard_map/ppermute | solution.py:203
  9.0 0.5 %collective-permute-start.3 = (bf16[3,128,128]{2,1,0:T(8,128)(2,1)S(1)}, bf16[3,128,128]{2,1,0:T(8,128)(2,1)S(1)}, u32[]{:S(2)}, u32[]{:S(2)}) collective-permute-start(bf16[3,128,128]{2,1,0:T(8,128)(2,1)S(1)} %get-tuple-element.21), channel_id=1, source_target_pairs={{0,1},{1,0},{2,3},{3,2},{4,5},{5,4},{6,7},{7,6},{8,9},{9,8},{10,11... | collective-permute-start | bytes 294920 | tf_op jit(solution)/shard_map/ppermute | solution.py:203
  9.5 0.5 %collective-permute-start.6 = (bf16[3,128,128]{2,1,0:T(8,128)(2,1)S(1)}, bf16[3,128,128]{2,1,0:T(8,128)(2,1)S(1)}, u32[]{:S(2)}, u32[]{:S(2)}) collective-permute-start(bf16[3,128,128]{2,1,0:T(8,128)(2,1)S(1)} %get-tuple-element.17.refs_3_), channel_id=1, source_target_pairs={{0,16},{8,24},{16,0},{24,8},{1,17},{9,25},{17,1},{25,9},{2,18},{10... | collective-permute-start | bytes 294920 | tf_op jit(solution)/shard_map/ppermute | solution.py:197
  10.1 0.0 copy-done.1
  10.1 0.0 copy-done.2
  10.1 1.9 %shard_map.46.codes_ref = s32[48]{0:T(128)S(1)} custom-call(s32[6,4,8]{2,1,0:T(4,128)S(1)} %bitcast.10, s32[4,3,2,8]{3,2,1,0:T(2,128)S(1)} %bitcast.11), custom_call_target="tpu_custom_call" | custom-call | tf_op jit(solution)/shard_map/pallas_call | solution.py:46
  12.0 0.0 collective-permute-done.1.refs_1_
  12.0 2.6 %collective-permute-done.refs_2_ = bf16[6,128,128]{2,1,0:T(8,128)(2,1)S(1)} collective-permute-done((bf16[6,128,128]{2,1,0:T(8,128)(2,1)}, bf16[6,128,128]{2,1,0:T(8,128)(2,1)S(1)}, u32[]{:S(2)}, u32[]{:S(2)}) %collective-permute-start) | collective-permute-done | bytes 196640 | tf_op jit(solution)/shard_map/ppermute | solution.py:197
  14.6 0.6 %collective-permute-start.2 = (bf16[6,128,128]{2,1,0:T(8,128)(2,1)S(1)}, bf16[6,128,128]{2,1,0:T(8,128)(2,1)S(1)}, u32[]{:S(2)}, u32[]{:S(2)}) collective-permute-start(bf16[6,128,128]{2,1,0:T(8,128)(2,1)S(1)} %collective-permute-done.refs_2_), channel_id=1, source_target_pairs={{0,2},{1,3},{2,0},{3,1},{4,6},{5,7},{6,4},{7,5},{8,10},{9,11},{10,... | collective-permute-start | bytes 589832 | tf_op jit(solution)/shard_map/ppermute | solution.py:197
  15.3 0.0 collective-permute-done.7.refs_8_
  15.3 0.0 collective-permute-start.9
  15.3 0.0 collective-permute-done.3.refs_4_
  15.3 0.5 %collective-permute-start.5 = (bf16[3,128,128]{2,1,0:T(8,128)(2,1)S(1)}, bf16[3,128,128]{2,1,0:T(8,128)(2,1)S(1)}, u32[]{:S(2)}, u32[]{:S(2)}) collective-permute-start(bf16[3,128,128]{2,1,0:T(8,128)(2,1)S(1)} %collective-permute-done.3.refs_4_), channel_id=1, source_target_pairs={{0,8},{8,0},{16,24},{24,16},{1,9},{9,1},{17,25},{25,17},{2,10},{10... | collective-permute-start | bytes 294920 | tf_op jit(solution)/shard_map/ppermute | solution.py:197
  15.8 0.0 collective-permute-done.6.refs_7_
  15.8 0.1 collective-permute-start.8
  15.8 0.4 %collective-permute-start.4 = (bf16[3,128,128]{2,1,0:T(8,128)(2,1)S(1)}, bf16[3,128,128]{2,1,0:T(8,128)(2,1)S(1)}, u32[]{:S(2)}, u32[]{:S(2)}) collective-permute-start(bf16[3,128,128]{2,1,0:T(8,128)(2,1)S(1)} %get-tuple-element.17.refs_3_), channel_id=1, source_target_pairs={{0,8},{8,0},{16,24},{24,16},{1,9},{9,1},{17,25},{25,17},{2,10},{10... | collective-permute-start | bytes 294920 | tf_op jit(solution)/shard_map/ppermute | solution.py:197
  16.3 0.3 %collective-permute-done.9.refs_10_ = bf16[3,128,128]{2,1,0:T(8,128)(2,1)S(1)} collective-permute-done((bf16[3,128,128]{2,1,0:T(8,128)(2,1)S(1)}, bf16[3,128,128]{2,1,0:T(8,128)(2,1)S(1)}, u32[]{:S(2)}, u32[]{:S(2)}) %collective-permute-start.9) | collective-permute-done | bytes 98336 | tf_op jit(solution)/shard_map/ppermute | solution.py:197
  16.6 0.2 collective-permute-done.5.refs_6_
  16.7 0.4 %collective-permute-done.8.refs_9_ = bf16[3,128,128]{2,1,0:T(8,128)(2,1)S(1)} collective-permute-done((bf16[3,128,128]{2,1,0:T(8,128)(2,1)S(1)}, bf16[3,128,128]{2,1,0:T(8,128)(2,1)S(1)}, u32[]{:S(2)}, u32[]{:S(2)}) %collective-permute-start.8) | collective-permute-done | bytes 98336 | tf_op jit(solution)/shard_map/ppermute | solution.py:197
  17.1 0.2 collective-permute-done.4.refs_5_
  17.2 0.0 copy-done
  17.2 1.6 %shard_map.47 = (f32[256,128]{1,0:T(8,128)S(1)}, f32[256,128]{1,0:T(8,128)S(1)}, bf16[2,768,256]{2,1,0:T(8,128)(2,1)S(1)}) custom-call(s32[48]{0:T(128)S(1)} %shard_map.46.codes_ref, bf16[6,128,128]{2,1,0:T(8,128)(2,1)S(1)} %bitcast.9, bf16[6,128,128]{2,1,0:T(8,128)(2,1)S(1)} %collective-permute-done.1.refs_1_, ...), custom_call_target="tpu_custom_call" | custom-call | flops 201326592 | bytes 786432 | tf_op jit(solution)/shard_map/pallas_call | solution.py:113
  18.9 1.5 %collective-permute-done.2.left_ref = bf16[6,128,128]{2,1,0:T(8,128)(2,1)S(1)} collective-permute-done((bf16[6,128,128]{2,1,0:T(8,128)(2,1)S(1)}, bf16[6,128,128]{2,1,0:T(8,128)(2,1)S(1)}, u32[]{:S(2)}, u32[]{:S(2)}) %collective-permute-start.2) | collective-permute-done | bytes 196640 | tf_op jit(solution)/shard_map/ppermute | solution.py:197
  20.4 0.3 %shard_map.49 = s16[272,128]{1,0:T(8,128)(2,1)S(1)} custom-call(bf16[6,128,128]{2,1,0:T(8,128)(2,1)S(1)} %collective-permute-done.2.left_ref, bf16[2,768,256]{2,1,0:T(8,128)(2,1)S(1)} %get-tuple-element.18.right_ref, f32[256,128]{1,0:T(8,128)S(1)} %get-tuple-element.20.total_ref), custom_call_target="tpu_custom_call" | custom-call | flops 25165824 | bytes 196608 | tf_op jit(solution)/shard_map/pallas_call | solution.py:146
  20.6 1.6 %collective-permute-start.10 = (s16[272,128]{1,0:T(8,128)(2,1)S(1)}, s16[272,128]{1,0:T(8,128)(2,1)S(1)}, u32[]{:S(2)}, u32[]{:S(2)}) collective-permute-start(s16[272,128]{1,0:T(8,128)(2,1)S(1)} %shard_map.49), channel_id=1, source_target_pairs={{0,1},{1,0},{2,3},{3,2},{4,5},{5,4},{6,7},{7,6},{8,9},{9,8},{10,11... | collective-permute-start | bytes 208904 | tf_op jit(solution)/shard_map/ppermute | solution.py:197
  22.2 0.2 shard_map.48.total_ref
  22.4 2.6 %collective-permute-done.10.coded_ref = s16[272,128]{1,0:T(8,128)(2,1)S(1)} collective-permute-done((s16[272,128]{1,0:T(8,128)(2,1)S(1)}, s16[272,128]{1,0:T(8,128)(2,1)S(1)}, u32[]{:S(2)}, u32[]{:S(2)}) %collective-permute-start.10) | collective-permute-done | bytes 69664 | tf_op jit(solution)/shard_map/ppermute | solution.py:197
  25.0 0.7 %shard_map.50 = bf16[256,128]{1,0:T(8,128)(2,1)} custom-call(f32[256,128]{1,0:T(8,128)S(1)} %shard_map.48.total_ref, s16[272,128]{1,0:T(8,128)(2,1)S(1)} %collective-permute-done.10.coded_ref), custom_call_target="tpu_custom_call" | custom-call | tf_op jit(solution)/shard_map/pallas_call | solution.py:186
Async XLA Ops:
  0.0 12.0 %collective-permute-start.1 = (bf16[6,128,128]{2,1,0:T(8,128)(2,1)}, bf16[6,128,128]{2,1,0:T(8,128)(2,1)S(1)}, u32[]{:S(2)}, u32[]{:S(2)}) collective-permute-start(bf16[6,128,128]{2,1,0:T(8,128)(2,1)} %bitcast.7), channel_id=1, source_target_pairs={{0,2},{1,3},{2,0},{3,1},{4,6},{5,7},{6,4},{7,5},{8,10},{9,11},{10,... | collective-permute-start | bytes 589832 | tf_op jit(solution)/shard_map/ppermute | solution.py:197
  3.0 11.6 %collective-permute-start = (bf16[6,128,128]{2,1,0:T(8,128)(2,1)}, bf16[6,128,128]{2,1,0:T(8,128)(2,1)S(1)}, u32[]{:S(2)}, u32[]{:S(2)}) collective-permute-start(bf16[6,128,128]{2,1,0:T(8,128)(2,1)} %bitcast.8), channel_id=1, source_target_pairs={{0,6},{1,7},{2,4},{3,5},{4,2},{5,3},{6,0},{7,1},{8,14},{9,15},{10,... | collective-permute-start | bytes 589832 | tf_op jit(solution)/shard_map/ppermute | solution.py:197
  5.5 4.6 %copy-start.1 = (s32[4,8,6]{1,0,2:T(4,128)S(1)}, s32[4,8,6]{1,0,2:T(4,128)}, u32[]{:S(2)}) copy-start(s32[4,8,6]{1,0,2:T(4,128)} %param.5) | copy-start | bytes 2308
  5.5 4.6 %copy-start.2 = (s32[4,8,2,3]{1,2,3,0:T(2,128)S(1)}, s32[4,8,2,3]{1,2,3,0:T(2,128)}, u32[]{:S(2)}) copy-start(s32[4,8,2,3]{1,2,3,0:T(2,128)} %param.7) | copy-start | bytes 2308
  5.5 11.7 %copy-start = (bf16[1,1,6,128,128]{4,3,2,1,0:T(8,128)(2,1)S(1)}, bf16[1,1,6,128,128]{4,3,2,1,0:T(8,128)(2,1)}, u32[]{:S(2)}) copy-start(bf16[1,1,6,128,128]{4,3,2,1,0:T(8,128)(2,1)} %param.4) | copy-start | bytes 589828
  6.5 8.8 %collective-permute-start.7 = (bf16[3,128,128]{2,1,0:T(8,128)(2,1)S(1)}, bf16[3,128,128]{2,1,0:T(8,128)(2,1)S(1)}, u32[]{:S(2)}, u32[]{:S(2)}) collective-permute-start(bf16[3,128,128]{2,1,0:T(8,128)(2,1)S(1)} %get-tuple-element.21), channel_id=1, source_target_pairs={{0,17},{1,16},{2,19},{3,18},{4,21},{5,20},{6,23},{7,22},{8,25},{9,... | collective-permute-start | bytes 294920 | tf_op jit(solution)/shard_map/ppermute | solution.py:203
  9.0 6.2 %collective-permute-start.3 = (bf16[3,128,128]{2,1,0:T(8,128)(2,1)S(1)}, bf16[3,128,128]{2,1,0:T(8,128)(2,1)S(1)}, u32[]{:S(2)}, u32[]{:S(2)}) collective-permute-start(bf16[3,128,128]{2,1,0:T(8,128)(2,1)S(1)} %get-tuple-element.21), channel_id=1, source_target_pairs={{0,1},{1,0},{2,3},{3,2},{4,5},{5,4},{6,7},{7,6},{8,9},{9,8},{10,11... | collective-permute-start | bytes 294920 | tf_op jit(solution)/shard_map/ppermute | solution.py:203
  9.5 6.3 %collective-permute-start.6 = (bf16[3,128,128]{2,1,0:T(8,128)(2,1)S(1)}, bf16[3,128,128]{2,1,0:T(8,128)(2,1)S(1)}, u32[]{:S(2)}, u32[]{:S(2)}) collective-permute-start(bf16[3,128,128]{2,1,0:T(8,128)(2,1)S(1)} %get-tuple-element.17.refs_3_), channel_id=1, source_target_pairs={{0,16},{8,24},{16,0},{24,8},{1,17},{9,25},{17,1},{25,9},{2,18},{10... | collective-permute-start | bytes 294920 | tf_op jit(solution)/shard_map/ppermute | solution.py:197
  14.6 5.7 %collective-permute-start.2 = (bf16[6,128,128]{2,1,0:T(8,128)(2,1)S(1)}, bf16[6,128,128]{2,1,0:T(8,128)(2,1)S(1)}, u32[]{:S(2)}, u32[]{:S(2)}) collective-permute-start(bf16[6,128,128]{2,1,0:T(8,128)(2,1)S(1)} %collective-permute-done.refs_2_), channel_id=1, source_target_pairs={{0,2},{1,3},{2,0},{3,1},{4,6},{5,7},{6,4},{7,5},{8,10},{9,11},{10,... | collective-permute-start | bytes 589832 | tf_op jit(solution)/shard_map/ppermute | solution.py:197
  15.3 1.3 %collective-permute-start.9 = (bf16[3,128,128]{2,1,0:T(8,128)(2,1)S(1)}, bf16[3,128,128]{2,1,0:T(8,128)(2,1)S(1)}, u32[]{:S(2)}, u32[]{:S(2)}) collective-permute-start(bf16[3,128,128]{2,1,0:T(8,128)(2,1)S(1)} %collective-permute-done.7.refs_8_), channel_id=1, source_target_pairs={{0,8},{8,0},{16,24},{24,16},{1,9},{9,1},{17,25},{25,17},{2,10},{10... | collective-permute-start | bytes 294920 | tf_op jit(solution)/shard_map/ppermute | solution.py:197
  15.3 1.5 %collective-permute-start.5 = (bf16[3,128,128]{2,1,0:T(8,128)(2,1)S(1)}, bf16[3,128,128]{2,1,0:T(8,128)(2,1)S(1)}, u32[]{:S(2)}, u32[]{:S(2)}) collective-permute-start(bf16[3,128,128]{2,1,0:T(8,128)(2,1)S(1)} %collective-permute-done.3.refs_4_), channel_id=1, source_target_pairs={{0,8},{8,0},{16,24},{24,16},{1,9},{9,1},{17,25},{25,17},{2,10},{10... | collective-permute-start | bytes 294920 | tf_op jit(solution)/shard_map/ppermute | solution.py:197
  15.8 1.3 %collective-permute-start.8 = (bf16[3,128,128]{2,1,0:T(8,128)(2,1)S(1)}, bf16[3,128,128]{2,1,0:T(8,128)(2,1)S(1)}, u32[]{:S(2)}, u32[]{:S(2)}) collective-permute-start(bf16[3,128,128]{2,1,0:T(8,128)(2,1)S(1)} %collective-permute-done.6.refs_7_), channel_id=1, source_target_pairs={{0,8},{8,0},{16,24},{24,16},{1,9},{9,1},{17,25},{25,17},{2,10},{10... | collective-permute-start | bytes 294920 | tf_op jit(solution)/shard_map/ppermute | solution.py:197
  15.8 1.4 %collective-permute-start.4 = (bf16[3,128,128]{2,1,0:T(8,128)(2,1)S(1)}, bf16[3,128,128]{2,1,0:T(8,128)(2,1)S(1)}, u32[]{:S(2)}, u32[]{:S(2)}) collective-permute-start(bf16[3,128,128]{2,1,0:T(8,128)(2,1)S(1)} %get-tuple-element.17.refs_3_), channel_id=1, source_target_pairs={{0,8},{8,0},{16,24},{24,16},{1,9},{9,1},{17,25},{25,17},{2,10},{10... | collective-permute-start | bytes 294920 | tf_op jit(solution)/shard_map/ppermute | solution.py:197
  20.6 4.4 %collective-permute-start.10 = (s16[272,128]{1,0:T(8,128)(2,1)S(1)}, s16[272,128]{1,0:T(8,128)(2,1)S(1)}, u32[]{:S(2)}, u32[]{:S(2)}) collective-permute-start(s16[272,128]{1,0:T(8,128)(2,1)S(1)} %shard_map.49), channel_id=1, source_target_pairs={{0,1},{1,0},{2,3},{3,2},{4,5},{5,4},{6,7},{7,6},{8,9},{9,8},{10,11... | collective-permute-start | bytes 208904 | tf_op jit(solution)/shard_map/ppermute | solution.py:197

commit v22 on v20

--- a/solution.py
+++ b/solution.py
@@ -203,10 +203,10 @@
     return lax.ppermute(block, ("row", "col"), route)
 
 
-def gather(block, beside, place):
+def gather(block, beside, ahead):
     places = lax.axis_size("col") // 2
     steps = [places >> n for n in range(1, places.bit_length() - 2)] + [3, 1]
-    later, _ = lax.optimization_barrier((block, place))
+    later, ahead = lax.optimization_barrier((block, ahead))
     came = [across(later if d == 1 else block, "col", 2 * d) for d in steps]
     came[:-1], beside = lax.optimization_barrier((came[:-1], beside))
     blocks = {0: block, **dict(zip(steps, came))}
@@ -217,7 +217,7 @@
         spanned += [s ^ d for s in spanned]
     last = spanned[-1]
     order = [s for s in sorted(blocks) if s != last] + [last]
-    return [(s, (blocks[s],)) for s in order], beside
+    return [(s, (blocks[s],)) for s in order], beside, ahead
 
 
 def shards(left_tiles, left_index, right_tiles, right_index):
@@ -229,7 +229,7 @@
     codes = find_matches(left_index, right_index)
     given = lax.dynamic_index_in_dim(right, 1 - y, 0, keepdims=False)
     own = lax.dynamic_index_in_dim(right, y, 0, keepdims=False)
-    lefts, codes = gather(left, codes, y)
+    lefts, codes, (own, given) = gather(left, codes, (own, given))
     rights = []
     for t in range(0, lax.axis_size("row"), 2):
         pair = [across(own, "row", t) if t else own, crossed(given, t)]

time: 24.1 us -> 24.1 us (level)
    ppermute x2, starting transfers between devices: 3.02 us -> 2 us  [crossed(): return lax.ppermute(block, ('row', 'col'), route)]
    ppermute x9, starting transfers between devices: 10.7 us -> 11.7 us  [across(): return lax.ppermute(block, axis, route)]
    ppermute x9, waiting for transfers between devices: 4.3 us -> 4.03 us  [across(): return lax.ppermute(block, axis, route)]
  transfers between devices with their start and end apart: 11 -> 11, of which waited for: 6 -> 7; matrix products, arithmetic and copies ran while one was open for 4% -> 4% of each run, Pallas kernels for 17% -> 17%
where the time goes in v22:
time: 24.1 us; the launch traced here: 24 us
  starting transfers between devices  13.7 us (57%)
  Pallas kernels  5.05 us (21%)
  waiting for transfers between devices  4.13 us (17%)
  local copies, waits for them, and re-layouts  1.02 us (4%)
    ppermute x9, starting transfers between devices, across(): return lax.ppermute(block, axis, route)  11.7 us
    ppermute x9, waiting for transfers between devices, across(): return lax.ppermute(block, axis, route)  4.03 us
    pallas_call x1, Pallas kernels, first_products(): pl.pallas_call(kernel, out_shape=[jax.ShapeDtypeStruct((RT * tile, tile),...  2.01 us
    ppermute x2, starting transfers between devices, crossed(): return lax.ppermute(block, ('row', 'col'), route)  2 us
    pallas_call x1, Pallas kernels, find_matches(): pl.pallas_call(kernel, out_shape=jax.ShapeDtypeStruct((inner * 2 * slots,...  1.92 us
    squeeze x1, local copies, waits for them, and re-layouts, shards(): given = lax.dynamic_index_in_dim(right, 1 - y, 0, keepdims=False)  0.99 us
    pallas_call x1, Pallas kernels, add_coded(): pl.pallas_call(kernel, out_shape=jax.ShapeDtypeStruct(total.shape, jnp.bf...  0.65 us
  transfers between devices with their start and end apart: 11, of which 7 were waited for; matrix products, arithmetic and copies ran while one was open for 4% of the time, Pallas kernels for 17%

profile of v22, /device:TPU:0, one launch (start us, length us, event | category | flops | bytes accessed | tf_op | source)
XLA Modules:
  0.0 24.0 jit_solution(9262569346490457018)
XLA Ops:
  0.0 5.0 %collective-permute-start = (bf16[6,128,128]{2,1,0:T(8,128)(2,1)}, bf16[6,128,128]{2,1,0:T(8,128)(2,1)S(1)}, u32[]{:S(2)}, u32[]{:S(2)}) collective-permute-start(bf16[6,128,128]{2,1,0:T(8,128)(2,1)} %bitcast.7), channel_id=1, source_target_pairs={{0,6},{1,7},{2,4},{3,5},{4,2},{5,3},{6,0},{7,1},{8,14},{9,15},{10,... | collective-permute-start | bytes 589832 | tf_op jit(solution)/shard_map/ppermute | solution.py:197
  5.0 0.0 copy-start
  5.1 0.0 copy-start.1
  5.1 0.0 copy-start.2
  5.1 1.0 %dynamic-slice_bitcast_fusion = (bf16[3,128,128]{2,1,0:T(8,128)(2,1)S(1)}, bf16[3,128,128]{2,1,0:T(8,128)(2,1)S(1)}) fusion(bf16[1,1,2,3,128,128]{5,4,3,2,1,0:T(8,128)(2,1)} %param.6, s32[]{:T(128)S(6)} %select_n.8, s32[]{:T(128)S(6)} %select_n.7), kind=kLoop, calls=%fused_computation | loop fusion | bytes 393224 | tf_op jit(solution)/shard_map/jit(dynamic_index_in_dim)/squeeze | solution.py:230
  6.1 0.0 copy-done
  6.1 0.1 collective-permute-start.2
  6.1 1.6 %collective-permute-start.6 = (bf16[3,128,128]{2,1,0:T(8,128)(2,1)S(1)}, bf16[3,128,128]{2,1,0:T(8,128)(2,1)S(1)}, u32[]{:S(2)}, u32[]{:S(2)}) collective-permute-start(bf16[3,128,128]{2,1,0:T(8,128)(2,1)S(1)} %get-tuple-element.20.refs_3_), channel_id=1, source_target_pairs={{0,16},{8,24},{16,0},{24,8},{1,17},{9,25},{17,1},{25,9},{2,18},{10... | collective-permute-start | bytes 294920 | tf_op jit(solution)/shard_map/ppermute | solution.py:197
  7.7 1.5 %collective-permute-start.7 = (bf16[3,128,128]{2,1,0:T(8,128)(2,1)S(1)}, bf16[3,128,128]{2,1,0:T(8,128)(2,1)S(1)}, u32[]{:S(2)}, u32[]{:S(2)}) collective-permute-start(bf16[3,128,128]{2,1,0:T(8,128)(2,1)S(1)} %get-tuple-element.21), channel_id=1, source_target_pairs={{0,17},{1,16},{2,19},{3,18},{4,21},{5,20},{6,23},{7,22},{8,25},{9,... | collective-permute-start | bytes 294920 | tf_op jit(solution)/shard_map/ppermute | solution.py:203
  9.2 0.5 %collective-permute-start.3 = (bf16[3,128,128]{2,1,0:T(8,128)(2,1)S(1)}, bf16[3,128,128]{2,1,0:T(8,128)(2,1)S(1)}, u32[]{:S(2)}, u32[]{:S(2)}) collective-permute-start(bf16[3,128,128]{2,1,0:T(8,128)(2,1)S(1)} %get-tuple-element.21), channel_id=1, source_target_pairs={{0,1},{1,0},{2,3},{3,2},{4,5},{5,4},{6,7},{7,6},{8,9},{9,8},{10,11... | collective-permute-start | bytes 294920 | tf_op jit(solution)/shard_map/ppermute | solution.py:203
  9.7 0.0 copy-done.1
  9.7 0.0 copy-done.2
  9.7 1.9 %shard_map.46.codes_ref = s32[48]{0:T(128)S(1)} custom-call(s32[6,4,8]{2,1,0:T(4,128)S(1)} %bitcast.10, s32[4,3,2,8]{3,2,1,0:T(2,128)S(1)} %bitcast.11), custom_call_target="tpu_custom_call" | custom-call | tf_op jit(solution)/shard_map/pallas_call | solution.py:46
  11.6 0.0 collective-permute-done.refs_2_
  11.6 2.5 %collective-permute-start.1 = (bf16[6,128,128]{2,1,0:T(8,128)(2,1)S(1)}, bf16[6,128,128]{2,1,0:T(8,128)(2,1)S(1)}, u32[]{:S(2)}, u32[]{:S(2)}) collective-permute-start(bf16[6,128,128]{2,1,0:T(8,128)(2,1)S(1)} %collective-permute-done.refs_2_), channel_id=1, source_target_pairs={{0,2},{1,3},{2,0},{3,1},{4,6},{5,7},{6,4},{7,5},{8,10},{9,11},{10,... | collective-permute-start | bytes 589832 | tf_op jit(solution)/shard_map/ppermute | solution.py:197
  14.1 0.0 collective-permute-done.6.refs_7_
  14.1 0.0 collective-permute-start.8
  14.1 0.0 collective-permute-done.7.refs_8_
  14.1 0.5 %collective-permute-start.9 = (bf16[3,128,128]{2,1,0:T(8,128)(2,1)S(1)}, bf16[3,128,128]{2,1,0:T(8,128)(2,1)S(1)}, u32[]{:S(2)}, u32[]{:S(2)}) collective-permute-start(bf16[3,128,128]{2,1,0:T(8,128)(2,1)S(1)} %collective-permute-done.7.refs_8_), channel_id=1, source_target_pairs={{0,8},{8,0},{16,24},{24,16},{1,9},{9,1},{17,25},{25,17},{2,10},{10... | collective-permute-start | bytes 294920 | tf_op jit(solution)/shard_map/ppermute | solution.py:197
  14.6 0.1 collective-permute-done.3.refs_4_
  14.7 0.0 collective-permute-start.5
  14.7 0.0 collective-permute-done.2.refs_1_
  14.7 0.5 %collective-permute-start.4 = (bf16[3,128,128]{2,1,0:T(8,128)(2,1)S(1)}, bf16[3,128,128]{2,1,0:T(8,128)(2,1)S(1)}, u32[]{:S(2)}, u32[]{:S(2)}) collective-permute-start(bf16[3,128,128]{2,1,0:T(8,128)(2,1)S(1)} %get-tuple-element.20.refs_3_), channel_id=1, source_target_pairs={{0,8},{8,0},{16,24},{24,16},{1,9},{9,1},{17,25},{25,17},{2,10},{10... | collective-permute-start | bytes 294920 | tf_op jit(solution)/shard_map/ppermute | solution.py:197
  15.2 0.2 collective-permute-done.8.refs_9_
  15.4 0.2 collective-permute-done.9.refs_10_
  15.6 0.5 %collective-permute-done.5.refs_6_ = bf16[3,128,128]{2,1,0:T(8,128)(2,1)S(1)} collective-permute-done((bf16[3,128,128]{2,1,0:T(8,128)(2,1)S(1)}, bf16[3,128,128]{2,1,0:T(8,128)(2,1)S(1)}, u32[]{:S(2)}, u32[]{:S(2)}) %collective-permute-start.5) | collective-permute-done | bytes 98336 | tf_op jit(solution)/shard_map/ppermute | solution.py:197
  16.0 0.2 collective-permute-done.4.refs_5_
  16.2 2.0 %shard_map.47 = (f32[256,128]{1,0:T(8,128)S(1)}, f32[256,128]{1,0:T(8,128)S(1)}, bf16[2,768,256]{2,1,0:T(8,128)(2,1)S(1)}) custom-call(s32[48]{0:T(128)S(1)} %shard_map.46.codes_ref, bf16[6,128,128]{2,1,0:T(8,128)(2,1)S(1)} %bitcast.9, bf16[6,128,128]{2,1,0:T(8,128)(2,1)S(1)} %collective-permute-done.2.refs_1_, ...), custom_call_target="tpu_custom_call" | custom-call | flops 201326592 | bytes 786432 | tf_op jit(solution)/shard_map/pallas_call | solution.py:113
  18.2 0.5 %collective-permute-done.1.left_ref = bf16[6,128,128]{2,1,0:T(8,128)(2,1)S(1)} collective-permute-done((bf16[6,128,128]{2,1,0:T(8,128)(2,1)S(1)}, bf16[6,128,128]{2,1,0:T(8,128)(2,1)S(1)}, u32[]{:S(2)}, u32[]{:S(2)}) %collective-permute-start.1) | collective-permute-done | bytes 196640 | tf_op jit(solution)/shard_map/ppermute | solution.py:197
  18.7 0.3 %shard_map.49 = s16[272,128]{1,0:T(8,128)(2,1)S(1)} custom-call(bf16[6,128,128]{2,1,0:T(8,128)(2,1)S(1)} %collective-permute-done.1.left_ref, bf16[2,768,256]{2,1,0:T(8,128)(2,1)S(1)} %get-tuple-element.22.right_ref, f32[256,128]{1,0:T(8,128)S(1)} %get-tuple-element.24.total_ref), custom_call_target="tpu_custom_call" | custom-call | flops 25165824 | bytes 196608 | tf_op jit(solution)/shard_map/pallas_call | solution.py:146
  19.0 1.6 %collective-permute-start.10 = (s16[272,128]{1,0:T(8,128)(2,1)S(1)}, s16[272,128]{1,0:T(8,128)(2,1)S(1)}, u32[]{:S(2)}, u32[]{:S(2)}) collective-permute-start(s16[272,128]{1,0:T(8,128)(2,1)S(1)} %shard_map.49), channel_id=1, source_target_pairs={{0,1},{1,0},{2,3},{3,2},{4,5},{5,4},{6,7},{7,6},{8,9},{9,8},{10,11... | collective-permute-start | bytes 208904 | tf_op jit(solution)/shard_map/ppermute | solution.py:197
  20.5 0.2 shard_map.48.total_ref
  20.8 2.6 %collective-permute-done.10.coded_ref = s16[272,128]{1,0:T(8,128)(2,1)S(1)} collective-permute-done((s16[272,128]{1,0:T(8,128)(2,1)S(1)}, s16[272,128]{1,0:T(8,128)(2,1)S(1)}, u32[]{:S(2)}, u32[]{:S(2)}) %collective-permute-start.10) | collective-permute-done | bytes 69664 | tf_op jit(solution)/shard_map/ppermute | solution.py:197
  23.3 0.7 %shard_map.50 = bf16[256,128]{1,0:T(8,128)(2,1)} custom-call(f32[256,128]{1,0:T(8,128)S(1)} %shard_map.48.total_ref, s16[272,128]{1,0:T(8,128)(2,1)S(1)} %collective-permute-done.10.coded_ref), custom_call_target="tpu_custom_call" | custom-call | tf_op jit(solution)/shard_map/pallas_call | solution.py:186
Async XLA Ops:
  0.0 11.6 %collective-permute-start = (bf16[6,128,128]{2,1,0:T(8,128)(2,1)}, bf16[6,128,128]{2,1,0:T(8,128)(2,1)S(1)}, u32[]{:S(2)}, u32[]{:S(2)}) collective-permute-start(bf16[6,128,128]{2,1,0:T(8,128)(2,1)} %bitcast.7), channel_id=1, source_target_pairs={{0,6},{1,7},{2,4},{3,5},{4,2},{5,3},{6,0},{7,1},{8,14},{9,15},{10,... | collective-permute-start | bytes 589832 | tf_op jit(solution)/shard_map/ppermute | solution.py:197
  5.0 1.0 %copy-start = (bf16[1,1,6,128,128]{4,3,2,1,0:T(8,128)(2,1)S(1)}, bf16[1,1,6,128,128]{4,3,2,1,0:T(8,128)(2,1)}, u32[]{:S(2)}) copy-start(bf16[1,1,6,128,128]{4,3,2,1,0:T(8,128)(2,1)} %param.4) | copy-start | bytes 589828
  5.1 4.6 %copy-start.1 = (s32[4,8,6]{1,0,2:T(4,128)S(1)}, s32[4,8,6]{1,0,2:T(4,128)}, u32[]{:S(2)}) copy-start(s32[4,8,6]{1,0,2:T(4,128)} %param.5) | copy-start | bytes 2308
  5.1 4.6 %copy-start.2 = (s32[4,8,2,3]{1,2,3,0:T(2,128)S(1)}, s32[4,8,2,3]{1,2,3,0:T(2,128)}, u32[]{:S(2)}) copy-start(s32[4,8,2,3]{1,2,3,0:T(2,128)} %param.7) | copy-start | bytes 2308
  6.1 8.6 %collective-permute-start.2 = (bf16[6,128,128]{2,1,0:T(8,128)(2,1)S(1)}, bf16[6,128,128]{2,1,0:T(8,128)(2,1)S(1)}, u32[]{:S(2)}, u32[]{:S(2)}) collective-permute-start(bf16[6,128,128]{2,1,0:T(8,128)(2,1)S(1)} %bitcast.8), channel_id=1, source_target_pairs={{0,2},{1,3},{2,0},{3,1},{4,6},{5,7},{6,4},{7,5},{8,10},{9,11},{10,... | collective-permute-start | bytes 589832 | tf_op jit(solution)/shard_map/ppermute | solution.py:197
  6.1 8.0 %collective-permute-start.6 = (bf16[3,128,128]{2,1,0:T(8,128)(2,1)S(1)}, bf16[3,128,128]{2,1,0:T(8,128)(2,1)S(1)}, u32[]{:S(2)}, u32[]{:S(2)}) collective-permute-start(bf16[3,128,128]{2,1,0:T(8,128)(2,1)S(1)} %get-tuple-element.20.refs_3_), channel_id=1, source_target_pairs={{0,16},{8,24},{16,0},{24,8},{1,17},{9,25},{17,1},{25,9},{2,18},{10... | collective-permute-start | bytes 294920 | tf_op jit(solution)/shard_map/ppermute | solution.py:197
  7.7 6.4 %collective-permute-start.7 = (bf16[3,128,128]{2,1,0:T(8,128)(2,1)S(1)}, bf16[3,128,128]{2,1,0:T(8,128)(2,1)S(1)}, u32[]{:S(2)}, u32[]{:S(2)}) collective-permute-start(bf16[3,128,128]{2,1,0:T(8,128)(2,1)S(1)} %get-tuple-element.21), channel_id=1, source_target_pairs={{0,17},{1,16},{2,19},{3,18},{4,21},{5,20},{6,23},{7,22},{8,25},{9,... | collective-permute-start | bytes 294920 | tf_op jit(solution)/shard_map/ppermute | solution.py:203
  9.2 5.5 %collective-permute-start.3 = (bf16[3,128,128]{2,1,0:T(8,128)(2,1)S(1)}, bf16[3,128,128]{2,1,0:T(8,128)(2,1)S(1)}, u32[]{:S(2)}, u32[]{:S(2)}) collective-permute-start(bf16[3,128,128]{2,1,0:T(8,128)(2,1)S(1)} %get-tuple-element.21), channel_id=1, source_target_pairs={{0,1},{1,0},{2,3},{3,2},{4,5},{5,4},{6,7},{7,6},{8,9},{9,8},{10,11... | collective-permute-start | bytes 294920 | tf_op jit(solution)/shard_map/ppermute | solution.py:203
  11.6 7.1 %collective-permute-start.1 = (bf16[6,128,128]{2,1,0:T(8,128)(2,1)S(1)}, bf16[6,128,128]{2,1,0:T(8,128)(2,1)S(1)}, u32[]{:S(2)}, u32[]{:S(2)}) collective-permute-start(bf16[6,128,128]{2,1,0:T(8,128)(2,1)S(1)} %collective-permute-done.refs_2_), channel_id=1, source_target_pairs={{0,2},{1,3},{2,0},{3,1},{4,6},{5,7},{6,4},{7,5},{8,10},{9,11},{10,... | collective-permute-start | bytes 589832 | tf_op jit(solution)/shard_map/ppermute | solution.py:197
  14.1 1.3 %collective-permute-start.8 = (bf16[3,128,128]{2,1,0:T(8,128)(2,1)S(1)}, bf16[3,128,128]{2,1,0:T(8,128)(2,1)S(1)}, u32[]{:S(2)}, u32[]{:S(2)}) collective-permute-start(bf16[3,128,128]{2,1,0:T(8,128)(2,1)S(1)} %collective-permute-done.6.refs_7_), channel_id=1, source_target_pairs={{0,8},{8,0},{16,24},{24,16},{1,9},{9,1},{17,25},{25,17},{2,10},{10... | collective-permute-start | bytes 294920 | tf_op jit(solution)/shard_map/ppermute | solution.py:197
  14.1 1.5 %collective-permute-start.9 = (bf16[3,128,128]{2,1,0:T(8,128)(2,1)S(1)}, bf16[3,128,128]{2,1,0:T(8,128)(2,1)S(1)}, u32[]{:S(2)}, u32[]{:S(2)}) collective-permute-start(bf16[3,128,128]{2,1,0:T(8,128)(2,1)S(1)} %collective-permute-done.7.refs_8_), channel_id=1, source_target_pairs={{0,8},{8,0},{16,24},{24,16},{1,9},{9,1},{17,25},{25,17},{2,10},{10... | collective-permute-start | bytes 294920 | tf_op jit(solution)/shard_map/ppermute | solution.py:197
  14.7 1.3 %collective-permute-start.5 = (bf16[3,128,128]{2,1,0:T(8,128)(2,1)S(1)}, bf16[3,128,128]{2,1,0:T(8,128)(2,1)S(1)}, u32[]{:S(2)}, u32[]{:S(2)}) collective-permute-start(bf16[3,128,128]{2,1,0:T(8,128)(2,1)S(1)} %collective-permute-done.3.refs_4_), channel_id=1, source_target_pairs={{0,8},{8,0},{16,24},{24,16},{1,9},{9,1},{17,25},{25,17},{2,10},{10... | collective-permute-start | bytes 294920 | tf_op jit(solution)/shard_map/ppermute | solution.py:197
  14.7 1.5 %collective-permute-start.4 = (bf16[3,128,128]{2,1,0:T(8,128)(2,1)S(1)}, bf16[3,128,128]{2,1,0:T(8,128)(2,1)S(1)}, u32[]{:S(2)}, u32[]{:S(2)}) collective-permute-start(bf16[3,128,128]{2,1,0:T(8,128)(2,1)S(1)} %get-tuple-element.20.refs_3_), channel_id=1, source_target_pairs={{0,8},{8,0},{16,24},{24,16},{1,9},{9,1},{17,25},{25,17},{2,10},{10... | collective-permute-start | bytes 294920 | tf_op jit(solution)/shard_map/ppermute | solution.py:197
  19.0 4.4 %collective-permute-start.10 = (s16[272,128]{1,0:T(8,128)(2,1)S(1)}, s16[272,128]{1,0:T(8,128)(2,1)S(1)}, u32[]{:S(2)}, u32[]{:S(2)}) collective-permute-start(s16[272,128]{1,0:T(8,128)(2,1)S(1)} %shard_map.49), channel_id=1, source_target_pairs={{0,1},{1,0},{2,3},{3,2},{4,5},{5,4},{6,7},{7,6},{8,9},{9,8},{10,11... | collective-permute-start | bytes 208904 | tf_op jit(solution)/shard_map/ppermute | solution.py:197

commit v23 on v20

--- a/solution.py
+++ b/solution.py
@@ -55,7 +55,7 @@
 def add_part(codes_ref, s, side, start, slots, left_ref, right_at, right_slots, total_ref):
     tile = total_ref.shape[1]
 
-    @pl.loop(0, left_ref.shape[0])
+    @pl.loop(0, left_ref.shape[0], unroll=True)
     def _(slot):
         code = codes_ref[(s * 2 + side) * slots + start + slot]
 
@@ -88,7 +88,7 @@
         last_ref[...] = jnp.zeros_like(last_ref)
         for side in range(2):
 
-            @pl.loop(0, slots)
+            @pl.loop(0, slots, unroll=True)
             def _(slot):
                 code = codes_ref[(last * 2 + side) * slots + slot]
 

time: 24.1 us -> 24.1 us (level)
  Pallas kernels: 4.87 us -> 4.57 us
  waiting for transfers between devices: 4.31 us -> 4.6 us
    pallas_call x1, Pallas kernels: 1.83 us -> 1.53 us  [first_products(): pl.pallas_call(kernel, out_shape=[jax.ShapeDtypeStruct((RT * tile, tile),...]
    ppermute x9, waiting for transfers between devices: 4.3 us -> 4.6 us  [across(): return lax.ppermute(block, axis, route)]
  transfers between devices with their start and end apart: 11 -> 11, of which waited for: 6 -> 6; matrix products, arithmetic and copies ran while one was open for 4% -> 4% of each run, Pallas kernels for 17% -> 15%
where the time goes in v23:
time: 24.1 us; the launch traced here: 24 us
  starting transfers between devices  13.7 us (57%)
  waiting for transfers between devices  4.6 us (19%)
  Pallas kernels  4.57 us (19%)
  local copies, waits for them, and re-layouts  1.01 us (4%)
    ppermute x9, starting transfers between devices, across(): return lax.ppermute(block, axis, route)  10.7 us
    ppermute x9, waiting for transfers between devices, across(): return lax.ppermute(block, axis, route)  4.6 us
    ppermute x2, starting transfers between devices, crossed(): return lax.ppermute(block, ('row', 'col'), route)  3.02 us
    pallas_call x1, Pallas kernels, find_matches(): pl.pallas_call(kernel, out_shape=jax.ShapeDtypeStruct((inner * 2 * slots,...  1.92 us
    pallas_call x1, Pallas kernels, first_products(): pl.pallas_call(kernel, out_shape=[jax.ShapeDtypeStruct((RT * tile, tile),...  1.53 us
    squeeze x1, local copies, waits for them, and re-layouts, shards(): given = lax.dynamic_index_in_dim(right, 1 - y, 0, keepdims=False)  1 us
    pallas_call x1, Pallas kernels, add_coded(): pl.pallas_call(kernel, out_shape=jax.ShapeDtypeStruct(total.shape, jnp.bf...  0.65 us
  transfers between devices with their start and end apart: 11, of which 6 were waited for; matrix products, arithmetic and copies ran while one was open for 4% of the time, Pallas kernels for 15%

profile of v23, /device:TPU:0, one launch (start us, length us, event | category | flops | bytes accessed | tf_op | source)
XLA Modules:
  0.0 24.0 jit_solution(14016280794630946020)
XLA Ops:
  0.0 5.0 %collective-permute-start = (bf16[6,128,128]{2,1,0:T(8,128)(2,1)}, bf16[6,128,128]{2,1,0:T(8,128)(2,1)S(1)}, u32[]{:S(2)}, u32[]{:S(2)}) collective-permute-start(bf16[6,128,128]{2,1,0:T(8,128)(2,1)} %bitcast.7), channel_id=1, source_target_pairs={{0,6},{1,7},{2,4},{3,5},{4,2},{5,3},{6,0},{7,1},{8,14},{9,15},{10,... | collective-permute-start | bytes 589832 | tf_op jit(solution)/shard_map/ppermute | solution.py:197
  5.0 0.0 collective-permute-start.2
  5.1 0.0 copy-start.1
  5.1 0.0 copy-start.2
  5.1 0.0 copy-start
  5.1 1.0 %dynamic-slice_bitcast_fusion = (bf16[3,128,128]{2,1,0:T(8,128)(2,1)S(1)}, bf16[3,128,128]{2,1,0:T(8,128)(2,1)S(1)}) fusion(bf16[1,1,2,3,128,128]{5,4,3,2,1,0:T(8,128)(2,1)} %param.6, s32[]{:T(128)S(6)} %select_n.8, s32[]{:T(128)S(6)} %select_n.7), kind=kLoop, calls=%fused_computation | loop fusion | bytes 393224 | tf_op jit(solution)/shard_map/jit(dynamic_index_in_dim)/squeeze | solution.py:230
  6.1 2.5 %collective-permute-start.7 = (bf16[3,128,128]{2,1,0:T(8,128)(2,1)S(1)}, bf16[3,128,128]{2,1,0:T(8,128)(2,1)S(1)}, u32[]{:S(2)}, u32[]{:S(2)}) collective-permute-start(bf16[3,128,128]{2,1,0:T(8,128)(2,1)S(1)} %get-tuple-element.21), channel_id=1, source_target_pairs={{0,17},{1,16},{2,19},{3,18},{4,21},{5,20},{6,23},{7,22},{8,25},{9,... | collective-permute-start | bytes 294920 | tf_op jit(solution)/shard_map/ppermute | solution.py:203
  8.6 0.5 %collective-permute-start.3 = (bf16[3,128,128]{2,1,0:T(8,128)(2,1)S(1)}, bf16[3,128,128]{2,1,0:T(8,128)(2,1)S(1)}, u32[]{:S(2)}, u32[]{:S(2)}) collective-permute-start(bf16[3,128,128]{2,1,0:T(8,128)(2,1)S(1)} %get-tuple-element.21), channel_id=1, source_target_pairs={{0,1},{1,0},{2,3},{3,2},{4,5},{5,4},{6,7},{7,6},{8,9},{9,8},{10,11... | collective-permute-start | bytes 294920 | tf_op jit(solution)/shard_map/ppermute | solution.py:203
  9.1 0.5 %collective-permute-start.6 = (bf16[3,128,128]{2,1,0:T(8,128)(2,1)S(1)}, bf16[3,128,128]{2,1,0:T(8,128)(2,1)S(1)}, u32[]{:S(2)}, u32[]{:S(2)}) collective-permute-start(bf16[3,128,128]{2,1,0:T(8,128)(2,1)S(1)} %get-tuple-element.17.refs_3_), channel_id=1, source_target_pairs={{0,16},{8,24},{16,0},{24,8},{1,17},{9,25},{17,1},{25,9},{2,18},{10... | collective-permute-start | bytes 294920 | tf_op jit(solution)/shard_map/ppermute | solution.py:197
  9.6 0.0 copy-done.1
  9.6 0.0 copy-done.2
  9.6 1.9 %shard_map.46.codes_ref = s32[48]{0:T(128)S(1)} custom-call(s32[6,4,8]{2,1,0:T(4,128)S(1)} %bitcast.10, s32[4,3,2,8]{3,2,1,0:T(2,128)S(1)} %bitcast.11), custom_call_target="tpu_custom_call" | custom-call | tf_op jit(solution)/shard_map/pallas_call | solution.py:46
  11.6 0.0 collective-permute-done.refs_2_
  11.6 2.5 %collective-permute-start.1 = (bf16[6,128,128]{2,1,0:T(8,128)(2,1)S(1)}, bf16[6,128,128]{2,1,0:T(8,128)(2,1)S(1)}, u32[]{:S(2)}, u32[]{:S(2)}) collective-permute-start(bf16[6,128,128]{2,1,0:T(8,128)(2,1)S(1)} %collective-permute-done.refs_2_), channel_id=1, source_target_pairs={{0,2},{1,3},{2,0},{3,1},{4,6},{5,7},{6,4},{7,5},{8,10},{9,11},{10,... | collective-permute-start | bytes 589832 | tf_op jit(solution)/shard_map/ppermute | solution.py:197
  14.1 0.0 collective-permute-done.7.refs_8_
  14.1 0.0 collective-permute-start.9
  14.1 0.0 collective-permute-done.3.refs_4_
  14.1 0.5 %collective-permute-start.5 = (bf16[3,128,128]{2,1,0:T(8,128)(2,1)S(1)}, bf16[3,128,128]{2,1,0:T(8,128)(2,1)S(1)}, u32[]{:S(2)}, u32[]{:S(2)}) collective-permute-start(bf16[3,128,128]{2,1,0:T(8,128)(2,1)S(1)} %collective-permute-done.3.refs_4_), channel_id=1, source_target_pairs={{0,8},{8,0},{16,24},{24,16},{1,9},{9,1},{17,25},{25,17},{2,10},{10... | collective-permute-start | bytes 294920 | tf_op jit(solution)/shard_map/ppermute | solution.py:197
  14.6 0.0 collective-permute-done.6.refs_7_
  14.6 0.1 collective-permute-start.8
  14.7 0.0 collective-permute-done.2.refs_1_
  14.7 0.4 %collective-permute-start.4 = (bf16[3,128,128]{2,1,0:T(8,128)(2,1)S(1)}, bf16[3,128,128]{2,1,0:T(8,128)(2,1)S(1)}, u32[]{:S(2)}, u32[]{:S(2)}) collective-permute-start(bf16[3,128,128]{2,1,0:T(8,128)(2,1)S(1)} %get-tuple-element.17.refs_3_), channel_id=1, source_target_pairs={{0,8},{8,0},{16,24},{24,16},{1,9},{9,1},{17,25},{25,17},{2,10},{10... | collective-permute-start | bytes 294920 | tf_op jit(solution)/shard_map/ppermute | solution.py:197
  15.1 0.3 %collective-permute-done.9.refs_10_ = bf16[3,128,128]{2,1,0:T(8,128)(2,1)S(1)} collective-permute-done((bf16[3,128,128]{2,1,0:T(8,128)(2,1)S(1)}, bf16[3,128,128]{2,1,0:T(8,128)(2,1)S(1)}, u32[]{:S(2)}, u32[]{:S(2)}) %collective-permute-start.9) | collective-permute-done | bytes 98336 | tf_op jit(solution)/shard_map/ppermute | solution.py:197
  15.4 0.2 collective-permute-done.5.refs_6_
  15.6 0.4 %collective-permute-done.8.refs_9_ = bf16[3,128,128]{2,1,0:T(8,128)(2,1)S(1)} collective-permute-done((bf16[3,128,128]{2,1,0:T(8,128)(2,1)S(1)}, bf16[3,128,128]{2,1,0:T(8,128)(2,1)S(1)}, u32[]{:S(2)}, u32[]{:S(2)}) %collective-permute-start.8) | collective-permute-done | bytes 98336 | tf_op jit(solution)/shard_map/ppermute | solution.py:197
  15.9 0.2 collective-permute-done.4.refs_5_
  16.1 0.0 copy-done
  16.1 1.5 %shard_map.47 = (f32[256,128]{1,0:T(8,128)S(1)}, f32[256,128]{1,0:T(8,128)S(1)}, bf16[2,768,256]{2,1,0:T(8,128)(2,1)S(1)}) custom-call(s32[48]{0:T(128)S(1)} %shard_map.46.codes_ref, bf16[6,128,128]{2,1,0:T(8,128)(2,1)S(1)} %bitcast.9, bf16[6,128,128]{2,1,0:T(8,128)(2,1)S(1)} %collective-permute-done.2.refs_1_, ...), custom_call_target="tpu_custom_call" | custom-call | flops 201326592 | bytes 786432 | tf_op jit(solution)/shard_map/pallas_call | solution.py:113
  17.6 1.1 %collective-permute-done.1.left_ref = bf16[6,128,128]{2,1,0:T(8,128)(2,1)S(1)} collective-permute-done((bf16[6,128,128]{2,1,0:T(8,128)(2,1)S(1)}, bf16[6,128,128]{2,1,0:T(8,128)(2,1)S(1)}, u32[]{:S(2)}, u32[]{:S(2)}) %collective-permute-start.1) | collective-permute-done | bytes 196640 | tf_op jit(solution)/shard_map/ppermute | solution.py:197
  18.7 0.3 %shard_map.49 = s16[272,128]{1,0:T(8,128)(2,1)S(1)} custom-call(bf16[6,128,128]{2,1,0:T(8,128)(2,1)S(1)} %collective-permute-done.1.left_ref, bf16[2,768,256]{2,1,0:T(8,128)(2,1)S(1)} %get-tuple-element.18.right_ref, f32[256,128]{1,0:T(8,128)S(1)} %get-tuple-element.20.total_ref), custom_call_target="tpu_custom_call" | custom-call | flops 25165824 | bytes 196608 | tf_op jit(solution)/shard_map/pallas_call | solution.py:146
  19.0 1.6 %collective-permute-start.10 = (s16[272,128]{1,0:T(8,128)(2,1)S(1)}, s16[272,128]{1,0:T(8,128)(2,1)S(1)}, u32[]{:S(2)}, u32[]{:S(2)}) collective-permute-start(s16[272,128]{1,0:T(8,128)(2,1)S(1)} %shard_map.49), channel_id=1, source_target_pairs={{0,1},{1,0},{2,3},{3,2},{4,5},{5,4},{6,7},{7,6},{8,9},{9,8},{10,11... | collective-permute-start | bytes 208904 | tf_op jit(solution)/shard_map/ppermute | solution.py:197
  20.5 0.2 shard_map.48.total_ref
  20.8 2.6 %collective-permute-done.10.coded_ref = s16[272,128]{1,0:T(8,128)(2,1)S(1)} collective-permute-done((s16[272,128]{1,0:T(8,128)(2,1)S(1)}, s16[272,128]{1,0:T(8,128)(2,1)S(1)}, u32[]{:S(2)}, u32[]{:S(2)}) %collective-permute-start.10) | collective-permute-done | bytes 69664 | tf_op jit(solution)/shard_map/ppermute | solution.py:197
  23.3 0.7 %shard_map.50 = bf16[256,128]{1,0:T(8,128)(2,1)} custom-call(f32[256,128]{1,0:T(8,128)S(1)} %shard_map.48.total_ref, s16[272,128]{1,0:T(8,128)(2,1)S(1)} %collective-permute-done.10.coded_ref), custom_call_target="tpu_custom_call" | custom-call | tf_op jit(solution)/shard_map/pallas_call | solution.py:186
Async XLA Ops:
  0.0 11.6 %collective-permute-start = (bf16[6,128,128]{2,1,0:T(8,128)(2,1)}, bf16[6,128,128]{2,1,0:T(8,128)(2,1)S(1)}, u32[]{:S(2)}, u32[]{:S(2)}) collective-permute-start(bf16[6,128,128]{2,1,0:T(8,128)(2,1)} %bitcast.7), channel_id=1, source_target_pairs={{0,6},{1,7},{2,4},{3,5},{4,2},{5,3},{6,0},{7,1},{8,14},{9,15},{10,... | collective-permute-start | bytes 589832 | tf_op jit(solution)/shard_map/ppermute | solution.py:197
  5.0 9.6 %collective-permute-start.2 = (bf16[6,128,128]{2,1,0:T(8,128)(2,1)}, bf16[6,128,128]{2,1,0:T(8,128)(2,1)S(1)}, u32[]{:S(2)}, u32[]{:S(2)}) collective-permute-start(bf16[6,128,128]{2,1,0:T(8,128)(2,1)} %bitcast.8), channel_id=1, source_target_pairs={{0,2},{1,3},{2,0},{3,1},{4,6},{5,7},{6,4},{7,5},{8,10},{9,11},{10,... | collective-permute-start | bytes 589832 | tf_op jit(solution)/shard_map/ppermute | solution.py:197
  5.1 4.6 %copy-start.1 = (s32[4,8,6]{1,0,2:T(4,128)S(1)}, s32[4,8,6]{1,0,2:T(4,128)}, u32[]{:S(2)}) copy-start(s32[4,8,6]{1,0,2:T(4,128)} %param.5) | copy-start | bytes 2308
  5.1 4.6 %copy-start.2 = (s32[4,8,2,3]{1,2,3,0:T(2,128)S(1)}, s32[4,8,2,3]{1,2,3,0:T(2,128)}, u32[]{:S(2)}) copy-start(s32[4,8,2,3]{1,2,3,0:T(2,128)} %param.7) | copy-start | bytes 2308
  5.1 11.0 %copy-start = (bf16[1,1,6,128,128]{4,3,2,1,0:T(8,128)(2,1)S(1)}, bf16[1,1,6,128,128]{4,3,2,1,0:T(8,128)(2,1)}, u32[]{:S(2)}) copy-start(bf16[1,1,6,128,128]{4,3,2,1,0:T(8,128)(2,1)} %param.4) | copy-start | bytes 589828
  6.1 8.0 %collective-permute-start.7 = (bf16[3,128,128]{2,1,0:T(8,128)(2,1)S(1)}, bf16[3,128,128]{2,1,0:T(8,128)(2,1)S(1)}, u32[]{:S(2)}, u32[]{:S(2)}) collective-permute-start(bf16[3,128,128]{2,1,0:T(8,128)(2,1)S(1)} %get-tuple-element.21), channel_id=1, source_target_pairs={{0,17},{1,16},{2,19},{3,18},{4,21},{5,20},{6,23},{7,22},{8,25},{9,... | collective-permute-start | bytes 294920 | tf_op jit(solution)/shard_map/ppermute | solution.py:203
  8.6 5.5 %collective-permute-start.3 = (bf16[3,128,128]{2,1,0:T(8,128)(2,1)S(1)}, bf16[3,128,128]{2,1,0:T(8,128)(2,1)S(1)}, u32[]{:S(2)}, u32[]{:S(2)}) collective-permute-start(bf16[3,128,128]{2,1,0:T(8,128)(2,1)S(1)} %get-tuple-element.21), channel_id=1, source_target_pairs={{0,1},{1,0},{2,3},{3,2},{4,5},{5,4},{6,7},{7,6},{8,9},{9,8},{10,11... | collective-permute-start | bytes 294920 | tf_op jit(solution)/shard_map/ppermute | solution.py:203
  9.1 5.5 %collective-permute-start.6 = (bf16[3,128,128]{2,1,0:T(8,128)(2,1)S(1)}, bf16[3,128,128]{2,1,0:T(8,128)(2,1)S(1)}, u32[]{:S(2)}, u32[]{:S(2)}) collective-permute-start(bf16[3,128,128]{2,1,0:T(8,128)(2,1)S(1)} %get-tuple-element.17.refs_3_), channel_id=1, source_target_pairs={{0,16},{8,24},{16,0},{24,8},{1,17},{9,25},{17,1},{25,9},{2,18},{10... | collective-permute-start | bytes 294920 | tf_op jit(solution)/shard_map/ppermute | solution.py:197
  11.6 7.1 %collective-permute-start.1 = (bf16[6,128,128]{2,1,0:T(8,128)(2,1)S(1)}, bf16[6,128,128]{2,1,0:T(8,128)(2,1)S(1)}, u32[]{:S(2)}, u32[]{:S(2)}) collective-permute-start(bf16[6,128,128]{2,1,0:T(8,128)(2,1)S(1)} %collective-permute-done.refs_2_), channel_id=1, source_target_pairs={{0,2},{1,3},{2,0},{3,1},{4,6},{5,7},{6,4},{7,5},{8,10},{9,11},{10,... | collective-permute-start | bytes 589832 | tf_op jit(solution)/shard_map/ppermute | solution.py:197
  14.1 1.3 %collective-permute-start.9 = (bf16[3,128,128]{2,1,0:T(8,128)(2,1)S(1)}, bf16[3,128,128]{2,1,0:T(8,128)(2,1)S(1)}, u32[]{:S(2)}, u32[]{:S(2)}) collective-permute-start(bf16[3,128,128]{2,1,0:T(8,128)(2,1)S(1)} %collective-permute-done.7.refs_8_), channel_id=1, source_target_pairs={{0,8},{8,0},{16,24},{24,16},{1,9},{9,1},{17,25},{25,17},{2,10},{10... | collective-permute-start | bytes 294920 | tf_op jit(solution)/shard_map/ppermute | solution.py:197
  14.1 1.5 %collective-permute-start.5 = (bf16[3,128,128]{2,1,0:T(8,128)(2,1)S(1)}, bf16[3,128,128]{2,1,0:T(8,128)(2,1)S(1)}, u32[]{:S(2)}, u32[]{:S(2)}) collective-permute-start(bf16[3,128,128]{2,1,0:T(8,128)(2,1)S(1)} %collective-permute-done.3.refs_4_), channel_id=1, source_target_pairs={{0,8},{8,0},{16,24},{24,16},{1,9},{9,1},{17,25},{25,17},{2,10},{10... | collective-permute-start | bytes 294920 | tf_op jit(solution)/shard_map/ppermute | solution.py:197
  14.6 1.3 %collective-permute-start.8 = (bf16[3,128,128]{2,1,0:T(8,128)(2,1)S(1)}, bf16[3,128,128]{2,1,0:T(8,128)(2,1)S(1)}, u32[]{:S(2)}, u32[]{:S(2)}) collective-permute-start(bf16[3,128,128]{2,1,0:T(8,128)(2,1)S(1)} %collective-permute-done.6.refs_7_), channel_id=1, source_target_pairs={{0,8},{8,0},{16,24},{24,16},{1,9},{9,1},{17,25},{25,17},{2,10},{10... | collective-permute-start | bytes 294920 | tf_op jit(solution)/shard_map/ppermute | solution.py:197
  14.7 1.4 %collective-permute-start.4 = (bf16[3,128,128]{2,1,0:T(8,128)(2,1)S(1)}, bf16[3,128,128]{2,1,0:T(8,128)(2,1)S(1)}, u32[]{:S(2)}, u32[]{:S(2)}) collective-permute-start(bf16[3,128,128]{2,1,0:T(8,128)(2,1)S(1)} %get-tuple-element.17.refs_3_), channel_id=1, source_target_pairs={{0,8},{8,0},{16,24},{24,16},{1,9},{9,1},{17,25},{25,17},{2,10},{10... | collective-permute-start | bytes 294920 | tf_op jit(solution)/shard_map/ppermute | solution.py:197
  19.0 4.4 %collective-permute-start.10 = (s16[272,128]{1,0:T(8,128)(2,1)S(1)}, s16[272,128]{1,0:T(8,128)(2,1)S(1)}, u32[]{:S(2)}, u32[]{:S(2)}) collective-permute-start(s16[272,128]{1,0:T(8,128)(2,1)S(1)} %shard_map.49), channel_id=1, source_target_pairs={{0,1},{1,0},{2,3},{3,2},{4,5},{5,4},{6,7},{7,6},{8,9},{9,8},{10,11... | collective-permute-start | bytes 208904 | tf_op jit(solution)/shard_map/ppermute | solution.py:197

commit v24 on v23

--- a/solution.py
+++ b/solution.py
@@ -174,20 +174,30 @@
 
 
 def add_coded(total, coded):
-    def kernel(total_ref, coded_ref, out_ref):
+    def kernel(total_ref, coded_ref, out_ref, sums, done):
         tile = total_ref.shape[1]
         exponents = coded_ref[RT * tile :, :].astype(jnp.int32).astype(jnp.float32)
+        copies = []
         for i in range(RT):
             rows = slice(i * tile, (i + 1) * tile)
             scale = jnp.exp2(exponents[i : i + 1, :] - BITS)
             values = coded_ref[rows, :].astype(jnp.int32).astype(jnp.float32)
-            out_ref[rows, :] = (total_ref[rows, :] + values * scale).astype(out_ref.dtype)
+            sums[i] = (total_ref[rows, :] + values * scale).astype(sums.dtype)
+            copy = pltpu.make_async_copy(sums.at[i], out_ref.at[pl.ds(i * tile, tile)], done.at[i])
+            copy.start()
+            copies.append(copy)
+        for copy in copies:
+            copy.wait()
 
     return pl.pallas_call(
         kernel,
         out_shape=jax.ShapeDtypeStruct(total.shape, jnp.bfloat16),
         in_specs=[VMEM] * 2,
-        out_specs=VMEM,
+        out_specs=pl.BlockSpec(memory_space=pl.ANY),
+        scratch_shapes=[
+            pltpu.VMEM((RT, total.shape[0] // RT, total.shape[1]), jnp.bfloat16),
+            pltpu.SemaphoreType.DMA((RT,)),
+        ],
         compiler_params=pltpu.CompilerParams(vmem_limit_bytes=8 * 1024 * 1024),
     )(total, coded)
 

time: 24.1 us -> 24.2 us (level)
  transfers between devices with their start and end apart: 11 -> 11, of which waited for: 6 -> 6; matrix products, arithmetic and copies ran while one was open for 4% -> 4% of each run, Pallas kernels for 15% -> 16%
where the time goes in v24:
time: 24.2 us; the launch traced here: 24 us
  starting transfers between devices  13.7 us (57%)
  Pallas kernels  4.68 us (19%)
  waiting for transfers between devices  4.51 us (19%)
  local copies, waits for them, and re-layouts  1.01 us (4%)
    ppermute x9, starting transfers between devices, across(): return lax.ppermute(block, axis, route)  10.7 us
    ppermute x9, waiting for transfers between devices, across(): return lax.ppermute(block, axis, route)  4.51 us
    ppermute x2, starting transfers between devices, crossed(): return lax.ppermute(block, ('row', 'col'), route)  3.02 us
    pallas_call x1, Pallas kernels, find_matches(): pl.pallas_call(kernel, out_shape=jax.ShapeDtypeStruct((inner * 2 * slots,...  1.92 us
    pallas_call x1, Pallas kernels, first_products(): pl.pallas_call(kernel, out_shape=[jax.ShapeDtypeStruct((RT * tile, tile),...  1.63 us
    squeeze x1, local copies, waits for them, and re-layouts, shards(): given = lax.dynamic_index_in_dim(right, 1 - y, 0, keepdims=False)  1 us
    pallas_call x1, Pallas kernels, add_coded(): pl.pallas_call(kernel, out_shape=jax.ShapeDtypeStruct(total.shape, jnp.bf...  0.66 us
  transfers between devices with their start and end apart: 11, of which 6 were waited for; matrix products, arithmetic and copies ran while one was open for 4% of the time, Pallas kernels for 16%

profile of v24, /device:TPU:0, one launch (start us, length us, event | category | flops | bytes accessed | tf_op | source)
XLA Modules:
  0.0 24.0 jit_solution(8813896679336459274)
XLA Ops:
  0.0 5.0 %collective-permute-start = (bf16[6,128,128]{2,1,0:T(8,128)(2,1)}, bf16[6,128,128]{2,1,0:T(8,128)(2,1)S(1)}, u32[]{:S(2)}, u32[]{:S(2)}) collective-permute-start(bf16[6,128,128]{2,1,0:T(8,128)(2,1)} %bitcast.7), channel_id=1, source_target_pairs={{0,6},{1,7},{2,4},{3,5},{4,2},{5,3},{6,0},{7,1},{8,14},{9,15},{10,... | collective-permute-start | bytes 589832 | tf_op jit(solution)/shard_map/ppermute | solution.py:207
  5.0 0.0 collective-permute-start.2
  5.1 0.0 copy-start.1
  5.1 0.0 copy-start.2
  5.1 0.0 copy-start
  5.1 1.0 %dynamic-slice_bitcast_fusion = (bf16[3,128,128]{2,1,0:T(8,128)(2,1)S(1)}, bf16[3,128,128]{2,1,0:T(8,128)(2,1)S(1)}) fusion(bf16[1,1,2,3,128,128]{5,4,3,2,1,0:T(8,128)(2,1)} %param.6, s32[]{:T(128)S(6)} %select_n.8, s32[]{:T(128)S(6)} %select_n.7), kind=kLoop, calls=%fused_computation | loop fusion | bytes 393224 | tf_op jit(solution)/shard_map/jit(dynamic_index_in_dim)/squeeze | solution.py:240
  6.1 2.5 %collective-permute-start.7 = (bf16[3,128,128]{2,1,0:T(8,128)(2,1)S(1)}, bf16[3,128,128]{2,1,0:T(8,128)(2,1)S(1)}, u32[]{:S(2)}, u32[]{:S(2)}) collective-permute-start(bf16[3,128,128]{2,1,0:T(8,128)(2,1)S(1)} %get-tuple-element.21), channel_id=1, source_target_pairs={{0,17},{1,16},{2,19},{3,18},{4,21},{5,20},{6,23},{7,22},{8,25},{9,... | collective-permute-start | bytes 294920 | tf_op jit(solution)/shard_map/ppermute | solution.py:213
  8.6 0.5 %collective-permute-start.3 = (bf16[3,128,128]{2,1,0:T(8,128)(2,1)S(1)}, bf16[3,128,128]{2,1,0:T(8,128)(2,1)S(1)}, u32[]{:S(2)}, u32[]{:S(2)}) collective-permute-start(bf16[3,128,128]{2,1,0:T(8,128)(2,1)S(1)} %get-tuple-element.21), channel_id=1, source_target_pairs={{0,1},{1,0},{2,3},{3,2},{4,5},{5,4},{6,7},{7,6},{8,9},{9,8},{10,11... | collective-permute-start | bytes 294920 | tf_op jit(solution)/shard_map/ppermute | solution.py:213
  9.1 0.5 %collective-permute-start.6 = (bf16[3,128,128]{2,1,0:T(8,128)(2,1)S(1)}, bf16[3,128,128]{2,1,0:T(8,128)(2,1)S(1)}, u32[]{:S(2)}, u32[]{:S(2)}) collective-permute-start(bf16[3,128,128]{2,1,0:T(8,128)(2,1)S(1)} %get-tuple-element.17.refs_3_), channel_id=1, source_target_pairs={{0,16},{8,24},{16,0},{24,8},{1,17},{9,25},{17,1},{25,9},{2,18},{10... | collective-permute-start | bytes 294920 | tf_op jit(solution)/shard_map/ppermute | solution.py:207
  9.6 0.0 copy-done.1
  9.6 0.0 copy-done.2
  9.6 1.9 %shard_map.46.codes_ref = s32[48]{0:T(128)S(1)} custom-call(s32[6,4,8]{2,1,0:T(4,128)S(1)} %bitcast.10, s32[4,3,2,8]{3,2,1,0:T(2,128)S(1)} %bitcast.11), custom_call_target="tpu_custom_call" | custom-call | tf_op jit(solution)/shard_map/pallas_call | solution.py:46
  11.6 0.0 collective-permute-done.refs_2_
  11.6 2.5 %collective-permute-start.1 = (bf16[6,128,128]{2,1,0:T(8,128)(2,1)S(1)}, bf16[6,128,128]{2,1,0:T(8,128)(2,1)S(1)}, u32[]{:S(2)}, u32[]{:S(2)}) collective-permute-start(bf16[6,128,128]{2,1,0:T(8,128)(2,1)S(1)} %collective-permute-done.refs_2_), channel_id=1, source_target_pairs={{0,2},{1,3},{2,0},{3,1},{4,6},{5,7},{6,4},{7,5},{8,10},{9,11},{10,... | collective-permute-start | bytes 589832 | tf_op jit(solution)/shard_map/ppermute | solution.py:207
  14.1 0.0 collective-permute-done.7.refs_8_
  14.1 0.0 collective-permute-start.9
  14.1 0.0 collective-permute-done.3.refs_4_
  14.1 0.5 %collective-permute-start.5 = (bf16[3,128,128]{2,1,0:T(8,128)(2,1)S(1)}, bf16[3,128,128]{2,1,0:T(8,128)(2,1)S(1)}, u32[]{:S(2)}, u32[]{:S(2)}) collective-permute-start(bf16[3,128,128]{2,1,0:T(8,128)(2,1)S(1)} %collective-permute-done.3.refs_4_), channel_id=1, source_target_pairs={{0,8},{8,0},{16,24},{24,16},{1,9},{9,1},{17,25},{25,17},{2,10},{10... | collective-permute-start | bytes 294920 | tf_op jit(solution)/shard_map/ppermute | solution.py:207
  14.6 0.0 collective-permute-done.6.refs_7_
  14.6 0.1 collective-permute-start.8
  14.7 0.0 collective-permute-done.2.refs_1_
  14.7 0.4 %collective-permute-start.4 = (bf16[3,128,128]{2,1,0:T(8,128)(2,1)S(1)}, bf16[3,128,128]{2,1,0:T(8,128)(2,1)S(1)}, u32[]{:S(2)}, u32[]{:S(2)}) collective-permute-start(bf16[3,128,128]{2,1,0:T(8,128)(2,1)S(1)} %get-tuple-element.17.refs_3_), channel_id=1, source_target_pairs={{0,8},{8,0},{16,24},{24,16},{1,9},{9,1},{17,25},{25,17},{2,10},{10... | collective-permute-start | bytes 294920 | tf_op jit(solution)/shard_map/ppermute | solution.py:207
  15.1 0.3 %collective-permute-done.9.refs_10_ = bf16[3,128,128]{2,1,0:T(8,128)(2,1)S(1)} collective-permute-done((bf16[3,128,128]{2,1,0:T(8,128)(2,1)S(1)}, bf16[3,128,128]{2,1,0:T(8,128)(2,1)S(1)}, u32[]{:S(2)}, u32[]{:S(2)}) %collective-permute-start.9) | collective-permute-done | bytes 98336 | tf_op jit(solution)/shard_map/ppermute | solution.py:207
  15.4 0.2 collective-permute-done.5.refs_6_
  15.6 0.4 %collective-permute-done.8.refs_9_ = bf16[3,128,128]{2,1,0:T(8,128)(2,1)S(1)} collective-permute-done((bf16[3,128,128]{2,1,0:T(8,128)(2,1)S(1)}, bf16[3,128,128]{2,1,0:T(8,128)(2,1)S(1)}, u32[]{:S(2)}, u32[]{:S(2)}) %collective-permute-start.8) | collective-permute-done | bytes 98336 | tf_op jit(solution)/shard_map/ppermute | solution.py:207
  15.9 0.2 collective-permute-done.4.refs_5_
  16.1 0.0 copy-done
  16.1 1.6 %shard_map.47 = (f32[256,128]{1,0:T(8,128)S(1)}, f32[256,128]{1,0:T(8,128)S(1)}, bf16[2,768,256]{2,1,0:T(8,128)(2,1)S(1)}) custom-call(s32[48]{0:T(128)S(1)} %shard_map.46.codes_ref, bf16[6,128,128]{2,1,0:T(8,128)(2,1)S(1)} %bitcast.9, bf16[6,128,128]{2,1,0:T(8,128)(2,1)S(1)} %collective-permute-done.2.refs_1_, ...), custom_call_target="tpu_custom_call" | custom-call | flops 201326592 | bytes 786432 | tf_op jit(solution)/shard_map/pallas_call | solution.py:113
  17.7 1.0 %collective-permute-done.1.left_ref = bf16[6,128,128]{2,1,0:T(8,128)(2,1)S(1)} collective-permute-done((bf16[6,128,128]{2,1,0:T(8,128)(2,1)S(1)}, bf16[6,128,128]{2,1,0:T(8,128)(2,1)S(1)}, u32[]{:S(2)}, u32[]{:S(2)}) %collective-permute-start.1) | collective-permute-done | bytes 196640 | tf_op jit(solution)/shard_map/ppermute | solution.py:207
  18.7 0.3 %shard_map.49 = s16[272,128]{1,0:T(8,128)(2,1)S(1)} custom-call(bf16[6,128,128]{2,1,0:T(8,128)(2,1)S(1)} %collective-permute-done.1.left_ref, bf16[2,768,256]{2,1,0:T(8,128)(2,1)S(1)} %get-tuple-element.18.right_ref, f32[256,128]{1,0:T(8,128)S(1)} %get-tuple-element.20.total_ref), custom_call_target="tpu_custom_call" | custom-call | flops 25165824 | bytes 196608 | tf_op jit(solution)/shard_map/pallas_call | solution.py:146
  19.0 1.6 %collective-permute-start.10 = (s16[272,128]{1,0:T(8,128)(2,1)S(1)}, s16[272,128]{1,0:T(8,128)(2,1)S(1)}, u32[]{:S(2)}, u32[]{:S(2)}) collective-permute-start(s16[272,128]{1,0:T(8,128)(2,1)S(1)} %shard_map.49), channel_id=1, source_target_pairs={{0,1},{1,0},{2,3},{3,2},{4,5},{5,4},{6,7},{7,6},{8,9},{9,8},{10,11... | collective-permute-start | bytes 208904 | tf_op jit(solution)/shard_map/ppermute | solution.py:207
  20.5 0.2 shard_map.48.total_ref
  20.8 2.6 %collective-permute-done.10.coded_ref = s16[272,128]{1,0:T(8,128)(2,1)S(1)} collective-permute-done((s16[272,128]{1,0:T(8,128)(2,1)S(1)}, s16[272,128]{1,0:T(8,128)(2,1)S(1)}, u32[]{:S(2)}, u32[]{:S(2)}) %collective-permute-start.10) | collective-permute-done | bytes 69664 | tf_op jit(solution)/shard_map/ppermute | solution.py:207
  23.3 0.7 %shard_map.50 = bf16[256,128]{1,0:T(8,128)(2,1)} custom-call(f32[256,128]{1,0:T(8,128)S(1)} %shard_map.48.total_ref, s16[272,128]{1,0:T(8,128)(2,1)S(1)} %collective-permute-done.10.coded_ref), custom_call_target="tpu_custom_call" | custom-call | tf_op jit(solution)/shard_map/pallas_call | solution.py:192
Async XLA Ops:
  0.0 11.6 %collective-permute-start = (bf16[6,128,128]{2,1,0:T(8,128)(2,1)}, bf16[6,128,128]{2,1,0:T(8,128)(2,1)S(1)}, u32[]{:S(2)}, u32[]{:S(2)}) collective-permute-start(bf16[6,128,128]{2,1,0:T(8,128)(2,1)} %bitcast.7), channel_id=1, source_target_pairs={{0,6},{1,7},{2,4},{3,5},{4,2},{5,3},{6,0},{7,1},{8,14},{9,15},{10,... | collective-permute-start | bytes 589832 | tf_op jit(solution)/shard_map/ppermute | solution.py:207
  5.0 9.6 %collective-permute-start.2 = (bf16[6,128,128]{2,1,0:T(8,128)(2,1)}, bf16[6,128,128]{2,1,0:T(8,128)(2,1)S(1)}, u32[]{:S(2)}, u32[]{:S(2)}) collective-permute-start(bf16[6,128,128]{2,1,0:T(8,128)(2,1)} %bitcast.8), channel_id=1, source_target_pairs={{0,2},{1,3},{2,0},{3,1},{4,6},{5,7},{6,4},{7,5},{8,10},{9,11},{10,... | collective-permute-start | bytes 589832 | tf_op jit(solution)/shard_map/ppermute | solution.py:207
  5.1 4.6 %copy-start.1 = (s32[4,8,6]{1,0,2:T(4,128)S(1)}, s32[4,8,6]{1,0,2:T(4,128)}, u32[]{:S(2)}) copy-start(s32[4,8,6]{1,0,2:T(4,128)} %param.5) | copy-start | bytes 2308
  5.1 4.6 %copy-start.2 = (s32[4,8,2,3]{1,2,3,0:T(2,128)S(1)}, s32[4,8,2,3]{1,2,3,0:T(2,128)}, u32[]{:S(2)}) copy-start(s32[4,8,2,3]{1,2,3,0:T(2,128)} %param.7) | copy-start | bytes 2308
  5.1 11.0 %copy-start = (bf16[1,1,6,128,128]{4,3,2,1,0:T(8,128)(2,1)S(1)}, bf16[1,1,6,128,128]{4,3,2,1,0:T(8,128)(2,1)}, u32[]{:S(2)}) copy-start(bf16[1,1,6,128,128]{4,3,2,1,0:T(8,128)(2,1)} %param.4) | copy-start | bytes 589828
  6.1 8.0 %collective-permute-start.7 = (bf16[3,128,128]{2,1,0:T(8,128)(2,1)S(1)}, bf16[3,128,128]{2,1,0:T(8,128)(2,1)S(1)}, u32[]{:S(2)}, u32[]{:S(2)}) collective-permute-start(bf16[3,128,128]{2,1,0:T(8,128)(2,1)S(1)} %get-tuple-element.21), channel_id=1, source_target_pairs={{0,17},{1,16},{2,19},{3,18},{4,21},{5,20},{6,23},{7,22},{8,25},{9,... | collective-permute-start | bytes 294920 | tf_op jit(solution)/shard_map/ppermute | solution.py:213
  8.6 5.5 %collective-permute-start.3 = (bf16[3,128,128]{2,1,0:T(8,128)(2,1)S(1)}, bf16[3,128,128]{2,1,0:T(8,128)(2,1)S(1)}, u32[]{:S(2)}, u32[]{:S(2)}) collective-permute-start(bf16[3,128,128]{2,1,0:T(8,128)(2,1)S(1)} %get-tuple-element.21), channel_id=1, source_target_pairs={{0,1},{1,0},{2,3},{3,2},{4,5},{5,4},{6,7},{7,6},{8,9},{9,8},{10,11... | collective-permute-start | bytes 294920 | tf_op jit(solution)/shard_map/ppermute | solution.py:213
  9.1 5.5 %collective-permute-start.6 = (bf16[3,128,128]{2,1,0:T(8,128)(2,1)S(1)}, bf16[3,128,128]{2,1,0:T(8,128)(2,1)S(1)}, u32[]{:S(2)}, u32[]{:S(2)}) collective-permute-start(bf16[3,128,128]{2,1,0:T(8,128)(2,1)S(1)} %get-tuple-element.17.refs_3_), channel_id=1, source_target_pairs={{0,16},{8,24},{16,0},{24,8},{1,17},{9,25},{17,1},{25,9},{2,18},{10... | collective-permute-start | bytes 294920 | tf_op jit(solution)/shard_map/ppermute | solution.py:207
  11.6 7.1 %collective-permute-start.1 = (bf16[6,128,128]{2,1,0:T(8,128)(2,1)S(1)}, bf16[6,128,128]{2,1,0:T(8,128)(2,1)S(1)}, u32[]{:S(2)}, u32[]{:S(2)}) collective-permute-start(bf16[6,128,128]{2,1,0:T(8,128)(2,1)S(1)} %collective-permute-done.refs_2_), channel_id=1, source_target_pairs={{0,2},{1,3},{2,0},{3,1},{4,6},{5,7},{6,4},{7,5},{8,10},{9,11},{10,... | collective-permute-start | bytes 589832 | tf_op jit(solution)/shard_map/ppermute | solution.py:207
  14.1 1.3 %collective-permute-start.9 = (bf16[3,128,128]{2,1,0:T(8,128)(2,1)S(1)}, bf16[3,128,128]{2,1,0:T(8,128)(2,1)S(1)}, u32[]{:S(2)}, u32[]{:S(2)}) collective-permute-start(bf16[3,128,128]{2,1,0:T(8,128)(2,1)S(1)} %collective-permute-done.7.refs_8_), channel_id=1, source_target_pairs={{0,8},{8,0},{16,24},{24,16},{1,9},{9,1},{17,25},{25,17},{2,10},{10... | collective-permute-start | bytes 294920 | tf_op jit(solution)/shard_map/ppermute | solution.py:207
  14.1 1.5 %collective-permute-start.5 = (bf16[3,128,128]{2,1,0:T(8,128)(2,1)S(1)}, bf16[3,128,128]{2,1,0:T(8,128)(2,1)S(1)}, u32[]{:S(2)}, u32[]{:S(2)}) collective-permute-start(bf16[3,128,128]{2,1,0:T(8,128)(2,1)S(1)} %collective-permute-done.3.refs_4_), channel_id=1, source_target_pairs={{0,8},{8,0},{16,24},{24,16},{1,9},{9,1},{17,25},{25,17},{2,10},{10... | collective-permute-start | bytes 294920 | tf_op jit(solution)/shard_map/ppermute | solution.py:207
  14.6 1.3 %collective-permute-start.8 = (bf16[3,128,128]{2,1,0:T(8,128)(2,1)S(1)}, bf16[3,128,128]{2,1,0:T(8,128)(2,1)S(1)}, u32[]{:S(2)}, u32[]{:S(2)}) collective-permute-start(bf16[3,128,128]{2,1,0:T(8,128)(2,1)S(1)} %collective-permute-done.6.refs_7_), channel_id=1, source_target_pairs={{0,8},{8,0},{16,24},{24,16},{1,9},{9,1},{17,25},{25,17},{2,10},{10... | collective-permute-start | bytes 294920 | tf_op jit(solution)/shard_map/ppermute | solution.py:207
  14.7 1.4 %collective-permute-start.4 = (bf16[3,128,128]{2,1,0:T(8,128)(2,1)S(1)}, bf16[3,128,128]{2,1,0:T(8,128)(2,1)S(1)}, u32[]{:S(2)}, u32[]{:S(2)}) collective-permute-start(bf16[3,128,128]{2,1,0:T(8,128)(2,1)S(1)} %get-tuple-element.17.refs_3_), channel_id=1, source_target_pairs={{0,8},{8,0},{16,24},{24,16},{1,9},{9,1},{17,25},{25,17},{2,10},{10... | collective-permute-start | bytes 294920 | tf_op jit(solution)/shard_map/ppermute | solution.py:207
  19.0 4.4 %collective-permute-start.10 = (s16[272,128]{1,0:T(8,128)(2,1)S(1)}, s16[272,128]{1,0:T(8,128)(2,1)S(1)}, u32[]{:S(2)}, u32[]{:S(2)}) collective-permute-start(s16[272,128]{1,0:T(8,128)(2,1)S(1)} %shard_map.49), channel_id=1, source_target_pairs={{0,1},{1,0},{2,3},{3,2},{4,5},{5,4},{6,7},{7,6},{8,9},{9,8},{10,11... | collective-permute-start | bytes 208904 | tf_op jit(solution)/shard_map/ppermute | solution.py:207

commit v25 on v23

--- a/solution.py
+++ b/solution.py
@@ -232,6 +232,8 @@
     lefts, codes = gather(left, codes, y)
     rights = []
     for t in range(0, lax.axis_size("row"), 2):
+        if t:
+            given, rights[1] = lax.optimization_barrier((given, rights[1]))
         pair = [across(own, "row", t) if t else own, crossed(given, t)]
         if not t:
             pair[0], near = lax.optimization_barrier((pair[0], lefts[1][1]))

time: 24.1 us -> 26.3 us (1.091)
  waiting for transfers between devices: 4.6 us -> 8.12 us
  starting transfers between devices: 13.7 us -> 12.5 us
    ppermute x9, starting transfers between devices: 10.7 us -> 8.51 us  [across(): return lax.ppermute(block, axis, route)]
    ppermute x2, waiting for transfers between devices: 0.01 us -> 2.06 us  [crossed(): return lax.ppermute(block, ('row', 'col'), route)]
    ppermute x9, waiting for transfers between devices: 4.6 us -> 6.06 us  [across(): return lax.ppermute(block, axis, route)]
    ppermute x2, starting transfers between devices: 3.02 us -> 4.03 us  [crossed(): return lax.ppermute(block, ('row', 'col'), route)]
  transfers between devices with their start and end apart: 11 -> 11, of which waited for: 6 -> 6; matrix products, arithmetic and copies ran while one was open for 4% -> 4% of each run, Pallas kernels for 15% -> 13%
where the time goes in v25:
time: 26.3 us; the launch traced here: 26.2 us
  starting transfers between devices  12.5 us (48%)
  waiting for transfers between devices  8.12 us (31%)
  Pallas kernels  4.41 us (17%)
  local copies, waits for them, and re-layouts  1 us (4%)
    ppermute x9, starting transfers between devices, across(): return lax.ppermute(block, axis, route)  8.51 us
    ppermute x9, waiting for transfers between devices, across(): return lax.ppermute(block, axis, route)  6.06 us
    ppermute x2, starting transfers between devices, crossed(): return lax.ppermute(block, ('row', 'col'), route)  4.03 us
    ppermute x2, waiting for transfers between devices, crossed(): return lax.ppermute(block, ('row', 'col'), route)  2.06 us
    pallas_call x1, Pallas kernels, find_matches(): pl.pallas_call(kernel, out_shape=jax.ShapeDtypeStruct((inner * 2 * slots,...  1.92 us
    pallas_call x1, Pallas kernels, first_products(): pl.pallas_call(kernel, out_shape=[jax.ShapeDtypeStruct((RT * tile, tile),...  1.37 us
    squeeze x1, local copies, waits for them, and re-layouts, shards(): given = lax.dynamic_index_in_dim(right, 1 - y, 0, keepdims=False)  0.99 us
    pallas_call x1, Pallas kernels, add_coded(): pl.pallas_call(kernel, out_shape=jax.ShapeDtypeStruct(total.shape, jnp.bf...  0.65 us
  transfers between devices with their start and end apart: 11, of which 6 were waited for; matrix products, arithmetic and copies ran while one was open for 4% of the time, Pallas kernels for 13%

profile of v25, /device:TPU:0, one launch (start us, length us, event | category | flops | bytes accessed | tf_op | source)
XLA Modules:
  0.0 26.2 jit_solution(11079930871517228316)
XLA Ops:
  0.0 5.0 %collective-permute-start = (bf16[6,128,128]{2,1,0:T(8,128)(2,1)}, bf16[6,128,128]{2,1,0:T(8,128)(2,1)S(1)}, u32[]{:S(2)}, u32[]{:S(2)}) collective-permute-start(bf16[6,128,128]{2,1,0:T(8,128)(2,1)} %bitcast.7), channel_id=1, source_target_pairs={{0,6},{1,7},{2,4},{3,5},{4,2},{5,3},{6,0},{7,1},{8,14},{9,15},{10,... | collective-permute-start | bytes 589832 | tf_op jit(solution)/shard_map/ppermute | solution.py:197
  5.0 0.0 copy-start
  5.1 0.0 copy-start.1
  5.1 0.0 copy-start.2
  5.1 1.0 %dynamic-slice_bitcast_fusion = (bf16[3,128,128]{2,1,0:T(8,128)(2,1)S(1)}, bf16[3,128,128]{2,1,0:T(8,128)(2,1)S(1)}) fusion(bf16[1,1,2,3,128,128]{5,4,3,2,1,0:T(8,128)(2,1)} %param.6, s32[]{:T(128)S(6)} %select_n.8, s32[]{:T(128)S(6)} %select_n.7), kind=kLoop, calls=%fused_computation | loop fusion | bytes 393224 | tf_op jit(solution)/shard_map/jit(dynamic_index_in_dim)/squeeze | solution.py:230
  6.1 1.6 %collective-permute-start.3 = (bf16[3,128,128]{2,1,0:T(8,128)(2,1)S(1)}, bf16[3,128,128]{2,1,0:T(8,128)(2,1)S(1)}, u32[]{:S(2)}, u32[]{:S(2)}) collective-permute-start(bf16[3,128,128]{2,1,0:T(8,128)(2,1)S(1)} %get-tuple-element.21), channel_id=1, source_target_pairs={{0,1},{1,0},{2,3},{3,2},{4,5},{5,4},{6,7},{7,6},{8,9},{9,8},{10,11... | collective-permute-start | bytes 294920 | tf_op jit(solution)/shard_map/ppermute | solution.py:203
  7.6 0.0 copy-done
  7.6 0.0 collective-permute-start.2
  7.6 1.5 %collective-permute-start.6 = (bf16[3,128,128]{2,1,0:T(8,128)(2,1)S(1)}, bf16[3,128,128]{2,1,0:T(8,128)(2,1)S(1)}, u32[]{:S(2)}, u32[]{:S(2)}) collective-permute-start(bf16[3,128,128]{2,1,0:T(8,128)(2,1)S(1)} %get-tuple-element.19.refs_3_), channel_id=1, source_target_pairs={{0,16},{8,24},{16,0},{24,8},{1,17},{9,25},{17,1},{25,9},{2,18},{10... | collective-permute-start | bytes 294920 | tf_op jit(solution)/shard_map/ppermute | solution.py:197
  9.1 1.6 %collective-permute-done.3.refs_4_ = bf16[3,128,128]{2,1,0:T(8,128)(2,1)S(1)} collective-permute-done((bf16[3,128,128]{2,1,0:T(8,128)(2,1)S(1)}, bf16[3,128,128]{2,1,0:T(8,128)(2,1)S(1)}, u32[]{:S(2)}, u32[]{:S(2)}) %collective-permute-start.3) | collective-permute-done | bytes 98336 | tf_op jit(solution)/shard_map/ppermute | solution.py:203
  10.7 2.4 %collective-permute-start.7 = (bf16[3,128,128]{2,1,0:T(8,128)(2,1)S(1)}, bf16[3,128,128]{2,1,0:T(8,128)(2,1)S(1)}, u32[]{:S(2)}, u32[]{:S(2)}) collective-permute-start(bf16[3,128,128]{2,1,0:T(8,128)(2,1)S(1)} %get-tuple-element.21), channel_id=1, source_target_pairs={{0,17},{1,16},{2,19},{3,18},{4,21},{5,20},{6,23},{7,22},{8,25},{9,... | collective-permute-start | bytes 294920 | tf_op jit(solution)/shard_map/ppermute | solution.py:203
  13.2 0.0 copy-done.1
  13.2 0.0 copy-done.2
  13.2 1.9 %shard_map.46.codes_ref = s32[48]{0:T(128)S(1)} custom-call(s32[6,4,8]{2,1,0:T(4,128)S(1)} %bitcast.10, s32[4,3,2,8]{3,2,1,0:T(2,128)S(1)} %bitcast.11), custom_call_target="tpu_custom_call" | custom-call | tf_op jit(solution)/shard_map/pallas_call | solution.py:46
  15.1 0.0 collective-permute-done.refs_2_
  15.1 0.1 collective-permute-start.1
  15.2 0.1 collective-permute-start.5
  15.3 0.0 collective-permute-done.6.refs_7_
  15.3 0.5 %collective-permute-start.8 = (bf16[3,128,128]{2,1,0:T(8,128)(2,1)S(1)}, bf16[3,128,128]{2,1,0:T(8,128)(2,1)S(1)}, u32[]{:S(2)}, u32[]{:S(2)}) collective-permute-start(bf16[3,128,128]{2,1,0:T(8,128)(2,1)S(1)} %collective-permute-done.6.refs_7_), channel_id=1, source_target_pairs={{0,8},{8,0},{16,24},{24,16},{1,9},{9,1},{17,25},{25,17},{2,10},{10... | collective-permute-start | bytes 294920 | tf_op jit(solution)/shard_map/ppermute | solution.py:197
  15.8 0.0 collective-permute-done.2.refs_1_
  15.8 0.5 %collective-permute-done.7.refs_8_ = bf16[3,128,128]{2,1,0:T(8,128)(2,1)S(1)} collective-permute-done((bf16[3,128,128]{2,1,0:T(8,128)(2,1)S(1)}, bf16[3,128,128]{2,1,0:T(8,128)(2,1)S(1)}, u32[]{:S(2)}, u32[]{:S(2)}) %collective-permute-start.7) | collective-permute-done | bytes 98336 | tf_op jit(solution)/shard_map/ppermute | solution.py:203
  16.3 0.0 collective-permute-start.9
  16.3 0.5 %collective-permute-start.4 = (bf16[3,128,128]{2,1,0:T(8,128)(2,1)S(1)}, bf16[3,128,128]{2,1,0:T(8,128)(2,1)S(1)}, u32[]{:S(2)}, u32[]{:S(2)}) collective-permute-start(bf16[3,128,128]{2,1,0:T(8,128)(2,1)S(1)} %get-tuple-element.19.refs_3_), channel_id=1, source_target_pairs={{0,8},{8,0},{16,24},{24,16},{1,9},{9,1},{17,25},{25,17},{2,10},{10... | collective-permute-start | bytes 294920 | tf_op jit(solution)/shard_map/ppermute | solution.py:197
  16.8 0.0 collective-permute-done.5.refs_6_
  16.8 0.0 collective-permute-done.8.refs_9_
  16.8 0.8 %collective-permute-done.9.refs_10_ = bf16[3,128,128]{2,1,0:T(8,128)(2,1)S(1)} collective-permute-done((bf16[3,128,128]{2,1,0:T(8,128)(2,1)S(1)}, bf16[3,128,128]{2,1,0:T(8,128)(2,1)S(1)}, u32[]{:S(2)}, u32[]{:S(2)}) %collective-permute-start.9) | collective-permute-done | bytes 98336 | tf_op jit(solution)/shard_map/ppermute | solution.py:197
  17.6 0.2 collective-permute-done.4.refs_5_
  17.7 1.4 %shard_map.47 = (f32[256,128]{1,0:T(8,128)S(1)}, f32[256,128]{1,0:T(8,128)S(1)}, bf16[2,768,256]{2,1,0:T(8,128)(2,1)S(1)}) custom-call(s32[48]{0:T(128)S(1)} %shard_map.46.codes_ref, bf16[6,128,128]{2,1,0:T(8,128)(2,1)S(1)} %bitcast.9, bf16[6,128,128]{2,1,0:T(8,128)(2,1)S(1)} %collective-permute-done.2.refs_1_, ...), custom_call_target="tpu_custom_call" | custom-call | flops 201326592 | bytes 786432 | tf_op jit(solution)/shard_map/pallas_call | solution.py:113
  19.1 1.8 %collective-permute-done.1.left_ref = bf16[6,128,128]{2,1,0:T(8,128)(2,1)S(1)} collective-permute-done((bf16[6,128,128]{2,1,0:T(8,128)(2,1)S(1)}, bf16[6,128,128]{2,1,0:T(8,128)(2,1)S(1)}, u32[]{:S(2)}, u32[]{:S(2)}) %collective-permute-start.1) | collective-permute-done | bytes 196640 | tf_op jit(solution)/shard_map/ppermute | solution.py:197
  20.9 0.3 shard_map.49
  21.1 0.8 %collective-permute-start.10 = (s16[272,128]{1,0:T(8,128)(2,1)S(1)}, s16[272,128]{1,0:T(8,128)(2,1)S(1)}, u32[]{:S(2)}, u32[]{:S(2)}) collective-permute-start(s16[272,128]{1,0:T(8,128)(2,1)S(1)} %shard_map.49), channel_id=1, source_target_pairs={{0,1},{1,0},{2,3},{3,2},{4,5},{5,4},{6,7},{7,6},{8,9},{9,8},{10,11... | collective-permute-start | bytes 208904 | tf_op jit(solution)/shard_map/ppermute | solution.py:197
  22.0 0.2 shard_map.48.total_ref
  22.2 3.3 %collective-permute-done.10.coded_ref = s16[272,128]{1,0:T(8,128)(2,1)S(1)} collective-permute-done((s16[272,128]{1,0:T(8,128)(2,1)S(1)}, s16[272,128]{1,0:T(8,128)(2,1)S(1)}, u32[]{:S(2)}, u32[]{:S(2)}) %collective-permute-start.10) | collective-permute-done | bytes 69664 | tf_op jit(solution)/shard_map/ppermute | solution.py:197
  25.5 0.7 %shard_map.50 = bf16[256,128]{1,0:T(8,128)(2,1)} custom-call(f32[256,128]{1,0:T(8,128)S(1)} %shard_map.48.total_ref, s16[272,128]{1,0:T(8,128)(2,1)S(1)} %collective-permute-done.10.coded_ref), custom_call_target="tpu_custom_call" | custom-call | tf_op jit(solution)/shard_map/pallas_call | solution.py:186
Async XLA Ops:
  0.0 15.1 %collective-permute-start = (bf16[6,128,128]{2,1,0:T(8,128)(2,1)}, bf16[6,128,128]{2,1,0:T(8,128)(2,1)S(1)}, u32[]{:S(2)}, u32[]{:S(2)}) collective-permute-start(bf16[6,128,128]{2,1,0:T(8,128)(2,1)} %bitcast.7), channel_id=1, source_target_pairs={{0,6},{1,7},{2,4},{3,5},{4,2},{5,3},{6,0},{7,1},{8,14},{9,15},{10,... | collective-permute-start | bytes 589832 | tf_op jit(solution)/shard_map/ppermute | solution.py:197
  5.0 2.6 %copy-start = (bf16[1,1,6,128,128]{4,3,2,1,0:T(8,128)(2,1)S(1)}, bf16[1,1,6,128,128]{4,3,2,1,0:T(8,128)(2,1)}, u32[]{:S(2)}) copy-start(bf16[1,1,6,128,128]{4,3,2,1,0:T(8,128)(2,1)} %param.4) | copy-start | bytes 589828
  5.1 8.1 %copy-start.1 = (s32[4,8,6]{1,0,2:T(4,128)S(1)}, s32[4,8,6]{1,0,2:T(4,128)}, u32[]{:S(2)}) copy-start(s32[4,8,6]{1,0,2:T(4,128)} %param.5) | copy-start | bytes 2308
  5.1 8.1 %copy-start.2 = (s32[4,8,2,3]{1,2,3,0:T(2,128)S(1)}, s32[4,8,2,3]{1,2,3,0:T(2,128)}, u32[]{:S(2)}) copy-start(s32[4,8,2,3]{1,2,3,0:T(2,128)} %param.7) | copy-start | bytes 2308
  6.1 4.7 %collective-permute-start.3 = (bf16[3,128,128]{2,1,0:T(8,128)(2,1)S(1)}, bf16[3,128,128]{2,1,0:T(8,128)(2,1)S(1)}, u32[]{:S(2)}, u32[]{:S(2)}) collective-permute-start(bf16[3,128,128]{2,1,0:T(8,128)(2,1)S(1)} %get-tuple-element.21), channel_id=1, source_target_pairs={{0,1},{1,0},{2,3},{3,2},{4,5},{5,4},{6,7},{7,6},{8,9},{9,8},{10,11... | collective-permute-start | bytes 294920 | tf_op jit(solution)/shard_map/ppermute | solution.py:203
  7.6 8.1 %collective-permute-start.2 = (bf16[6,128,128]{2,1,0:T(8,128)(2,1)S(1)}, bf16[6,128,128]{2,1,0:T(8,128)(2,1)S(1)}, u32[]{:S(2)}, u32[]{:S(2)}) collective-permute-start(bf16[6,128,128]{2,1,0:T(8,128)(2,1)S(1)} %bitcast.8), channel_id=1, source_target_pairs={{0,2},{1,3},{2,0},{3,1},{4,6},{5,7},{6,4},{7,5},{8,10},{9,11},{10,... | collective-permute-start | bytes 589832 | tf_op jit(solution)/shard_map/ppermute | solution.py:197
  7.6 7.6 %collective-permute-start.6 = (bf16[3,128,128]{2,1,0:T(8,128)(2,1)S(1)}, bf16[3,128,128]{2,1,0:T(8,128)(2,1)S(1)}, u32[]{:S(2)}, u32[]{:S(2)}) collective-permute-start(bf16[3,128,128]{2,1,0:T(8,128)(2,1)S(1)} %get-tuple-element.19.refs_3_), channel_id=1, source_target_pairs={{0,16},{8,24},{16,0},{24,8},{1,17},{9,25},{17,1},{25,9},{2,18},{10... | collective-permute-start | bytes 294920 | tf_op jit(solution)/shard_map/ppermute | solution.py:197
  10.7 5.5 %collective-permute-start.7 = (bf16[3,128,128]{2,1,0:T(8,128)(2,1)S(1)}, bf16[3,128,128]{2,1,0:T(8,128)(2,1)S(1)}, u32[]{:S(2)}, u32[]{:S(2)}) collective-permute-start(bf16[3,128,128]{2,1,0:T(8,128)(2,1)S(1)} %get-tuple-element.21), channel_id=1, source_target_pairs={{0,17},{1,16},{2,19},{3,18},{4,21},{5,20},{6,23},{7,22},{8,25},{9,... | collective-permute-start | bytes 294920 | tf_op jit(solution)/shard_map/ppermute | solution.py:203
  15.1 5.7 %collective-permute-start.1 = (bf16[6,128,128]{2,1,0:T(8,128)(2,1)S(1)}, bf16[6,128,128]{2,1,0:T(8,128)(2,1)S(1)}, u32[]{:S(2)}, u32[]{:S(2)}) collective-permute-start(bf16[6,128,128]{2,1,0:T(8,128)(2,1)S(1)} %collective-permute-done.refs_2_), channel_id=1, source_target_pairs={{0,2},{1,3},{2,0},{3,1},{4,6},{5,7},{6,4},{7,5},{8,10},{9,11},{10,... | collective-permute-start | bytes 589832 | tf_op jit(solution)/shard_map/ppermute | solution.py:197
  15.2 1.6 %collective-permute-start.5 = (bf16[3,128,128]{2,1,0:T(8,128)(2,1)S(1)}, bf16[3,128,128]{2,1,0:T(8,128)(2,1)S(1)}, u32[]{:S(2)}, u32[]{:S(2)}) collective-permute-start(bf16[3,128,128]{2,1,0:T(8,128)(2,1)S(1)} %collective-permute-done.3.refs_4_), channel_id=1, source_target_pairs={{0,8},{8,0},{16,24},{24,16},{1,9},{9,1},{17,25},{25,17},{2,10},{10... | collective-permute-start | bytes 294920 | tf_op jit(solution)/shard_map/ppermute | solution.py:197
  15.3 1.5 %collective-permute-start.8 = (bf16[3,128,128]{2,1,0:T(8,128)(2,1)S(1)}, bf16[3,128,128]{2,1,0:T(8,128)(2,1)S(1)}, u32[]{:S(2)}, u32[]{:S(2)}) collective-permute-start(bf16[3,128,128]{2,1,0:T(8,128)(2,1)S(1)} %collective-permute-done.6.refs_7_), channel_id=1, source_target_pairs={{0,8},{8,0},{16,24},{24,16},{1,9},{9,1},{17,25},{25,17},{2,10},{10... | collective-permute-start | bytes 294920 | tf_op jit(solution)/shard_map/ppermute | solution.py:197
  16.3 1.3 %collective-permute-start.9 = (bf16[3,128,128]{2,1,0:T(8,128)(2,1)S(1)}, bf16[3,128,128]{2,1,0:T(8,128)(2,1)S(1)}, u32[]{:S(2)}, u32[]{:S(2)}) collective-permute-start(bf16[3,128,128]{2,1,0:T(8,128)(2,1)S(1)} %collective-permute-done.7.refs_8_), channel_id=1, source_target_pairs={{0,8},{8,0},{16,24},{24,16},{1,9},{9,1},{17,25},{25,17},{2,10},{10... | collective-permute-start | bytes 294920 | tf_op jit(solution)/shard_map/ppermute | solution.py:197
  16.3 1.5 %collective-permute-start.4 = (bf16[3,128,128]{2,1,0:T(8,128)(2,1)S(1)}, bf16[3,128,128]{2,1,0:T(8,128)(2,1)S(1)}, u32[]{:S(2)}, u32[]{:S(2)}) collective-permute-start(bf16[3,128,128]{2,1,0:T(8,128)(2,1)S(1)} %get-tuple-element.19.refs_3_), channel_id=1, source_target_pairs={{0,8},{8,0},{16,24},{24,16},{1,9},{9,1},{17,25},{25,17},{2,10},{10... | collective-permute-start | bytes 294920 | tf_op jit(solution)/shard_map/ppermute | solution.py:197
  21.1 4.4 %collective-permute-start.10 = (s16[272,128]{1,0:T(8,128)(2,1)S(1)}, s16[272,128]{1,0:T(8,128)(2,1)S(1)}, u32[]{:S(2)}, u32[]{:S(2)}) collective-permute-start(s16[272,128]{1,0:T(8,128)(2,1)S(1)} %shard_map.49), channel_id=1, source_target_pairs={{0,1},{1,0},{2,3},{3,2},{4,5},{5,4},{6,7},{7,6},{8,9},{9,8},{10,11... | collective-permute-start | bytes 208904 | tf_op jit(solution)/shard_map/ppermute | solution.py:197

commit v26 on v22

--- a/solution.py
+++ b/solution.py
@@ -55,7 +55,7 @@
 def add_part(codes_ref, s, side, start, slots, left_ref, right_at, right_slots, total_ref):
     tile = total_ref.shape[1]
 
-    @pl.loop(0, left_ref.shape[0])
+    @pl.loop(0, left_ref.shape[0], unroll=True)
     def _(slot):
         code = codes_ref[(s * 2 + side) * slots + start + slot]
 

time: 24.1 us -> 24.1 us (level)
  Pallas kernels: 5.05 us -> 5.49 us
  waiting for transfers between devices: 4.13 us -> 3.69 us
    ppermute x9, waiting for transfers between devices: 4.03 us -> 3.59 us  [across(): return lax.ppermute(block, axis, route)]
    pallas_call x1, Pallas kernels: 2.01 us -> 2.45 us  [first_products(): pl.pallas_call(kernel, out_shape=[jax.ShapeDtypeStruct((RT * tile, tile),...]
  transfers between devices with their start and end apart: 11 -> 11, of which waited for: 7 -> 7; matrix products, arithmetic and copies ran while one was open for 4% -> 4% of each run, Pallas kernels for 17% -> 19%
where the time goes in v26:
time: 24.1 us; the launch traced here: 24 us
  starting transfers between devices  13.7 us (57%)
  Pallas kernels  5.49 us (23%)
  waiting for transfers between devices  3.69 us (15%)
  local copies, waits for them, and re-layouts  1.02 us (4%)
    ppermute x9, starting transfers between devices, across(): return lax.ppermute(block, axis, route)  11.7 us
    ppermute x9, waiting for transfers between devices, across(): return lax.ppermute(block, axis, route)  3.59 us
    pallas_call x1, Pallas kernels, first_products(): pl.pallas_call(kernel, out_shape=[jax.ShapeDtypeStruct((RT * tile, tile),...  2.45 us
    ppermute x2, starting transfers between devices, crossed(): return lax.ppermute(block, ('row', 'col'), route)  2 us
    pallas_call x1, Pallas kernels, find_matches(): pl.pallas_call(kernel, out_shape=jax.ShapeDtypeStruct((inner * 2 * slots,...  1.92 us
    squeeze x1, local copies, waits for them, and re-layouts, shards(): given = lax.dynamic_index_in_dim(right, 1 - y, 0, keepdims=False)  0.99 us
    pallas_call x1, Pallas kernels, add_coded(): pl.pallas_call(kernel, out_shape=jax.ShapeDtypeStruct(total.shape, jnp.bf...  0.65 us
  transfers between devices with their start and end apart: 11, of which 7 were waited for; matrix products, arithmetic and copies ran while one was open for 4% of the time, Pallas kernels for 19%

profile of v26, /device:TPU:0, one launch (start us, length us, event | category | flops | bytes accessed | tf_op | source)
XLA Modules:
  0.0 24.0 jit_solution(13625172291054972624)
XLA Ops:
  0.0 5.0 %collective-permute-start = (bf16[6,128,128]{2,1,0:T(8,128)(2,1)}, bf16[6,128,128]{2,1,0:T(8,128)(2,1)S(1)}, u32[]{:S(2)}, u32[]{:S(2)}) collective-permute-start(bf16[6,128,128]{2,1,0:T(8,128)(2,1)} %bitcast.7), channel_id=1, source_target_pairs={{0,6},{1,7},{2,4},{3,5},{4,2},{5,3},{6,0},{7,1},{8,14},{9,15},{10,... | collective-permute-start | bytes 589832 | tf_op jit(solution)/shard_map/ppermute | solution.py:197
  5.0 0.0 copy-start
  5.1 0.0 copy-start.1
  5.1 0.0 copy-start.2
  5.1 1.0 %dynamic-slice_bitcast_fusion = (bf16[3,128,128]{2,1,0:T(8,128)(2,1)S(1)}, bf16[3,128,128]{2,1,0:T(8,128)(2,1)S(1)}) fusion(bf16[1,1,2,3,128,128]{5,4,3,2,1,0:T(8,128)(2,1)} %param.6, s32[]{:T(128)S(6)} %select_n.8, s32[]{:T(128)S(6)} %select_n.7), kind=kLoop, calls=%fused_computation | loop fusion | bytes 393224 | tf_op jit(solution)/shard_map/jit(dynamic_index_in_dim)/squeeze | solution.py:230
  6.1 0.0 copy-done
  6.1 0.1 collective-permute-start.2
  6.1 1.6 %collective-permute-start.6 = (bf16[3,128,128]{2,1,0:T(8,128)(2,1)S(1)}, bf16[3,128,128]{2,1,0:T(8,128)(2,1)S(1)}, u32[]{:S(2)}, u32[]{:S(2)}) collective-permute-start(bf16[3,128,128]{2,1,0:T(8,128)(2,1)S(1)} %get-tuple-element.20.refs_3_), channel_id=1, source_target_pairs={{0,16},{8,24},{16,0},{24,8},{1,17},{9,25},{17,1},{25,9},{2,18},{10... | collective-permute-start | bytes 294920 | tf_op jit(solution)/shard_map/ppermute | solution.py:197
  7.7 1.5 %collective-permute-start.7 = (bf16[3,128,128]{2,1,0:T(8,128)(2,1)S(1)}, bf16[3,128,128]{2,1,0:T(8,128)(2,1)S(1)}, u32[]{:S(2)}, u32[]{:S(2)}) collective-permute-start(bf16[3,128,128]{2,1,0:T(8,128)(2,1)S(1)} %get-tuple-element.21), channel_id=1, source_target_pairs={{0,17},{1,16},{2,19},{3,18},{4,21},{5,20},{6,23},{7,22},{8,25},{9,... | collective-permute-start | bytes 294920 | tf_op jit(solution)/shard_map/ppermute | solution.py:203
  9.2 0.5 %collective-permute-start.3 = (bf16[3,128,128]{2,1,0:T(8,128)(2,1)S(1)}, bf16[3,128,128]{2,1,0:T(8,128)(2,1)S(1)}, u32[]{:S(2)}, u32[]{:S(2)}) collective-permute-start(bf16[3,128,128]{2,1,0:T(8,128)(2,1)S(1)} %get-tuple-element.21), channel_id=1, source_target_pairs={{0,1},{1,0},{2,3},{3,2},{4,5},{5,4},{6,7},{7,6},{8,9},{9,8},{10,11... | collective-permute-start | bytes 294920 | tf_op jit(solution)/shard_map/ppermute | solution.py:203
  9.7 0.0 copy-done.1
  9.7 0.0 copy-done.2
  9.7 1.9 %shard_map.46.codes_ref = s32[48]{0:T(128)S(1)} custom-call(s32[6,4,8]{2,1,0:T(4,128)S(1)} %bitcast.10, s32[4,3,2,8]{3,2,1,0:T(2,128)S(1)} %bitcast.11), custom_call_target="tpu_custom_call" | custom-call | tf_op jit(solution)/shard_map/pallas_call | solution.py:46
  11.6 0.0 collective-permute-done.refs_2_
  11.6 2.5 %collective-permute-start.1 = (bf16[6,128,128]{2,1,0:T(8,128)(2,1)S(1)}, bf16[6,128,128]{2,1,0:T(8,128)(2,1)S(1)}, u32[]{:S(2)}, u32[]{:S(2)}) collective-permute-start(bf16[6,128,128]{2,1,0:T(8,128)(2,1)S(1)} %collective-permute-done.refs_2_), channel_id=1, source_target_pairs={{0,2},{1,3},{2,0},{3,1},{4,6},{5,7},{6,4},{7,5},{8,10},{9,11},{10,... | collective-permute-start | bytes 589832 | tf_op jit(solution)/shard_map/ppermute | solution.py:197
  14.1 0.0 collective-permute-done.6.refs_7_
  14.1 0.0 collective-permute-start.8
  14.1 0.0 collective-permute-done.7.refs_8_
  14.1 0.5 %collective-permute-start.9 = (bf16[3,128,128]{2,1,0:T(8,128)(2,1)S(1)}, bf16[3,128,128]{2,1,0:T(8,128)(2,1)S(1)}, u32[]{:S(2)}, u32[]{:S(2)}) collective-permute-start(bf16[3,128,128]{2,1,0:T(8,128)(2,1)S(1)} %collective-permute-done.7.refs_8_), channel_id=1, source_target_pairs={{0,8},{8,0},{16,24},{24,16},{1,9},{9,1},{17,25},{25,17},{2,10},{10... | collective-permute-start | bytes 294920 | tf_op jit(solution)/shard_map/ppermute | solution.py:197
  14.6 0.1 collective-permute-done.3.refs_4_
  14.7 0.0 collective-permute-start.5
  14.7 0.0 collective-permute-done.2.refs_1_
  14.7 0.5 %collective-permute-start.4 = (bf16[3,128,128]{2,1,0:T(8,128)(2,1)S(1)}, bf16[3,128,128]{2,1,0:T(8,128)(2,1)S(1)}, u32[]{:S(2)}, u32[]{:S(2)}) collective-permute-start(bf16[3,128,128]{2,1,0:T(8,128)(2,1)S(1)} %get-tuple-element.20.refs_3_), channel_id=1, source_target_pairs={{0,8},{8,0},{16,24},{24,16},{1,9},{9,1},{17,25},{25,17},{2,10},{10... | collective-permute-start | bytes 294920 | tf_op jit(solution)/shard_map/ppermute | solution.py:197
  15.2 0.2 collective-permute-done.8.refs_9_
  15.4 0.2 collective-permute-done.9.refs_10_
  15.6 0.5 %collective-permute-done.5.refs_6_ = bf16[3,128,128]{2,1,0:T(8,128)(2,1)S(1)} collective-permute-done((bf16[3,128,128]{2,1,0:T(8,128)(2,1)S(1)}, bf16[3,128,128]{2,1,0:T(8,128)(2,1)S(1)}, u32[]{:S(2)}, u32[]{:S(2)}) %collective-permute-start.5) | collective-permute-done | bytes 98336 | tf_op jit(solution)/shard_map/ppermute | solution.py:197
  16.0 0.2 collective-permute-done.4.refs_5_
  16.2 2.4 %shard_map.47 = (f32[256,128]{1,0:T(8,128)S(1)}, f32[256,128]{1,0:T(8,128)S(1)}, bf16[2,768,256]{2,1,0:T(8,128)(2,1)S(1)}) custom-call(s32[48]{0:T(128)S(1)} %shard_map.46.codes_ref, bf16[6,128,128]{2,1,0:T(8,128)(2,1)S(1)} %bitcast.9, bf16[6,128,128]{2,1,0:T(8,128)(2,1)S(1)} %collective-permute-done.2.refs_1_, ...), custom_call_target="tpu_custom_call" | custom-call | flops 201326592 | bytes 786432 | tf_op jit(solution)/shard_map/pallas_call | solution.py:113
  18.6 0.1 collective-permute-done.1.left_ref
  18.7 0.3 %shard_map.49 = s16[272,128]{1,0:T(8,128)(2,1)S(1)} custom-call(bf16[6,128,128]{2,1,0:T(8,128)(2,1)S(1)} %collective-permute-done.1.left_ref, bf16[2,768,256]{2,1,0:T(8,128)(2,1)S(1)} %get-tuple-element.22.right_ref, f32[256,128]{1,0:T(8,128)S(1)} %get-tuple-element.24.total_ref), custom_call_target="tpu_custom_call" | custom-call | flops 25165824 | bytes 196608 | tf_op jit(solution)/shard_map/pallas_call | solution.py:146
  19.0 1.6 %collective-permute-start.10 = (s16[272,128]{1,0:T(8,128)(2,1)S(1)}, s16[272,128]{1,0:T(8,128)(2,1)S(1)}, u32[]{:S(2)}, u32[]{:S(2)}) collective-permute-start(s16[272,128]{1,0:T(8,128)(2,1)S(1)} %shard_map.49), channel_id=1, source_target_pairs={{0,1},{1,0},{2,3},{3,2},{4,5},{5,4},{6,7},{7,6},{8,9},{9,8},{10,11... | collective-permute-start | bytes 208904 | tf_op jit(solution)/shard_map/ppermute | solution.py:197
  20.5 0.2 shard_map.48.total_ref
  20.8 2.6 %collective-permute-done.10.coded_ref = s16[272,128]{1,0:T(8,128)(2,1)S(1)} collective-permute-done((s16[272,128]{1,0:T(8,128)(2,1)S(1)}, s16[272,128]{1,0:T(8,128)(2,1)S(1)}, u32[]{:S(2)}, u32[]{:S(2)}) %collective-permute-start.10) | collective-permute-done | bytes 69664 | tf_op jit(solution)/shard_map/ppermute | solution.py:197
  23.3 0.7 %shard_map.50 = bf16[256,128]{1,0:T(8,128)(2,1)} custom-call(f32[256,128]{1,0:T(8,128)S(1)} %shard_map.48.total_ref, s16[272,128]{1,0:T(8,128)(2,1)S(1)} %collective-permute-done.10.coded_ref), custom_call_target="tpu_custom_call" | custom-call | tf_op jit(solution)/shard_map/pallas_call | solution.py:186
Async XLA Ops:
  0.0 11.6 %collective-permute-start = (bf16[6,128,128]{2,1,0:T(8,128)(2,1)}, bf16[6,128,128]{2,1,0:T(8,128)(2,1)S(1)}, u32[]{:S(2)}, u32[]{:S(2)}) collective-permute-start(bf16[6,128,128]{2,1,0:T(8,128)(2,1)} %bitcast.7), channel_id=1, source_target_pairs={{0,6},{1,7},{2,4},{3,5},{4,2},{5,3},{6,0},{7,1},{8,14},{9,15},{10,... | collective-permute-start | bytes 589832 | tf_op jit(solution)/shard_map/ppermute | solution.py:197
  5.0 1.0 %copy-start = (bf16[1,1,6,128,128]{4,3,2,1,0:T(8,128)(2,1)S(1)}, bf16[1,1,6,128,128]{4,3,2,1,0:T(8,128)(2,1)}, u32[]{:S(2)}) copy-start(bf16[1,1,6,128,128]{4,3,2,1,0:T(8,128)(2,1)} %param.4) | copy-start | bytes 589828
  5.1 4.6 %copy-start.1 = (s32[4,8,6]{1,0,2:T(4,128)S(1)}, s32[4,8,6]{1,0,2:T(4,128)}, u32[]{:S(2)}) copy-start(s32[4,8,6]{1,0,2:T(4,128)} %param.5) | copy-start | bytes 2308
  5.1 4.6 %copy-start.2 = (s32[4,8,2,3]{1,2,3,0:T(2,128)S(1)}, s32[4,8,2,3]{1,2,3,0:T(2,128)}, u32[]{:S(2)}) copy-start(s32[4,8,2,3]{1,2,3,0:T(2,128)} %param.7) | copy-start | bytes 2308
  6.1 8.6 %collective-permute-start.2 = (bf16[6,128,128]{2,1,0:T(8,128)(2,1)S(1)}, bf16[6,128,128]{2,1,0:T(8,128)(2,1)S(1)}, u32[]{:S(2)}, u32[]{:S(2)}) collective-permute-start(bf16[6,128,128]{2,1,0:T(8,128)(2,1)S(1)} %bitcast.8), channel_id=1, source_target_pairs={{0,2},{1,3},{2,0},{3,1},{4,6},{5,7},{6,4},{7,5},{8,10},{9,11},{10,... | collective-permute-start | bytes 589832 | tf_op jit(solution)/shard_map/ppermute | solution.py:197
  6.1 8.0 %collective-permute-start.6 = (bf16[3,128,128]{2,1,0:T(8,128)(2,1)S(1)}, bf16[3,128,128]{2,1,0:T(8,128)(2,1)S(1)}, u32[]{:S(2)}, u32[]{:S(2)}) collective-permute-start(bf16[3,128,128]{2,1,0:T(8,128)(2,1)S(1)} %get-tuple-element.20.refs_3_), channel_id=1, source_target_pairs={{0,16},{8,24},{16,0},{24,8},{1,17},{9,25},{17,1},{25,9},{2,18},{10... | collective-permute-start | bytes 294920 | tf_op jit(solution)/shard_map/ppermute | solution.py:197
  7.7 6.4 %collective-permute-start.7 = (bf16[3,128,128]{2,1,0:T(8,128)(2,1)S(1)}, bf16[3,128,128]{2,1,0:T(8,128)(2,1)S(1)}, u32[]{:S(2)}, u32[]{:S(2)}) collective-permute-start(bf16[3,128,128]{2,1,0:T(8,128)(2,1)S(1)} %get-tuple-element.21), channel_id=1, source_target_pairs={{0,17},{1,16},{2,19},{3,18},{4,21},{5,20},{6,23},{7,22},{8,25},{9,... | collective-permute-start | bytes 294920 | tf_op jit(solution)/shard_map/ppermute | solution.py:203
  9.2 5.5 %collective-permute-start.3 = (bf16[3,128,128]{2,1,0:T(8,128)(2,1)S(1)}, bf16[3,128,128]{2,1,0:T(8,128)(2,1)S(1)}, u32[]{:S(2)}, u32[]{:S(2)}) collective-permute-start(bf16[3,128,128]{2,1,0:T(8,128)(2,1)S(1)} %get-tuple-element.21), channel_id=1, source_target_pairs={{0,1},{1,0},{2,3},{3,2},{4,5},{5,4},{6,7},{7,6},{8,9},{9,8},{10,11... | collective-permute-start | bytes 294920 | tf_op jit(solution)/shard_map/ppermute | solution.py:203
  11.6 7.1 %collective-permute-start.1 = (bf16[6,128,128]{2,1,0:T(8,128)(2,1)S(1)}, bf16[6,128,128]{2,1,0:T(8,128)(2,1)S(1)}, u32[]{:S(2)}, u32[]{:S(2)}) collective-permute-start(bf16[6,128,128]{2,1,0:T(8,128)(2,1)S(1)} %collective-permute-done.refs_2_), channel_id=1, source_target_pairs={{0,2},{1,3},{2,0},{3,1},{4,6},{5,7},{6,4},{7,5},{8,10},{9,11},{10,... | collective-permute-start | bytes 589832 | tf_op jit(solution)/shard_map/ppermute | solution.py:197
  14.1 1.3 %collective-permute-start.8 = (bf16[3,128,128]{2,1,0:T(8,128)(2,1)S(1)}, bf16[3,128,128]{2,1,0:T(8,128)(2,1)S(1)}, u32[]{:S(2)}, u32[]{:S(2)}) collective-permute-start(bf16[3,128,128]{2,1,0:T(8,128)(2,1)S(1)} %collective-permute-done.6.refs_7_), channel_id=1, source_target_pairs={{0,8},{8,0},{16,24},{24,16},{1,9},{9,1},{17,25},{25,17},{2,10},{10... | collective-permute-start | bytes 294920 | tf_op jit(solution)/shard_map/ppermute | solution.py:197
  14.1 1.5 %collective-permute-start.9 = (bf16[3,128,128]{2,1,0:T(8,128)(2,1)S(1)}, bf16[3,128,128]{2,1,0:T(8,128)(2,1)S(1)}, u32[]{:S(2)}, u32[]{:S(2)}) collective-permute-start(bf16[3,128,128]{2,1,0:T(8,128)(2,1)S(1)} %collective-permute-done.7.refs_8_), channel_id=1, source_target_pairs={{0,8},{8,0},{16,24},{24,16},{1,9},{9,1},{17,25},{25,17},{2,10},{10... | collective-permute-start | bytes 294920 | tf_op jit(solution)/shard_map/ppermute | solution.py:197
  14.7 1.3 %collective-permute-start.5 = (bf16[3,128,128]{2,1,0:T(8,128)(2,1)S(1)}, bf16[3,128,128]{2,1,0:T(8,128)(2,1)S(1)}, u32[]{:S(2)}, u32[]{:S(2)}) collective-permute-start(bf16[3,128,128]{2,1,0:T(8,128)(2,1)S(1)} %collective-permute-done.3.refs_4_), channel_id=1, source_target_pairs={{0,8},{8,0},{16,24},{24,16},{1,9},{9,1},{17,25},{25,17},{2,10},{10... | collective-permute-start | bytes 294920 | tf_op jit(solution)/shard_map/ppermute | solution.py:197
  14.7 1.5 %collective-permute-start.4 = (bf16[3,128,128]{2,1,0:T(8,128)(2,1)S(1)}, bf16[3,128,128]{2,1,0:T(8,128)(2,1)S(1)}, u32[]{:S(2)}, u32[]{:S(2)}) collective-permute-start(bf16[3,128,128]{2,1,0:T(8,128)(2,1)S(1)} %get-tuple-element.20.refs_3_), channel_id=1, source_target_pairs={{0,8},{8,0},{16,24},{24,16},{1,9},{9,1},{17,25},{25,17},{2,10},{10... | collective-permute-start | bytes 294920 | tf_op jit(solution)/shard_map/ppermute | solution.py:197
  19.0 4.4 %collective-permute-start.10 = (s16[272,128]{1,0:T(8,128)(2,1)S(1)}, s16[272,128]{1,0:T(8,128)(2,1)S(1)}, u32[]{:S(2)}, u32[]{:S(2)}) collective-permute-start(s16[272,128]{1,0:T(8,128)(2,1)S(1)} %shard_map.49), channel_id=1, source_target_pairs={{0,1},{1,0},{2,3},{3,2},{4,5},{5,4},{6,7},{7,6},{8,9},{9,8},{10,11... | collective-permute-start | bytes 208904 | tf_op jit(solution)/shard_map/ppermute | solution.py:197
